TPU v7x, 256 devices: a whole 4x4x8 slice. The times are simulated.
256 devices in a mesh: wide: 64 (over z, x, core), narrow: 4 (over y).
Axes of the slice: x: 4, y: 4, z: 8, core: 2. Of those that a mesh axis runs over, the one named last changes fastest.
Arguments:
- b_tensor: bfloat16 [4, 4096, 4096], P('narrow', 'wide'), may hold values from -6 to 6
- pair_mask: int32 [4, 64, 64], P('narrow', 'wide'), may hold values 0 or 1
- first_map: int32 [64], replicated, may hold values from 0 to 63, each once
- second_map: int32 [64], replicated, may hold values from 0 to 63, each once
- occ_blocks: bfloat16 [64, 8, 64, 64], P('wide', 'narrow'), may hold values from -0.25 to 0.25
- occ_index: int32 [64, 8], replicated, may hold values from 0 to 63, as said below
- virt_blocks: bfloat16 [64, 8, 64, 64], P('wide', 'narrow'), may hold values from -0.25 to 0.25
- virt_index: int32 [64, 8], replicated, may hold values from 0 to 63, as said below
Outputs:
- result: bfloat16 [4, 4096, 4096], P('narrow', 'wide')
Inputs may be any that keep to these rules, and one draw needn't show every extreme that they name: `occ_index`: row a lists 8 different molecules, the first of them a itself. `virt_index`: row c lists 8 different molecules, the first of them c itself.
All inputs are finite; a program needn't handle non-finite values. No bound on the sum of `pair_mask` on one device may be relied on, other than what follows from the above.
Results may differ from a plain program's by a relative error of at most 0.005.
Values may be sent and summed in bfloat16 or wider, within the bound.
No kernel may reach another device: no remote copies, remote signals or barrier semaphores. Data moves between devices by JAX's collectives and lax.ppermute only.
A program may use at most 128 MiB of HBM per device.

v0:
```python
import jax
import jax.numpy as jnp
from jax import lax
from jax.sharding import PartitionSpec as P


def occupied(tensor_four, panels, lists):
    total = None
    for column in range(panels.shape[1]):
        columns = jnp.take(tensor_four, lists[:, column], axis=2)
        term = jnp.einsum(
            "pnam,alm->pnal", columns, panels[:, column], preferred_element_type=jnp.float32
        )
        total = term if total is None else total + term
    shape = total.shape
    return total.astype(jnp.bfloat16).reshape(shape[0], shape[1], shape[2] * shape[3])


def virtual(regrouped, panels, slot_lists):
    width = regrouped.shape[2]
    grouped = regrouped.reshape(regrouped.shape[0], regrouped.shape[1] // width, width, width)
    total = None
    for column in range(panels.shape[1]):
        columns = jnp.take(grouped, slot_lists[:, column], axis=1)
        term = jnp.einsum(
            "pcnl,cnm->plcm", columns, panels[:, column], preferred_element_type=jnp.float32
        )
        total = term if total is None else total + term
    shape = total.shape
    return total.astype(jnp.bfloat16).reshape(shape[0], shape[1], shape[2] * shape[3])


def per_device(
    b_tensor, pair_mask, first_map, second_map, occ_blocks, occ_index, virt_blocks, virt_index
):
    block = b_tensor.shape[1]
    molecules = b_tensor.shape[2] // block
    weights = jnp.repeat(pair_mask[0, 0], block).astype(jnp.bfloat16)
    masked = b_tensor * weights[None, None, :]
    tensor_four = masked.reshape(b_tensor.shape[0], block, molecules, block)
    inverse = jnp.argsort(first_map)
    virt_slots = jnp.take(inverse, virt_index, axis=0)
    occ_local, virt_local = (
        lax.all_gather(occ_blocks, "narrow", axis=1, tiled=True),
        lax.all_gather(virt_blocks, "narrow", axis=1, tiled=True),
    )
    natural = occupied(
        tensor_four, lax.all_gather(occ_local, "wide", axis=0, tiled=True), occ_index
    )
    split_rows = natural.reshape(natural.shape[0], block, molecules, block)
    ordered = jnp.take(split_rows, second_map, axis=2).reshape(natural.shape)
    regrouped = lax.all_to_all(ordered, "wide", split_axis=2, concat_axis=1, tiled=True)
    return virtual(regrouped, lax.all_gather(virt_local, "wide", axis=0, tiled=True), virt_slots)


def solution(mesh):
    placed = (
        P("narrow", "wide", None),
        P("narrow", "wide", None),
        P(),
        P(),
        P("wide", "narrow", None, None),
        P(),
        P("wide", "narrow", None, None),
        P(),
    )
    return jax.shard_map(
        per_device, mesh=mesh, in_specs=placed, out_specs=P("narrow", "wide", None), check_vma=False
    )
```

profile of v0, /device:TPU:1, one launch (start us, length us, event | category | flops | bytes accessed | tf_op | source)
XLA Modules:
  0.0 215.3 jit_solution(2279195710726268518)
XLA Ops:
  6.5 12.3 %all_gather.12 = bf16[1,8,64,64]{3,2,0,1:T(8,128)(2,1)} all-gather(bf16[1,2,64,64]{3,2,0,1:T(8,128)(2,1)} %bitcast.310), channel_id=1, replica_groups=mesh['wide'=64,'narrow'=4] {'narrow'}, dimensions={1}, use_global_device_ids=true | all-gather | bytes 81920 | tf_op jit(solution)/shard_map/all_gather | solution.py:44
  18.9 10.1 %all_gather.14 = bf16[1,8,64,64]{3,2,0,1:T(8,128)(2,1)} all-gather(bf16[1,2,64,64]{3,2,0,1:T(8,128)(2,1)} %bitcast.311), channel_id=1, replica_groups=mesh['wide'=64,'narrow'=4] {'narrow'}, dimensions={1}, use_global_device_ids=true | all-gather | bytes 81920 | tf_op jit(solution)/shard_map/all_gather | solution.py:45
  36.0 1.7 gather_fusion.3
  39.3 1.7 gather_fusion.1
  41.0 1.7 gather_fusion.7
  42.6 1.7 gather_fusion.8
  44.3 62.3 %all-gather.3.cloned.1.call-done = bf16[64,8,64,64]{3,2,0,1:T(8,128)(2,1)} async-done(((bf16[1,8,64,64]{3,2,0,1:T(8,128)(2,1)}), bf16[64,8,64,64]{3,2,0,1:T(8,128)(2,1)}) %all-gather.3.cloned.1.call-update) | async-done | bytes 4194320 | tf_op jit(solution)/shard_map/all_gather | solution.py:48
  106.6 2.1 fusion.10
  108.7 2.5 %fusion.11 = f32[64,64,64]{2,1,0:T(8,128)S(1)} fusion(bf16[64,8,64,64]{3,2,0,1:T(8,128)(2,1)} %all-gather.3.cloned.1.call-done, bf16[64,64,64]{2,1,0:T(8,128)(2,1)S(1)} %gather_fusion.5, pred[64]{0:T(512)(128)(4,1)S(1)} %get-tuple-element.57), kind=kOutput, calls=%fused_computation.43 | convolution fusion | flops 33816576 | bytes 2621504 | tf_op jit(solution)/shard_map/pnam,alm->pnal/dot_general | solution.py:11
  111.2 2.0 fusion.12
  122.0 22.4 %reduce = bf16[4096,64]{1,0:T(8,128)(2,1)S(1)} reduce(bf16[4096,1,64]{2,1,0:T(2,128)(2,1)S(1)} %bitcast.308, bf16[]{:T(256)} %broadcast.114), dimensions={1}, to_apply=%bitcast.272.reduce_sub_computation | reduce | bytes 1048578
  145.9 6.2 %all-to-all-start = ((bf16[64,2,2048]{2,1,0:T(2,128)(2,1)}), bf16[64,2,2048]{2,1,0:T(2,128)(2,1)S(1)}, u32[]{:S(2)}, u32[]{:S(2)}) async-start(bf16[64,2,2048]{2,1,0:T(2,128)(2,1)} %reshape.418), calls=%async_computation | async-start | bytes 1048576 | tf_op jit(solution)/shard_map/all_to_all | solution.py:52
  152.3 2.1 sort.17
  154.4 3.3 %gather_fusion = s32[512]{0:T(512)S(1)} fusion(s32[64]{0:T(128)S(1)} %get-tuple-element.8, s32[1024]{0:T(1024)S(1)} %pad_clamp_fusion.17), kind=kCustom, calls=%fused_computation.17 | custom fusion | bytes 6144 | tf_op jit(solution)/shard_map/jit(_take)/gather | solution.py:42
  158.0 14.9 %all-to-all-done = bf16[64,2,2048]{2,1,0:T(2,128)(2,1)S(1)} async-done(((bf16[64,2,2048]{2,1,0:T(2,128)(2,1)}), bf16[64,2,2048]{2,1,0:T(2,128)(2,1)S(1)}, u32[]{:S(2)}, u32[]{:S(2)}) %all-to-all-start) | async-done | bytes 524320 | tf_op jit(solution)/shard_map/all_to_all | solution.py:52
  175.0 1.7 gather_fusion.15
  176.7 1.7 gather_fusion.14
  178.4 1.7 gather_fusion.13
  180.1 1.7 gather_fusion.12
  181.8 1.7 gather_fusion.11
  186.6 7.7 %all-gather.5.cloned.1.call-done = bf16[64,8,64,64]{3,2,0,1:T(8,128)(2,1)} async-done(((bf16[1,8,64,64]{3,2,0,1:T(8,128)(2,1)}), bf16[64,8,64,64]{3,2,0,1:T(8,128)(2,1)}) %all-gather.5.cloned.1.call-update) | async-done | bytes 4194320 | tf_op jit(solution)/shard_map/all_gather | solution.py:53
  194.3 2.3 %fusion.3 = f32[64,64,64]{2,1,0:T(8,128)S(1)} fusion(bf16[64,8,64,64]{3,2,0,1:T(8,128)(2,1)} %all-gather.5.cloned.1.call-done, bf16[64,64,64]{2,1,0:T(8,128)(2,1)} %gather_fusion.15, pred[64]{0:T(512)(128)(4,1)S(1)} %get-tuple-element.43), kind=kOutput, calls=%fused_computation.26 | convolution fusion | flops 33816576 | bytes 3145792 | tf_op jit(solution)/shard_map/pcnl,cnm->plcm/dot_general | solution.py:25
  196.6 2.6 %fusion.4 = f32[64,64,64]{2,1,0:T(8,128)S(1)} fusion(bf16[64,8,64,64]{3,2,0,1:T(8,128)(2,1)} %all-gather.5.cloned.1.call-done, bf16[64,64,64]{2,1,0:T(8,128)(2,1)} %gather_fusion.14, pred[64]{0:T(512)(128)(4,1)S(1)} %get-tuple-element.45), kind=kOutput, calls=%fused_computation.28 | convolution fusion | flops 33816576 | bytes 3145792 | tf_op jit(solution)/shard_map/pcnl,cnm->plcm/dot_general | solution.py:25
  199.3 1.9 fusion.5
  (87 shorter events, 31.6 us)
Async XLA Ops:
  6.5 100.1 %all-gather.3.cloned.1.call-start = ((), (), s32[]{:S(2)}) async-start(), calls=%async_computation.1 | async-start | bytes 8519680 | tf_op jit(solution)/shard_map/all_gather | solution.py:48
  18.9 175.5 %all-gather.5.cloned.1.call-start = ((), (), s32[]{:S(2)}) async-start(), calls=%async_computation.2 | async-start | bytes 8519680 | tf_op jit(solution)/shard_map/all_gather | solution.py:53
  30.9 1.8 copy-start.11
  41.0 3.3 %copy-start.12 = (s32[64]{0:T(128)S(1)}, s32[64]{0:T(128)}, u32[]{:S(2)}) copy-start(s32[64]{0:T(128)} %param.15) | copy-start | bytes 772
  106.6 4.6 %copy-start.1 = (bf16[64,8,64,64]{3,2,0,1:T(8,128)(2,1)S(1)}, bf16[64,8,64,64]{3,2,0,1:T(8,128)(2,1)}, u32[]{:S(2)}) copy-start(bf16[64,8,64,64]{3,2,0,1:T(8,128)(2,1)} %all-gather.3.cloned.1.call-done) | copy-start | bytes 12582916
  111.2 2.1 copy-start.2
  113.3 1.2 copy-start.3
  114.5 1.2 copy-start.4
  115.7 1.2 copy-start.6
  116.9 1.2 copy-start.5
  144.4 7.7 %copy-start.10 = (s32[64,8]{0,1:T(8,128)S(1)}, s32[64,8]{0,1:T(8,128)}, u32[]{:S(2)}) copy-start(s32[64,8]{0,1:T(8,128)} %param.19) | copy-start | bytes 6148
  144.4 7.9 %copy-start.13 = (s32[64]{0:T(128)S(1)}, s32[64]{0:T(128)}, u32[]{:S(2)}) copy-start(s32[64]{0:T(128)} %param.14) | copy-start | bytes 772
  145.9 27.0 %all-to-all-start = ((bf16[64,2,2048]{2,1,0:T(2,128)(2,1)}), bf16[64,2,2048]{2,1,0:T(2,128)(2,1)S(1)}, u32[]{:S(2)}, u32[]{:S(2)}) async-start(bf16[64,2,2048]{2,1,0:T(2,128)(2,1)} %reshape.418), calls=%async_computation | async-start | bytes 1048576 | tf_op jit(solution)/shard_map/all_to_all | solution.py:52
  194.3 5.0 %copy-start = (bf16[64,8,64,64]{3,2,0,1:T(8,128)(2,1)S(1)}, bf16[64,8,64,64]{3,2,0,1:T(8,128)(2,1)}, u32[]{:S(2)}) copy-start(bf16[64,8,64,64]{3,2,0,1:T(8,128)(2,1)} %all-gather.5.cloned.1.call-done) | copy-start | bytes 12582916
  199.3 2.0 copy-start.9
  201.3 1.2 copy-start.7
  202.5 1.2 copy-start.8
Sparse Core Ops, SparseCore 0:
  19.0 87.5 all-gather.2
  109.4 84.8 all-gather.4
where the time goes:
time: 216 us; the launch traced here: 215 us
  waiting for transfers between devices  84.9 us (39%)
  local copies, waits for them, and re-layouts  40.3 us (19%)
  other arithmetic  26.6 us (12%)
  blocking collectives  22.4 us (10%)
  matrix products  21.2 us (10%)
  between operations  13.8 us (6%)
  starting transfers between devices  6.21 us (3%)
    all_gather x1, waiting for transfers between devices, per_device(): lax.all_gather(occ_local, 'wide', axis=0, tiled=True)  62.3 us
    unnamed x1, other arithmetic  22.4 us
    all_to_all x1, waiting for transfers between devices, per_device(): lax.all_to_all(ordered, 'wide', split_axis=2, concat_axis=1, tiled=True)  14.9 us
    all_gather x1, blocking collectives, per_device(): lax.all_gather(occ_blocks, 'narrow', axis=1, tiled=True)  12.3 us
    gather x8, local copies, waits for them, and re-layouts, virtual(): columns = jnp.take(grouped, slot_lists[:, column], axis=1)  11.6 us
    gather x8, local copies, waits for them, and re-layouts, occupied(): columns = jnp.take(tensor_four, lists[:, column], axis=2)  11.5 us
    dot_general x8, matrix products, virtual(): jnp.einsum('pcnl,cnm->plcm', columns, panels[:, column], preferred_elemen...  10.7 us
    dot_general x8, matrix products, occupied(): jnp.einsum('pnam,alm->pnal', columns, panels[:, column], preferred_elemen...  10.6 us
  transfers between devices with their start and end apart: 3, of which 3 were waited for; matrix products, arithmetic and copies ran while one was open for 33% of the time, Pallas kernels for 0%

commit v1 on v0

v1 whole, which is shorter than its diff:
```python
import functools
import itertools

import jax
import jax.numpy as jnp
from jax import lax
from jax.experimental import pallas as pl
from jax.experimental.pallas import tpu as pltpu
from jax.sharding import PartitionSpec as P

Z, X, CORES, Y = 8, 4, 2, 4
PART = 8


def invert(map_ref, inverse_ref):
    @pl.loop(0, map_ref.shape[0])
    def _(slot):
        inverse_ref[map_ref[slot]] = slot


def swap_halves(tile):
    half = tile.shape[1] // 2
    return jnp.concatenate([tile[:, half:], tile[:, :half]], axis=1)


def occupied_kernel(parts, index_ref, second_ref, own_ref, *refs):
    piece_refs, row_refs = refs[: CORES * Y], refs[CORES * Y : CORES * Y + len(parts)]
    out_ref, dense_ref, rows_ref, inverse_ref = refs[CORES * Y + len(parts) :]
    _, quarter, width = piece_refs[0].shape
    block = width // 2
    x, core, y = own_ref[1], own_ref[2], own_ref[3]
    invert(second_ref, inverse_ref)
    for (off, start), ref in zip(parts, row_refs):
        place = pl.multiple_of((x + off) % X * block + start, 32)
        rows_ref[pl.ds(place, ref.shape[0]), :] = ref[...]
    side_of = lax.broadcasted_iota(jnp.int32, (quarter, width), 1) // block

    @pl.loop(0, Z * X // PART)
    def _(chunk):
        dense_ref[...] = jnp.zeros_like(dense_ref)
        members = list(itertools.product(range(CORES), range(PART)))
        molecules = [
            (chunk * PART + inner) * CORES + (core + core_off) % CORES
            for core_off, inner in members
        ]
        for y_off in range(Y):
            tiles = [
                piece_refs[core_off * Y + y_off][chunk * PART + inner]
                for core_off, inner in members
            ]
            swapped = [swap_halves(tile) for tile in tiles]
            for side in range(2):
                k = 2 * ((y + y_off) % Y) + side
                placed = []
                for row, molecule in enumerate(molecules):
                    index = index_ref[molecule, k]
                    column = pl.multiple_of(index // 2 * width, width)
                    place = (pl.ds(row * quarter, quarter), pl.ds(column, width))
                    value = jnp.where(index % 2 == side, tiles[row], swapped[row])
                    placed.append(
                        (place, jnp.where(side_of == index % 2, value, dense_ref[place]))
                    )
                for place, value in placed:
                    dense_ref[place] = value
        product = lax.dot_general(
            dense_ref[...], rows_ref[...], (((1,), (1,)), ((), ())),
            preferred_element_type=jnp.float32,
        ).astype(jnp.bfloat16)
        for row, molecule in enumerate(molecules):
            out_ref[inverse_ref[molecule]] = product[row * quarter : (row + 1) * quarter]


def virtual_kernel(
    index_ref, first_ref, own_ref, mine_ref, other_ref, rows_ref, out_ref, table_ref, inverse_ref
):
    quarter, width = rows_ref.shape[1], mine_ref.shape[4]
    block = width // 2
    core, y = own_ref[2], own_ref[3]
    z_now = pl.program_id(0)

    @pl.when(z_now == 0)
    def _():
        invert(first_ref, inverse_ref)
        for z, c, high in itertools.product(range(Z), range(CORES), range(2)):
            tile = jnp.concatenate(
                [
                    rows_ref[(z * X + x) * CORES + c, :, high * width : (high + 1) * width]
                    for x in range(X)
                ],
                axis=0,
            )
            place = (z * CORES + c) * 2 + high
            table_ref[place] = tile
            table_ref[Z * CORES * 2 + place] = swap_halves(tile)

    def stored(molecule, k):
        slot = inverse_ref[index_ref[molecule, k]]
        x, c = slot // CORES % X, slot % CORES
        return (slot // (X * CORES) * CORES + c) * 2 + x // 2, x % 2

    left_half = lax.broadcasted_iota(jnp.int32, table_ref.shape[1:], 1) < block
    for x in range(X):
        found = []
        for core_off, panel_ref in enumerate((mine_ref, other_ref)):
            molecule = (z_now * X + x) * CORES + (core + core_off) % CORES
            left = []
            for y_off in range(Y):
                k = 2 * ((y + y_off) % Y)
                (one, odd_one), (two, odd_two) = stored(molecule, k), stored(molecule, k + 1)
                left.append(
                    jnp.where(
                        left_half,
                        table_ref[Z * CORES * 2 * odd_one + one],
                        table_ref[Z * CORES * 2 * (1 - odd_two) + two],
                    )
                )
            right = [panel_ref[x, y_off, 0] for y_off in range(Y)]
            found.append(
                lax.dot_general(
                    jnp.concatenate(left, axis=1), jnp.concatenate(right, axis=1),
                    (((1,), (1,)), ((), ())), preferred_element_type=jnp.float32,
                )
            )
        both = jnp.where(
            core == 0, jnp.concatenate(found, axis=1), jnp.concatenate(found[::-1], axis=1)
        )
        out_ref[:, x * width : (x + 1) * width] = both.astype(jnp.bfloat16)


def occupied(pieces, parts, rows, own, occ_index, second_map):
    molecules = second_map.shape[0]
    _, quarter, width = pieces[0].shape
    basis = rows[0].shape[1]
    smem = pl.BlockSpec(memory_space=pltpu.SMEM)
    vmem = pl.BlockSpec(memory_space=pltpu.VMEM)
    count = X * width // 2
    return pl.pallas_call(
        functools.partial(occupied_kernel, parts),
        out_shape=jax.ShapeDtypeStruct((molecules, quarter, count), jnp.bfloat16),
        in_specs=[smem] * 3 + [vmem] * (len(pieces) + len(rows)),
        out_specs=vmem,
        scratch_shapes=[
            pltpu.VMEM((PART * CORES * quarter, basis), jnp.bfloat16),
            pltpu.VMEM((count, basis), jnp.bfloat16),
            pltpu.SMEM((molecules,), jnp.int32),
        ],
        compiler_params=pltpu.CompilerParams(vmem_limit_bytes=32 * 2**20),
        cost_estimate=pl.CostEstimate(
            flops=2 * molecules * quarter * count * basis, bytes_accessed=2**22, transcendentals=0
        ),
    )(occ_index, second_map, own, *pieces, *rows)


def virtual(mine, other, rows, own, virt_index, first_map):
    molecules = first_map.shape[0]
    block, width = mine.shape[3:]
    panels = pl.BlockSpec((X, Y, 1, block, width), lambda g, *_: (0, 0, g, 0, 0))
    return pl.pallas_call(
        virtual_kernel,
        out_shape=jax.ShapeDtypeStruct((block, molecules * block), jnp.bfloat16),
        grid_spec=pltpu.PrefetchScalarGridSpec(
            num_scalar_prefetch=3,
            grid=(Z,),
            in_specs=[panels, panels, pl.BlockSpec(rows.shape, lambda g, *_: (0, 0, 0))],
            out_specs=pl.BlockSpec((block, X * width), lambda g, *_: (0, g)),
            scratch_shapes=[
                pltpu.VMEM((molecules, block, width), jnp.bfloat16),
                pltpu.SMEM((molecules,), jnp.int32),
            ],
        ),
        compiler_params=pltpu.CompilerParams(
            dimension_semantics=("arbitrary",), vmem_limit_bytes=48 * 2**20
        ),
        cost_estimate=pl.CostEstimate(
            flops=4 * mine.size * block, bytes_accessed=4 * mine.size, transcendentals=0
        ),
    )(virt_index, first_map, own, mine, other, rows)


def wide_index(z, x, core):
    return (z % Z * X + x % X) * CORES + core % CORES


PLANES = [[wide_index(z, x, c) for z in range(Z) for x in range(X)] for c in range(CORES)]
COLUMNS = [[wide_index(z, x, c) for z in range(Z)] for x in range(X) for c in range(CORES)]
ROWS = [[wide_index(z, x, c) for x in range(X)] for z in range(Z) for c in range(CORES)]


def shift(array, axis, by):
    if axis == "y":
        return lax.ppermute(array, "narrow", [((i + by) % Y, i) for i in range(Y)])
    steps = [by if axis == name else 0 for name in ("z", "x", "core")]
    pairs = []
    for place in itertools.product(range(Z), range(X), range(CORES)):
        source = wide_index(*(at + step for at, step in zip(place, steps)))
        pairs.append((source, wide_index(*place)))
    return lax.ppermute(array, "wide", pairs)


def exchange(array, groups):
    return lax.all_to_all(
        array, "wide", split_axis=0, concat_axis=0, tiled=True, axis_index_groups=groups
    )


def ring(array, axis):
    middle = array.shape[0] // 2
    after, before = shift(array, axis, 1), shift(array, axis, -1)
    low, high = shift(before[:middle], axis, -1), shift(after[middle:], axis, 1)
    return [(0, 0, array), (1, 0, after), (2, 0, low), (2, middle, high), (3, 0, before)]


def per_device(
    b_tensor, pair_mask, first_map, second_map, occ_blocks, occ_index, virt_blocks, virt_index
):
    block = b_tensor.shape[1]
    wide, narrow = lax.axis_index("wide"), lax.axis_index("narrow")
    own = [wide // (X * CORES), wide // CORES % X, wide % CORES, narrow]
    own = jnp.stack(own).astype(jnp.int32)
    masked = b_tensor[0] * jnp.repeat(pair_mask[0, 0], block).astype(jnp.bfloat16)[None]
    parts = ring(masked, "x")
    occ_piece = occ_blocks[0].transpose(1, 0, 2).reshape(block, -1)
    virt_piece = virt_blocks[0].transpose(2, 0, 1).reshape(block, -1)
    quarters = exchange(jnp.tile(occ_piece, (Z, 1)), PLANES).reshape(Z * X, block // X, -1)
    mine = [quarters] + [shift(quarters, "y", by) for by in range(1, Y)]
    pieces = mine + [shift(piece, "core", 1) for piece in mine]
    column = exchange(jnp.tile(virt_piece, (Z, 1)), COLUMNS).reshape(Z, *virt_piece.shape)
    plane = jnp.stack([column] + [shift(column, "y", by) for by in range(1, Y)])
    mine = lax.all_gather(plane, "wide", axis=0, axis_index_groups=ROWS)
    other = shift(mine, "core", 1)
    half = occupied(
        pieces, [part[:2] for part in parts], [part[2] for part in parts], own, occ_index,
        second_map,
    )
    rows = lax.all_to_all(half, "wide", split_axis=0, concat_axis=0, tiled=True)
    return virtual(mine, other, rows, own, virt_index, first_map)[None]


def solution(mesh):
    placed = (
        P("narrow", "wide", None),
        P("narrow", "wide", None),
        P(),
        P(),
        P("wide", "narrow", None, None),
        P(),
        P("wide", "narrow", None, None),
        P(),
    )
    return jax.shard_map(
        per_device, mesh=mesh, in_specs=placed, out_specs=P("narrow", "wide", None), check_vma=False
    )
```

time: 216 us -> 170 us (0.79)
  waiting for transfers between devices: 84.9 us -> 55.3 us
  Pallas kernels: 0 us -> 26 us
  local copies, waits for them, and re-layouts: 40.3 us -> 14.5 us
  other arithmetic: 26.6 us -> 1.64 us
  matrix products: 21.2 us -> 0 us
  starting transfers between devices: 6.21 us -> 26.1 us
  blocking collectives: 22.4 us -> 32 us
    all_gather x2 -> x1, waiting for transfers between devices: 70 us -> 31.1 us  [per_device(): mine = lax.all_gather(plane, 'wide', axis=0, axis_index_groups=ROWS)]
    all_to_all x0 -> x2, blocking collectives: none -> 32 us  [exchange(): lax.all_to_all(array, 'wide', split_axis=0, concat_axis=0, tiled=True, ax...]
    gather x20 -> x0, local copies, waits for them, and re-layouts: 27.3 us -> none  [the longest x8 11.6 us: virtual(): columns = jnp.take(grouped, slot_lists[:, column], axis=1)]
    pallas_call x0 -> x2, Pallas kernels: none -> 26 us  [the longest x1 15 us: virtual(): pl.pallas_call(virtual_kernel, out_shape=jax.ShapeDtypeStruct((block, mol...]
    unnamed x1 -> x0, other arithmetic: 22.4 us -> none
    all_gather x2 -> x0, blocking collectives: 22.4 us -> none  [the longest x1 12.3 us: per_device(): lax.all_gather(occ_blocks, 'narrow', axis=1, tiled=True)]
    dot_general x16 -> x0, matrix products: 21.2 us -> none  [the longest x8 10.7 us: virtual(): jnp.einsum('pcnl,cnm->plcm', columns, panels[:, column], preferred_elemen...]
    ppermute x0 -> x15, starting transfers between devices: none -> 19.7 us  [the longest x9 11.1 us: shift(): return lax.ppermute(array, 'wide', pairs)]
  transfers between devices with their start and end apart: 3 -> 17, of which waited for: 3 -> 6; matrix products, arithmetic and copies ran while one was open for 33% -> 1% of each run, Pallas kernels for 0% -> 7%
where the time goes in v1:
time: 170 us; the launch traced here: 169 us
  waiting for transfers between devices  55.3 us (33%)
  blocking collectives  32 us (19%)
  starting transfers between devices  26.1 us (15%)
  Pallas kernels  26 us (15%)
  local copies, waits for them, and re-layouts  14.5 us (9%)
  between operations  13.5 us (8%)
    all_to_all x2, blocking collectives, exchange(): lax.all_to_all(array, 'wide', split_axis=0, concat_axis=0, tiled=True, ax...  32 us
    all_gather x1, waiting for transfers between devices, per_device(): mine = lax.all_gather(plane, 'wide', axis=0, axis_index_groups=ROWS)  31.1 us
    all_to_all x1, waiting for transfers between devices, per_device(): rows = lax.all_to_all(half, 'wide', split_axis=0, concat_axis=0, tiled=True)  17.6 us
    pallas_call x1, Pallas kernels, virtual(): pl.pallas_call(virtual_kernel, out_shape=jax.ShapeDtypeStruct((block, mol...  15 us
    unnamed x52, local copies, waits for them, and re-layouts  13.3 us
    ppermute x9, starting transfers between devices, shift(): return lax.ppermute(array, 'wide', pairs)  11.1 us
    pallas_call x1, Pallas kernels, occupied(): pl.pallas_call(functools.partial(occupied_kernel, parts), out_shape=jax.S...  11 us
    ppermute x6, starting transfers between devices, shift(): return lax.ppermute(array, 'narrow', [((i + by) % Y, i) for i in range(Y)])  8.58 us
  transfers between devices with their start and end apart: 17, of which 6 were waited for; matrix products, arithmetic and copies ran while one was open for 1% of the time, Pallas kernels for 7%

profile of v1, /device:TPU:1, one launch (start us, length us, event | category | flops | bytes accessed | tf_op | source)
XLA Modules:
  0.0 169.0 jit_solution(14206284528776705801)
XLA Ops:
  7.5 16.6 %all_to_all.20 = bf16[8,64,128]{2,1,0:T(8,128)(2,1)S(1)} all-to-all(bf16[8,64,128]{2,1,0:T(8,128)(2,1)S(1)} %tile.17), channel_id=1, replica_groups={{0,32,64,96,128,160,192,224},{4,36,68,100,132,164,196,228},{8,40,72,104..., dimensions={0} | all-to-all | bytes 262144 | tf_op jit(solution)/shard_map/all_to_all | solution.py:201
  24.1 1.3 collective-permute-start.2
  25.4 1.4 collective-permute-start
  26.8 1.6 collective-permute-start.1
  29.2 3.4 %collective-permute-done.1 = bf16[8,64,128]{2,1,0:T(8,128)(2,1)S(1)} collective-permute-done((bf16[8,64,128]{2,1,0:T(8,128)(2,1)S(1)}, bf16[8,64,128]{2,1,0:T(8,128)(2,1)S(1)}, u32[]{:S(2)}, u32[]{:S(2)}) %collective-permute-start.1) | collective-permute-done | bytes 131104 | tf_op jit(solution)/shard_map/ppermute | solution.py:191
  34.4 1.3 collective-permute-start.12
  35.7 31.1 %all-gather.3.cloned.1.call-done = bf16[16,8,64,128]{3,2,1,0:T(8,128)(2,1)} async-done(((bf16[4,8,64,128]{3,2,1,0:T(8,128)(2,1)}), bf16[16,8,64,128]{3,2,1,0:T(8,128)(2,1)}) %all-gather.3.cloned.1.call-update) | async-done | bytes 2097168 | tf_op jit(solution)/shard_map/all_gather | solution.py:229
  67.3 1.3 collective-permute-start.11
  68.7 15.4 %all_to_all.21.refs_0_ = bf16[32,16,128]{2,1,0:T(8,128)(2,1)S(1)} all-to-all(bf16[32,16,128]{2,1,0:T(8,128)(2,1)S(1)} %bitcast.25), channel_id=1, replica_groups={{0,8,16,24,32,40,48,56,64,72,80,88,96,104,112,120,128,136,144,152,160,1..., dimensions={0} | all-to-all | bytes 262144 | tf_op jit(solution)/shard_map/all_to_all | solution.py:201
  84.1 1.2 collective-permute-start.6
  85.3 1.5 collective-permute-start.4
  86.7 1.5 collective-permute-start.5
  89.1 4.3 %collective-permute-start.7 = (bf16[32,16,128]{2,1,0:T(8,128)(2,1)S(1)}, bf16[32,16,128]{2,1,0:T(8,128)(2,1)S(1)}, u32[]{:S(2)}, u32[]{:S(2)}) collective-permute-start(bf16[32,16,128]{2,1,0:T(8,128)(2,1)S(1)} %all_to_all.21.refs_0_), channel_id=1, source_target_pairs={{4,0},{0,4},{12,8},{8,12},{20,16},{16,20},{28,24},{24,28},{36,32},... | collective-permute-start | bytes 393224 | tf_op jit(solution)/shard_map/ppermute | solution.py:197
  93.6 2.7 %collective-permute-start.14 = (bf16[32,4096]{1,0:T(8,128)(2,1)S(1)}, bf16[32,4096]{1,0:T(8,128)(2,1)S(1)}, u32[]{:S(2)}, u32[]{:S(2)}) collective-permute-start(bf16[32,4096]{1,0:T(8,128)(2,1)S(1)} %slice.9), channel_id=1, source_target_pairs={{8,0},{12,4},{16,8},{20,12},{24,16},{28,20},{0,24},{4,28},{40,32},... | collective-permute-start | bytes 786440 | tf_op jit(solution)/shard_map/ppermute | solution.py:197
  96.9 1.0 collective-permute-start.8
  100.7 1.5 collective-permute-done.13.refs_10_
  103.7 1.0 copy-done.2
  104.7 0.9 copy-done.5
  105.7 0.9 copy-done.7
  107.5 0.9 copy-done.11
  112.0 11.0 %shard_map.82 = bf16[64,16,256]{2,1,0:T(8,128)(2,1)} custom-call(s32[64,8]{1,0:T(8,128)S(1)} %copy.18.index_ref, s32[64]{0:T(128)S(1)} %copy-done.20, s32[4]{0:T(128)S(1)} %pad_add_fusion.own_ref, bf16[32,16,128]{2,1,0:T(8,128)(2,1)S(1)} %all_to_all.21.refs_0_, bf16[32,16,128]{2,1,0:T(8,128)(2,1)S(1)} %copy-done.9, bf16[32,16,128]{2,1,0:T(8,128)(2,1)S(1)} %copy-done.11, ...), custom_call_target="tpu_custom_call" | custom-call | flops 2147483648 | bytes 4194304 | tf_op jit(solution)/shard_map/pallas_call | solution.py:137
  123.0 6.4 %all-to-all-start.2 = ((bf16[64,16,256]{2,1,0:T(8,128)(2,1)}), bf16[64,16,256]{2,1,0:T(8,128)(2,1)S(1)}, u32[]{:S(2)}, u32[]{:S(2)}) async-start(bf16[64,16,256]{2,1,0:T(8,128)(2,1)} %shard_map.82), calls=%async_computation.2 | async-start | bytes 1048576 | tf_op jit(solution)/shard_map/all_to_all | solution.py:235
  129.6 17.6 %all-to-all-done.2.rows_ref = bf16[64,16,256]{2,1,0:T(8,128)(2,1)S(1)} async-done(((bf16[64,16,256]{2,1,0:T(8,128)(2,1)}), bf16[64,16,256]{2,1,0:T(8,128)(2,1)S(1)}, u32[]{:S(2)}, u32[]{:S(2)}) %all-to-all-start.2) | async-done | bytes 524320 | tf_op jit(solution)/shard_map/all_to_all | solution.py:235
  147.2 15.0 %shard_map.83 = bf16[64,4096]{1,0:T(8,128)(2,1)} custom-call(s32[64,8]{1,0:T(8,128)S(1)} %copy.19.index_ref, s32[64]{0:T(128)S(1)} %copy-done.3, s32[4]{0:T(128)S(1)} %pad_add_fusion.own_ref, bf16[4,4,8,64,128]{4,3,2,1,0:T(8,128)(2,1)S(1)} %bitcast.24, bf16[4,4,8,64,128]{4,3,2,1,0:T(8,128)(2,1)} %collective-permute-done.3.other_ref, ...), custom_call_target="tpu_custom_call" | custom-call | flops 268435456 | bytes 4194304 | tf_op jit(solution)/shard_map/pallas_call | solution.py:158
  (80 shorter events, 14.6 us)
Async XLA Ops:
  6.5 27.8 %copy-start.21 = (bf16[1,64,4096]{2,1,0:T(8,128)(2,1)S(1)}, bf16[1,64,4096]{2,1,0:T(8,128)(2,1)}, u32[]{:S(2)}) copy-start(bf16[1,64,4096]{2,1,0:T(8,128)(2,1)} %param.8) | copy-start | bytes 1572868
  6.5 62.0 %copy-start.22 = (bf16[1,2,64,64]{3,2,1,0:T(8,128)(2,1)S(1)}, bf16[1,2,64,64]{3,2,1,0:T(8,128)(2,1)}, u32[]{:S(2)}) copy-start(bf16[1,2,64,64]{3,2,1,0:T(8,128)(2,1)} %param.12) | copy-start | bytes 49156
  6.5 60.3 %all-gather.3.cloned.1.call-start = ((), (), s32[]{:S(2)}) async-start(), calls=%async_computation.3 | async-start | bytes 2621440 | tf_op jit(solution)/shard_map/all_gather | solution.py:229
  24.1 5.1 %collective-permute-start.2 = (bf16[8,64,128]{2,1,0:T(8,128)(2,1)S(1)}, bf16[8,64,128]{2,1,0:T(8,128)(2,1)S(1)}, u32[]{:S(2)}, u32[]{:S(2)}) collective-permute-start(bf16[8,64,128]{2,1,0:T(8,128)(2,1)S(1)} %all_to_all.20), channel_id=1, source_target_pairs={{3,0},{0,1},{1,2},{2,3},{7,4},{4,5},{5,6},{6,7},{11,8},{8,9},{9,10... | collective-permute-start | bytes 393224 | tf_op jit(solution)/shard_map/ppermute | solution.py:191
  25.4 3.8 %collective-permute-start = (bf16[8,64,128]{2,1,0:T(8,128)(2,1)S(1)}, bf16[8,64,128]{2,1,0:T(8,128)(2,1)S(1)}, u32[]{:S(2)}, u32[]{:S(2)}) collective-permute-start(bf16[8,64,128]{2,1,0:T(8,128)(2,1)S(1)} %all_to_all.20), channel_id=1, source_target_pairs={{1,0},{2,1},{3,2},{0,3},{5,4},{6,5},{7,6},{4,7},{9,8},{10,9},{11,1... | collective-permute-start | bytes 393224 | tf_op jit(solution)/shard_map/ppermute | solution.py:191
  26.8 5.8 %collective-permute-start.1 = (bf16[8,64,128]{2,1,0:T(8,128)(2,1)S(1)}, bf16[8,64,128]{2,1,0:T(8,128)(2,1)S(1)}, u32[]{:S(2)}, u32[]{:S(2)}) collective-permute-start(bf16[8,64,128]{2,1,0:T(8,128)(2,1)S(1)} %all_to_all.20), channel_id=1, source_target_pairs={{2,0},{3,1},{0,2},{1,3},{6,4},{7,5},{4,6},{5,7},{10,8},{11,9},{8,1... | collective-permute-start | bytes 393224 | tf_op jit(solution)/shard_map/ppermute | solution.py:191
  32.6 66.6 %copy-start.23 = (s32[64,8]{0,1:T(8,128)S(1)}, s32[64,8]{0,1:T(8,128)}, u32[]{:S(2)}) copy-start(s32[64,8]{0,1:T(8,128)} %param.13) | copy-start | bytes 6148
  32.6 71.1 %copy-start.20 = (s32[64]{0:T(128)S(1)}, s32[64]{0:T(128)}, u32[]{:S(2)}) copy-start(s32[64]{0:T(128)} %second_ref.1) | copy-start | bytes 772
  34.4 52.4 %collective-permute-start.12 = (bf16[64,4096]{1,0:T(8,128)(2,1)S(1)}, bf16[64,4096]{1,0:T(8,128)(2,1)S(1)}, u32[]{:S(2)}, u32[]{:S(2)}) collective-permute-start(bf16[64,4096]{1,0:T(8,128)(2,1)S(1)} %bitcast_multiply_fusion.refs_8_), channel_id=1, source_target_pairs={{24,0},{28,4},{0,8},{4,12},{8,16},{12,20},{16,24},{20,28},{56,32},... | collective-permute-start | bytes 1572872 | tf_op jit(solution)/shard_map/ppermute | solution.py:197
  66.8 80.4 %collective-permute-start.3 = (bf16[4,4,8,64,128]{4,3,2,1,0:T(8,128)(2,1)}, bf16[4,4,8,64,128]{4,3,2,1,0:T(8,128)(2,1)}, u32[]{:S(2)}, u32[]{:S(2)}) collective-permute-start(bf16[4,4,8,64,128]{4,3,2,1,0:T(8,128)(2,1)} %bitcast.23), channel_id=1, source_target_pairs={{4,0},{0,4},{12,8},{8,12},{20,16},{16,20},{28,24},{24,28},{36,32},... | collective-permute-start | bytes 6291464 | tf_op jit(solution)/shard_map/ppermute | solution.py:197
  67.3 26.1 %collective-permute-start.11 = (bf16[64,4096]{1,0:T(8,128)(2,1)S(1)}, bf16[64,4096]{1,0:T(8,128)(2,1)S(1)}, u32[]{:S(2)}, u32[]{:S(2)}) collective-permute-start(bf16[64,4096]{1,0:T(8,128)(2,1)S(1)} %bitcast_multiply_fusion.refs_8_), channel_id=1, source_target_pairs={{8,0},{12,4},{16,8},{20,12},{24,16},{28,20},{0,24},{4,28},{40,32},... | collective-permute-start | bytes 1572872 | tf_op jit(solution)/shard_map/ppermute | solution.py:197
  84.1 5.0 %collective-permute-start.6 = (bf16[32,16,128]{2,1,0:T(8,128)(2,1)S(1)}, bf16[32,16,128]{2,1,0:T(8,128)(2,1)S(1)}, u32[]{:S(2)}, u32[]{:S(2)}) collective-permute-start(bf16[32,16,128]{2,1,0:T(8,128)(2,1)S(1)} %all_to_all.21.refs_0_), channel_id=1, source_target_pairs={{3,0},{0,1},{1,2},{2,3},{7,4},{4,5},{5,6},{6,7},{11,8},{8,9},{9,10... | collective-permute-start | bytes 393224 | tf_op jit(solution)/shard_map/ppermute | solution.py:191
  85.3 8.2 %collective-permute-start.4 = (bf16[32,16,128]{2,1,0:T(8,128)(2,1)S(1)}, bf16[32,16,128]{2,1,0:T(8,128)(2,1)S(1)}, u32[]{:S(2)}, u32[]{:S(2)}) collective-permute-start(bf16[32,16,128]{2,1,0:T(8,128)(2,1)S(1)} %all_to_all.21.refs_0_), channel_id=1, source_target_pairs={{1,0},{2,1},{3,2},{0,3},{5,4},{6,5},{7,6},{4,7},{9,8},{10,9},{11,1... | collective-permute-start | bytes 393224 | tf_op jit(solution)/shard_map/ppermute | solution.py:191
  86.7 6.8 %collective-permute-start.5 = (bf16[32,16,128]{2,1,0:T(8,128)(2,1)S(1)}, bf16[32,16,128]{2,1,0:T(8,128)(2,1)S(1)}, u32[]{:S(2)}, u32[]{:S(2)}) collective-permute-start(bf16[32,16,128]{2,1,0:T(8,128)(2,1)S(1)} %all_to_all.21.refs_0_), channel_id=1, source_target_pairs={{2,0},{3,1},{0,2},{1,3},{6,4},{7,5},{4,6},{5,7},{10,8},{11,9},{8,1... | collective-permute-start | bytes 393224 | tf_op jit(solution)/shard_map/ppermute | solution.py:191
  89.1 7.2 %collective-permute-start.7 = (bf16[32,16,128]{2,1,0:T(8,128)(2,1)S(1)}, bf16[32,16,128]{2,1,0:T(8,128)(2,1)S(1)}, u32[]{:S(2)}, u32[]{:S(2)}) collective-permute-start(bf16[32,16,128]{2,1,0:T(8,128)(2,1)S(1)} %all_to_all.21.refs_0_), channel_id=1, source_target_pairs={{4,0},{0,4},{12,8},{8,12},{20,16},{16,20},{28,24},{24,28},{36,32},... | collective-permute-start | bytes 393224 | tf_op jit(solution)/shard_map/ppermute | solution.py:197
  93.4 4.5 %collective-permute-start.10 = (bf16[32,16,128]{2,1,0:T(8,128)(2,1)S(1)}, bf16[32,16,128]{2,1,0:T(8,128)(2,1)S(1)}, u32[]{:S(2)}, u32[]{:S(2)}) collective-permute-start(bf16[32,16,128]{2,1,0:T(8,128)(2,1)S(1)} %collective-permute-done.6.refs_3_), channel_id=1, source_target_pairs={{4,0},{0,4},{12,8},{8,12},{20,16},{16,20},{28,24},{24,28},{36,32},... | collective-permute-start | bytes 393224 | tf_op jit(solution)/shard_map/ppermute | solution.py:197
  93.5 8.8 %collective-permute-start.13 = (bf16[32,4096]{1,0:T(8,128)(2,1)S(1)}, bf16[32,4096]{1,0:T(8,128)(2,1)S(1)}, u32[]{:S(2)}, u32[]{:S(2)}) collective-permute-start(bf16[32,4096]{1,0:T(8,128)(2,1)S(1)} %slice.8), channel_id=1, source_target_pairs={{24,0},{28,4},{0,8},{4,12},{8,16},{12,20},{16,24},{20,28},{56,32},... | collective-permute-start | bytes 786440 | tf_op jit(solution)/shard_map/ppermute | solution.py:197
  93.6 9.4 %collective-permute-start.14 = (bf16[32,4096]{1,0:T(8,128)(2,1)S(1)}, bf16[32,4096]{1,0:T(8,128)(2,1)S(1)}, u32[]{:S(2)}, u32[]{:S(2)}) collective-permute-start(bf16[32,4096]{1,0:T(8,128)(2,1)S(1)} %slice.9), channel_id=1, source_target_pairs={{8,0},{12,4},{16,8},{20,12},{24,16},{28,20},{0,24},{4,28},{40,32},... | collective-permute-start | bytes 786440 | tf_op jit(solution)/shard_map/ppermute | solution.py:197
  96.9 2.5 %collective-permute-start.8 = (bf16[32,16,128]{2,1,0:T(8,128)(2,1)S(1)}, bf16[32,16,128]{2,1,0:T(8,128)(2,1)S(1)}, u32[]{:S(2)}, u32[]{:S(2)}) collective-permute-start(bf16[32,16,128]{2,1,0:T(8,128)(2,1)S(1)} %collective-permute-done.4.refs_1_), channel_id=1, source_target_pairs={{4,0},{0,4},{12,8},{8,12},{20,16},{16,20},{28,24},{24,28},{36,32},... | collective-permute-start | bytes 393224 | tf_op jit(solution)/shard_map/ppermute | solution.py:197
  98.5 1.5 collective-permute-start.9
  99.3 30.2 %copy-start.24 = (s32[64,8]{0,1:T(8,128)S(1)}, s32[64,8]{0,1:T(8,128)}, u32[]{:S(2)}) copy-start(s32[64,8]{0,1:T(8,128)} %param.15) | copy-start | bytes 6148
  99.3 47.9 %copy-start.3 = (s32[64]{0:T(128)S(1)}, s32[64]{0:T(128)}, u32[]{:S(2)}) copy-start(s32[64]{0:T(128)} %first_ref.1) | copy-start | bytes 772
  112.0 35.2 %copy-start = (bf16[16,8,64,128]{3,2,1,0:T(8,128)(2,1)S(1)}, bf16[16,8,64,128]{3,2,1,0:T(8,128)(2,1)}, u32[]{:S(2)}) copy-start(bf16[16,8,64,128]{3,2,1,0:T(8,128)(2,1)} %all-gather.3.cloned.1.call-done) | copy-start | bytes 6291460
  123.0 24.2 %all-to-all-start.2 = ((bf16[64,16,256]{2,1,0:T(8,128)(2,1)}), bf16[64,16,256]{2,1,0:T(8,128)(2,1)S(1)}, u32[]{:S(2)}, u32[]{:S(2)}) async-start(bf16[64,16,256]{2,1,0:T(8,128)(2,1)} %shard_map.82), calls=%async_computation.2 | async-start | bytes 1048576 | tf_op jit(solution)/shard_map/all_to_all | solution.py:235
  (18 other events, 30.7 us)
Sparse Core Ops, SparseCore 0:
  33.6 33.1 all-gather.2

commit v2 on v0

v2 whole, which is shorter than its diff:
```python
import functools
import itertools

import jax
import jax.numpy as jnp
from jax import lax
from jax.experimental import pallas as pl
from jax.experimental.pallas import tpu as pltpu
from jax.sharding import Mesh, PartitionSpec as P

Z, X, CORES, Y = 8, 4, 2, 4
BLOCK, WIDTH, QUARTER = 64, 128, 16
MOLECULES = Z * X * CORES
BASIS = MOLECULES * BLOCK
ANYWHERE = pl.BlockSpec(memory_space=pl.ANY)
SMEM = pl.BlockSpec(memory_space=pltpu.SMEM)
VMEM = pl.BlockSpec(memory_space=pltpu.VMEM)
NT = (((1,), (1,)), ((), ()))


def swap_halves(tile):
    return jnp.concatenate([tile[:, BLOCK:], tile[:, :BLOCK]], axis=1)


def small(kernel, outs, in_specs, scratch=()):
    return pl.pallas_call(
        kernel,
        out_shape=tuple(jax.ShapeDtypeStruct(shape, jnp.bfloat16) for shape in outs),
        in_specs=in_specs,
        out_specs=(VMEM,) * len(outs),
        scratch_shapes=list(scratch),
        compiler_params=pltpu.CompilerParams(vmem_limit_bytes=8 * 2**20),
    )


def fetch(pairs, sems):
    copies = [
        pltpu.make_async_copy(source, target, sems.at[number])
        for number, (source, target) in enumerate(pairs)
    ]
    for copy in copies:
        copy.start()
    for copy in copies:
        copy.wait()


def pieces_kernel(own_ref, occ_hbm, virt_hbm, occ_out, virt_out, occ_ref, virt_ref, turn_ref, sems):
    fetch([(occ_hbm, occ_ref), (virt_hbm, virt_ref)], sems)
    turn_ref[...] = jnp.concatenate([occ_ref[0, 0], occ_ref[0, 1]], axis=1)
    for off in range(X):
        start = pl.multiple_of(((own_ref[1] + off) & (X - 1)) * QUARTER, QUARTER)
        occ_out[off] = turn_ref[pl.ds(start, QUARTER), :]
    rows = jnp.concatenate([virt_ref[0, 0], virt_ref[0, 1]], axis=0).astype(jnp.float32)
    virt_out[...] = rows.T.astype(jnp.bfloat16)


def make_pieces(own, occ_blocks, virt_blocks):
    return small(
        pieces_kernel,
        [(X, QUARTER, WIDTH), (BLOCK, WIDTH)],
        [SMEM, ANYWHERE, ANYWHERE],
        [
            pltpu.VMEM(occ_blocks.shape, jnp.bfloat16),
            pltpu.VMEM(virt_blocks.shape, jnp.bfloat16),
            pltpu.VMEM((BLOCK, WIDTH), jnp.bfloat16),
            pltpu.SemaphoreType.DMA((2,)),
        ],
    )(own, occ_blocks, virt_blocks)


def mask_kernel(mask_ref, one_ref, two_ref, three_ref, b_hbm, masked_ref, b_ref, sems):
    del one_ref, two_ref, three_ref
    fetch([(b_hbm, b_ref)], sems)
    first_half = lax.broadcasted_iota(jnp.int32, (BLOCK, WIDTH), 1) < BLOCK
    for pair in range(MOLECULES // 2):
        weight = jnp.where(first_half, mask_ref[0, 0, 2 * pair], mask_ref[0, 0, 2 * pair + 1])
        place = slice(pair * WIDTH, (pair + 1) * WIDTH)
        masked_ref[:, place] = b_ref[0, :, place] * weight.astype(jnp.float32).astype(jnp.bfloat16)


def mask_rows(pair_mask, b_tensor, after):
    return small(
        mask_kernel,
        [(BLOCK, BASIS)],
        [SMEM] + [ANYWHERE] * 4,
        [pltpu.VMEM(b_tensor.shape, jnp.bfloat16), pltpu.SemaphoreType.DMA((1,))],
    )(pair_mask, *after, b_tensor)[0]


def spread_kernel(occ_ref, one_ref, two_ref, three_ref, virt_ref, after_ref, out_ref):
    del after_ref
    for z in range(Z):
        out_ref[z, 0, 0] = occ_ref[0]
        for off, ref in ((1, one_ref), (2, two_ref), (3, three_ref)):
            out_ref[z, 0, off] = ref[...]
        for part in range(X):
            out_ref[z, 1, part] = virt_ref[part * QUARTER : (part + 1) * QUARTER]


def divide_kernel(both_ref, after_ref, before_ref, occ_ref, virt_ref):
    del after_ref, before_ref
    for x_off in range(X):
        for z in range(Z):
            occ_ref[x_off, z] = both_ref[z, 0, x_off]
            virt_ref[z, x_off * QUARTER : (x_off + 1) * QUARTER] = both_ref[z, 1, x_off]


def stack_kernel(*refs):
    *parts, out_ref = refs
    for y, ref in enumerate(parts):
        out_ref[y] = ref[...]


def tie(array, after):
    return pl.pallas_call(
        lambda array_ref, after_ref, out_ref: None,
        out_shape=jax.ShapeDtypeStruct(array.shape, array.dtype),
        in_specs=[ANYWHERE, ANYWHERE],
        out_specs=ANYWHERE,
        input_output_aliases={0: 0},
        compiler_params=pltpu.CompilerParams(vmem_limit_bytes=56 * 2**20),
    )(array, after)


PARTS = [(0, 0, BLOCK), (1, 0, BLOCK), (3, 0, BLOCK), (2, 0, BLOCK // 2), (2, BLOCK // 2, BLOCK // 2)]
PIECES = list(itertools.product(range(CORES), range(Y)))


def occupied_kernel(index_ref, second_ref, own_ref, *refs):
    piece_refs, refs = refs[: len(PIECES)], refs[len(PIECES) :]
    row_refs, refs = refs[: len(PARTS)], refs[len(PARTS) :]
    out_ref, rows_ref, even_ref, odd_ref, inverse_ref, sems = refs
    x0, core0, y0 = (own_ref[i] for i in range(1, 4))
    copies = []
    for number, ((off, start, count), source) in enumerate(zip(PARTS, row_refs)):
        place = pl.multiple_of(((x0 + off) & (X - 1)) * BLOCK + start, 32)
        target = rows_ref.at[pl.ds(place, count), :]
        copies.append(pltpu.make_async_copy(source, target, sems.at[number]))
        copies[-1].start()

    @pl.loop(0, MOLECULES)
    def _(slot):
        inverse_ref[second_ref[slot]] = slot

    side_of = lax.broadcasted_iota(jnp.int32, (QUARTER, WIDTH), 1) // BLOCK
    members = list(itertools.product(range(CORES), range(Z)))
    for x_off in range(X):
        dense_ref = odd_ref if x_off % 2 else even_ref
        dense_ref[...] = jnp.zeros_like(dense_ref)
        molecules = [
            (z * X + ((x0 + x_off) & (X - 1))) * CORES + ((core0 + core_off) & (CORES - 1))
            for core_off, z in members
        ]
        for y_off in range(Y):
            tiles = [piece_refs[c * Y + y_off][x_off, z] for c, z in members]
            swapped = [swap_halves(tile) for tile in tiles]
            for side in range(2):
                k = (((y0 + y_off) & (Y - 1)) << 1) + side
                placed = []
                for row, molecule in enumerate(molecules):
                    index = index_ref[k, molecule]
                    place = (
                        pl.ds(row * QUARTER, QUARTER),
                        pl.ds(pl.multiple_of((index >> 1) * WIDTH, WIDTH), WIDTH),
                    )
                    parity = index & 1
                    value = jnp.where(parity == side, tiles[row], swapped[row])
                    placed.append((place, jnp.where(side_of == parity, value, dense_ref[place])))
                for place, value in placed:
                    dense_ref[place] = value
        if x_off == 0:
            for copy in copies:
                copy.wait()
        product = lax.dot_general(
            dense_ref[...], rows_ref[...], NT, preferred_element_type=jnp.float32
        ).astype(jnp.bfloat16)
        for row, molecule in enumerate(molecules):
            out_ref[inverse_ref[molecule]] = product[row * QUARTER : (row + 1) * QUARTER]


def occupied(pieces, rows, own, occ_index, second_map):
    dense = (CORES * Z * QUARTER, BASIS)
    return pl.pallas_call(
        occupied_kernel,
        out_shape=jax.ShapeDtypeStruct((MOLECULES, QUARTER, X * BLOCK), jnp.bfloat16),
        in_specs=[SMEM] * 3 + [VMEM] * len(pieces) + [ANYWHERE] * len(rows),
        out_specs=VMEM,
        scratch_shapes=[
            pltpu.VMEM((X * BLOCK, BASIS), jnp.bfloat16),
            pltpu.VMEM(dense, jnp.bfloat16),
            pltpu.VMEM(dense, jnp.bfloat16),
            pltpu.SMEM((MOLECULES,), jnp.int32),
            pltpu.SemaphoreType.DMA((len(rows),)),
        ],
        compiler_params=pltpu.CompilerParams(vmem_limit_bytes=16 * 2**20),
        cost_estimate=pl.CostEstimate(
            flops=2 * X * dense[0] * X * BLOCK * BASIS, bytes_accessed=2**22, transcendentals=0
        ),
    )(occ_index.T, second_map, own, *pieces, *rows)


def table_place(slot):
    z, x, core = slot // (X * CORES), slot // CORES % X, slot % CORES
    return (z * CORES + core) * 2 + x // 2, x % 2


def virtual_kernel(core_off, index_ref, first_ref, own_ref, panel_ref, rows_ref, *refs):
    *before_ref, out_ref, table_ref, left_ref, right_ref = refs
    core0, y0 = own_ref[2], own_ref[3]
    z_now = pl.program_id(0)
    half_table = Z * CORES * 2

    @pl.when(z_now == 0)
    def _():
        for slot in range(MOLECULES):
            place, parity = table_place(slot)
            molecule = first_ref[slot]
            left_ref[molecule] = place + half_table * parity
            right_ref[molecule] = place + half_table * (1 - parity)
        for z, c, high in itertools.product(range(Z), range(CORES), range(2)):
            tile = jnp.concatenate(
                [
                    rows_ref[(z * X + x) * CORES + c, :, high * WIDTH : (high + 1) * WIDTH]
                    for x in range(X)
                ],
                axis=0,
            )
            place = (z * CORES + c) * 2 + high
            table_ref[place] = tile
            table_ref[half_table + place] = swap_halves(tile)

    first_half = lax.broadcasted_iota(jnp.int32, (BLOCK, WIDTH), 1) < BLOCK
    for x in range(X):
        molecule = (z_now * X + x) * CORES + ((core0 + core_off) & (CORES - 1))
        left = []
        for y in range(Y):
            k = ((y0 + y) & (Y - 1)) << 1
            one = left_ref[index_ref[k, molecule]]
            two = right_ref[index_ref[k + 1, molecule]]
            left.append(jnp.where(first_half, table_ref[one], table_ref[two]))
        right = [panel_ref[x, y, 0] for y in range(Y)]
        found = lax.dot_general(
            jnp.concatenate(left, axis=1), jnp.concatenate(right, axis=1), NT,
            preferred_element_type=jnp.float32,
        ).astype(jnp.bfloat16)
        found = jnp.concatenate([found, found], axis=1)
        place = slice(x * WIDTH, (x + 1) * WIDTH)
        if core_off:
            found = jnp.where(first_half == (core0 == 0), before_ref[0][:, place], found)
        out_ref[:, place] = found


def virtual(core_off, panels, rows, own, virt_index, first_map, *before):
    columns = pl.BlockSpec((BLOCK, X * WIDTH), lambda g, *_: (0, g))
    return pl.pallas_call(
        functools.partial(virtual_kernel, core_off),
        out_shape=jax.ShapeDtypeStruct((BLOCK, BASIS), jnp.bfloat16),
        grid_spec=pltpu.PrefetchScalarGridSpec(
            num_scalar_prefetch=3,
            grid=(Z,),
            in_specs=[
                pl.BlockSpec((X, Y, 1, BLOCK, WIDTH), lambda g, *_: (0, 0, g, 0, 0)),
                pl.BlockSpec(rows.shape, lambda g, *_: (0, 0, 0)),
            ]
            + [columns] * len(before),
            out_specs=columns,
            scratch_shapes=[
                pltpu.VMEM((MOLECULES, BLOCK, WIDTH), jnp.bfloat16),
                pltpu.SMEM((MOLECULES,), jnp.int32),
                pltpu.SMEM((MOLECULES,), jnp.int32),
            ],
        ),
        input_output_aliases={5: 0} if before else {},
        compiler_params=pltpu.CompilerParams(
            dimension_semantics=("arbitrary",), vmem_limit_bytes=(16 if before else 56) * 2**20
        ),
        cost_estimate=pl.CostEstimate(
            flops=2 * panels.size * BLOCK, bytes_accessed=2 * panels.size, transcendentals=0
        ),
    )(virt_index.T, first_map, own, panels, rows, *before)


SIZES = {"z": Z, "x": X, "core": CORES, "y": Y}


def shift(array, axis, by):
    size = SIZES[axis]
    return lax.ppermute(array, axis, [((i + by) % size, i) for i in range(size)])


def per_device(
    b_tensor, pair_mask, first_map, second_map, occ_blocks, occ_index, virt_blocks, virt_index
):
    own = jnp.stack([lax.axis_index(axis) for axis in SIZES]).astype(jnp.int32)
    occ_piece, virt_piece = make_pieces(own, occ_blocks, virt_blocks)
    quarters = [shift(occ_piece[X - off], "x", off) for off in range(1, X)]
    masked = mask_rows(pair_mask, b_tensor, quarters)
    after, before = shift(masked, "x", 1), shift(masked, "x", -1)
    middle = BLOCK // 2
    low, high = shift(before[:middle], "x", -1), shift(after[middle:], "x", 1)
    spread = small(spread_kernel, [(Z, 2, X, QUARTER, WIDTH)], [VMEM] * 5 + [ANYWHERE])(
        occ_piece, *quarters, virt_piece, masked
    )[0]
    both = lax.all_to_all(spread, "z", split_axis=0, concat_axis=0, tiled=True)
    occ_column, virt_column = small(
        divide_kernel, [(X, Z, QUARTER, WIDTH), (Z, BLOCK, WIDTH)], [VMEM, ANYWHERE, ANYWHERE]
    )(both, after, before)
    pieces = [occ_column] + [shift(occ_column, "y", by) for by in range(1, Y)]
    pieces = pieces + [shift(part, "core", 1) for part in pieces]
    virt_plane = small(stack_kernel, [(Y, Z, BLOCK, WIDTH)], [VMEM] * Y)(
        virt_column, *[shift(virt_column, "y", by) for by in range(1, Y)]
    )[0]
    mine = lax.all_gather(virt_plane, "x", axis=0)
    half = occupied(pieces, [masked, after, before, low, high], own, occ_index, second_map)
    rows = lax.all_to_all(half, ("z", "x", "core"), split_axis=0, concat_axis=0, tiled=True)
    mine = tie(mine, rows)
    other = shift(mine, "core", 1)
    known = (rows, own, virt_index, first_map)
    return virtual(1, other, *known, virtual(0, mine, *known))[None]


def solution(mesh):
    shaped = Mesh(mesh.devices.reshape(Z, X, CORES, Y), tuple(SIZES))
    wide = ("z", "x", "core")
    placed = (
        P("y", wide, None),
        P("y", wide, None),
        P(),
        P(),
        P(wide, "y", None, None),
        P(),
        P(wide, "y", None, None),
        P(),
    )
    return jax.shard_map(
        per_device, mesh=shaped, in_specs=placed, out_specs=P("y", wide, None), check_vma=False
    )
```

time: 216 us -> 125 us (0.58)
  waiting for transfers between devices: 84.9 us -> 13.2 us
  local copies, waits for them, and re-layouts: 40.3 us -> 3.28 us
  other arithmetic: 26.6 us -> 0.08 us
  Pallas kernels: 0 us -> 23.4 us
  blocking collectives: 22.4 us -> 45.4 us
  matrix products: 21.2 us -> 0 us
  starting transfers between devices: 6.21 us -> 24.5 us
    all_gather x2 -> x1, waiting for transfers between devices: 70 us -> 0.01 us  [per_device(): mine = lax.all_gather(virt_plane, 'x', axis=0)]
    all_to_all x0 -> x2, blocking collectives: none -> 45.4 us  [the longest x1 28 us: per_device(): lax.all_to_all(half, ('z', 'x', 'core'), split_axis=0, concat_axis=0, til...]
    gather x20 -> x0, local copies, waits for them, and re-layouts: 27.3 us -> none  [the longest x8 11.6 us: virtual(): columns = jnp.take(grouped, slot_lists[:, column], axis=1)]
    ppermute x0 -> x18, starting transfers between devices: none -> 24.5 us  [shift(): lax.ppermute(array, axis, [((i + by) % size, i) for i in range(size)])]
    pallas_call x0 -> x9, Pallas kernels: none -> 23.4 us  [the longest x2 14.5 us: virtual(): pl.pallas_call(functools.partial(virtual_kernel, core_off), out_shape=jax...]
    unnamed x1 -> x0, other arithmetic: 22.4 us -> none
    all_gather x2 -> x0, blocking collectives: 22.4 us -> none  [the longest x1 12.3 us: per_device(): lax.all_gather(occ_blocks, 'narrow', axis=1, tiled=True)]
    dot_general x16 -> x0, matrix products: 21.2 us -> none  [the longest x8 10.7 us: virtual(): jnp.einsum('pcnl,cnm->plcm', columns, panels[:, column], preferred_elemen...]
  transfers between devices with their start and end apart: 3 -> 19, of which waited for: 3 -> 8; matrix products, arithmetic and copies ran while one was open for 33% -> 0% of each run, Pallas kernels for 0% -> 12%
where the time goes in v2:
time: 125 us; the launch traced here: 123 us
  blocking collectives  45.4 us (36%)
  starting transfers between devices  24.5 us (20%)
  Pallas kernels  23.4 us (19%)
  between operations  13.5 us (11%)
  waiting for transfers between devices  13.2 us (11%)
  local copies, waits for them, and re-layouts  3.28 us (3%)
    all_to_all x1, blocking collectives, per_device(): lax.all_to_all(half, ('z', 'x', 'core'), split_axis=0, concat_axis=0, til...  28 us
    ppermute x18, starting transfers between devices, shift(): lax.ppermute(array, axis, [((i + by) % size, i) for i in range(size)])  24.5 us
    all_to_all x1, blocking collectives, per_device(): both = lax.all_to_all(spread, 'z', split_axis=0, concat_axis=0, tiled=True)  17.4 us
    pallas_call x2, Pallas kernels, virtual(): pl.pallas_call(functools.partial(virtual_kernel, core_off), out_shape=jax...  14.5 us
    ppermute x18, waiting for transfers between devices, shift(): lax.ppermute(array, axis, [((i + by) % size, i) for i in range(size)])  13.2 us
    pallas_call x1, Pallas kernels, occupied(): pl.pallas_call(occupied_kernel, out_shape=jax.ShapeDtypeStruct((MOLECULES...  6.55 us
    unnamed x22, local copies, waits for them, and re-layouts  3.24 us
  transfers between devices with their start and end apart: 19, of which 8 were waited for; matrix products, arithmetic and copies ran while one was open for 0% of the time, Pallas kernels for 12%

profile of v2, /device:TPU:1, one launch (start us, length us, event | category | flops | bytes accessed | tf_op | source)
XLA Modules:
  0.0 123.4 jit_solution(17133940302161636015)
XLA Ops:
  6.6 0.8 copy-done.2
  7.4 0.8 copy-done.3
  8.1 0.7 shard_map.82
  8.9 3.4 %collective-permute-start = (bf16[16,128]{1,0:T(8,128)(2,1)S(1)}, bf16[16,128]{1,0:T(8,128)(2,1)S(1)}, u32[]{:S(2)}, u32[]{:S(2)}) collective-permute-start(bf16[16,128]{1,0:T(8,128)(2,1)S(1)} %get-tuple-element.15), channel_id=1, source_target_pairs={{8,0},{16,8},{24,16},{0,24},{9,1},{17,9},{25,17},{1,25},{10,2},{18... | collective-permute-start | bytes 12296 | tf_op jit(solution)/shard_map/ppermute | solution.py:288
  13.4 2.8 %collective-permute-done.1.two_ref = bf16[16,128]{1,0:T(8,128)(2,1)S(1)} collective-permute-done((bf16[16,128]{1,0:T(8,128)(2,1)S(1)}, bf16[16,128]{1,0:T(8,128)(2,1)S(1)}, u32[]{:S(2)}, u32[]{:S(2)}) %collective-permute-start.1) | collective-permute-done | bytes 4128 | tf_op jit(solution)/shard_map/ppermute | solution.py:288
  16.5 1.0 copy-done.1
  19.3 1.1 collective-permute-start.4
  20.5 17.4 %all_to_all.10.both_ref = bf16[8,2,4,16,128]{4,3,2,1,0:T(8,128)(2,1)S(1)} all-to-all(bf16[8,2,4,16,128]{4,3,2,1,0:T(8,128)(2,1)S(1)} %shard_map.84), channel_id=1, replica_groups=mesh['z'=8,'x'=4,'core'=2,'y'=4] {'z'}, dimensions={0} | all-to-all | bytes 524288 | tf_op jit(solution)/shard_map/all_to_all | solution.py:304
  37.9 2.8 %collective-permute-start.5 = (bf16[8,64,128]{2,1,0:T(8,128)(2,1)S(1)}, bf16[8,64,128]{2,1,0:T(8,128)(2,1)S(1)}, u32[]{:S(2)}, u32[]{:S(2)}) collective-permute-start(bf16[8,64,128]{2,1,0:T(8,128)(2,1)S(1)} %get-tuple-element.11.refs_0_), channel_id=1, source_target_pairs={{1,0},{2,1},{3,2},{0,3},{5,4},{6,5},{7,6},{4,7},{9,8},{10,9},{11,1... | collective-permute-start | bytes 393224 | tf_op jit(solution)/shard_map/ppermute | solution.py:288
  41.8 2.3 %collective-permute-done.5.refs_1_ = bf16[8,64,128]{2,1,0:T(8,128)(2,1)S(1)} collective-permute-done((bf16[8,64,128]{2,1,0:T(8,128)(2,1)S(1)}, bf16[8,64,128]{2,1,0:T(8,128)(2,1)S(1)}, u32[]{:S(2)}, u32[]{:S(2)}) %collective-permute-start.5) | collective-permute-done | bytes 131104 | tf_op jit(solution)/shard_map/ppermute | solution.py:288
  44.0 2.1 %collective-permute-done.6.refs_2_ = bf16[8,64,128]{2,1,0:T(8,128)(2,1)S(1)} collective-permute-done((bf16[8,64,128]{2,1,0:T(8,128)(2,1)S(1)}, bf16[8,64,128]{2,1,0:T(8,128)(2,1)S(1)}, u32[]{:S(2)}, u32[]{:S(2)}) %collective-permute-start.6) | collective-permute-done | bytes 131104 | tf_op jit(solution)/shard_map/ppermute | solution.py:288
  46.2 1.3 %collective-permute-done.7.refs_3_ = bf16[8,64,128]{2,1,0:T(8,128)(2,1)S(1)} collective-permute-done((bf16[8,64,128]{2,1,0:T(8,128)(2,1)S(1)}, bf16[8,64,128]{2,1,0:T(8,128)(2,1)S(1)}, u32[]{:S(2)}, u32[]{:S(2)}) %collective-permute-start.7) | collective-permute-done | bytes 131104 | tf_op jit(solution)/shard_map/ppermute | solution.py:288
  47.5 0.8 shard_map.86
  49.0 0.8 collective-permute-start.10
  49.9 6.3 %collective-permute-start.11 = (bf16[4,8,16,128]{3,2,1,0:T(8,128)(2,1)S(1)}, bf16[4,8,16,128]{3,2,1,0:T(8,128)(2,1)S(1)}, u32[]{:S(2)}, u32[]{:S(2)}) collective-permute-start(bf16[4,8,16,128]{3,2,1,0:T(8,128)(2,1)S(1)} %get-tuple-element.12.refs_0_), channel_id=1, source_target_pairs={{4,0},{0,4},{5,1},{1,5},{6,2},{2,6},{7,3},{3,7},{12,8},{8,12},{13,... | collective-permute-start | bytes 393224 | tf_op jit(solution)/shard_map/ppermute | solution.py:288
  56.3 2.7 %collective-permute-start.16 = (bf16[32,4096]{1,0:T(8,128)(2,1)S(1)}, bf16[32,4096]{1,0:T(8,128)(2,1)S(1)}, u32[]{:S(2)}, u32[]{:S(2)}) collective-permute-start(bf16[32,4096]{1,0:T(8,128)(2,1)S(1)} %slice.21), channel_id=1, source_target_pairs={{8,0},{16,8},{24,16},{0,24},{9,1},{17,9},{25,17},{1,25},{10,2},{18... | collective-permute-start | bytes 786440 | tf_op jit(solution)/shard_map/ppermute | solution.py:288
  59.0 2.2 %collective-permute-start.12 = (bf16[4,8,16,128]{3,2,1,0:T(8,128)(2,1)S(1)}, bf16[4,8,16,128]{3,2,1,0:T(8,128)(2,1)S(1)}, u32[]{:S(2)}, u32[]{:S(2)}) collective-permute-start(bf16[4,8,16,128]{3,2,1,0:T(8,128)(2,1)S(1)} %collective-permute-done.8.refs_1_), channel_id=1, source_target_pairs={{4,0},{0,4},{5,1},{1,5},{6,2},{2,6},{7,3},{3,7},{12,8},{8,12},{13,... | collective-permute-start | bytes 393224 | tf_op jit(solution)/shard_map/ppermute | solution.py:288
  61.2 1.3 %collective-permute-start.13 = (bf16[4,8,16,128]{3,2,1,0:T(8,128)(2,1)S(1)}, bf16[4,8,16,128]{3,2,1,0:T(8,128)(2,1)S(1)}, u32[]{:S(2)}, u32[]{:S(2)}) collective-permute-start(bf16[4,8,16,128]{3,2,1,0:T(8,128)(2,1)S(1)} %collective-permute-done.9.refs_2_), channel_id=1, source_target_pairs={{4,0},{0,4},{5,1},{1,5},{6,2},{2,6},{7,3},{3,7},{12,8},{8,12},{13,... | collective-permute-start | bytes 393224 | tf_op jit(solution)/shard_map/ppermute | solution.py:288
  62.5 1.0 collective-permute-done.13.refs_6_
  63.9 3.1 %collective-permute-done.15.refs_11_ = bf16[32,4096]{1,0:T(8,128)(2,1)S(1)} collective-permute-done((bf16[32,4096]{1,0:T(8,128)(2,1)S(1)}, bf16[32,4096]{1,0:T(8,128)(2,1)S(1)}, u32[]{:S(2)}, u32[]{:S(2)}) %collective-permute-start.15) | collective-permute-done | bytes 262176 | tf_op jit(solution)/shard_map/ppermute | solution.py:288
  67.0 6.5 %shard_map.87 = bf16[64,16,256]{2,1,0:T(8,128)(2,1)S(1)} custom-call(s32[8,64]{1,0:T(8,128)S(1)} %bitcast.16, s32[64]{0:T(128)S(1)} %copy-done.10, s32[4]{0:T(128)S(1)} %pad_add_fusion.own_ref, bf16[4,8,16,128]{3,2,1,0:T(8,128)(2,1)S(1)} %get-tuple-element.12.refs_0_, bf16[4,8,16,128]{3,2,1,0:T(8,128)(2,1)S(1)} %collective-permute-done.8.refs_1_, ...), custom_call_target="tpu_custom_call" | custom-call | flops 2147483648 | bytes 4194304 | tf_op jit(solution)/shard_map/pallas_call | solution.py:183
  73.6 28.0 %all_to_all.11.after_ref.rows_ref = bf16[64,16,256]{2,1,0:T(8,128)(2,1)} all-to-all(bf16[64,16,256]{2,1,0:T(8,128)(2,1)S(1)} %shard_map.87), channel_id=1, replica_groups=mesh['z'=8,'x'=4,'core'=2,'y'=4] {'z','x','core'}, dimensions={0} | all-to-all | bytes 1048576 | tf_op jit(solution)/shard_map/all_to_all | solution.py:315
  102.0 7.6 %shard_map.89.refs_0_ = bf16[64,4096]{1,0:T(8,128)(2,1)} custom-call(s32[8,64]{1,0:T(8,128)} %bitcast.14, s32[64]{0:T(128)} %first_ref.3, s32[4]{0:T(128)} %copy-done.5, bf16[4,4,8,64,128]{4,3,2,1,0:T(8,128)(2,1)} %shard_map.88.panel_ref, bf16[64,16,256]{2,1,0:T(8,128)(2,1)} %all_to_all.11.after_ref.rows_ref), custom_call_target="tpu_custom_call" | custom-call | flops 134217728 | bytes 2097152 | tf_op jit(solution)/shard_map/pallas_call | solution.py:255
  109.7 6.9 %shard_map.90 = bf16[64,4096]{1,0:T(8,128)(2,1)} custom-call(s32[8,64]{1,0:T(8,128)S(1)} %bitcast.15, s32[64]{0:T(128)S(1)} %copy-done.7, s32[4]{0:T(128)S(1)} %copy-done.6, bf16[4,4,8,64,128]{4,3,2,1,0:T(8,128)(2,1)S(1)} %collective-permute-done.17.panel_ref, bf16[64,16,256]{2,1,0:T(8,128)(2,1)S(1)} %copy-done, ...), custom_call_target="tpu_custom_call", output_to_operand_aliasing={{}: (5, {})} | custom-call | flops 134217728 | bytes 2097152 | tf_op jit(solution)/shard_map/pallas_call | solution.py:255
  (52 shorter events, 6.1 us)
Async XLA Ops:
  6.5 95.0 %all-gather.3.cloned.1.call-start = ((), (), s32[]{:S(2)}) async-start(), calls=%async_computation.2 | async-start | bytes 2621440 | tf_op jit(solution)/shard_map/all_gather | solution.py:313
  8.1 58.9 %copy-start.5 = (s32[4]{0:T(128)}, s32[4]{0:T(128)S(1)}, u32[]{:S(2)}) copy-start(s32[4]{0:T(128)S(1)} %pad_add_fusion.own_ref) | copy-start | bytes 52
  8.9 4.5 %collective-permute-start = (bf16[16,128]{1,0:T(8,128)(2,1)S(1)}, bf16[16,128]{1,0:T(8,128)(2,1)S(1)}, u32[]{:S(2)}, u32[]{:S(2)}) collective-permute-start(bf16[16,128]{1,0:T(8,128)(2,1)S(1)} %get-tuple-element.15), channel_id=1, source_target_pairs={{8,0},{16,8},{24,16},{0,24},{9,1},{17,9},{25,17},{1,25},{10,2},{18... | collective-permute-start | bytes 12296 | tf_op jit(solution)/shard_map/ppermute | solution.py:288
  12.3 4.0 %collective-permute-start.1 = (bf16[16,128]{1,0:T(8,128)(2,1)S(1)}, bf16[16,128]{1,0:T(8,128)(2,1)S(1)}, u32[]{:S(2)}, u32[]{:S(2)}) collective-permute-start(bf16[16,128]{1,0:T(8,128)(2,1)S(1)} %get-tuple-element.14), channel_id=1, source_target_pairs={{16,0},{24,8},{0,16},{8,24},{17,1},{25,9},{1,17},{9,25},{18,2},{26... | collective-permute-start | bytes 12296 | tf_op jit(solution)/shard_map/ppermute | solution.py:288
  12.8 3.7 %collective-permute-start.2 = (bf16[16,128]{1,0:T(8,128)(2,1)S(1)}, bf16[16,128]{1,0:T(8,128)(2,1)S(1)}, u32[]{:S(2)}, u32[]{:S(2)}) collective-permute-start(bf16[16,128]{1,0:T(8,128)(2,1)S(1)} %get-tuple-element.13), channel_id=1, source_target_pairs={{24,0},{0,8},{8,16},{16,24},{25,1},{1,9},{9,17},{17,25},{26,2},{2,... | collective-permute-start | bytes 12296 | tf_op jit(solution)/shard_map/ppermute | solution.py:288
  18.9 19.0 %collective-permute-start.3 = (bf16[64,4096]{1,0:T(8,128)(2,1)S(1)}, bf16[64,4096]{1,0:T(8,128)(2,1)S(1)}, u32[]{:S(2)}, u32[]{:S(2)}) collective-permute-start(bf16[64,4096]{1,0:T(8,128)(2,1)S(1)} %shard_map.83.after_ref.refs_8_), channel_id=1, source_target_pairs={{8,0},{16,8},{24,16},{0,24},{9,1},{17,9},{25,17},{1,25},{10,2},{18... | collective-permute-start | bytes 1572872 | tf_op jit(solution)/shard_map/ppermute | solution.py:288
  19.3 18.5 %collective-permute-start.4 = (bf16[64,4096]{1,0:T(8,128)(2,1)S(1)}, bf16[64,4096]{1,0:T(8,128)(2,1)S(1)}, u32[]{:S(2)}, u32[]{:S(2)}) collective-permute-start(bf16[64,4096]{1,0:T(8,128)(2,1)S(1)} %shard_map.83.after_ref.refs_8_), channel_id=1, source_target_pairs={{24,0},{0,8},{8,16},{16,24},{25,1},{1,9},{9,17},{17,25},{26,2},{2,... | collective-permute-start | bytes 1572872 | tf_op jit(solution)/shard_map/ppermute | solution.py:288
  37.9 29.1 %copy-start.9 = (s32[64,8]{0,1:T(8,128)S(1)}, s32[64,8]{0,1:T(8,128)}, u32[]{:S(2)}) copy-start(s32[64,8]{0,1:T(8,128)} %param.13) | copy-start | bytes 6148
  37.9 29.1 %copy-start.10 = (s32[64]{0:T(128)S(1)}, s32[64]{0:T(128)}, u32[]{:S(2)}) copy-start(s32[64]{0:T(128)} %second_ref.1) | copy-start | bytes 772
  37.9 6.1 %collective-permute-start.5 = (bf16[8,64,128]{2,1,0:T(8,128)(2,1)S(1)}, bf16[8,64,128]{2,1,0:T(8,128)(2,1)S(1)}, u32[]{:S(2)}, u32[]{:S(2)}) collective-permute-start(bf16[8,64,128]{2,1,0:T(8,128)(2,1)S(1)} %get-tuple-element.11.refs_0_), channel_id=1, source_target_pairs={{1,0},{2,1},{3,2},{0,3},{5,4},{6,5},{7,6},{4,7},{9,8},{10,9},{11,1... | collective-permute-start | bytes 393224 | tf_op jit(solution)/shard_map/ppermute | solution.py:288
  40.7 5.4 %collective-permute-start.6 = (bf16[8,64,128]{2,1,0:T(8,128)(2,1)S(1)}, bf16[8,64,128]{2,1,0:T(8,128)(2,1)S(1)}, u32[]{:S(2)}, u32[]{:S(2)}) collective-permute-start(bf16[8,64,128]{2,1,0:T(8,128)(2,1)S(1)} %get-tuple-element.11.refs_0_), channel_id=1, source_target_pairs={{2,0},{3,1},{0,2},{1,3},{6,4},{7,5},{4,6},{5,7},{10,8},{11,9},{8,1... | collective-permute-start | bytes 393224 | tf_op jit(solution)/shard_map/ppermute | solution.py:288
  41.1 6.4 %collective-permute-start.7 = (bf16[8,64,128]{2,1,0:T(8,128)(2,1)S(1)}, bf16[8,64,128]{2,1,0:T(8,128)(2,1)S(1)}, u32[]{:S(2)}, u32[]{:S(2)}) collective-permute-start(bf16[8,64,128]{2,1,0:T(8,128)(2,1)S(1)} %get-tuple-element.11.refs_0_), channel_id=1, source_target_pairs={{3,0},{0,1},{1,2},{2,3},{7,4},{4,5},{5,6},{6,7},{11,8},{8,9},{9,10... | collective-permute-start | bytes 393224 | tf_op jit(solution)/shard_map/ppermute | solution.py:288
  48.3 8.0 %collective-permute-start.8 = (bf16[4,8,16,128]{3,2,1,0:T(8,128)(2,1)S(1)}, bf16[4,8,16,128]{3,2,1,0:T(8,128)(2,1)S(1)}, u32[]{:S(2)}, u32[]{:S(2)}) collective-permute-start(bf16[4,8,16,128]{3,2,1,0:T(8,128)(2,1)S(1)} %get-tuple-element.12.refs_0_), channel_id=1, source_target_pairs={{1,0},{2,1},{3,2},{0,3},{5,4},{6,5},{7,6},{4,7},{9,8},{10,9},{11,1... | collective-permute-start | bytes 393224 | tf_op jit(solution)/shard_map/ppermute | solution.py:288
  48.7 10.4 %collective-permute-start.9 = (bf16[4,8,16,128]{3,2,1,0:T(8,128)(2,1)S(1)}, bf16[4,8,16,128]{3,2,1,0:T(8,128)(2,1)S(1)}, u32[]{:S(2)}, u32[]{:S(2)}) collective-permute-start(bf16[4,8,16,128]{3,2,1,0:T(8,128)(2,1)S(1)} %get-tuple-element.12.refs_0_), channel_id=1, source_target_pairs={{2,0},{3,1},{0,2},{1,3},{6,4},{7,5},{4,6},{5,7},{10,8},{11,9},{8,1... | collective-permute-start | bytes 393224 | tf_op jit(solution)/shard_map/ppermute | solution.py:288
  49.0 12.2 %collective-permute-start.10 = (bf16[4,8,16,128]{3,2,1,0:T(8,128)(2,1)S(1)}, bf16[4,8,16,128]{3,2,1,0:T(8,128)(2,1)S(1)}, u32[]{:S(2)}, u32[]{:S(2)}) collective-permute-start(bf16[4,8,16,128]{3,2,1,0:T(8,128)(2,1)S(1)} %get-tuple-element.12.refs_0_), channel_id=1, source_target_pairs={{3,0},{0,1},{1,2},{2,3},{7,4},{4,5},{5,6},{6,7},{11,8},{8,9},{9,10... | collective-permute-start | bytes 393224 | tf_op jit(solution)/shard_map/ppermute | solution.py:288
  49.9 12.7 %collective-permute-start.11 = (bf16[4,8,16,128]{3,2,1,0:T(8,128)(2,1)S(1)}, bf16[4,8,16,128]{3,2,1,0:T(8,128)(2,1)S(1)}, u32[]{:S(2)}, u32[]{:S(2)}) collective-permute-start(bf16[4,8,16,128]{3,2,1,0:T(8,128)(2,1)S(1)} %get-tuple-element.12.refs_0_), channel_id=1, source_target_pairs={{4,0},{0,4},{5,1},{1,5},{6,2},{2,6},{7,3},{3,7},{12,8},{8,12},{13,... | collective-permute-start | bytes 393224 | tf_op jit(solution)/shard_map/ppermute | solution.py:288
  56.2 10.8 %collective-permute-start.15 = (bf16[32,4096]{1,0:T(8,128)(2,1)S(1)}, bf16[32,4096]{1,0:T(8,128)(2,1)S(1)}, u32[]{:S(2)}, u32[]{:S(2)}) collective-permute-start(bf16[32,4096]{1,0:T(8,128)(2,1)S(1)} %slice.20), channel_id=1, source_target_pairs={{24,0},{0,8},{8,16},{16,24},{25,1},{1,9},{9,17},{17,25},{26,2},{2,... | collective-permute-start | bytes 786440 | tf_op jit(solution)/shard_map/ppermute | solution.py:288
  56.3 10.7 %collective-permute-start.16 = (bf16[32,4096]{1,0:T(8,128)(2,1)S(1)}, bf16[32,4096]{1,0:T(8,128)(2,1)S(1)}, u32[]{:S(2)}, u32[]{:S(2)}) collective-permute-start(bf16[32,4096]{1,0:T(8,128)(2,1)S(1)} %slice.21), channel_id=1, source_target_pairs={{8,0},{16,8},{24,16},{0,24},{9,1},{17,9},{25,17},{1,25},{10,2},{18... | collective-permute-start | bytes 786440 | tf_op jit(solution)/shard_map/ppermute | solution.py:288
  59.0 3.5 %collective-permute-start.12 = (bf16[4,8,16,128]{3,2,1,0:T(8,128)(2,1)S(1)}, bf16[4,8,16,128]{3,2,1,0:T(8,128)(2,1)S(1)}, u32[]{:S(2)}, u32[]{:S(2)}) collective-permute-start(bf16[4,8,16,128]{3,2,1,0:T(8,128)(2,1)S(1)} %collective-permute-done.8.refs_1_), channel_id=1, source_target_pairs={{4,0},{0,4},{5,1},{1,5},{6,2},{2,6},{7,3},{3,7},{12,8},{8,12},{13,... | collective-permute-start | bytes 393224 | tf_op jit(solution)/shard_map/ppermute | solution.py:288
  61.2 2.3 %collective-permute-start.13 = (bf16[4,8,16,128]{3,2,1,0:T(8,128)(2,1)S(1)}, bf16[4,8,16,128]{3,2,1,0:T(8,128)(2,1)S(1)}, u32[]{:S(2)}, u32[]{:S(2)}) collective-permute-start(bf16[4,8,16,128]{3,2,1,0:T(8,128)(2,1)S(1)} %collective-permute-done.9.refs_2_), channel_id=1, source_target_pairs={{4,0},{0,4},{5,1},{1,5},{6,2},{2,6},{7,3},{3,7},{12,8},{8,12},{13,... | collective-permute-start | bytes 393224 | tf_op jit(solution)/shard_map/ppermute | solution.py:288
  62.5 1.3 %collective-permute-start.14 = (bf16[4,8,16,128]{3,2,1,0:T(8,128)(2,1)S(1)}, bf16[4,8,16,128]{3,2,1,0:T(8,128)(2,1)S(1)}, u32[]{:S(2)}, u32[]{:S(2)}) collective-permute-start(bf16[4,8,16,128]{3,2,1,0:T(8,128)(2,1)S(1)} %collective-permute-done.10.refs_3_), channel_id=1, source_target_pairs={{4,0},{0,4},{5,1},{1,5},{6,2},{2,6},{7,3},{3,7},{12,8},{8,12},{13,... | collective-permute-start | bytes 393224 | tf_op jit(solution)/shard_map/ppermute | solution.py:288
  101.5 8.1 %copy-start.6 = (s32[4]{0:T(128)S(1)}, s32[4]{0:T(128)}, u32[]{:S(2)}) copy-start(s32[4]{0:T(128)} %copy-done.5) | copy-start | bytes 52
  101.5 8.2 %copy-start.7 = (s32[64]{0:T(128)S(1)}, s32[64]{0:T(128)}, u32[]{:S(2)}) copy-start(s32[64]{0:T(128)} %first_ref.3) | copy-start | bytes 772
  101.5 8.1 %collective-permute-start.17 = (bf16[4,4,8,64,128]{4,3,2,1,0:T(8,128)(2,1)}, bf16[4,4,8,64,128]{4,3,2,1,0:T(8,128)(2,1)S(1)}, u32[]{:S(2)}, u32[]{:S(2)}) collective-permute-start(bf16[4,4,8,64,128]{4,3,2,1,0:T(8,128)(2,1)} %shard_map.88.panel_ref), channel_id=1, source_target_pairs={{4,0},{0,4},{5,1},{1,5},{6,2},{2,6},{7,3},{3,7},{12,8},{8,12},{13,... | collective-permute-start | bytes 6291464 | tf_op jit(solution)/shard_map/ppermute | solution.py:288
  (6 other events, 19.5 us)
Sparse Core Ops, SparseCore 0:
  48.4 34.4 all-gather.2

commit v3 on v0

v3 whole, which is shorter than its diff:
```python
import functools
import itertools

import jax
import jax.numpy as jnp
from jax import lax
from jax.experimental import pallas as pl
from jax.experimental.pallas import tpu as pltpu
from jax.sharding import Mesh, PartitionSpec as P

Z, X, CORES, Y = 8, 4, 2, 4
SIZES = {"z": Z, "x": X, "core": CORES, "y": Y}
CHIPS = Z * X
BLOCK, WIDTH, QUARTER = 64, 128, 16
MOLECULES = CHIPS * CORES
BASIS = MOLECULES * BLOCK
ANYWHERE = pl.BlockSpec(memory_space=pl.ANY)
SMEM = pl.BlockSpec(memory_space=pltpu.SMEM)
VMEM = pl.BlockSpec(memory_space=pltpu.VMEM)
NT = (((1,), (1,)), ((), ()))


def swap_halves(tile):
    return jnp.concatenate([tile[:, BLOCK:], tile[:, :BLOCK]], axis=1)


def call(kernel, outs, in_specs, out_specs, scratch=(), mib=16, flops=2**18, moved=2**20):
    return pl.pallas_call(
        kernel,
        out_shape=tuple(jax.ShapeDtypeStruct(shape, jnp.bfloat16) for shape in outs),
        in_specs=in_specs,
        out_specs=out_specs,
        scratch_shapes=list(scratch),
        compiler_params=pltpu.CompilerParams(vmem_limit_bytes=mib * 2**20),
        cost_estimate=pl.CostEstimate(flops=flops, bytes_accessed=moved, transcendentals=0),
    )


def started(pairs, sems):
    copies = [
        pltpu.make_async_copy(source, target, sems.at[number])
        for number, (source, target) in enumerate(pairs)
    ]
    for copy in copies:
        copy.start()
    return copies


def prepare_kernel(
    mask_ref, b_hbm, occ_hbm, virt_hbm, masked_ref, spread_ref, b_ref, occ_ref, virt_ref, sems
):
    b_copy, *others = started([(b_hbm, b_ref), (occ_hbm, occ_ref), (virt_hbm, virt_ref)], sems)
    for copy in others:
        copy.wait()
    occ = jnp.concatenate([occ_ref[0, 0], occ_ref[0, 1]], axis=1)
    rows = jnp.concatenate([virt_ref[0, 0], virt_ref[0, 1]], axis=0).astype(jnp.float32)
    virt = rows.T.astype(jnp.bfloat16)
    for z, x in itertools.product(range(Z), range(X)):
        spread_ref[z * X + x, :QUARTER] = occ[x * QUARTER : (x + 1) * QUARTER]
        spread_ref[z * X + x, QUARTER:] = virt
    b_copy.wait()
    first_half = lax.broadcasted_iota(jnp.int32, (BLOCK, WIDTH), 1) < BLOCK
    for pair in range(MOLECULES // 2):
        weight = jnp.where(first_half, mask_ref[0, 0, 2 * pair], mask_ref[0, 0, 2 * pair + 1])
        place = slice(pair * WIDTH, (pair + 1) * WIDTH)
        masked_ref[:, place] = b_ref[0, :, place] * weight.astype(jnp.float32).astype(jnp.bfloat16)


def prepare(pair_mask, b_tensor, occ_blocks, virt_blocks):
    arrays = (b_tensor, occ_blocks, virt_blocks)
    return call(
        prepare_kernel,
        [(BLOCK, BASIS), (CHIPS, QUARTER + BLOCK, WIDTH)],
        [SMEM] + [ANYWHERE] * 3,
        (VMEM, VMEM),
        [pltpu.VMEM(array.shape, jnp.bfloat16) for array in arrays]
        + [pltpu.SemaphoreType.DMA((3,))],
    )(pair_mask, *arrays)


def divide_kernel(both_ref, occ_ref, virt_ref):
    for chip in range(CHIPS):
        occ_ref[chip] = both_ref[chip, :QUARTER]
        virt_ref[chip] = both_ref[chip, QUARTER:]


def divide(both):
    return call(
        divide_kernel, [(CHIPS, QUARTER, WIDTH), (CHIPS, BLOCK, WIDTH)], [VMEM], (VMEM, VMEM)
    )(both)


def tie(arrays, after):
    count = len(arrays)
    return pl.pallas_call(
        lambda *refs: None,
        out_shape=tuple(jax.ShapeDtypeStruct(array.shape, array.dtype) for array in arrays),
        in_specs=[ANYWHERE] * (count + 1),
        out_specs=(ANYWHERE,) * count,
        input_output_aliases={number: number for number in range(count)},
        compiler_params=pltpu.CompilerParams(vmem_limit_bytes=2**20),
    )(*arrays, after)


PARTS = [(0, None), (1, None), (3, None), (2, 0), (2, 1)]
MEMBERS = 16


def occupied_kernel(index_ref, second_ref, own_ref, *refs):
    piece_refs, refs = refs[: CORES * Y], refs[CORES * Y :]
    row_refs, refs = refs[: CORES * len(PARTS)], refs[CORES * len(PARTS) :]
    *_, out_ref, piece_ref, rows_ref, even_ref, odd_ref = refs
    x0, core0, y0 = (own_ref[i] for i in range(1, 4))
    for number, ref in enumerate(piece_refs):
        piece_ref[number * CHIPS : (number + 1) * CHIPS] = ref[...]
    for core_off in range(CORES):
        for (off, part), ref in zip(PARTS, row_refs[core_off * len(PARTS) :]):
            block = ((core0 ^ core_off) << 2) + ((x0 + off) & (X - 1))
            place = pl.multiple_of((block << 6) + (part or 0) * (BLOCK // 2), 32)
            rows_ref[pl.ds(place, ref.shape[0]), :] = ref[...]
    side_of = lax.broadcasted_iota(jnp.int32, (QUARTER, WIDTH), 1) // BLOCK
    even_ref[...] = jnp.zeros_like(even_ref)
    odd_ref[...] = jnp.zeros_like(odd_ref)
    for chunk, dense_ref in enumerate((even_ref, odd_ref)):
        molecules = [
            second_ref[(chunk * MEMBERS + member) * CORES + core0] for member in range(MEMBERS)
        ]
        places = [
            (((molecule & 1) ^ core0) << 7) + (molecule >> 1) for molecule in molecules
        ]
        for y_off in range(Y):
            tiles = [piece_ref[place + y_off * CHIPS] for place in places]
            swapped = [swap_halves(tile) for tile in tiles]
            for side in range(2):
                k = (((y0 + y_off) & (Y - 1)) << 1) + side
                placed = []
                for row, molecule in enumerate(molecules):
                    index = index_ref[k, molecule]
                    place = (
                        pl.ds(row * QUARTER, QUARTER),
                        pl.ds(pl.multiple_of((index >> 1) << 7, WIDTH), WIDTH),
                    )
                    parity = index & 1
                    value = jnp.where(parity == side, tiles[row], swapped[row])
                    placed.append((place, jnp.where(side_of == parity, value, dense_ref[place])))
                for place, value in placed:
                    dense_ref[place] = value
        product = lax.dot_general(
            dense_ref[...], rows_ref[...], NT, preferred_element_type=jnp.float32
        ).astype(jnp.bfloat16)
        for row in range(MEMBERS):
            out_ref[chunk * MEMBERS + row] = product[row * QUARTER : (row + 1) * QUARTER]


def occupied(pieces, rows, own, occ_index, second_map, *early):
    dense = (MEMBERS * QUARTER, BASIS)
    lanes = CORES * X * BLOCK
    return call(
        occupied_kernel,
        [(CHIPS, QUARTER, lanes)],
        [SMEM] * 3 + [VMEM] * (len(pieces) + len(rows)) + [ANYWHERE] * len(early),
        (VMEM,),
        [
            pltpu.VMEM((len(pieces) * CHIPS, QUARTER, WIDTH), jnp.bfloat16),
            pltpu.VMEM((lanes, BASIS), jnp.bfloat16),
            pltpu.VMEM(dense, jnp.bfloat16),
            pltpu.VMEM(dense, jnp.bfloat16),
        ],
        mib=24,
        flops=4 * dense[0] * BASIS * lanes,
        moved=2**23,
    )(occ_index.T, second_map, own, *pieces, *rows, *early)[0]


def virtual_kernel(core_off, index_ref, first_ref, own_ref, *refs):
    panel_refs, refs = refs[: len(PARTS)], refs[len(PARTS) :]
    if core_off:
        table_ref, before_ref, out_hbm, out_ref, left_ref, right_ref, out_sems = refs
    else:
        rows_ref, out_ref, table_ref, left_ref, right_ref = refs
    core0, y0 = own_ref[2], own_ref[3]
    half_table = CHIPS * CORES // 2
    for slot in range(MOLECULES):
        z, x, core = slot // (X * CORES), slot // CORES % X, slot % CORES
        place = z * X + core * 2 + x // 2
        molecule = first_ref[slot]
        left_ref[molecule] = place + half_table * (x % 2)
        right_ref[molecule] = place + half_table * (1 - x % 2)
    if not core_off:
        for z, tile_at in itertools.product(range(Z), range(X)):
            lanes = slice(tile_at * WIDTH, (tile_at + 1) * WIDTH)
            tile = jnp.concatenate([rows_ref[z * X + x, :, lanes] for x in range(X)], axis=0)
            table_ref[z * X + tile_at] = tile
            table_ref[half_table + z * X + tile_at] = swap_halves(tile)

    def panel(y_off, chip):
        if y_off == 2:
            return panel_refs[3 + chip // (CHIPS // 2)][chip % (CHIPS // 2)]
        return panel_refs[{0: 0, 1: 1, 3: 2}[y_off]][chip]

    first_half = lax.broadcasted_iota(jnp.int32, (BLOCK, WIDTH), 1) < BLOCK
    written = []
    for z in range(Z):
        for x in range(X):
            molecule = (z * X + x) * CORES + (core0 ^ core_off)
            left = []
            for y in range(Y):
                k = ((y0 + y) & (Y - 1)) << 1
                one = left_ref[index_ref[k, molecule]]
                two = right_ref[index_ref[k + 1, molecule]]
                left.append(jnp.where(first_half, table_ref[one], table_ref[two]))
            right = [panel(y, z * X + x) for y in range(Y)]
            found = lax.dot_general(
                jnp.concatenate(left, axis=1), jnp.concatenate(right, axis=1), NT,
                preferred_element_type=jnp.float32,
            ).astype(jnp.bfloat16)
            found = jnp.concatenate([found, found], axis=1)
            place = slice((z * X + x) * WIDTH, (z * X + x + 1) * WIDTH)
            if core_off:
                found = jnp.where(first_half == (core0 == 0), before_ref[:, place], found)
            out_ref[:, place] = found
        if core_off:
            place = (slice(None), pl.ds(z * X * WIDTH, X * WIDTH))
            written.append(
                pltpu.make_async_copy(out_ref.at[place], out_hbm.at[place], out_sems.at[z])
            )
            written[-1].start()
    for copy in written:
        copy.wait()


def virtual(core_off, panels, own, virt_index, first_map, *rest):
    shape, table = (BLOCK, BASIS), (MOLECULES, BLOCK, WIDTH)
    scratch = [pltpu.SMEM((MOLECULES,), jnp.int32)] * 2
    if core_off:
        scratch = [pltpu.VMEM(shape, jnp.bfloat16), *scratch, pltpu.SemaphoreType.DMA((Z,))]
    return call(
        functools.partial(virtual_kernel, core_off),
        [shape] if core_off else [shape, table],
        [SMEM] * 3 + [VMEM] * (len(panels) + len(rest)),
        (ANYWHERE,) if core_off else (VMEM, VMEM),
        scratch,
        flops=2 * MOLECULES // 2 * BLOCK * BASIS // 8 * BLOCK,
        moved=2**22,
    )(virt_index.T, first_map, own, *panels, *rest)


def shift(array, axis, by):
    size = SIZES[axis]
    return lax.ppermute(array, axis, [((i + by) % size, i) for i in range(size)])


def ring(array, axis):
    after, before = shift(array, axis, 1), shift(array, axis, -1)
    middle = array.shape[0] // 2
    low, high = shift(before[:middle], axis, -1), shift(after[middle:], axis, 1)
    return [array, after, before, low, high]


def exchange(array):
    return lax.all_to_all(array, ("z", "x"), split_axis=0, concat_axis=0, tiled=True)


def per_device(
    b_tensor, pair_mask, first_map, second_map, occ_blocks, occ_index, virt_blocks, virt_index
):
    own = jnp.stack([lax.axis_index(axis) for axis in SIZES]).astype(jnp.int32)
    masked, spread = prepare(pair_mask, b_tensor, occ_blocks, virt_blocks)
    both = exchange(spread)
    rows = ring(masked, "x")
    rows = rows + [shift(part, "core", 1) for part in rows]
    occ_plane, virt_plane = divide(both)
    pieces = [occ_plane] + [shift(occ_plane, "y", by) for by in range(1, Y)]
    pieces = pieces + [shift(piece, "core", 1) for piece in pieces]
    mine = ring(virt_plane, "y")
    half = occupied(pieces, rows, own, occ_index, second_map, *mine[1:3])
    turned = exchange(half)
    mine = tie(mine, turned)
    other = [shift(panel, "core", 1) for panel in mine]
    known = (own, virt_index, first_map)
    columns, table = virtual(0, mine, *known, turned)
    return virtual(1, other, *known, table, columns)[0][None]


def solution(mesh):
    shaped = Mesh(mesh.devices.reshape(Z, X, CORES, Y), tuple(SIZES))
    wide = ("z", "x", "core")
    placed = (
        P("y", wide, None),
        P("y", wide, None),
        P(),
        P(),
        P(wide, "y", None, None),
        P(),
        P(wide, "y", None, None),
        P(),
    )
    return jax.shard_map(
        per_device, mesh=shaped, in_specs=placed, out_specs=P("y", wide, None), check_vma=False
    )
```

time: 216 us -> 119 us (0.55)
  starting transfers between devices: 6.21 us -> 51.7 us
  waiting for transfers between devices: 84.9 us -> 47.8 us
  local copies, waits for them, and re-layouts: 40.3 us -> 6.12 us
  other arithmetic: 26.6 us -> 0.08 us
  blocking collectives: 22.4 us -> 0 us
  matrix products: 21.2 us -> 0 us
  between operations: 13.8 us -> 0.32 us
  Pallas kernels: 0 us -> 12.5 us
    all_gather x2 -> x0, waiting for transfers between devices: 70 us -> none  [the longest x1 62.3 us: per_device(): lax.all_gather(occ_local, 'wide', axis=0, tiled=True)]
    ppermute x0 -> x25, waiting for transfers between devices: none -> 39.7 us  [shift(): lax.ppermute(array, axis, [((i + by) % size, i) for i in range(size)])]
    ppermute x0 -> x25, starting transfers between devices: none -> 30 us  [shift(): lax.ppermute(array, axis, [((i + by) % size, i) for i in range(size)])]
    gather x20 -> x0, local copies, waits for them, and re-layouts: 27.3 us -> none  [the longest x8 11.6 us: virtual(): columns = jnp.take(grouped, slot_lists[:, column], axis=1)]
    unnamed x1 -> x0, other arithmetic: 22.4 us -> none
    all_gather x2 -> x0, blocking collectives: 22.4 us -> none  [the longest x1 12.3 us: per_device(): lax.all_gather(occ_blocks, 'narrow', axis=1, tiled=True)]
    dot_general x16 -> x0, matrix products: 21.2 us -> none  [the longest x8 10.7 us: virtual(): jnp.einsum('pcnl,cnm->plcm', columns, panels[:, column], preferred_elemen...]
    all_to_all x1 -> x2, starting transfers between devices: 6.16 us -> 21.7 us  [exchange(): lax.all_to_all(array, ('z', 'x'), split_axis=0, concat_axis=0, tiled=True)]
  transfers between devices with their start and end apart: 3 -> 27, of which waited for: 3 -> 10; matrix products, arithmetic and copies ran while one was open for 33% -> 0% of each run, Pallas kernels for 0% -> 2%
where the time goes in v3:
time: 119 us
  starting transfers between devices  51.7 us (43%)
  waiting for transfers between devices  47.8 us (40%)
  Pallas kernels  12.5 us (11%)
  local copies, waits for them, and re-layouts  6.12 us (5%)
    ppermute x25, waiting for transfers between devices, shift(): lax.ppermute(array, axis, [((i + by) % size, i) for i in range(size)])  39.7 us
    ppermute x25, starting transfers between devices, shift(): lax.ppermute(array, axis, [((i + by) % size, i) for i in range(size)])  30 us
    all_to_all x2, starting transfers between devices, exchange(): lax.all_to_all(array, ('z', 'x'), split_axis=0, concat_axis=0, tiled=True)  21.7 us
    all_to_all x2, waiting for transfers between devices, exchange(): lax.all_to_all(array, ('z', 'x'), split_axis=0, concat_axis=0, tiled=True)  8.06 us
    pallas_call x1, Pallas kernels, occupied(): call(occupied_kernel, [(CHIPS, QUARTER, lanes)], [SMEM] * 3 + [VMEM] * (l...  6.54 us
    unnamed x24, local copies, waits for them, and re-layouts  6.05 us
    pallas_call x2, Pallas kernels, virtual(): call(functools.partial(virtual_kernel, core_off), [shape] if core_off els...  4.21 us
  transfers between devices with their start and end apart: 27, of which 10 were waited for; matrix products, arithmetic and copies ran while one was open for 0% of the time, Pallas kernels for 2%

profile of v3, /device:TPU:1, one launch (start us, length us, event | category | flops | bytes accessed | tf_op | source)
XLA Modules:
  0.0 118.5 jit_solution(10913911497328608704)
XLA Ops:
  3.2 1.7 %shard_map.82 = (bf16[64,4096]{1,0:T(8,128)(2,1)S(1)}, bf16[32,80,128]{2,1,0:T(8,128)(2,1)}) custom-call(s32[1,1,64]{2,1,0:T(1,128)S(1)} %copy-done.5, bf16[1,64,4096]{2,1,0:T(8,128)(2,1)S(1)} %copy-done, bf16[1,2,64,64]{3,2,1,0:T(8,128)(2,1)S(1)} %copy-done.1, bf16[1,2,64,64]{3,2,1,0:T(8,128)(2,1)S(1)} %copy-done.2), custom_call_target="tpu_custom_call" | custom-call | flops 262144 | bytes 1048576 | tf_op jit(solution)/shard_map/pallas_call | solution.py:71
  5.0 11.9 %all-to-all-start = ((bf16[32,80,128]{2,1,0:T(8,128)(2,1)}), bf16[32,80,128]{2,1,0:T(8,128)(2,1)S(1)}, u32[]{:S(2)}, u32[]{:S(2)}) async-start(bf16[32,80,128]{2,1,0:T(8,128)(2,1)} %get-tuple-element.16), calls=%async_computation | async-start | bytes 1310720 | tf_op jit(solution)/shard_map/all_to_all | solution.py:261
  16.9 1.3 %collective-permute-start.12 = (bf16[64,4096]{1,0:T(8,128)(2,1)S(1)}, bf16[64,4096]{1,0:T(8,128)(2,1)S(1)}, u32[]{:S(2)}, u32[]{:S(2)}) collective-permute-start(bf16[64,4096]{1,0:T(8,128)(2,1)S(1)} %get-tuple-element.19.refs_8_), channel_id=1, source_target_pairs={{24,0},{0,8},{8,16},{16,24},{25,1},{1,9},{9,17},{17,25},{26,2},{2,... | collective-permute-start | bytes 1572872 | tf_op jit(solution)/shard_map/ppermute | solution.py:250
  18.2 1.4 %collective-permute-start.11 = (bf16[64,4096]{1,0:T(8,128)(2,1)S(1)}, bf16[64,4096]{1,0:T(8,128)(2,1)S(1)}, u32[]{:S(2)}, u32[]{:S(2)}) collective-permute-start(bf16[64,4096]{1,0:T(8,128)(2,1)S(1)} %get-tuple-element.19.refs_8_), channel_id=1, source_target_pairs={{8,0},{16,8},{24,16},{0,24},{9,1},{17,9},{25,17},{1,25},{10,2},{18... | collective-permute-start | bytes 1572872 | tf_op jit(solution)/shard_map/ppermute | solution.py:250
  19.6 1.5 %collective-permute-start.15 = (bf16[64,4096]{1,0:T(8,128)(2,1)S(1)}, bf16[64,4096]{1,0:T(8,128)(2,1)}, u32[]{:S(2)}, u32[]{:S(2)}) collective-permute-start(bf16[64,4096]{1,0:T(8,128)(2,1)S(1)} %get-tuple-element.19.refs_8_), channel_id=1, source_target_pairs={{4,0},{0,4},{5,1},{1,5},{6,2},{2,6},{7,3},{3,7},{12,8},{8,12},{13,... | collective-permute-start | bytes 1572872 | tf_op jit(solution)/shard_map/ppermute | solution.py:250
  21.1 16.5 %collective-permute-done.12.refs_10_ = bf16[64,4096]{1,0:T(8,128)(2,1)S(1)} collective-permute-done((bf16[64,4096]{1,0:T(8,128)(2,1)S(1)}, bf16[64,4096]{1,0:T(8,128)(2,1)S(1)}, u32[]{:S(2)}, u32[]{:S(2)}) %collective-permute-start.12) | collective-permute-done | bytes 524320 | tf_op jit(solution)/shard_map/ppermute | solution.py:250
  37.8 2.7 %collective-permute-start.14 = (bf16[32,4096]{1,0:T(8,128)(2,1)S(1)}, bf16[32,4096]{1,0:T(8,128)(2,1)}, u32[]{:S(2)}, u32[]{:S(2)}) collective-permute-start(bf16[32,4096]{1,0:T(8,128)(2,1)S(1)} %slice.19), channel_id=1, source_target_pairs={{8,0},{16,8},{24,16},{0,24},{9,1},{17,9},{25,17},{1,25},{10,2},{18... | collective-permute-start | bytes 786440 | tf_op jit(solution)/shard_map/ppermute | solution.py:250
  40.5 2.2 %collective-permute-start.16 = (bf16[64,4096]{1,0:T(8,128)(2,1)S(1)}, bf16[64,4096]{1,0:T(8,128)(2,1)}, u32[]{:S(2)}, u32[]{:S(2)}) collective-permute-start(bf16[64,4096]{1,0:T(8,128)(2,1)S(1)} %collective-permute-done.11.refs_9_), channel_id=1, source_target_pairs={{4,0},{0,4},{5,1},{1,5},{6,2},{2,6},{7,3},{3,7},{12,8},{8,12},{13,... | collective-permute-start | bytes 1572872 | tf_op jit(solution)/shard_map/ppermute | solution.py:250
  42.7 2.4 %collective-permute-done.13.refs_11_ = bf16[32,4096]{1,0:T(8,128)(2,1)S(1)} collective-permute-done((bf16[32,4096]{1,0:T(8,128)(2,1)S(1)}, bf16[32,4096]{1,0:T(8,128)(2,1)S(1)}, u32[]{:S(2)}, u32[]{:S(2)}) %collective-permute-start.13) | collective-permute-done | bytes 262176 | tf_op jit(solution)/shard_map/ppermute | solution.py:250
  45.1 2.6 %collective-permute-start.18 = (bf16[32,4096]{1,0:T(8,128)(2,1)S(1)}, bf16[32,4096]{1,0:T(8,128)(2,1)S(1)}, u32[]{:S(2)}, u32[]{:S(2)}) collective-permute-start(bf16[32,4096]{1,0:T(8,128)(2,1)S(1)} %collective-permute-done.13.refs_11_), channel_id=1, source_target_pairs={{4,0},{0,4},{5,1},{1,5},{6,2},{2,6},{7,3},{3,7},{12,8},{8,12},{13,... | collective-permute-start | bytes 786440 | tf_op jit(solution)/shard_map/ppermute | solution.py:250
  47.7 2.8 %collective-permute-start = (bf16[32,64,128]{2,1,0:T(8,128)(2,1)S(1)}, bf16[32,64,128]{2,1,0:T(8,128)(2,1)S(1)}, u32[]{:S(2)}, u32[]{:S(2)}) collective-permute-start(bf16[32,64,128]{2,1,0:T(8,128)(2,1)S(1)} %get-tuple-element.17.refs_0_), channel_id=1, source_target_pairs={{1,0},{2,1},{3,2},{0,3},{5,4},{6,5},{7,6},{4,7},{9,8},{10,9},{11,1... | collective-permute-start | bytes 1572872 | tf_op jit(solution)/shard_map/ppermute | solution.py:250
  51.3 1.2 collective-permute-start.6
  52.4 1.6 %collective-permute-start.4 = (bf16[32,16,128]{2,1,0:T(8,128)(2,1)S(1)}, bf16[32,16,128]{2,1,0:T(8,128)(2,1)S(1)}, u32[]{:S(2)}, u32[]{:S(2)}) collective-permute-start(bf16[32,16,128]{2,1,0:T(8,128)(2,1)S(1)} %get-tuple-element.18.refs_0_), channel_id=1, source_target_pairs={{1,0},{2,1},{3,2},{0,3},{5,4},{6,5},{7,6},{4,7},{9,8},{10,9},{11,1... | collective-permute-start | bytes 393224 | tf_op jit(solution)/shard_map/ppermute | solution.py:250
  54.0 1.2 %collective-permute-start.5 = (bf16[32,16,128]{2,1,0:T(8,128)(2,1)S(1)}, bf16[32,16,128]{2,1,0:T(8,128)(2,1)S(1)}, u32[]{:S(2)}, u32[]{:S(2)}) collective-permute-start(bf16[32,16,128]{2,1,0:T(8,128)(2,1)S(1)} %get-tuple-element.18.refs_0_), channel_id=1, source_target_pairs={{2,0},{3,1},{0,2},{1,3},{6,4},{7,5},{4,6},{5,7},{10,8},{11,9},{8,1... | collective-permute-start | bytes 393224 | tf_op jit(solution)/shard_map/ppermute | solution.py:250
  55.2 12.7 %collective-permute-done.6.refs_3_ = bf16[32,16,128]{2,1,0:T(8,128)(2,1)S(1)} collective-permute-done((bf16[32,16,128]{2,1,0:T(8,128)(2,1)S(1)}, bf16[32,16,128]{2,1,0:T(8,128)(2,1)S(1)}, u32[]{:S(2)}, u32[]{:S(2)}) %collective-permute-start.6) | collective-permute-done | bytes 131104 | tf_op jit(solution)/shard_map/ppermute | solution.py:250
  67.9 4.5 %collective-permute-start.7 = (bf16[32,16,128]{2,1,0:T(8,128)(2,1)S(1)}, bf16[32,16,128]{2,1,0:T(8,128)(2,1)S(1)}, u32[]{:S(2)}, u32[]{:S(2)}) collective-permute-start(bf16[32,16,128]{2,1,0:T(8,128)(2,1)S(1)} %get-tuple-element.18.refs_0_), channel_id=1, source_target_pairs={{4,0},{0,4},{5,1},{1,5},{6,2},{2,6},{7,3},{3,7},{12,8},{8,12},{13,... | collective-permute-start | bytes 393224 | tf_op jit(solution)/shard_map/ppermute | solution.py:250
  77.0 6.5 %shard_map.84 = bf16[32,16,512]{2,1,0:T(8,128)(2,1)} custom-call(s32[8,64]{1,0:T(8,128)S(1)} %bitcast.9, s32[64]{0:T(128)S(1)} %copy-done.11, s32[4]{0:T(128)S(1)} %pad_add_fusion.own_ref, bf16[32,16,128]{2,1,0:T(8,128)(2,1)S(1)} %get-tuple-element.18.refs_0_, bf16[32,16,128]{2,1,0:T(8,128)(2,1)S(1)} %collective-permute-done.4.refs_1_, ...), custom_call_target="tpu_custom_call" | custom-call | flops 2147483648 | bytes 8388608 | tf_op jit(solution)/shard_map/pallas_call | solution.py:158
  83.6 9.8 %all-to-all-start.1 = ((bf16[32,16,512]{2,1,0:T(8,128)(2,1)}), bf16[32,16,512]{2,1,0:T(8,128)(2,1)S(1)}, u32[]{:S(2)}, u32[]{:S(2)}) async-start(bf16[32,16,512]{2,1,0:T(8,128)(2,1)} %shard_map.84), calls=%async_computation.1 | async-start | bytes 1048576 | tf_op jit(solution)/shard_map/all_to_all | solution.py:261
  93.5 2.7 %collective-permute-start.3 = (bf16[16,64,128]{2,1,0:T(8,128)(2,1)S(1)}, bf16[16,64,128]{2,1,0:T(8,128)(2,1)S(1)}, u32[]{:S(2)}, u32[]{:S(2)}) collective-permute-start(bf16[16,64,128]{2,1,0:T(8,128)(2,1)S(1)} %slice.17), channel_id=1, source_target_pairs={{1,0},{2,1},{3,2},{0,3},{5,4},{6,5},{7,6},{4,7},{9,8},{10,9},{11,1... | collective-permute-start | bytes 786440 | tf_op jit(solution)/shard_map/ppermute | solution.py:250
  96.3 5.6 %collective-permute-done.2.refs_3_ = bf16[16,64,128]{2,1,0:T(8,128)(2,1)S(1)} collective-permute-done((bf16[16,64,128]{2,1,0:T(8,128)(2,1)S(1)}, bf16[16,64,128]{2,1,0:T(8,128)(2,1)S(1)}, u32[]{:S(2)}, u32[]{:S(2)}) %collective-permute-start.2) | collective-permute-done | bytes 262176 | tf_op jit(solution)/shard_map/ppermute | solution.py:250
  101.9 8.1 %all-to-all-done.1.refs_5_ = bf16[32,16,512]{2,1,0:T(8,128)(2,1)S(1)} async-done(((bf16[32,16,512]{2,1,0:T(8,128)(2,1)}), bf16[32,16,512]{2,1,0:T(8,128)(2,1)S(1)}, u32[]{:S(2)}, u32[]{:S(2)}) %all-to-all-start.1) | async-done | bytes 524320 | tf_op jit(solution)/shard_map/all_to_all | solution.py:261
  110.0 2.2 %collective-permute-start.20 = (bf16[32,64,128]{2,1,0:T(8,128)(2,1)S(1)}, bf16[32,64,128]{2,1,0:T(8,128)(2,1)S(1)}, u32[]{:S(2)}, u32[]{:S(2)}) collective-permute-start(bf16[32,64,128]{2,1,0:T(8,128)(2,1)S(1)} %get-tuple-element.20.refs_0_), channel_id=1, source_target_pairs={{4,0},{0,4},{5,1},{1,5},{6,2},{2,6},{7,3},{3,7},{12,8},{8,12},{13,... | collective-permute-start | bytes 1572872 | tf_op jit(solution)/shard_map/ppermute | solution.py:250
  113.3 1.8 %shard_map.86 = (bf16[64,4096]{1,0:T(8,128)(2,1)S(1)}, bf16[64,64,128]{2,1,0:T(8,128)(2,1)S(1)}) custom-call(s32[8,64]{1,0:T(8,128)S(1)} %bitcast.7, s32[64]{0:T(128)S(1)} %copy-done.4, s32[4]{0:T(128)S(1)} %pad_add_fusion.own_ref, bf16[32,64,128]{2,1,0:T(8,128)(2,1)S(1)} %get-tuple-element.20.refs_0_, bf16[32,64,128]{2,1,0:T(8,128)(2,1)S(1)} %get-tuple-element.21.refs_1_, ...), custom_call_target="tpu_custom_call" | custom-call | flops 134217728 | bytes 4194304 | tf_op jit(solution)/shard_map/pallas_call | solution.py:237
  116.0 2.4 %shard_map.87 = bf16[64,4096]{1,0:T(8,128)(2,1)} custom-call(s32[8,64]{1,0:T(8,128)S(1)} %bitcast.8, s32[64]{0:T(128)S(1)} %copy-done.4, s32[4]{0:T(128)S(1)} %pad_add_fusion.own_ref, bf16[32,64,128]{2,1,0:T(8,128)(2,1)S(1)} %collective-permute-done.20.refs_0_, bf16[32,64,128]{2,1,0:T(8,128)(2,1)S(1)} %collective-permute-done.21.refs_1_, ...), custom_call_target="tpu_custom_call" | custom-call | flops 134217728 | bytes 4194304 | tf_op jit(solution)/shard_map/pallas_call | solution.py:237
  (65 shorter events, 10.8 us)
Async XLA Ops:
  5.0 42.7 %all-to-all-start = ((bf16[32,80,128]{2,1,0:T(8,128)(2,1)}), bf16[32,80,128]{2,1,0:T(8,128)(2,1)S(1)}, u32[]{:S(2)}, u32[]{:S(2)}) async-start(bf16[32,80,128]{2,1,0:T(8,128)(2,1)} %get-tuple-element.16), calls=%async_computation | async-start | bytes 1310720 | tf_op jit(solution)/shard_map/all_to_all | solution.py:261
  16.9 20.8 %collective-permute-start.12 = (bf16[64,4096]{1,0:T(8,128)(2,1)S(1)}, bf16[64,4096]{1,0:T(8,128)(2,1)S(1)}, u32[]{:S(2)}, u32[]{:S(2)}) collective-permute-start(bf16[64,4096]{1,0:T(8,128)(2,1)S(1)} %get-tuple-element.19.refs_8_), channel_id=1, source_target_pairs={{24,0},{0,8},{8,16},{16,24},{25,1},{1,9},{9,17},{17,25},{26,2},{2,... | collective-permute-start | bytes 1572872 | tf_op jit(solution)/shard_map/ppermute | solution.py:250
  18.2 19.6 %collective-permute-start.11 = (bf16[64,4096]{1,0:T(8,128)(2,1)S(1)}, bf16[64,4096]{1,0:T(8,128)(2,1)S(1)}, u32[]{:S(2)}, u32[]{:S(2)}) collective-permute-start(bf16[64,4096]{1,0:T(8,128)(2,1)S(1)} %get-tuple-element.19.refs_8_), channel_id=1, source_target_pairs={{8,0},{16,8},{24,16},{0,24},{9,1},{17,9},{25,17},{1,25},{10,2},{18... | collective-permute-start | bytes 1572872 | tf_op jit(solution)/shard_map/ppermute | solution.py:250
  19.6 28.1 %collective-permute-start.15 = (bf16[64,4096]{1,0:T(8,128)(2,1)S(1)}, bf16[64,4096]{1,0:T(8,128)(2,1)}, u32[]{:S(2)}, u32[]{:S(2)}) collective-permute-start(bf16[64,4096]{1,0:T(8,128)(2,1)S(1)} %get-tuple-element.19.refs_8_), channel_id=1, source_target_pairs={{4,0},{0,4},{5,1},{1,5},{6,2},{2,6},{7,3},{3,7},{12,8},{8,12},{13,... | collective-permute-start | bytes 1572872 | tf_op jit(solution)/shard_map/ppermute | solution.py:250
  37.7 7.4 %collective-permute-start.13 = (bf16[32,4096]{1,0:T(8,128)(2,1)S(1)}, bf16[32,4096]{1,0:T(8,128)(2,1)S(1)}, u32[]{:S(2)}, u32[]{:S(2)}) collective-permute-start(bf16[32,4096]{1,0:T(8,128)(2,1)S(1)} %slice.18), channel_id=1, source_target_pairs={{24,0},{0,8},{8,16},{16,24},{25,1},{1,9},{9,17},{17,25},{26,2},{2,... | collective-permute-start | bytes 786440 | tf_op jit(solution)/shard_map/ppermute | solution.py:250
  37.8 9.9 %collective-permute-start.14 = (bf16[32,4096]{1,0:T(8,128)(2,1)S(1)}, bf16[32,4096]{1,0:T(8,128)(2,1)}, u32[]{:S(2)}, u32[]{:S(2)}) collective-permute-start(bf16[32,4096]{1,0:T(8,128)(2,1)S(1)} %slice.19), channel_id=1, source_target_pairs={{8,0},{16,8},{24,16},{0,24},{9,1},{17,9},{25,17},{1,25},{10,2},{18... | collective-permute-start | bytes 786440 | tf_op jit(solution)/shard_map/ppermute | solution.py:250
  40.5 11.9 %collective-permute-start.16 = (bf16[64,4096]{1,0:T(8,128)(2,1)S(1)}, bf16[64,4096]{1,0:T(8,128)(2,1)}, u32[]{:S(2)}, u32[]{:S(2)}) collective-permute-start(bf16[64,4096]{1,0:T(8,128)(2,1)S(1)} %collective-permute-done.11.refs_9_), channel_id=1, source_target_pairs={{4,0},{0,4},{5,1},{1,5},{6,2},{2,6},{7,3},{3,7},{12,8},{8,12},{13,... | collective-permute-start | bytes 1572872 | tf_op jit(solution)/shard_map/ppermute | solution.py:250
  42.7 11.3 %collective-permute-start.17 = (bf16[64,4096]{1,0:T(8,128)(2,1)S(1)}, bf16[64,4096]{1,0:T(8,128)(2,1)}, u32[]{:S(2)}, u32[]{:S(2)}) collective-permute-start(bf16[64,4096]{1,0:T(8,128)(2,1)S(1)} %collective-permute-done.12.refs_10_), channel_id=1, source_target_pairs={{4,0},{0,4},{5,1},{1,5},{6,2},{2,6},{7,3},{3,7},{12,8},{8,12},{13,... | collective-permute-start | bytes 1572872 | tf_op jit(solution)/shard_map/ppermute | solution.py:250
  45.1 5.5 %collective-permute-start.18 = (bf16[32,4096]{1,0:T(8,128)(2,1)S(1)}, bf16[32,4096]{1,0:T(8,128)(2,1)S(1)}, u32[]{:S(2)}, u32[]{:S(2)}) collective-permute-start(bf16[32,4096]{1,0:T(8,128)(2,1)S(1)} %collective-permute-done.13.refs_11_), channel_id=1, source_target_pairs={{4,0},{0,4},{5,1},{1,5},{6,2},{2,6},{7,3},{3,7},{12,8},{8,12},{13,... | collective-permute-start | bytes 786440 | tf_op jit(solution)/shard_map/ppermute | solution.py:250
  47.7 3.6 %collective-permute-start.19 = (bf16[32,4096]{1,0:T(8,128)(2,1)}, bf16[32,4096]{1,0:T(8,128)(2,1)}, u32[]{:S(2)}, u32[]{:S(2)}) collective-permute-start(bf16[32,4096]{1,0:T(8,128)(2,1)} %collective-permute-done.14.refs_12_), channel_id=1, source_target_pairs={{4,0},{0,4},{5,1},{1,5},{6,2},{2,6},{7,3},{3,7},{12,8},{8,12},{13,... | collective-permute-start | bytes 786440 | tf_op jit(solution)/shard_map/ppermute | solution.py:250
  47.7 27.3 %collective-permute-start = (bf16[32,64,128]{2,1,0:T(8,128)(2,1)S(1)}, bf16[32,64,128]{2,1,0:T(8,128)(2,1)S(1)}, u32[]{:S(2)}, u32[]{:S(2)}) collective-permute-start(bf16[32,64,128]{2,1,0:T(8,128)(2,1)S(1)} %get-tuple-element.17.refs_0_), channel_id=1, source_target_pairs={{1,0},{2,1},{3,2},{0,3},{5,4},{6,5},{7,6},{4,7},{9,8},{10,9},{11,1... | collective-permute-start | bytes 1572872 | tf_op jit(solution)/shard_map/ppermute | solution.py:250
  51.3 23.7 %collective-permute-start.1 = (bf16[32,64,128]{2,1,0:T(8,128)(2,1)S(1)}, bf16[32,64,128]{2,1,0:T(8,128)(2,1)S(1)}, u32[]{:S(2)}, u32[]{:S(2)}) collective-permute-start(bf16[32,64,128]{2,1,0:T(8,128)(2,1)S(1)} %get-tuple-element.17.refs_0_), channel_id=1, source_target_pairs={{3,0},{0,1},{1,2},{2,3},{7,4},{4,5},{5,6},{6,7},{11,8},{8,9},{9,10... | collective-permute-start | bytes 1572872 | tf_op jit(solution)/shard_map/ppermute | solution.py:250
  51.3 16.7 %collective-permute-start.6 = (bf16[32,16,128]{2,1,0:T(8,128)(2,1)S(1)}, bf16[32,16,128]{2,1,0:T(8,128)(2,1)S(1)}, u32[]{:S(2)}, u32[]{:S(2)}) collective-permute-start(bf16[32,16,128]{2,1,0:T(8,128)(2,1)S(1)} %get-tuple-element.18.refs_0_), channel_id=1, source_target_pairs={{3,0},{0,1},{1,2},{2,3},{7,4},{4,5},{5,6},{6,7},{11,8},{8,9},{9,10... | collective-permute-start | bytes 393224 | tf_op jit(solution)/shard_map/ppermute | solution.py:250
  52.4 20.0 %collective-permute-start.4 = (bf16[32,16,128]{2,1,0:T(8,128)(2,1)S(1)}, bf16[32,16,128]{2,1,0:T(8,128)(2,1)S(1)}, u32[]{:S(2)}, u32[]{:S(2)}) collective-permute-start(bf16[32,16,128]{2,1,0:T(8,128)(2,1)S(1)} %get-tuple-element.18.refs_0_), channel_id=1, source_target_pairs={{1,0},{2,1},{3,2},{0,3},{5,4},{6,5},{7,6},{4,7},{9,8},{10,9},{11,1... | collective-permute-start | bytes 393224 | tf_op jit(solution)/shard_map/ppermute | solution.py:250
  54.0 18.4 %collective-permute-start.5 = (bf16[32,16,128]{2,1,0:T(8,128)(2,1)S(1)}, bf16[32,16,128]{2,1,0:T(8,128)(2,1)S(1)}, u32[]{:S(2)}, u32[]{:S(2)}) collective-permute-start(bf16[32,16,128]{2,1,0:T(8,128)(2,1)S(1)} %get-tuple-element.18.refs_0_), channel_id=1, source_target_pairs={{2,0},{3,1},{0,2},{1,3},{6,4},{7,5},{4,6},{5,7},{10,8},{11,9},{8,1... | collective-permute-start | bytes 393224 | tf_op jit(solution)/shard_map/ppermute | solution.py:250
  67.9 5.6 %collective-permute-start.7 = (bf16[32,16,128]{2,1,0:T(8,128)(2,1)S(1)}, bf16[32,16,128]{2,1,0:T(8,128)(2,1)S(1)}, u32[]{:S(2)}, u32[]{:S(2)}) collective-permute-start(bf16[32,16,128]{2,1,0:T(8,128)(2,1)S(1)} %get-tuple-element.18.refs_0_), channel_id=1, source_target_pairs={{4,0},{0,4},{5,1},{1,5},{6,2},{2,6},{7,3},{3,7},{12,8},{8,12},{13,... | collective-permute-start | bytes 393224 | tf_op jit(solution)/shard_map/ppermute | solution.py:250
  83.6 26.4 %all-to-all-start.1 = ((bf16[32,16,512]{2,1,0:T(8,128)(2,1)}), bf16[32,16,512]{2,1,0:T(8,128)(2,1)S(1)}, u32[]{:S(2)}, u32[]{:S(2)}) async-start(bf16[32,16,512]{2,1,0:T(8,128)(2,1)} %shard_map.84), calls=%async_computation.1 | async-start | bytes 1048576 | tf_op jit(solution)/shard_map/all_to_all | solution.py:261
  93.4 8.5 %collective-permute-start.2 = (bf16[16,64,128]{2,1,0:T(8,128)(2,1)S(1)}, bf16[16,64,128]{2,1,0:T(8,128)(2,1)S(1)}, u32[]{:S(2)}, u32[]{:S(2)}) collective-permute-start(bf16[16,64,128]{2,1,0:T(8,128)(2,1)S(1)} %slice.16), channel_id=1, source_target_pairs={{3,0},{0,1},{1,2},{2,3},{7,4},{4,5},{5,6},{6,7},{11,8},{8,9},{9,10... | collective-permute-start | bytes 786440 | tf_op jit(solution)/shard_map/ppermute | solution.py:250
  93.5 8.4 %collective-permute-start.3 = (bf16[16,64,128]{2,1,0:T(8,128)(2,1)S(1)}, bf16[16,64,128]{2,1,0:T(8,128)(2,1)S(1)}, u32[]{:S(2)}, u32[]{:S(2)}) collective-permute-start(bf16[16,64,128]{2,1,0:T(8,128)(2,1)S(1)} %slice.17), channel_id=1, source_target_pairs={{1,0},{2,1},{3,2},{0,3},{5,4},{6,5},{7,6},{4,7},{9,8},{10,9},{11,1... | collective-permute-start | bytes 786440 | tf_op jit(solution)/shard_map/ppermute | solution.py:250
  110.0 6.0 %collective-permute-start.20 = (bf16[32,64,128]{2,1,0:T(8,128)(2,1)S(1)}, bf16[32,64,128]{2,1,0:T(8,128)(2,1)S(1)}, u32[]{:S(2)}, u32[]{:S(2)}) collective-permute-start(bf16[32,64,128]{2,1,0:T(8,128)(2,1)S(1)} %get-tuple-element.20.refs_0_), channel_id=1, source_target_pairs={{4,0},{0,4},{5,1},{1,5},{6,2},{2,6},{7,3},{3,7},{12,8},{8,12},{13,... | collective-permute-start | bytes 1572872 | tf_op jit(solution)/shard_map/ppermute | solution.py:250
  112.2 3.8 %collective-permute-start.21 = (bf16[32,64,128]{2,1,0:T(8,128)(2,1)S(1)}, bf16[32,64,128]{2,1,0:T(8,128)(2,1)S(1)}, u32[]{:S(2)}, u32[]{:S(2)}) collective-permute-start(bf16[32,64,128]{2,1,0:T(8,128)(2,1)S(1)} %get-tuple-element.21.refs_1_), channel_id=1, source_target_pairs={{4,0},{0,4},{5,1},{1,5},{6,2},{2,6},{7,3},{3,7},{12,8},{8,12},{13,... | collective-permute-start | bytes 1572872 | tf_op jit(solution)/shard_map/ppermute | solution.py:250
  112.2 3.8 %collective-permute-start.22 = (bf16[32,64,128]{2,1,0:T(8,128)(2,1)S(1)}, bf16[32,64,128]{2,1,0:T(8,128)(2,1)S(1)}, u32[]{:S(2)}, u32[]{:S(2)}) collective-permute-start(bf16[32,64,128]{2,1,0:T(8,128)(2,1)S(1)} %get-tuple-element.22.refs_2_), channel_id=1, source_target_pairs={{4,0},{0,4},{5,1},{1,5},{6,2},{2,6},{7,3},{3,7},{12,8},{8,12},{13,... | collective-permute-start | bytes 1572872 | tf_op jit(solution)/shard_map/ppermute | solution.py:250
  112.7 2.9 %collective-permute-start.23 = (bf16[16,64,128]{2,1,0:T(8,128)(2,1)S(1)}, bf16[16,64,128]{2,1,0:T(8,128)(2,1)S(1)}, u32[]{:S(2)}, u32[]{:S(2)}) collective-permute-start(bf16[16,64,128]{2,1,0:T(8,128)(2,1)S(1)} %get-tuple-element.23.refs_3_), channel_id=1, source_target_pairs={{4,0},{0,4},{5,1},{1,5},{6,2},{2,6},{7,3},{3,7},{12,8},{8,12},{13,... | collective-permute-start | bytes 786440 | tf_op jit(solution)/shard_map/ppermute | solution.py:250
  112.7 3.3 %collective-permute-start.24 = (bf16[16,64,128]{2,1,0:T(8,128)(2,1)S(1)}, bf16[16,64,128]{2,1,0:T(8,128)(2,1)S(1)}, u32[]{:S(2)}, u32[]{:S(2)}) collective-permute-start(bf16[16,64,128]{2,1,0:T(8,128)(2,1)S(1)} %get-tuple-element.24.refs_4_), channel_id=1, source_target_pairs={{4,0},{0,4},{5,1},{1,5},{6,2},{2,6},{7,3},{3,7},{12,8},{8,12},{13,... | collective-permute-start | bytes 786440 | tf_op jit(solution)/shard_map/ppermute | solution.py:250
  (15 other events, 29.1 us)

commit v4 on v3

--- a/solution.py
+++ b/solution.py
@@ -36,46 +36,32 @@
     )
 
 
-def started(pairs, sems):
-    copies = [
-        pltpu.make_async_copy(source, target, sems.at[number])
-        for number, (source, target) in enumerate(pairs)
-    ]
-    for copy in copies:
-        copy.start()
-    return copies
-
-
-def prepare_kernel(
-    mask_ref, b_hbm, occ_hbm, virt_hbm, masked_ref, spread_ref, b_ref, occ_ref, virt_ref, sems
-):
-    b_copy, *others = started([(b_hbm, b_ref), (occ_hbm, occ_ref), (virt_hbm, virt_ref)], sems)
-    for copy in others:
-        copy.wait()
+def mask_kernel(mask_ref, b_ref, masked_ref):
+    first_half = lax.broadcasted_iota(jnp.int32, (BLOCK, WIDTH), 1) < BLOCK
+    for pair in range(MOLECULES // 2):
+        weight = jnp.where(first_half, mask_ref[0, 0, 2 * pair], mask_ref[0, 0, 2 * pair + 1])
+        place = slice(pair * WIDTH, (pair + 1) * WIDTH)
+        masked_ref[:, place] = b_ref[0, :, place] * weight.astype(jnp.float32).astype(jnp.bfloat16)
+
+
+def mask_rows(pair_mask, b_tensor):
+    return call(mask_kernel, [(BLOCK, BASIS)], [SMEM, VMEM], (VMEM,), mib=8)(pair_mask, b_tensor)[0]
+
+
+def spread_kernel(own_ref, occ_ref, virt_ref, spread_ref):
+    del own_ref
     occ = jnp.concatenate([occ_ref[0, 0], occ_ref[0, 1]], axis=1)
     rows = jnp.concatenate([virt_ref[0, 0], virt_ref[0, 1]], axis=0).astype(jnp.float32)
     virt = rows.T.astype(jnp.bfloat16)
     for z, x in itertools.product(range(Z), range(X)):
         spread_ref[z * X + x, :QUARTER] = occ[x * QUARTER : (x + 1) * QUARTER]
         spread_ref[z * X + x, QUARTER:] = virt
-    b_copy.wait()
-    first_half = lax.broadcasted_iota(jnp.int32, (BLOCK, WIDTH), 1) < BLOCK
-    for pair in range(MOLECULES // 2):
-        weight = jnp.where(first_half, mask_ref[0, 0, 2 * pair], mask_ref[0, 0, 2 * pair + 1])
-        place = slice(pair * WIDTH, (pair + 1) * WIDTH)
-        masked_ref[:, place] = b_ref[0, :, place] * weight.astype(jnp.float32).astype(jnp.bfloat16)
-
-
-def prepare(pair_mask, b_tensor, occ_blocks, virt_blocks):
-    arrays = (b_tensor, occ_blocks, virt_blocks)
-    return call(
-        prepare_kernel,
-        [(BLOCK, BASIS), (CHIPS, QUARTER + BLOCK, WIDTH)],
-        [SMEM] + [ANYWHERE] * 3,
-        (VMEM, VMEM),
-        [pltpu.VMEM(array.shape, jnp.bfloat16) for array in arrays]
-        + [pltpu.SemaphoreType.DMA((3,))],
-    )(pair_mask, *arrays)
+
+
+def spread(own, occ_blocks, virt_blocks):
+    return call(
+        spread_kernel, [(CHIPS, QUARTER + BLOCK, WIDTH)], [SMEM, VMEM, VMEM], (VMEM,), mib=8
+    )(own, occ_blocks, virt_blocks)[0]
 
 
 def divide_kernel(both_ref, occ_ref, virt_ref):
@@ -86,90 +72,99 @@
 
 def divide(both):
     return call(
-        divide_kernel, [(CHIPS, QUARTER, WIDTH), (CHIPS, BLOCK, WIDTH)], [VMEM], (VMEM, VMEM)
+        divide_kernel,
+        [(CHIPS, QUARTER, WIDTH), (CHIPS, BLOCK, WIDTH)],
+        [VMEM],
+        (VMEM, VMEM),
+        mib=8,
     )(both)
 
 
-def tie(arrays, after):
+def tie(arrays, *after):
     count = len(arrays)
     return pl.pallas_call(
         lambda *refs: None,
         out_shape=tuple(jax.ShapeDtypeStruct(array.shape, array.dtype) for array in arrays),
-        in_specs=[ANYWHERE] * (count + 1),
+        in_specs=[ANYWHERE] * (count + len(after)),
         out_specs=(ANYWHERE,) * count,
         input_output_aliases={number: number for number in range(count)},
         compiler_params=pltpu.CompilerParams(vmem_limit_bytes=2**20),
-    )(*arrays, after)
+    )(*arrays, *after)
 
 
 PARTS = [(0, None), (1, None), (3, None), (2, 0), (2, 1)]
 MEMBERS = 16
 
 
-def occupied_kernel(index_ref, second_ref, own_ref, *refs):
-    piece_refs, refs = refs[: CORES * Y], refs[CORES * Y :]
-    row_refs, refs = refs[: CORES * len(PARTS)], refs[CORES * len(PARTS) :]
-    *_, out_ref, piece_ref, rows_ref, even_ref, odd_ref = refs
-    x0, core0, y0 = (own_ref[i] for i in range(1, 4))
+def dense_kernel(index_ref, second_ref, own_ref, *refs):
+    *piece_refs, dense_ref, piece_ref = refs
+    core0, y0 = own_ref[2], own_ref[3]
     for number, ref in enumerate(piece_refs):
         piece_ref[number * CHIPS : (number + 1) * CHIPS] = ref[...]
-    for core_off in range(CORES):
-        for (off, part), ref in zip(PARTS, row_refs[core_off * len(PARTS) :]):
-            block = ((core0 ^ core_off) << 2) + ((x0 + off) & (X - 1))
-            place = pl.multiple_of((block << 6) + (part or 0) * (BLOCK // 2), 32)
-            rows_ref[pl.ds(place, ref.shape[0]), :] = ref[...]
     side_of = lax.broadcasted_iota(jnp.int32, (QUARTER, WIDTH), 1) // BLOCK
-    even_ref[...] = jnp.zeros_like(even_ref)
-    odd_ref[...] = jnp.zeros_like(odd_ref)
-    for chunk, dense_ref in enumerate((even_ref, odd_ref)):
-        molecules = [
-            second_ref[(chunk * MEMBERS + member) * CORES + core0] for member in range(MEMBERS)
-        ]
-        places = [
-            (((molecule & 1) ^ core0) << 7) + (molecule >> 1) for molecule in molecules
-        ]
+    dense_ref[...] = jnp.zeros_like(dense_ref)
+    for chunk in range(0, CHIPS, MEMBERS):
+        molecules = [second_ref[(chunk + member) * CORES + core0] for member in range(MEMBERS)]
+        places = [(((molecule & 1) ^ core0) << 7) + (molecule >> 1) for molecule in molecules]
         for y_off in range(Y):
             tiles = [piece_ref[place + y_off * CHIPS] for place in places]
             swapped = [swap_halves(tile) for tile in tiles]
             for side in range(2):
                 k = (((y0 + y_off) & (Y - 1)) << 1) + side
                 placed = []
-                for row, molecule in enumerate(molecules):
+                for row, molecule in enumerate(molecules, chunk):
                     index = index_ref[k, molecule]
                     place = (
                         pl.ds(row * QUARTER, QUARTER),
                         pl.ds(pl.multiple_of((index >> 1) << 7, WIDTH), WIDTH),
                     )
                     parity = index & 1
-                    value = jnp.where(parity == side, tiles[row], swapped[row])
+                    value = jnp.where(parity == side, tiles[row - chunk], swapped[row - chunk])
                     placed.append((place, jnp.where(side_of == parity, value, dense_ref[place])))
                 for place, value in placed:
                     dense_ref[place] = value
-        product = lax.dot_general(
-            dense_ref[...], rows_ref[...], NT, preferred_element_type=jnp.float32
-        ).astype(jnp.bfloat16)
-        for row in range(MEMBERS):
-            out_ref[chunk * MEMBERS + row] = product[row * QUARTER : (row + 1) * QUARTER]
-
-
-def occupied(pieces, rows, own, occ_index, second_map, *early):
-    dense = (MEMBERS * QUARTER, BASIS)
+
+
+def dense_panel(pieces, own, occ_index, second_map):
+    shape = (CHIPS * QUARTER, BASIS)
+    return call(
+        dense_kernel,
+        [shape],
+        [SMEM] * 3 + [VMEM] * len(pieces),
+        (VMEM,),
+        [pltpu.VMEM((len(pieces) * CHIPS, QUARTER, WIDTH), jnp.bfloat16)],
+        mib=8,
+        flops=2**20,
+        moved=2**23,
+    )(occ_index.T, second_map, own, *pieces)[0]
+
+
+def occupied_kernel(own_ref, dense_ref, *refs):
+    *row_refs, out_ref, rows_ref = refs
+    x0, core0 = own_ref[1], own_ref[2]
+    for core_off in range(CORES):
+        for (off, part), ref in zip(PARTS, row_refs[core_off * len(PARTS) :]):
+            block = ((core0 ^ core_off) << 2) + ((x0 + off) & (X - 1))
+            place = pl.multiple_of((block << 6) + (part or 0) * (BLOCK // 2), 32)
+            rows_ref[pl.ds(place, ref.shape[0]), :] = ref[...]
+    product = lax.dot_general(
+        dense_ref[...], rows_ref[...], NT, preferred_element_type=jnp.float32
+    ).astype(jnp.bfloat16)
+    for chip in range(CHIPS):
+        out_ref[chip] = product[chip * QUARTER : (chip + 1) * QUARTER]
+
+
+def occupied(dense, rows, own):
     lanes = CORES * X * BLOCK
     return call(
         occupied_kernel,
         [(CHIPS, QUARTER, lanes)],
-        [SMEM] * 3 + [VMEM] * (len(pieces) + len(rows)) + [ANYWHERE] * len(early),
+        [SMEM] + [VMEM] * (1 + len(rows)),
         (VMEM,),
-        [
-            pltpu.VMEM((len(pieces) * CHIPS, QUARTER, WIDTH), jnp.bfloat16),
-            pltpu.VMEM((lanes, BASIS), jnp.bfloat16),
-            pltpu.VMEM(dense, jnp.bfloat16),
-            pltpu.VMEM(dense, jnp.bfloat16),
-        ],
-        mib=24,
-        flops=4 * dense[0] * BASIS * lanes,
+        [pltpu.VMEM((lanes, BASIS), jnp.bfloat16)],
+        flops=2 * dense.size * lanes,
         moved=2**23,
-    )(occ_index.T, second_map, own, *pieces, *rows, *early)[0]
+    )(own, dense, *rows)[0]
 
 
 def virtual_kernel(core_off, index_ref, first_ref, own_ref, *refs):
@@ -250,8 +245,10 @@
     return lax.ppermute(array, axis, [((i + by) % size, i) for i in range(size)])
 
 
-def ring(array, axis):
+def ring(array, axis, *between):
     after, before = shift(array, axis, 1), shift(array, axis, -1)
+    if between:
+        after, before = tie([after, before], *between)
     middle = array.shape[0] // 2
     low, high = shift(before[:middle], axis, -1), shift(after[middle:], axis, 1)
     return [array, after, before, low, high]
@@ -265,16 +262,16 @@
     b_tensor, pair_mask, first_map, second_map, occ_blocks, occ_index, virt_blocks, virt_index
 ):
     own = jnp.stack([lax.axis_index(axis) for axis in SIZES]).astype(jnp.int32)
-    masked, spread = prepare(pair_mask, b_tensor, occ_blocks, virt_blocks)
-    both = exchange(spread)
-    rows = ring(masked, "x")
-    rows = rows + [shift(part, "core", 1) for part in rows]
+    both = exchange(spread(own, occ_blocks, virt_blocks))
     occ_plane, virt_plane = divide(both)
     pieces = [occ_plane] + [shift(occ_plane, "y", by) for by in range(1, Y)]
+    rows = ring(mask_rows(pair_mask, b_tensor), "x", *pieces[1:])
+    rows = rows + [shift(part, "core", 1) for part in rows]
+    (virt_plane,) = tie([virt_plane], *pieces[1:])
     pieces = pieces + [shift(piece, "core", 1) for piece in pieces]
-    mine = ring(virt_plane, "y")
-    half = occupied(pieces, rows, own, occ_index, second_map, *mine[1:3])
-    turned = exchange(half)
+    half = occupied(dense_panel(pieces, own, occ_index, second_map), rows, own)
+    mine = ring(virt_plane, "y", half)
+    turned = exchange(*tie([half], *mine[1:3]))
     mine = tie(mine, turned)
     other = [shift(panel, "core", 1) for panel in mine]
     known = (own, virt_index, first_map)

time: 119 us -> 104 us (0.87)
  waiting for transfers between devices: 47.8 us -> 37.9 us
  local copies, waits for them, and re-layouts: 6.12 us -> 3.3 us
  starting transfers between devices: 51.7 us -> 48.9 us
    ppermute x25, waiting for transfers between devices: 39.7 us -> 18 us  [shift(): lax.ppermute(array, axis, [((i + by) % size, i) for i in range(size)])]
    all_to_all x2, waiting for transfers between devices: 8.06 us -> 19.9 us  [exchange(): lax.all_to_all(array, ('z', 'x'), split_axis=0, concat_axis=0, tiled=True)]
    all_to_all x2, starting transfers between devices: 21.7 us -> 17.9 us  [exchange(): lax.all_to_all(array, ('z', 'x'), split_axis=0, concat_axis=0, tiled=True)]
    unnamed x24 -> x16, local copies, waits for them, and re-layouts: 6.05 us -> 3.22 us
    pallas_call x2 -> x4, Pallas kernels: 8.28 us -> 8.99 us  [the longest x1 4.49 us: occupied(): call(occupied_kernel, [(CHIPS, QUARTER, lanes)], [SMEM] + [VMEM] * (1 + l...]
  transfers between devices with their start and end apart: 27 -> 27, of which waited for: 10 -> 12; matrix products, arithmetic and copies ran while one was open for 0% -> 0% of each run, Pallas kernels for 2% -> 9%
where the time goes in v4:
time: 104 us
  starting transfers between devices  48.9 us (47%)
  waiting for transfers between devices  37.9 us (36%)
  Pallas kernels  13.2 us (13%)
  local copies, waits for them, and re-layouts  3.3 us (3%)
    ppermute x25, starting transfers between devices, shift(): lax.ppermute(array, axis, [((i + by) % size, i) for i in range(size)])  31 us
    all_to_all x2, waiting for transfers between devices, exchange(): lax.all_to_all(array, ('z', 'x'), split_axis=0, concat_axis=0, tiled=True)  19.9 us
    ppermute x25, waiting for transfers between devices, shift(): lax.ppermute(array, axis, [((i + by) % size, i) for i in range(size)])  18 us
    all_to_all x2, starting transfers between devices, exchange(): lax.all_to_all(array, ('z', 'x'), split_axis=0, concat_axis=0, tiled=True)  17.9 us
    pallas_call x1, Pallas kernels, occupied(): call(occupied_kernel, [(CHIPS, QUARTER, lanes)], [SMEM] + [VMEM] * (1 + l...  4.49 us
    pallas_call x2, Pallas kernels, virtual(): call(functools.partial(virtual_kernel, core_off), [shape] if core_off els...  4.21 us
    unnamed x16, local copies, waits for them, and re-layouts  3.22 us
    pallas_call x1, Pallas kernels, dense_panel(): call(dense_kernel, [shape], [SMEM] * 3 + [VMEM] * len(pieces), (VMEM,), [...  2.34 us
  transfers between devices with their start and end apart: 27, of which 12 were waited for; matrix products, arithmetic and copies ran while one was open for 0% of the time, Pallas kernels for 9%

profile of v4, /device:TPU:1, one launch (start us, length us, event | category | flops | bytes accessed | tf_op | source)
XLA Modules:
  0.0 103.7 jit_solution(17308535029761575670)
XLA Ops:
  1.6 1.5 %shard_map.82 = bf16[32,80,128]{2,1,0:T(8,128)(2,1)} custom-call(s32[4]{0:T(128)S(1)} %pad_add_fusion.own_ref, bf16[1,2,64,64]{3,2,1,0:T(8,128)(2,1)S(1)} %copy-done.1, bf16[1,2,64,64]{3,2,1,0:T(8,128)(2,1)S(1)} %copy-done.2), custom_call_target="tpu_custom_call" | custom-call | flops 262144 | bytes 1048576 | tf_op jit(solution)/shard_map/pallas_call | solution.py:62
  3.1 11.9 %all-to-all-start = ((bf16[32,80,128]{2,1,0:T(8,128)(2,1)}), bf16[32,80,128]{2,1,0:T(8,128)(2,1)S(1)}, u32[]{:S(2)}, u32[]{:S(2)}) async-start(bf16[32,80,128]{2,1,0:T(8,128)(2,1)} %shard_map.82), calls=%async_computation | async-start | bytes 1310720 | tf_op jit(solution)/shard_map/all_to_all | solution.py:258
  17.3 1.3 %collective-permute-start.10 = (bf16[64,4096]{1,0:T(8,128)(2,1)S(1)}, bf16[64,4096]{1,0:T(8,128)(2,1)S(1)}, u32[]{:S(2)}, u32[]{:S(2)}) collective-permute-start(bf16[64,4096]{1,0:T(8,128)(2,1)S(1)} %shard_map.86.refs_0_), channel_id=1, source_target_pairs={{24,0},{0,8},{8,16},{16,24},{25,1},{1,9},{9,17},{17,25},{26,2},{2,... | collective-permute-start | bytes 1572872 | tf_op jit(solution)/shard_map/ppermute | solution.py:245
  18.6 1.4 %collective-permute-start.9 = (bf16[64,4096]{1,0:T(8,128)(2,1)S(1)}, bf16[64,4096]{1,0:T(8,128)(2,1)S(1)}, u32[]{:S(2)}, u32[]{:S(2)}) collective-permute-start(bf16[64,4096]{1,0:T(8,128)(2,1)S(1)} %shard_map.86.refs_0_), channel_id=1, source_target_pairs={{8,0},{16,8},{24,16},{0,24},{9,1},{17,9},{25,17},{1,25},{10,2},{18... | collective-permute-start | bytes 1572872 | tf_op jit(solution)/shard_map/ppermute | solution.py:245
  20.1 1.5 %collective-permute-start.13 = (bf16[64,4096]{1,0:T(8,128)(2,1)S(1)}, bf16[64,4096]{1,0:T(8,128)(2,1)}, u32[]{:S(2)}, u32[]{:S(2)}) collective-permute-start(bf16[64,4096]{1,0:T(8,128)(2,1)S(1)} %shard_map.86.refs_0_), channel_id=1, source_target_pairs={{4,0},{0,4},{5,1},{1,5},{6,2},{2,6},{7,3},{3,7},{12,8},{8,12},{13,... | collective-permute-start | bytes 1572872 | tf_op jit(solution)/shard_map/ppermute | solution.py:245
  21.6 12.1 %all-to-all-done.both_ref = bf16[32,80,128]{2,1,0:T(8,128)(2,1)S(1)} async-done(((bf16[32,80,128]{2,1,0:T(8,128)(2,1)}), bf16[32,80,128]{2,1,0:T(8,128)(2,1)S(1)}, u32[]{:S(2)}, u32[]{:S(2)}) %all-to-all-start) | async-done | bytes 655392 | tf_op jit(solution)/shard_map/all_to_all | solution.py:258
  33.7 2.8 %collective-permute-start = (bf16[32,16,128]{2,1,0:T(8,128)(2,1)S(1)}, bf16[32,16,128]{2,1,0:T(8,128)(2,1)S(1)}, u32[]{:S(2)}, u32[]{:S(2)}) collective-permute-start(bf16[32,16,128]{2,1,0:T(8,128)(2,1)S(1)} %get-tuple-element.19.refs_0_), channel_id=1, source_target_pairs={{1,0},{2,1},{3,2},{0,3},{5,4},{6,5},{7,6},{4,7},{9,8},{10,9},{11,1... | collective-permute-start | bytes 393224 | tf_op jit(solution)/shard_map/ppermute | solution.py:245
  39.5 2.4 %collective-permute-done.1.refs_2_.refs_3_ = bf16[32,16,128]{2,1,0:T(8,128)(2,1)S(1)} collective-permute-done((bf16[32,16,128]{2,1,0:T(8,128)(2,1)S(1)}, bf16[32,16,128]{2,1,0:T(8,128)(2,1)S(1)}, u32[]{:S(2)}, u32[]{:S(2)}) %collective-permute-start.1) | collective-permute-done | bytes 131104 | tf_op jit(solution)/shard_map/ppermute | solution.py:245
  41.9 1.4 %collective-permute-done.2.refs_3_.refs_4_ = bf16[32,16,128]{2,1,0:T(8,128)(2,1)S(1)} collective-permute-done((bf16[32,16,128]{2,1,0:T(8,128)(2,1)S(1)}, bf16[32,16,128]{2,1,0:T(8,128)(2,1)S(1)}, u32[]{:S(2)}, u32[]{:S(2)}) %collective-permute-start.2) | collective-permute-done | bytes 131104 | tf_op jit(solution)/shard_map/ppermute | solution.py:245
  44.3 4.2 %collective-permute-start.5 = (bf16[32,16,128]{2,1,0:T(8,128)(2,1)S(1)}, bf16[32,16,128]{2,1,0:T(8,128)(2,1)S(1)}, u32[]{:S(2)}, u32[]{:S(2)}) collective-permute-start(bf16[32,16,128]{2,1,0:T(8,128)(2,1)S(1)} %get-tuple-element.19.refs_0_), channel_id=1, source_target_pairs={{4,0},{0,4},{5,1},{1,5},{6,2},{2,6},{7,3},{3,7},{12,8},{8,12},{13,... | collective-permute-start | bytes 393224 | tf_op jit(solution)/shard_map/ppermute | solution.py:245
  49.0 2.0 %collective-permute-start.12 = (bf16[32,4096]{1,0:T(8,128)(2,1)S(1)}, bf16[32,4096]{1,0:T(8,128)(2,1)S(1)}, u32[]{:S(2)}, u32[]{:S(2)}) collective-permute-start(bf16[32,4096]{1,0:T(8,128)(2,1)S(1)} %slice.13), channel_id=1, source_target_pairs={{8,0},{16,8},{24,16},{0,24},{9,1},{17,9},{25,17},{1,25},{10,2},{18... | collective-permute-start | bytes 786440 | tf_op jit(solution)/shard_map/ppermute | solution.py:245
  51.0 4.0 %collective-permute-start.16 = (bf16[32,4096]{1,0:T(8,128)(2,1)S(1)}, bf16[32,4096]{1,0:T(8,128)(2,1)S(1)}, u32[]{:S(2)}, u32[]{:S(2)}) collective-permute-start(bf16[32,4096]{1,0:T(8,128)(2,1)S(1)} %collective-permute-done.11.refs_3_), channel_id=1, source_target_pairs={{4,0},{0,4},{5,1},{1,5},{6,2},{2,6},{7,3},{3,7},{12,8},{8,12},{13,... | collective-permute-start | bytes 786440 | tf_op jit(solution)/shard_map/ppermute | solution.py:245
  55.6 2.2 %collective-permute-done.8.refs_7_ = bf16[32,16,128]{2,1,0:T(8,128)(2,1)S(1)} collective-permute-done((bf16[32,16,128]{2,1,0:T(8,128)(2,1)S(1)}, bf16[32,16,128]{2,1,0:T(8,128)(2,1)S(1)}, u32[]{:S(2)}, u32[]{:S(2)}) %collective-permute-start.8) | collective-permute-done | bytes 131104 | tf_op jit(solution)/shard_map/ppermute | solution.py:245
  60.3 2.3 %shard_map.85.dense_ref = bf16[512,4096]{1,0:T(8,128)(2,1)S(1)} custom-call(s32[8,64]{1,0:T(8,128)S(1)} %bitcast.9, s32[64]{0:T(128)S(1)} %copy-done.7, s32[4]{0:T(128)S(1)} %pad_add_fusion.own_ref, bf16[32,16,128]{2,1,0:T(8,128)(2,1)S(1)} %get-tuple-element.19.refs_0_, bf16[32,16,128]{2,1,0:T(8,128)(2,1)S(1)} %collective-permute-done.refs_1_.refs_2_, ...), custom_call_target="tpu_custom_call" | custom-call | flops 1048576 | bytes 8388608 | tf_op jit(solution)/shard_map/pallas_call | solution.py:130
  62.7 4.5 %shard_map.88.refs_2_.refs_0_ = bf16[32,16,512]{2,1,0:T(8,128)(2,1)} custom-call(s32[4]{0:T(128)S(1)} %pad_add_fusion.own_ref, bf16[512,4096]{1,0:T(8,128)(2,1)S(1)} %shard_map.85.dense_ref, bf16[64,4096]{1,0:T(8,128)(2,1)S(1)} %shard_map.86.refs_0_, bf16[64,4096]{1,0:T(8,128)(2,1)S(1)} %get-tuple-element.20.refs_1_, ...), custom_call_target="tpu_custom_call" | custom-call | flops 2147483648 | bytes 8388608 | tf_op jit(solution)/shard_map/pallas_call | solution.py:159
  67.2 3.9 %collective-permute-done.3.refs_0_ = bf16[32,64,128]{2,1,0:T(8,128)(2,1)S(1)} collective-permute-done((bf16[32,64,128]{2,1,0:T(8,128)(2,1)S(1)}, bf16[32,64,128]{2,1,0:T(8,128)(2,1)S(1)}, u32[]{:S(2)}, u32[]{:S(2)}) %collective-permute-start.3) | collective-permute-done | bytes 524320 | tf_op jit(solution)/shard_map/ppermute | solution.py:245
  71.0 1.5 %collective-permute-done.4.refs_1_ = bf16[32,64,128]{2,1,0:T(8,128)(2,1)S(1)} collective-permute-done((bf16[32,64,128]{2,1,0:T(8,128)(2,1)S(1)}, bf16[32,64,128]{2,1,0:T(8,128)(2,1)S(1)}, u32[]{:S(2)}, u32[]{:S(2)}) %collective-permute-start.4) | collective-permute-done | bytes 524320 | tf_op jit(solution)/shard_map/ppermute | solution.py:245
  72.5 6.0 %all-to-all-start.1 = ((bf16[32,16,512]{2,1,0:T(8,128)(2,1)}), bf16[32,16,512]{2,1,0:T(8,128)(2,1)S(1)}, u32[]{:S(2)}, u32[]{:S(2)}) async-start(bf16[32,16,512]{2,1,0:T(8,128)(2,1)} %shard_map.90), calls=%async_computation.1 | async-start | bytes 1048576 | tf_op jit(solution)/shard_map/all_to_all | solution.py:258
  78.7 2.7 %collective-permute-start.19 = (bf16[16,64,128]{2,1,0:T(8,128)(2,1)S(1)}, bf16[16,64,128]{2,1,0:T(8,128)(2,1)S(1)}, u32[]{:S(2)}, u32[]{:S(2)}) collective-permute-start(bf16[16,64,128]{2,1,0:T(8,128)(2,1)S(1)} %slice.15), channel_id=1, source_target_pairs={{1,0},{2,1},{3,2},{0,3},{5,4},{6,5},{7,6},{4,7},{9,8},{10,9},{11,1... | collective-permute-start | bytes 786440 | tf_op jit(solution)/shard_map/ppermute | solution.py:245
  81.3 4.4 %collective-permute-done.18.refs_3_ = bf16[16,64,128]{2,1,0:T(8,128)(2,1)S(1)} collective-permute-done((bf16[16,64,128]{2,1,0:T(8,128)(2,1)S(1)}, bf16[16,64,128]{2,1,0:T(8,128)(2,1)S(1)}, u32[]{:S(2)}, u32[]{:S(2)}) %collective-permute-start.18) | collective-permute-done | bytes 262176 | tf_op jit(solution)/shard_map/ppermute | solution.py:245
  85.7 7.8 %all-to-all-done.1.refs_5_ = bf16[32,16,512]{2,1,0:T(8,128)(2,1)S(1)} async-done(((bf16[32,16,512]{2,1,0:T(8,128)(2,1)}), bf16[32,16,512]{2,1,0:T(8,128)(2,1)S(1)}, u32[]{:S(2)}, u32[]{:S(2)}) %all-to-all-start.1) | async-done | bytes 524320 | tf_op jit(solution)/shard_map/all_to_all | solution.py:258
  93.5 3.8 %collective-permute-start.20 = (bf16[32,64,128]{2,1,0:T(8,128)(2,1)S(1)}, bf16[32,64,128]{2,1,0:T(8,128)(2,1)S(1)}, u32[]{:S(2)}, u32[]{:S(2)}) collective-permute-start(bf16[32,64,128]{2,1,0:T(8,128)(2,1)S(1)} %get-tuple-element.24.refs_0_), channel_id=1, source_target_pairs={{4,0},{0,4},{5,1},{1,5},{6,2},{2,6},{7,3},{3,7},{12,8},{8,12},{13,... | collective-permute-start | bytes 1572872 | tf_op jit(solution)/shard_map/ppermute | solution.py:245
  98.4 1.8 %shard_map.92 = (bf16[64,4096]{1,0:T(8,128)(2,1)S(1)}, bf16[64,64,128]{2,1,0:T(8,128)(2,1)S(1)}) custom-call(s32[8,64]{1,0:T(8,128)S(1)} %bitcast.7, s32[64]{0:T(128)S(1)} %copy-done.5, s32[4]{0:T(128)S(1)} %pad_add_fusion.own_ref, bf16[32,64,128]{2,1,0:T(8,128)(2,1)S(1)} %get-tuple-element.24.refs_0_, bf16[32,64,128]{2,1,0:T(8,128)(2,1)S(1)} %get-tuple-element.25.refs_1_, ...), custom_call_target="tpu_custom_call" | custom-call | flops 134217728 | bytes 4194304 | tf_op jit(solution)/shard_map/pallas_call | solution.py:232
  101.1 2.4 %shard_map.93 = bf16[64,4096]{1,0:T(8,128)(2,1)} custom-call(s32[8,64]{1,0:T(8,128)S(1)} %bitcast.8, s32[64]{0:T(128)S(1)} %copy-done.5, s32[4]{0:T(128)S(1)} %pad_add_fusion.own_ref, bf16[32,64,128]{2,1,0:T(8,128)(2,1)S(1)} %collective-permute-done.20.refs_0_, bf16[32,64,128]{2,1,0:T(8,128)(2,1)S(1)} %collective-permute-done.21.refs_1_, ...), custom_call_target="tpu_custom_call" | custom-call | flops 134217728 | bytes 4194304 | tf_op jit(solution)/shard_map/pallas_call | solution.py:232
  (63 shorter events, 13.6 us)
Async XLA Ops:
  3.1 30.6 %all-to-all-start = ((bf16[32,80,128]{2,1,0:T(8,128)(2,1)}), bf16[32,80,128]{2,1,0:T(8,128)(2,1)S(1)}, u32[]{:S(2)}, u32[]{:S(2)}) async-start(bf16[32,80,128]{2,1,0:T(8,128)(2,1)} %shard_map.82), calls=%async_computation | async-start | bytes 1310720 | tf_op jit(solution)/shard_map/all_to_all | solution.py:258
  17.3 20.5 %collective-permute-start.10 = (bf16[64,4096]{1,0:T(8,128)(2,1)S(1)}, bf16[64,4096]{1,0:T(8,128)(2,1)S(1)}, u32[]{:S(2)}, u32[]{:S(2)}) collective-permute-start(bf16[64,4096]{1,0:T(8,128)(2,1)S(1)} %shard_map.86.refs_0_), channel_id=1, source_target_pairs={{24,0},{0,8},{8,16},{16,24},{25,1},{1,9},{9,17},{17,25},{26,2},{2,... | collective-permute-start | bytes 1572872 | tf_op jit(solution)/shard_map/ppermute | solution.py:245
  18.6 20.5 %collective-permute-start.9 = (bf16[64,4096]{1,0:T(8,128)(2,1)S(1)}, bf16[64,4096]{1,0:T(8,128)(2,1)S(1)}, u32[]{:S(2)}, u32[]{:S(2)}) collective-permute-start(bf16[64,4096]{1,0:T(8,128)(2,1)S(1)} %shard_map.86.refs_0_), channel_id=1, source_target_pairs={{8,0},{16,8},{24,16},{0,24},{9,1},{17,9},{25,17},{1,25},{10,2},{18... | collective-permute-start | bytes 1572872 | tf_op jit(solution)/shard_map/ppermute | solution.py:245
  20.1 28.9 %collective-permute-start.13 = (bf16[64,4096]{1,0:T(8,128)(2,1)S(1)}, bf16[64,4096]{1,0:T(8,128)(2,1)}, u32[]{:S(2)}, u32[]{:S(2)}) collective-permute-start(bf16[64,4096]{1,0:T(8,128)(2,1)S(1)} %shard_map.86.refs_0_), channel_id=1, source_target_pairs={{4,0},{0,4},{5,1},{1,5},{6,2},{2,6},{7,3},{3,7},{12,8},{8,12},{13,... | collective-permute-start | bytes 1572872 | tf_op jit(solution)/shard_map/ppermute | solution.py:245
  33.7 5.8 %collective-permute-start = (bf16[32,16,128]{2,1,0:T(8,128)(2,1)S(1)}, bf16[32,16,128]{2,1,0:T(8,128)(2,1)S(1)}, u32[]{:S(2)}, u32[]{:S(2)}) collective-permute-start(bf16[32,16,128]{2,1,0:T(8,128)(2,1)S(1)} %get-tuple-element.19.refs_0_), channel_id=1, source_target_pairs={{1,0},{2,1},{3,2},{0,3},{5,4},{6,5},{7,6},{4,7},{9,8},{10,9},{11,1... | collective-permute-start | bytes 393224 | tf_op jit(solution)/shard_map/ppermute | solution.py:245
  36.5 5.4 %collective-permute-start.1 = (bf16[32,16,128]{2,1,0:T(8,128)(2,1)S(1)}, bf16[32,16,128]{2,1,0:T(8,128)(2,1)S(1)}, u32[]{:S(2)}, u32[]{:S(2)}) collective-permute-start(bf16[32,16,128]{2,1,0:T(8,128)(2,1)S(1)} %get-tuple-element.19.refs_0_), channel_id=1, source_target_pairs={{2,0},{3,1},{0,2},{1,3},{6,4},{7,5},{4,6},{5,7},{10,8},{11,9},{8,1... | collective-permute-start | bytes 393224 | tf_op jit(solution)/shard_map/ppermute | solution.py:245
  37.9 5.4 %collective-permute-start.2 = (bf16[32,16,128]{2,1,0:T(8,128)(2,1)S(1)}, bf16[32,16,128]{2,1,0:T(8,128)(2,1)S(1)}, u32[]{:S(2)}, u32[]{:S(2)}) collective-permute-start(bf16[32,16,128]{2,1,0:T(8,128)(2,1)S(1)} %get-tuple-element.19.refs_0_), channel_id=1, source_target_pairs={{3,0},{0,1},{1,2},{2,3},{7,4},{4,5},{5,6},{6,7},{11,8},{8,9},{9,10... | collective-permute-start | bytes 393224 | tf_op jit(solution)/shard_map/ppermute | solution.py:245
  43.3 7.7 %collective-permute-start.11 = (bf16[32,4096]{1,0:T(8,128)(2,1)S(1)}, bf16[32,4096]{1,0:T(8,128)(2,1)S(1)}, u32[]{:S(2)}, u32[]{:S(2)}) collective-permute-start(bf16[32,4096]{1,0:T(8,128)(2,1)S(1)} %slice.12), channel_id=1, source_target_pairs={{24,0},{0,8},{8,16},{16,24},{25,1},{1,9},{9,17},{17,25},{26,2},{2,... | collective-permute-start | bytes 786440 | tf_op jit(solution)/shard_map/ppermute | solution.py:245
  44.3 10.7 %collective-permute-start.5 = (bf16[32,16,128]{2,1,0:T(8,128)(2,1)S(1)}, bf16[32,16,128]{2,1,0:T(8,128)(2,1)S(1)}, u32[]{:S(2)}, u32[]{:S(2)}) collective-permute-start(bf16[32,16,128]{2,1,0:T(8,128)(2,1)S(1)} %get-tuple-element.19.refs_0_), channel_id=1, source_target_pairs={{4,0},{0,4},{5,1},{1,5},{6,2},{2,6},{7,3},{3,7},{12,8},{8,12},{13,... | collective-permute-start | bytes 393224 | tf_op jit(solution)/shard_map/ppermute | solution.py:245
  48.5 6.5 %collective-permute-start.6 = (bf16[32,16,128]{2,1,0:T(8,128)(2,1)S(1)}, bf16[32,16,128]{2,1,0:T(8,128)(2,1)S(1)}, u32[]{:S(2)}, u32[]{:S(2)}) collective-permute-start(bf16[32,16,128]{2,1,0:T(8,128)(2,1)S(1)} %collective-permute-done.refs_1_.refs_2_), channel_id=1, source_target_pairs={{4,0},{0,4},{5,1},{1,5},{6,2},{2,6},{7,3},{3,7},{12,8},{8,12},{13,... | collective-permute-start | bytes 393224 | tf_op jit(solution)/shard_map/ppermute | solution.py:245
  48.5 7.0 %collective-permute-start.7 = (bf16[32,16,128]{2,1,0:T(8,128)(2,1)S(1)}, bf16[32,16,128]{2,1,0:T(8,128)(2,1)S(1)}, u32[]{:S(2)}, u32[]{:S(2)}) collective-permute-start(bf16[32,16,128]{2,1,0:T(8,128)(2,1)S(1)} %collective-permute-done.1.refs_2_.refs_3_), channel_id=1, source_target_pairs={{4,0},{0,4},{5,1},{1,5},{6,2},{2,6},{7,3},{3,7},{12,8},{8,12},{13,... | collective-permute-start | bytes 393224 | tf_op jit(solution)/shard_map/ppermute | solution.py:245
  49.0 9.4 %collective-permute-start.12 = (bf16[32,4096]{1,0:T(8,128)(2,1)S(1)}, bf16[32,4096]{1,0:T(8,128)(2,1)S(1)}, u32[]{:S(2)}, u32[]{:S(2)}) collective-permute-start(bf16[32,4096]{1,0:T(8,128)(2,1)S(1)} %slice.13), channel_id=1, source_target_pairs={{8,0},{16,8},{24,16},{0,24},{9,1},{17,9},{25,17},{1,25},{10,2},{18... | collective-permute-start | bytes 786440 | tf_op jit(solution)/shard_map/ppermute | solution.py:245
  51.0 8.3 %collective-permute-start.16 = (bf16[32,4096]{1,0:T(8,128)(2,1)S(1)}, bf16[32,4096]{1,0:T(8,128)(2,1)S(1)}, u32[]{:S(2)}, u32[]{:S(2)}) collective-permute-start(bf16[32,4096]{1,0:T(8,128)(2,1)S(1)} %collective-permute-done.11.refs_3_), channel_id=1, source_target_pairs={{4,0},{0,4},{5,1},{1,5},{6,2},{2,6},{7,3},{3,7},{12,8},{8,12},{13,... | collective-permute-start | bytes 786440 | tf_op jit(solution)/shard_map/ppermute | solution.py:245
  55.0 7.6 %collective-permute-start.14 = (bf16[64,4096]{1,0:T(8,128)(2,1)S(1)}, bf16[64,4096]{1,0:T(8,128)(2,1)S(1)}, u32[]{:S(2)}, u32[]{:S(2)}) collective-permute-start(bf16[64,4096]{1,0:T(8,128)(2,1)S(1)} %get-tuple-element.20.refs_1_), channel_id=1, source_target_pairs={{4,0},{0,4},{5,1},{1,5},{6,2},{2,6},{7,3},{3,7},{12,8},{8,12},{13,... | collective-permute-start | bytes 1572872 | tf_op jit(solution)/shard_map/ppermute | solution.py:245
  55.0 7.6 %collective-permute-start.15 = (bf16[64,4096]{1,0:T(8,128)(2,1)S(1)}, bf16[64,4096]{1,0:T(8,128)(2,1)S(1)}, u32[]{:S(2)}, u32[]{:S(2)}) collective-permute-start(bf16[64,4096]{1,0:T(8,128)(2,1)S(1)} %get-tuple-element.21.refs_2_), channel_id=1, source_target_pairs={{4,0},{0,4},{5,1},{1,5},{6,2},{2,6},{7,3},{3,7},{12,8},{8,12},{13,... | collective-permute-start | bytes 1572872 | tf_op jit(solution)/shard_map/ppermute | solution.py:245
  57.9 13.1 %collective-permute-start.3 = (bf16[32,64,128]{2,1,0:T(8,128)(2,1)S(1)}, bf16[32,64,128]{2,1,0:T(8,128)(2,1)S(1)}, u32[]{:S(2)}, u32[]{:S(2)}) collective-permute-start(bf16[32,64,128]{2,1,0:T(8,128)(2,1)S(1)} %shard_map.84.refs_0_), channel_id=1, source_target_pairs={{1,0},{2,1},{3,2},{0,3},{5,4},{6,5},{7,6},{4,7},{9,8},{10,9},{11,1... | collective-permute-start | bytes 1572872 | tf_op jit(solution)/shard_map/ppermute | solution.py:245
  58.5 14.0 %collective-permute-start.4 = (bf16[32,64,128]{2,1,0:T(8,128)(2,1)S(1)}, bf16[32,64,128]{2,1,0:T(8,128)(2,1)S(1)}, u32[]{:S(2)}, u32[]{:S(2)}) collective-permute-start(bf16[32,64,128]{2,1,0:T(8,128)(2,1)S(1)} %shard_map.84.refs_0_), channel_id=1, source_target_pairs={{3,0},{0,1},{1,2},{2,3},{7,4},{4,5},{5,6},{6,7},{11,8},{8,9},{9,10... | collective-permute-start | bytes 1572872 | tf_op jit(solution)/shard_map/ppermute | solution.py:245
  59.3 3.3 %collective-permute-start.17 = (bf16[32,4096]{1,0:T(8,128)(2,1)S(1)}, bf16[32,4096]{1,0:T(8,128)(2,1)S(1)}, u32[]{:S(2)}, u32[]{:S(2)}) collective-permute-start(bf16[32,4096]{1,0:T(8,128)(2,1)S(1)} %collective-permute-done.12.refs_4_), channel_id=1, source_target_pairs={{4,0},{0,4},{5,1},{1,5},{6,2},{2,6},{7,3},{3,7},{12,8},{8,12},{13,... | collective-permute-start | bytes 786440 | tf_op jit(solution)/shard_map/ppermute | solution.py:245
  72.5 21.0 %all-to-all-start.1 = ((bf16[32,16,512]{2,1,0:T(8,128)(2,1)}), bf16[32,16,512]{2,1,0:T(8,128)(2,1)S(1)}, u32[]{:S(2)}, u32[]{:S(2)}) async-start(bf16[32,16,512]{2,1,0:T(8,128)(2,1)} %shard_map.90), calls=%async_computation.1 | async-start | bytes 1048576 | tf_op jit(solution)/shard_map/all_to_all | solution.py:258
  78.6 7.1 %collective-permute-start.18 = (bf16[16,64,128]{2,1,0:T(8,128)(2,1)S(1)}, bf16[16,64,128]{2,1,0:T(8,128)(2,1)S(1)}, u32[]{:S(2)}, u32[]{:S(2)}) collective-permute-start(bf16[16,64,128]{2,1,0:T(8,128)(2,1)S(1)} %slice.14), channel_id=1, source_target_pairs={{3,0},{0,1},{1,2},{2,3},{7,4},{4,5},{5,6},{6,7},{11,8},{8,9},{9,10... | collective-permute-start | bytes 786440 | tf_op jit(solution)/shard_map/ppermute | solution.py:245
  78.7 7.0 %collective-permute-start.19 = (bf16[16,64,128]{2,1,0:T(8,128)(2,1)S(1)}, bf16[16,64,128]{2,1,0:T(8,128)(2,1)S(1)}, u32[]{:S(2)}, u32[]{:S(2)}) collective-permute-start(bf16[16,64,128]{2,1,0:T(8,128)(2,1)S(1)} %slice.15), channel_id=1, source_target_pairs={{1,0},{2,1},{3,2},{0,3},{5,4},{6,5},{7,6},{4,7},{9,8},{10,9},{11,1... | collective-permute-start | bytes 786440 | tf_op jit(solution)/shard_map/ppermute | solution.py:245
  93.5 7.6 %collective-permute-start.20 = (bf16[32,64,128]{2,1,0:T(8,128)(2,1)S(1)}, bf16[32,64,128]{2,1,0:T(8,128)(2,1)S(1)}, u32[]{:S(2)}, u32[]{:S(2)}) collective-permute-start(bf16[32,64,128]{2,1,0:T(8,128)(2,1)S(1)} %get-tuple-element.24.refs_0_), channel_id=1, source_target_pairs={{4,0},{0,4},{5,1},{1,5},{6,2},{2,6},{7,3},{3,7},{12,8},{8,12},{13,... | collective-permute-start | bytes 1572872 | tf_op jit(solution)/shard_map/ppermute | solution.py:245
  97.3 3.8 %collective-permute-start.21 = (bf16[32,64,128]{2,1,0:T(8,128)(2,1)S(1)}, bf16[32,64,128]{2,1,0:T(8,128)(2,1)S(1)}, u32[]{:S(2)}, u32[]{:S(2)}) collective-permute-start(bf16[32,64,128]{2,1,0:T(8,128)(2,1)S(1)} %get-tuple-element.25.refs_1_), channel_id=1, source_target_pairs={{4,0},{0,4},{5,1},{1,5},{6,2},{2,6},{7,3},{3,7},{12,8},{8,12},{13,... | collective-permute-start | bytes 1572872 | tf_op jit(solution)/shard_map/ppermute | solution.py:245
  97.3 3.8 %collective-permute-start.22 = (bf16[32,64,128]{2,1,0:T(8,128)(2,1)S(1)}, bf16[32,64,128]{2,1,0:T(8,128)(2,1)S(1)}, u32[]{:S(2)}, u32[]{:S(2)}) collective-permute-start(bf16[32,64,128]{2,1,0:T(8,128)(2,1)S(1)} %get-tuple-element.26.refs_2_), channel_id=1, source_target_pairs={{4,0},{0,4},{5,1},{1,5},{6,2},{2,6},{7,3},{3,7},{12,8},{8,12},{13,... | collective-permute-start | bytes 1572872 | tf_op jit(solution)/shard_map/ppermute | solution.py:245
  (11 other events, 194.7 us)

commit v5 on v4

--- a/solution.py
+++ b/solution.py
@@ -24,7 +24,7 @@
     return jnp.concatenate([tile[:, BLOCK:], tile[:, :BLOCK]], axis=1)
 
 
-def call(kernel, outs, in_specs, out_specs, scratch=(), mib=16, flops=2**18, moved=2**20):
+def call(kernel, outs, in_specs, out_specs, scratch=(), mib=16):
     return pl.pallas_call(
         kernel,
         out_shape=tuple(jax.ShapeDtypeStruct(shape, jnp.bfloat16) for shape in outs),
@@ -32,7 +32,7 @@
         out_specs=out_specs,
         scratch_shapes=list(scratch),
         compiler_params=pltpu.CompilerParams(vmem_limit_bytes=mib * 2**20),
-        cost_estimate=pl.CostEstimate(flops=flops, bytes_accessed=moved, transcendentals=0),
+        cost_estimate=pl.CostEstimate(flops=2**10, bytes_accessed=2**10, transcendentals=0),
     )
 
 
@@ -48,36 +48,23 @@
     return call(mask_kernel, [(BLOCK, BASIS)], [SMEM, VMEM], (VMEM,), mib=8)(pair_mask, b_tensor)[0]
 
 
-def spread_kernel(own_ref, occ_ref, virt_ref, spread_ref):
+def spread_occ_kernel(own_ref, occ_ref, spread_ref):
     del own_ref
     occ = jnp.concatenate([occ_ref[0, 0], occ_ref[0, 1]], axis=1)
+    for z, x in itertools.product(range(Z), range(X)):
+        spread_ref[z * X + x] = occ[x * QUARTER : (x + 1) * QUARTER]
+
+
+def spread_virt_kernel(virt_ref, after_ref, spread_ref):
+    del after_ref
     rows = jnp.concatenate([virt_ref[0, 0], virt_ref[0, 1]], axis=0).astype(jnp.float32)
     virt = rows.T.astype(jnp.bfloat16)
-    for z, x in itertools.product(range(Z), range(X)):
-        spread_ref[z * X + x, :QUARTER] = occ[x * QUARTER : (x + 1) * QUARTER]
-        spread_ref[z * X + x, QUARTER:] = virt
-
-
-def spread(own, occ_blocks, virt_blocks):
-    return call(
-        spread_kernel, [(CHIPS, QUARTER + BLOCK, WIDTH)], [SMEM, VMEM, VMEM], (VMEM,), mib=8
-    )(own, occ_blocks, virt_blocks)[0]
-
-
-def divide_kernel(both_ref, occ_ref, virt_ref):
     for chip in range(CHIPS):
-        occ_ref[chip] = both_ref[chip, :QUARTER]
-        virt_ref[chip] = both_ref[chip, QUARTER:]
-
-
-def divide(both):
-    return call(
-        divide_kernel,
-        [(CHIPS, QUARTER, WIDTH), (CHIPS, BLOCK, WIDTH)],
-        [VMEM],
-        (VMEM, VMEM),
-        mib=8,
-    )(both)
+        spread_ref[chip] = virt
+
+
+def spread(kernel, rows, specs, *arrays):
+    return call(kernel, [(CHIPS, rows, WIDTH)], specs, (VMEM,), mib=8)(*arrays)[0]
 
 
 def tie(arrays, *after):
@@ -134,8 +121,6 @@
         (VMEM,),
         [pltpu.VMEM((len(pieces) * CHIPS, QUARTER, WIDTH), jnp.bfloat16)],
         mib=8,
-        flops=2**20,
-        moved=2**23,
     )(occ_index.T, second_map, own, *pieces)[0]
 
 
@@ -162,8 +147,6 @@
         [SMEM] + [VMEM] * (1 + len(rows)),
         (VMEM,),
         [pltpu.VMEM((lanes, BASIS), jnp.bfloat16)],
-        flops=2 * dense.size * lanes,
-        moved=2**23,
     )(own, dense, *rows)[0]
 
 
@@ -235,8 +218,6 @@
         [SMEM] * 3 + [VMEM] * (len(panels) + len(rest)),
         (ANYWHERE,) if core_off else (VMEM, VMEM),
         scratch,
-        flops=2 * MOLECULES // 2 * BLOCK * BASIS // 8 * BLOCK,
-        moved=2**22,
     )(virt_index.T, first_map, own, *panels, *rest)
 
 
@@ -262,8 +243,9 @@
     b_tensor, pair_mask, first_map, second_map, occ_blocks, occ_index, virt_blocks, virt_index
 ):
     own = jnp.stack([lax.axis_index(axis) for axis in SIZES]).astype(jnp.int32)
-    both = exchange(spread(own, occ_blocks, virt_blocks))
-    occ_plane, virt_plane = divide(both)
+    occ_spread = spread(spread_occ_kernel, QUARTER, [SMEM, VMEM], own, occ_blocks)
+    virt_spread = spread(spread_virt_kernel, BLOCK, [VMEM, ANYWHERE], virt_blocks, occ_spread)
+    occ_plane, virt_plane = exchange(occ_spread), exchange(virt_spread)
     pieces = [occ_plane] + [shift(occ_plane, "y", by) for by in range(1, Y)]
     rows = ring(mask_rows(pair_mask, b_tensor), "x", *pieces[1:])
     rows = rows + [shift(part, "core", 1) for part in rows]

time: 104 us -> 110 us (1.058)
  local copies, waits for them, and re-layouts: 3.3 us -> 9.78 us
  waiting for transfers between devices: 37.9 us -> 32.5 us
  starting transfers between devices: 48.9 us -> 52.7 us
    unnamed x16 -> x36, local copies, waits for them, and re-layouts: 3.22 us -> 8.28 us
    all_to_all x2 -> x3, starting transfers between devices: 17.9 us -> 22.8 us  [exchange(): lax.all_to_all(array, ('z', 'x'), split_axis=0, concat_axis=0, tiled=True)]
    all_to_all x2 -> x3, waiting for transfers between devices: 19.9 us -> 15.5 us  [exchange(): lax.all_to_all(array, ('z', 'x'), split_axis=0, concat_axis=0, tiled=True)]
  transfers between devices with their start and end apart: 27 -> 28, of which waited for: 12 -> 11; matrix products, arithmetic and copies ran while one was open for 0% -> 1% of each run, Pallas kernels for 9% -> 10%
where the time goes in v5:
time: 110 us
  starting transfers between devices  52.7 us (48%)
  waiting for transfers between devices  32.5 us (30%)
  Pallas kernels  14.2 us (13%)
  local copies, waits for them, and re-layouts  9.78 us (9%)
    ppermute x25, starting transfers between devices, shift(): lax.ppermute(array, axis, [((i + by) % size, i) for i in range(size)])  29.9 us
    all_to_all x3, starting transfers between devices, exchange(): lax.all_to_all(array, ('z', 'x'), split_axis=0, concat_axis=0, tiled=True)  22.8 us
    ppermute x25, waiting for transfers between devices, shift(): lax.ppermute(array, axis, [((i + by) % size, i) for i in range(size)])  17.1 us
    all_to_all x3, waiting for transfers between devices, exchange(): lax.all_to_all(array, ('z', 'x'), split_axis=0, concat_axis=0, tiled=True)  15.5 us
    unnamed x36, local copies, waits for them, and re-layouts  8.28 us
    pallas_call x1, Pallas kernels, occupied(): call(occupied_kernel, [(CHIPS, QUARTER, lanes)], [SMEM] + [VMEM] * (1 + l...  4.48 us
    pallas_call x2, Pallas kernels, virtual(): call(functools.partial(virtual_kernel, core_off), [shape] if core_off els...  4.21 us
    pallas_call x1, Pallas kernels, dense_panel(): call(dense_kernel, [shape], [SMEM] * 3 + [VMEM] * len(pieces), (VMEM,), [...  2.64 us
  transfers between devices with their start and end apart: 28, of which 11 were waited for; matrix products, arithmetic and copies ran while one was open for 1% of the time, Pallas kernels for 10%

profile of v5, /device:TPU:1, one launch (start us, length us, event | category | flops | bytes accessed | tf_op | source)
XLA Modules:
  0.0 109.6 jit_solution(10303067776922453188)
XLA Ops:
  0.8 1.3 %shard_map.82.after_ref = bf16[32,16,128]{2,1,0:T(8,128)(2,1)} custom-call(s32[4]{0:T(128)S(1)} %pad_add_fusion.own_ref, bf16[1,2,64,64]{3,2,1,0:T(8,128)(2,1)S(1)} %copy-done.11), custom_call_target="tpu_custom_call" | custom-call | flops 1024 | bytes 1024 | tf_op jit(solution)/shard_map/pallas_call | solution.py:67
  2.1 11.9 %all-to-all-start.1 = ((bf16[32,16,128]{2,1,0:T(8,128)(2,1)}), bf16[32,16,128]{2,1,0:T(8,128)(2,1)S(1)}, u32[]{:S(2)}, u32[]{:S(2)}) async-start(bf16[32,16,128]{2,1,0:T(8,128)(2,1)} %shard_map.82.after_ref), calls=%async_computation.1 | async-start | bytes 262144 | tf_op jit(solution)/shard_map/all_to_all | solution.py:239
  15.7 7.7 %all-to-all-done.1.refs_0_ = bf16[32,16,128]{2,1,0:T(8,128)(2,1)S(1)} async-done(((bf16[32,16,128]{2,1,0:T(8,128)(2,1)}), bf16[32,16,128]{2,1,0:T(8,128)(2,1)S(1)}, u32[]{:S(2)}, u32[]{:S(2)}) %all-to-all-start.1) | async-done | bytes 131104 | tf_op jit(solution)/shard_map/all_to_all | solution.py:239
  23.3 3.9 %all-to-all-start = ((bf16[32,64,128]{2,1,0:T(8,128)(2,1)}), bf16[32,64,128]{2,1,0:T(8,128)(2,1)S(1)}, u32[]{:S(2)}, u32[]{:S(2)}) async-start(bf16[32,64,128]{2,1,0:T(8,128)(2,1)} %shard_map.83), calls=%async_computation | async-start | bytes 1048576 | tf_op jit(solution)/shard_map/all_to_all | solution.py:239
  29.6 1.2 %collective-permute-start.10 = (bf16[64,4096]{1,0:T(8,128)(2,1)S(1)}, bf16[64,4096]{1,0:T(8,128)(2,1)S(1)}, u32[]{:S(2)}, u32[]{:S(2)}) collective-permute-start(bf16[64,4096]{1,0:T(8,128)(2,1)S(1)} %shard_map.86.refs_0_), channel_id=1, source_target_pairs={{24,0},{0,8},{8,16},{16,24},{25,1},{1,9},{9,17},{17,25},{26,2},{2,... | collective-permute-start | bytes 1572872 | tf_op jit(solution)/shard_map/ppermute | solution.py:226
  30.8 1.6 %collective-permute-start.9 = (bf16[64,4096]{1,0:T(8,128)(2,1)S(1)}, bf16[64,4096]{1,0:T(8,128)(2,1)S(1)}, u32[]{:S(2)}, u32[]{:S(2)}) collective-permute-start(bf16[64,4096]{1,0:T(8,128)(2,1)S(1)} %shard_map.86.refs_0_), channel_id=1, source_target_pairs={{8,0},{16,8},{24,16},{0,24},{9,1},{17,9},{25,17},{1,25},{10,2},{18... | collective-permute-start | bytes 1572872 | tf_op jit(solution)/shard_map/ppermute | solution.py:226
  32.3 2.7 %collective-permute-start = (bf16[32,16,128]{2,1,0:T(8,128)(2,1)S(1)}, bf16[32,16,128]{2,1,0:T(8,128)(2,1)S(1)}, u32[]{:S(2)}, u32[]{:S(2)}) collective-permute-start(bf16[32,16,128]{2,1,0:T(8,128)(2,1)S(1)} %all-to-all-done.1.refs_0_), channel_id=1, source_target_pairs={{1,0},{2,1},{3,2},{0,3},{5,4},{6,5},{7,6},{4,7},{9,8},{10,9},{11,1... | collective-permute-start | bytes 393224 | tf_op jit(solution)/shard_map/ppermute | solution.py:226
  35.1 2.9 %collective-permute-start.13 = (bf16[64,4096]{1,0:T(8,128)(2,1)S(1)}, bf16[64,4096]{1,0:T(8,128)(2,1)S(1)}, u32[]{:S(2)}, u32[]{:S(2)}) collective-permute-start(bf16[64,4096]{1,0:T(8,128)(2,1)S(1)} %shard_map.86.refs_0_), channel_id=1, source_target_pairs={{4,0},{0,4},{5,1},{1,5},{6,2},{2,6},{7,3},{3,7},{12,8},{8,12},{13,... | collective-permute-start | bytes 1572872 | tf_op jit(solution)/shard_map/ppermute | solution.py:226
  39.0 5.6 %collective-permute-done.1.refs_2_.refs_3_ = bf16[32,16,128]{2,1,0:T(8,128)(2,1)S(1)} collective-permute-done((bf16[32,16,128]{2,1,0:T(8,128)(2,1)S(1)}, bf16[32,16,128]{2,1,0:T(8,128)(2,1)S(1)}, u32[]{:S(2)}, u32[]{:S(2)}) %collective-permute-start.1) | collective-permute-done | bytes 131104 | tf_op jit(solution)/shard_map/ppermute | solution.py:226
  46.4 2.3 %collective-permute-done.10.refs_1_ = bf16[64,4096]{1,0:T(8,128)(2,1)S(1)} collective-permute-done((bf16[64,4096]{1,0:T(8,128)(2,1)S(1)}, bf16[64,4096]{1,0:T(8,128)(2,1)S(1)}, u32[]{:S(2)}, u32[]{:S(2)}) %collective-permute-start.10) | collective-permute-done | bytes 524320 | tf_op jit(solution)/shard_map/ppermute | solution.py:226
  49.4 2.3 %collective-permute-start.6 = (bf16[32,16,128]{2,1,0:T(8,128)(2,1)S(1)}, bf16[32,16,128]{2,1,0:T(8,128)(2,1)S(1)}, u32[]{:S(2)}, u32[]{:S(2)}) collective-permute-start(bf16[32,16,128]{2,1,0:T(8,128)(2,1)S(1)} %collective-permute-done.refs_1_.refs_2_), channel_id=1, source_target_pairs={{4,0},{0,4},{5,1},{1,5},{6,2},{2,6},{7,3},{3,7},{12,8},{8,12},{13,... | collective-permute-start | bytes 393224 | tf_op jit(solution)/shard_map/ppermute | solution.py:226
  52.4 2.3 %collective-permute-start.12 = (bf16[32,4096]{1,0:T(8,128)(2,1)}, bf16[32,4096]{1,0:T(8,128)(2,1)}, u32[]{:S(2)}, u32[]{:S(2)}) collective-permute-start(bf16[32,4096]{1,0:T(8,128)(2,1)} %slice.13), channel_id=1, source_target_pairs={{8,0},{16,8},{24,16},{0,24},{9,1},{17,9},{25,17},{1,25},{10,2},{18... | collective-permute-start | bytes 786440 | tf_op jit(solution)/shard_map/ppermute | solution.py:226
  57.2 2.5 %collective-permute-start.16 = (bf16[32,4096]{1,0:T(8,128)(2,1)}, bf16[32,4096]{1,0:T(8,128)(2,1)S(1)}, u32[]{:S(2)}, u32[]{:S(2)}) collective-permute-start(bf16[32,4096]{1,0:T(8,128)(2,1)} %collective-permute-done.11.refs_3_), channel_id=1, source_target_pairs={{4,0},{0,4},{5,1},{1,5},{6,2},{2,6},{7,3},{3,7},{12,8},{8,12},{13,... | collective-permute-start | bytes 786440 | tf_op jit(solution)/shard_map/ppermute | solution.py:226
  60.5 2.7 %collective-permute-start.3 = (bf16[32,64,128]{2,1,0:T(8,128)(2,1)S(1)}, bf16[32,64,128]{2,1,0:T(8,128)(2,1)S(1)}, u32[]{:S(2)}, u32[]{:S(2)}) collective-permute-start(bf16[32,64,128]{2,1,0:T(8,128)(2,1)S(1)} %shard_map.84.refs_0_), channel_id=1, source_target_pairs={{1,0},{2,1},{3,2},{0,3},{5,4},{6,5},{7,6},{4,7},{9,8},{10,9},{11,1... | collective-permute-start | bytes 1572872 | tf_op jit(solution)/shard_map/ppermute | solution.py:226
  68.0 2.6 %shard_map.85.dense_ref = bf16[512,4096]{1,0:T(8,128)(2,1)S(1)} custom-call(s32[8,64]{1,0:T(8,128)S(1)} %bitcast.9, s32[64]{0:T(128)S(1)} %copy-done.17, s32[4]{0:T(128)S(1)} %pad_add_fusion.own_ref, bf16[32,16,128]{2,1,0:T(8,128)(2,1)S(1)} %copy-done.3, bf16[32,16,128]{2,1,0:T(8,128)(2,1)S(1)} %collective-permute-done.refs_1_.refs_2_, ...), custom_call_target="tpu_custom_call" | custom-call | flops 1024 | bytes 1024 | tf_op jit(solution)/shard_map/pallas_call | solution.py:117
  70.7 4.5 %shard_map.88.refs_2_.refs_0_ = bf16[32,16,512]{2,1,0:T(8,128)(2,1)} custom-call(s32[4]{0:T(128)S(1)} %pad_add_fusion.own_ref, bf16[512,4096]{1,0:T(8,128)(2,1)S(1)} %shard_map.85.dense_ref, bf16[64,4096]{1,0:T(8,128)(2,1)S(1)} %shard_map.86.refs_0_, bf16[64,4096]{1,0:T(8,128)(2,1)S(1)} %get-tuple-element.16.refs_1_, ...), custom_call_target="tpu_custom_call" | custom-call | flops 1024 | bytes 1024 | tf_op jit(solution)/shard_map/pallas_call | solution.py:144
  75.2 2.2 %collective-permute-done.4.refs_1_ = bf16[32,64,128]{2,1,0:T(8,128)(2,1)S(1)} collective-permute-done((bf16[32,64,128]{2,1,0:T(8,128)(2,1)S(1)}, bf16[32,64,128]{2,1,0:T(8,128)(2,1)S(1)}, u32[]{:S(2)}, u32[]{:S(2)}) %collective-permute-start.4) | collective-permute-done | bytes 524320 | tf_op jit(solution)/shard_map/ppermute | solution.py:226
  77.4 7.1 %all-to-all-start.2 = ((bf16[32,16,512]{2,1,0:T(8,128)(2,1)}), bf16[32,16,512]{2,1,0:T(8,128)(2,1)S(1)}, u32[]{:S(2)}, u32[]{:S(2)}) async-start(bf16[32,16,512]{2,1,0:T(8,128)(2,1)} %shard_map.90), calls=%async_computation.2 | async-start | bytes 1048576 | tf_op jit(solution)/shard_map/all_to_all | solution.py:239
  84.6 2.7 %collective-permute-start.19 = (bf16[16,64,128]{2,1,0:T(8,128)(2,1)S(1)}, bf16[16,64,128]{2,1,0:T(8,128)(2,1)S(1)}, u32[]{:S(2)}, u32[]{:S(2)}) collective-permute-start(bf16[16,64,128]{2,1,0:T(8,128)(2,1)S(1)} %slice.15), channel_id=1, source_target_pairs={{1,0},{2,1},{3,2},{0,3},{5,4},{6,5},{7,6},{4,7},{9,8},{10,9},{11,1... | collective-permute-start | bytes 786440 | tf_op jit(solution)/shard_map/ppermute | solution.py:226
  87.3 4.4 %collective-permute-done.18.refs_3_ = bf16[16,64,128]{2,1,0:T(8,128)(2,1)S(1)} collective-permute-done((bf16[16,64,128]{2,1,0:T(8,128)(2,1)S(1)}, bf16[16,64,128]{2,1,0:T(8,128)(2,1)S(1)}, u32[]{:S(2)}, u32[]{:S(2)}) %collective-permute-start.18) | collective-permute-done | bytes 262176 | tf_op jit(solution)/shard_map/ppermute | solution.py:226
  91.7 7.8 %all-to-all-done.2.refs_5_ = bf16[32,16,512]{2,1,0:T(8,128)(2,1)S(1)} async-done(((bf16[32,16,512]{2,1,0:T(8,128)(2,1)}), bf16[32,16,512]{2,1,0:T(8,128)(2,1)S(1)}, u32[]{:S(2)}, u32[]{:S(2)}) %all-to-all-start.2) | async-done | bytes 524320 | tf_op jit(solution)/shard_map/all_to_all | solution.py:239
  99.5 3.8 %collective-permute-start.20 = (bf16[32,64,128]{2,1,0:T(8,128)(2,1)S(1)}, bf16[32,64,128]{2,1,0:T(8,128)(2,1)S(1)}, u32[]{:S(2)}, u32[]{:S(2)}) collective-permute-start(bf16[32,64,128]{2,1,0:T(8,128)(2,1)S(1)} %get-tuple-element.20.refs_0_), channel_id=1, source_target_pairs={{4,0},{0,4},{5,1},{1,5},{6,2},{2,6},{7,3},{3,7},{12,8},{8,12},{13,... | collective-permute-start | bytes 1572872 | tf_op jit(solution)/shard_map/ppermute | solution.py:226
  104.3 1.8 %shard_map.92 = (bf16[64,4096]{1,0:T(8,128)(2,1)S(1)}, bf16[64,64,128]{2,1,0:T(8,128)(2,1)S(1)}) custom-call(s32[8,64]{1,0:T(8,128)S(1)} %bitcast.7, s32[64]{0:T(128)S(1)} %copy-done.15, s32[4]{0:T(128)S(1)} %pad_add_fusion.own_ref, bf16[32,64,128]{2,1,0:T(8,128)(2,1)S(1)} %get-tuple-element.20.refs_0_, bf16[32,64,128]{2,1,0:T(8,128)(2,1)S(1)} %get-tuple-element.21.refs_1_, ...), custom_call_target="tpu_custom_call" | custom-call | flops 1024 | bytes 1024 | tf_op jit(solution)/shard_map/pallas_call | solution.py:215
  107.1 2.4 %shard_map.93 = bf16[64,4096]{1,0:T(8,128)(2,1)} custom-call(s32[8,64]{1,0:T(8,128)S(1)} %bitcast.8, s32[64]{0:T(128)S(1)} %copy-done.15, s32[4]{0:T(128)S(1)} %pad_add_fusion.own_ref, bf16[32,64,128]{2,1,0:T(8,128)(2,1)S(1)} %collective-permute-done.20.refs_0_, bf16[32,64,128]{2,1,0:T(8,128)(2,1)S(1)} %collective-permute-done.21.refs_1_, ...), custom_call_target="tpu_custom_call" | custom-call | flops 1024 | bytes 1024 | tf_op jit(solution)/shard_map/pallas_call | solution.py:215
  (85 shorter events, 19.2 us)
Async XLA Ops:
  2.1 21.2 %all-to-all-start.1 = ((bf16[32,16,128]{2,1,0:T(8,128)(2,1)}), bf16[32,16,128]{2,1,0:T(8,128)(2,1)S(1)}, u32[]{:S(2)}, u32[]{:S(2)}) async-start(bf16[32,16,128]{2,1,0:T(8,128)(2,1)} %shard_map.82.after_ref), calls=%async_computation.1 | async-start | bytes 262144 | tf_op jit(solution)/shard_map/all_to_all | solution.py:239
  23.3 31.9 %all-to-all-start = ((bf16[32,64,128]{2,1,0:T(8,128)(2,1)}), bf16[32,64,128]{2,1,0:T(8,128)(2,1)S(1)}, u32[]{:S(2)}, u32[]{:S(2)}) async-start(bf16[32,64,128]{2,1,0:T(8,128)(2,1)} %shard_map.83), calls=%async_computation | async-start | bytes 1048576 | tf_op jit(solution)/shard_map/all_to_all | solution.py:239
  29.6 19.1 %collective-permute-start.10 = (bf16[64,4096]{1,0:T(8,128)(2,1)S(1)}, bf16[64,4096]{1,0:T(8,128)(2,1)S(1)}, u32[]{:S(2)}, u32[]{:S(2)}) collective-permute-start(bf16[64,4096]{1,0:T(8,128)(2,1)S(1)} %shard_map.86.refs_0_), channel_id=1, source_target_pairs={{24,0},{0,8},{8,16},{16,24},{25,1},{1,9},{9,17},{17,25},{26,2},{2,... | collective-permute-start | bytes 1572872 | tf_op jit(solution)/shard_map/ppermute | solution.py:226
  30.8 17.9 %collective-permute-start.9 = (bf16[64,4096]{1,0:T(8,128)(2,1)S(1)}, bf16[64,4096]{1,0:T(8,128)(2,1)S(1)}, u32[]{:S(2)}, u32[]{:S(2)}) collective-permute-start(bf16[64,4096]{1,0:T(8,128)(2,1)S(1)} %shard_map.86.refs_0_), channel_id=1, source_target_pairs={{8,0},{16,8},{24,16},{0,24},{9,1},{17,9},{25,17},{1,25},{10,2},{18... | collective-permute-start | bytes 1572872 | tf_op jit(solution)/shard_map/ppermute | solution.py:226
  32.3 6.0 %collective-permute-start = (bf16[32,16,128]{2,1,0:T(8,128)(2,1)S(1)}, bf16[32,16,128]{2,1,0:T(8,128)(2,1)S(1)}, u32[]{:S(2)}, u32[]{:S(2)}) collective-permute-start(bf16[32,16,128]{2,1,0:T(8,128)(2,1)S(1)} %all-to-all-done.1.refs_0_), channel_id=1, source_target_pairs={{1,0},{2,1},{3,2},{0,3},{5,4},{6,5},{7,6},{4,7},{9,8},{10,9},{11,1... | collective-permute-start | bytes 393224 | tf_op jit(solution)/shard_map/ppermute | solution.py:226
  35.1 24.6 %collective-permute-start.13 = (bf16[64,4096]{1,0:T(8,128)(2,1)S(1)}, bf16[64,4096]{1,0:T(8,128)(2,1)S(1)}, u32[]{:S(2)}, u32[]{:S(2)}) collective-permute-start(bf16[64,4096]{1,0:T(8,128)(2,1)S(1)} %shard_map.86.refs_0_), channel_id=1, source_target_pairs={{4,0},{0,4},{5,1},{1,5},{6,2},{2,6},{7,3},{3,7},{12,8},{8,12},{13,... | collective-permute-start | bytes 1572872 | tf_op jit(solution)/shard_map/ppermute | solution.py:226
  38.0 6.7 %collective-permute-start.1 = (bf16[32,16,128]{2,1,0:T(8,128)(2,1)S(1)}, bf16[32,16,128]{2,1,0:T(8,128)(2,1)S(1)}, u32[]{:S(2)}, u32[]{:S(2)}) collective-permute-start(bf16[32,16,128]{2,1,0:T(8,128)(2,1)S(1)} %all-to-all-done.1.refs_0_), channel_id=1, source_target_pairs={{2,0},{3,1},{0,2},{1,3},{6,4},{7,5},{4,6},{5,7},{10,8},{11,9},{8,1... | collective-permute-start | bytes 393224 | tf_op jit(solution)/shard_map/ppermute | solution.py:226
  38.3 8.1 %collective-permute-start.2 = (bf16[32,16,128]{2,1,0:T(8,128)(2,1)S(1)}, bf16[32,16,128]{2,1,0:T(8,128)(2,1)S(1)}, u32[]{:S(2)}, u32[]{:S(2)}) collective-permute-start(bf16[32,16,128]{2,1,0:T(8,128)(2,1)S(1)} %all-to-all-done.1.refs_0_), channel_id=1, source_target_pairs={{3,0},{0,1},{1,2},{2,3},{7,4},{4,5},{5,6},{6,7},{11,8},{8,9},{9,10... | collective-permute-start | bytes 393224 | tf_op jit(solution)/shard_map/ppermute | solution.py:226
  44.7 10.1 %collective-permute-start.5 = (bf16[32,16,128]{2,1,0:T(8,128)(2,1)S(1)}, bf16[32,16,128]{2,1,0:T(8,128)(2,1)S(1)}, u32[]{:S(2)}, u32[]{:S(2)}) collective-permute-start(bf16[32,16,128]{2,1,0:T(8,128)(2,1)S(1)} %all-to-all-done.1.refs_0_), channel_id=1, source_target_pairs={{4,0},{0,4},{5,1},{1,5},{6,2},{2,6},{7,3},{3,7},{12,8},{8,12},{13,... | collective-permute-start | bytes 393224 | tf_op jit(solution)/shard_map/ppermute | solution.py:226
  49.4 7.7 %collective-permute-start.11 = (bf16[32,4096]{1,0:T(8,128)(2,1)}, bf16[32,4096]{1,0:T(8,128)(2,1)}, u32[]{:S(2)}, u32[]{:S(2)}) collective-permute-start(bf16[32,4096]{1,0:T(8,128)(2,1)} %slice.12), channel_id=1, source_target_pairs={{24,0},{0,8},{8,16},{16,24},{25,1},{1,9},{9,17},{17,25},{26,2},{2,... | collective-permute-start | bytes 786440 | tf_op jit(solution)/shard_map/ppermute | solution.py:226
  49.4 5.6 %collective-permute-start.6 = (bf16[32,16,128]{2,1,0:T(8,128)(2,1)S(1)}, bf16[32,16,128]{2,1,0:T(8,128)(2,1)S(1)}, u32[]{:S(2)}, u32[]{:S(2)}) collective-permute-start(bf16[32,16,128]{2,1,0:T(8,128)(2,1)S(1)} %collective-permute-done.refs_1_.refs_2_), channel_id=1, source_target_pairs={{4,0},{0,4},{5,1},{1,5},{6,2},{2,6},{7,3},{3,7},{12,8},{8,12},{13,... | collective-permute-start | bytes 393224 | tf_op jit(solution)/shard_map/ppermute | solution.py:226
  52.4 10.8 %collective-permute-start.12 = (bf16[32,4096]{1,0:T(8,128)(2,1)}, bf16[32,4096]{1,0:T(8,128)(2,1)}, u32[]{:S(2)}, u32[]{:S(2)}) collective-permute-start(bf16[32,4096]{1,0:T(8,128)(2,1)} %slice.13), channel_id=1, source_target_pairs={{8,0},{16,8},{24,16},{0,24},{9,1},{17,9},{25,17},{1,25},{10,2},{18... | collective-permute-start | bytes 786440 | tf_op jit(solution)/shard_map/ppermute | solution.py:226
  55.0 4.7 %collective-permute-start.8 = (bf16[32,16,128]{2,1,0:T(8,128)(2,1)S(1)}, bf16[32,16,128]{2,1,0:T(8,128)(2,1)}, u32[]{:S(2)}, u32[]{:S(2)}) collective-permute-start(bf16[32,16,128]{2,1,0:T(8,128)(2,1)S(1)} %collective-permute-done.2.refs_3_.refs_4_), channel_id=1, source_target_pairs={{4,0},{0,4},{5,1},{1,5},{6,2},{2,6},{7,3},{3,7},{12,8},{8,12},{13,... | collective-permute-start | bytes 393224 | tf_op jit(solution)/shard_map/ppermute | solution.py:226
  56.7 14.0 %collective-permute-start.14 = (bf16[64,4096]{1,0:T(8,128)(2,1)S(1)}, bf16[64,4096]{1,0:T(8,128)(2,1)S(1)}, u32[]{:S(2)}, u32[]{:S(2)}) collective-permute-start(bf16[64,4096]{1,0:T(8,128)(2,1)S(1)} %get-tuple-element.16.refs_1_), channel_id=1, source_target_pairs={{4,0},{0,4},{5,1},{1,5},{6,2},{2,6},{7,3},{3,7},{12,8},{8,12},{13,... | collective-permute-start | bytes 1572872 | tf_op jit(solution)/shard_map/ppermute | solution.py:226
  57.2 6.4 %collective-permute-start.16 = (bf16[32,4096]{1,0:T(8,128)(2,1)}, bf16[32,4096]{1,0:T(8,128)(2,1)S(1)}, u32[]{:S(2)}, u32[]{:S(2)}) collective-permute-start(bf16[32,4096]{1,0:T(8,128)(2,1)} %collective-permute-done.11.refs_3_), channel_id=1, source_target_pairs={{4,0},{0,4},{5,1},{1,5},{6,2},{2,6},{7,3},{3,7},{12,8},{8,12},{13,... | collective-permute-start | bytes 786440 | tf_op jit(solution)/shard_map/ppermute | solution.py:226
  59.7 11.0 %collective-permute-start.15 = (bf16[64,4096]{1,0:T(8,128)(2,1)S(1)}, bf16[64,4096]{1,0:T(8,128)(2,1)S(1)}, u32[]{:S(2)}, u32[]{:S(2)}) collective-permute-start(bf16[64,4096]{1,0:T(8,128)(2,1)S(1)} %get-tuple-element.17.refs_2_), channel_id=1, source_target_pairs={{4,0},{0,4},{5,1},{1,5},{6,2},{2,6},{7,3},{3,7},{12,8},{8,12},{13,... | collective-permute-start | bytes 1572872 | tf_op jit(solution)/shard_map/ppermute | solution.py:226
  60.5 14.7 %collective-permute-start.3 = (bf16[32,64,128]{2,1,0:T(8,128)(2,1)S(1)}, bf16[32,64,128]{2,1,0:T(8,128)(2,1)S(1)}, u32[]{:S(2)}, u32[]{:S(2)}) collective-permute-start(bf16[32,64,128]{2,1,0:T(8,128)(2,1)S(1)} %shard_map.84.refs_0_), channel_id=1, source_target_pairs={{1,0},{2,1},{3,2},{0,3},{5,4},{6,5},{7,6},{4,7},{9,8},{10,9},{11,1... | collective-permute-start | bytes 1572872 | tf_op jit(solution)/shard_map/ppermute | solution.py:226
  63.3 14.1 %collective-permute-start.4 = (bf16[32,64,128]{2,1,0:T(8,128)(2,1)S(1)}, bf16[32,64,128]{2,1,0:T(8,128)(2,1)S(1)}, u32[]{:S(2)}, u32[]{:S(2)}) collective-permute-start(bf16[32,64,128]{2,1,0:T(8,128)(2,1)S(1)} %shard_map.84.refs_0_), channel_id=1, source_target_pairs={{3,0},{0,1},{1,2},{2,3},{7,4},{4,5},{5,6},{6,7},{11,8},{8,9},{9,10... | collective-permute-start | bytes 1572872 | tf_op jit(solution)/shard_map/ppermute | solution.py:226
  63.5 7.1 %collective-permute-start.17 = (bf16[32,4096]{1,0:T(8,128)(2,1)}, bf16[32,4096]{1,0:T(8,128)(2,1)S(1)}, u32[]{:S(2)}, u32[]{:S(2)}) collective-permute-start(bf16[32,4096]{1,0:T(8,128)(2,1)} %collective-permute-done.12.refs_4_), channel_id=1, source_target_pairs={{4,0},{0,4},{5,1},{1,5},{6,2},{2,6},{7,3},{3,7},{12,8},{8,12},{13,... | collective-permute-start | bytes 786440 | tf_op jit(solution)/shard_map/ppermute | solution.py:226
  77.4 22.1 %all-to-all-start.2 = ((bf16[32,16,512]{2,1,0:T(8,128)(2,1)}), bf16[32,16,512]{2,1,0:T(8,128)(2,1)S(1)}, u32[]{:S(2)}, u32[]{:S(2)}) async-start(bf16[32,16,512]{2,1,0:T(8,128)(2,1)} %shard_map.90), calls=%async_computation.2 | async-start | bytes 1048576 | tf_op jit(solution)/shard_map/all_to_all | solution.py:239
  84.5 7.1 %collective-permute-start.18 = (bf16[16,64,128]{2,1,0:T(8,128)(2,1)S(1)}, bf16[16,64,128]{2,1,0:T(8,128)(2,1)S(1)}, u32[]{:S(2)}, u32[]{:S(2)}) collective-permute-start(bf16[16,64,128]{2,1,0:T(8,128)(2,1)S(1)} %slice.14), channel_id=1, source_target_pairs={{3,0},{0,1},{1,2},{2,3},{7,4},{4,5},{5,6},{6,7},{11,8},{8,9},{9,10... | collective-permute-start | bytes 786440 | tf_op jit(solution)/shard_map/ppermute | solution.py:226
  84.6 7.0 %collective-permute-start.19 = (bf16[16,64,128]{2,1,0:T(8,128)(2,1)S(1)}, bf16[16,64,128]{2,1,0:T(8,128)(2,1)S(1)}, u32[]{:S(2)}, u32[]{:S(2)}) collective-permute-start(bf16[16,64,128]{2,1,0:T(8,128)(2,1)S(1)} %slice.15), channel_id=1, source_target_pairs={{1,0},{2,1},{3,2},{0,3},{5,4},{6,5},{7,6},{4,7},{9,8},{10,9},{11,1... | collective-permute-start | bytes 786440 | tf_op jit(solution)/shard_map/ppermute | solution.py:226
  99.5 7.6 %collective-permute-start.20 = (bf16[32,64,128]{2,1,0:T(8,128)(2,1)S(1)}, bf16[32,64,128]{2,1,0:T(8,128)(2,1)S(1)}, u32[]{:S(2)}, u32[]{:S(2)}) collective-permute-start(bf16[32,64,128]{2,1,0:T(8,128)(2,1)S(1)} %get-tuple-element.20.refs_0_), channel_id=1, source_target_pairs={{4,0},{0,4},{5,1},{1,5},{6,2},{2,6},{7,3},{3,7},{12,8},{8,12},{13,... | collective-permute-start | bytes 1572872 | tf_op jit(solution)/shard_map/ppermute | solution.py:226
  103.3 3.8 %collective-permute-start.21 = (bf16[32,64,128]{2,1,0:T(8,128)(2,1)S(1)}, bf16[32,64,128]{2,1,0:T(8,128)(2,1)S(1)}, u32[]{:S(2)}, u32[]{:S(2)}) collective-permute-start(bf16[32,64,128]{2,1,0:T(8,128)(2,1)S(1)} %get-tuple-element.21.refs_1_), channel_id=1, source_target_pairs={{4,0},{0,4},{5,1},{1,5},{6,2},{2,6},{7,3},{3,7},{12,8},{8,12},{13,... | collective-permute-start | bytes 1572872 | tf_op jit(solution)/shard_map/ppermute | solution.py:226
  (22 other events, 270.8 us)

commit v6 on v4

--- a/solution.py
+++ b/solution.py
@@ -24,7 +24,7 @@
     return jnp.concatenate([tile[:, BLOCK:], tile[:, :BLOCK]], axis=1)
 
 
-def call(kernel, outs, in_specs, out_specs, scratch=(), mib=16, flops=2**18, moved=2**20):
+def call(kernel, outs, in_specs, out_specs, scratch=(), mib=16):
     return pl.pallas_call(
         kernel,
         out_shape=tuple(jax.ShapeDtypeStruct(shape, jnp.bfloat16) for shape in outs),
@@ -32,7 +32,7 @@
         out_specs=out_specs,
         scratch_shapes=list(scratch),
         compiler_params=pltpu.CompilerParams(vmem_limit_bytes=mib * 2**20),
-        cost_estimate=pl.CostEstimate(flops=flops, bytes_accessed=moved, transcendentals=0),
+        cost_estimate=pl.CostEstimate(flops=2**10, bytes_accessed=2**10, transcendentals=0),
     )
 
 
@@ -134,8 +134,6 @@
         (VMEM,),
         [pltpu.VMEM((len(pieces) * CHIPS, QUARTER, WIDTH), jnp.bfloat16)],
         mib=8,
-        flops=2**20,
-        moved=2**23,
     )(occ_index.T, second_map, own, *pieces)[0]
 
 
@@ -162,8 +160,6 @@
         [SMEM] + [VMEM] * (1 + len(rows)),
         (VMEM,),
         [pltpu.VMEM((lanes, BASIS), jnp.bfloat16)],
-        flops=2 * dense.size * lanes,
-        moved=2**23,
     )(own, dense, *rows)[0]
 
 
@@ -235,8 +231,6 @@
         [SMEM] * 3 + [VMEM] * (len(panels) + len(rest)),
         (ANYWHERE,) if core_off else (VMEM, VMEM),
         scratch,
-        flops=2 * MOLECULES // 2 * BLOCK * BASIS // 8 * BLOCK,
-        moved=2**22,
     )(virt_index.T, first_map, own, *panels, *rest)
 
 
@@ -265,7 +259,7 @@
     both = exchange(spread(own, occ_blocks, virt_blocks))
     occ_plane, virt_plane = divide(both)
     pieces = [occ_plane] + [shift(occ_plane, "y", by) for by in range(1, Y)]
-    rows = ring(mask_rows(pair_mask, b_tensor), "x", *pieces[1:])
+    rows = ring(mask_rows(pair_mask, b_tensor), "x", occ_plane)
     rows = rows + [shift(part, "core", 1) for part in rows]
     (virt_plane,) = tie([virt_plane], *pieces[1:])
     pieces = pieces + [shift(piece, "core", 1) for piece in pieces]

time: 104 us -> 98.2 us (0.944)
  waiting for transfers between devices: 37.9 us -> 31.7 us
    ppermute x25, waiting for transfers between devices: 18 us -> 11.9 us  [shift(): lax.ppermute(array, axis, [((i + by) % size, i) for i in range(size)])]
    all_to_all x2, starting transfers between devices: 17.9 us -> 19.1 us  [exchange(): lax.all_to_all(array, ('z', 'x'), split_axis=0, concat_axis=0, tiled=True)]
  transfers between devices with their start and end apart: 27 -> 27, of which waited for: 12 -> 8; matrix products, arithmetic and copies ran while one was open for 0% -> 0% of each run, Pallas kernels for 9% -> 10%
where the time goes in v6:
time: 98.2 us; the launch traced here: 97.7 us
  starting transfers between devices  49.1 us (50%)
  waiting for transfers between devices  31.7 us (32%)
  Pallas kernels  13.2 us (13%)
  local copies, waits for them, and re-layouts  3.3 us (3%)
    ppermute x25, starting transfers between devices, shift(): lax.ppermute(array, axis, [((i + by) % size, i) for i in range(size)])  30 us
    all_to_all x2, waiting for transfers between devices, exchange(): lax.all_to_all(array, ('z', 'x'), split_axis=0, concat_axis=0, tiled=True)  19.9 us
    all_to_all x2, starting transfers between devices, exchange(): lax.all_to_all(array, ('z', 'x'), split_axis=0, concat_axis=0, tiled=True)  19.1 us
    ppermute x25, waiting for transfers between devices, shift(): lax.ppermute(array, axis, [((i + by) % size, i) for i in range(size)])  11.9 us
    pallas_call x1, Pallas kernels, occupied(): call(occupied_kernel, [(CHIPS, QUARTER, lanes)], [SMEM] + [VMEM] * (1 + l...  4.5 us
    pallas_call x2, Pallas kernels, virtual(): call(functools.partial(virtual_kernel, core_off), [shape] if core_off els...  4.21 us
    unnamed x16, local copies, waits for them, and re-layouts  3.22 us
    pallas_call x1, Pallas kernels, dense_panel(): call(dense_kernel, [shape], [SMEM] * 3 + [VMEM] * len(pieces), (VMEM,), [...  2.34 us
  transfers between devices with their start and end apart: 27, of which 8 were waited for; matrix products, arithmetic and copies ran while one was open for 0% of the time, Pallas kernels for 10%

profile of v6, /device:TPU:1, one launch (start us, length us, event | category | flops | bytes accessed | tf_op | source)
XLA Modules:
  0.0 97.7 jit_solution(17383058600186571566)
XLA Ops:
  1.6 1.5 %shard_map.82 = bf16[32,80,128]{2,1,0:T(8,128)(2,1)} custom-call(s32[4]{0:T(128)S(1)} %pad_add_fusion.own_ref, bf16[1,2,64,64]{3,2,1,0:T(8,128)(2,1)S(1)} %copy-done.1, bf16[1,2,64,64]{3,2,1,0:T(8,128)(2,1)S(1)} %copy-done.2), custom_call_target="tpu_custom_call" | custom-call | flops 1024 | bytes 1024 | tf_op jit(solution)/shard_map/pallas_call | solution.py:62
  3.1 11.9 %all-to-all-start = ((bf16[32,80,128]{2,1,0:T(8,128)(2,1)}), bf16[32,80,128]{2,1,0:T(8,128)(2,1)S(1)}, u32[]{:S(2)}, u32[]{:S(2)}) async-start(bf16[32,80,128]{2,1,0:T(8,128)(2,1)} %shard_map.82), calls=%async_computation | async-start | bytes 1310720 | tf_op jit(solution)/shard_map/all_to_all | solution.py:252
  17.3 1.3 %collective-permute-start.10 = (bf16[64,4096]{1,0:T(8,128)(2,1)S(1)}, bf16[64,4096]{1,0:T(8,128)(2,1)S(1)}, u32[]{:S(2)}, u32[]{:S(2)}) collective-permute-start(bf16[64,4096]{1,0:T(8,128)(2,1)S(1)} %shard_map.86.refs_0_), channel_id=1, source_target_pairs={{24,0},{0,8},{8,16},{16,24},{25,1},{1,9},{9,17},{17,25},{26,2},{2,... | collective-permute-start | bytes 1572872 | tf_op jit(solution)/shard_map/ppermute | solution.py:239
  18.6 1.4 %collective-permute-start.9 = (bf16[64,4096]{1,0:T(8,128)(2,1)S(1)}, bf16[64,4096]{1,0:T(8,128)(2,1)S(1)}, u32[]{:S(2)}, u32[]{:S(2)}) collective-permute-start(bf16[64,4096]{1,0:T(8,128)(2,1)S(1)} %shard_map.86.refs_0_), channel_id=1, source_target_pairs={{8,0},{16,8},{24,16},{0,24},{9,1},{17,9},{25,17},{1,25},{10,2},{18... | collective-permute-start | bytes 1572872 | tf_op jit(solution)/shard_map/ppermute | solution.py:239
  20.1 1.5 %collective-permute-start.13 = (bf16[64,4096]{1,0:T(8,128)(2,1)S(1)}, bf16[64,4096]{1,0:T(8,128)(2,1)}, u32[]{:S(2)}, u32[]{:S(2)}) collective-permute-start(bf16[64,4096]{1,0:T(8,128)(2,1)S(1)} %shard_map.86.refs_0_), channel_id=1, source_target_pairs={{4,0},{0,4},{5,1},{1,5},{6,2},{2,6},{7,3},{3,7},{12,8},{8,12},{13,... | collective-permute-start | bytes 1572872 | tf_op jit(solution)/shard_map/ppermute | solution.py:239
  21.6 12.1 %all-to-all-done.both_ref = bf16[32,80,128]{2,1,0:T(8,128)(2,1)S(1)} async-done(((bf16[32,80,128]{2,1,0:T(8,128)(2,1)}), bf16[32,80,128]{2,1,0:T(8,128)(2,1)S(1)}, u32[]{:S(2)}, u32[]{:S(2)}) %all-to-all-start) | async-done | bytes 655392 | tf_op jit(solution)/shard_map/all_to_all | solution.py:252
  33.7 2.8 %collective-permute-start = (bf16[32,16,128]{2,1,0:T(8,128)(2,1)S(1)}, bf16[32,16,128]{2,1,0:T(8,128)(2,1)S(1)}, u32[]{:S(2)}, u32[]{:S(2)}) collective-permute-start(bf16[32,16,128]{2,1,0:T(8,128)(2,1)S(1)} %get-tuple-element.19.refs_0_.refs_2_), channel_id=1, source_target_pairs={{1,0},{2,1},{3,2},{0,3},{5,4},{6,5},{7,6},{4,7},{9,8},{10,9},{11,1... | collective-permute-start | bytes 393224 | tf_op jit(solution)/shard_map/ppermute | solution.py:239
  37.9 1.3 %collective-permute-start.2 = (bf16[32,16,128]{2,1,0:T(8,128)(2,1)S(1)}, bf16[32,16,128]{2,1,0:T(8,128)(2,1)S(1)}, u32[]{:S(2)}, u32[]{:S(2)}) collective-permute-start(bf16[32,16,128]{2,1,0:T(8,128)(2,1)S(1)} %get-tuple-element.19.refs_0_.refs_2_), channel_id=1, source_target_pairs={{3,0},{0,1},{1,2},{2,3},{7,4},{4,5},{5,6},{6,7},{11,8},{8,9},{9,10... | collective-permute-start | bytes 393224 | tf_op jit(solution)/shard_map/ppermute | solution.py:239
  39.3 2.9 %collective-permute-start.5 = (bf16[32,16,128]{2,1,0:T(8,128)(2,1)S(1)}, bf16[32,16,128]{2,1,0:T(8,128)(2,1)S(1)}, u32[]{:S(2)}, u32[]{:S(2)}) collective-permute-start(bf16[32,16,128]{2,1,0:T(8,128)(2,1)S(1)} %get-tuple-element.19.refs_0_.refs_2_), channel_id=1, source_target_pairs={{4,0},{0,4},{5,1},{1,5},{6,2},{2,6},{7,3},{3,7},{12,8},{8,12},{13,... | collective-permute-start | bytes 393224 | tf_op jit(solution)/shard_map/ppermute | solution.py:239
  42.3 1.8 %collective-permute-start.12 = (bf16[32,4096]{1,0:T(8,128)(2,1)S(1)}, bf16[32,4096]{1,0:T(8,128)(2,1)S(1)}, u32[]{:S(2)}, u32[]{:S(2)}) collective-permute-start(bf16[32,4096]{1,0:T(8,128)(2,1)S(1)} %slice.13), channel_id=1, source_target_pairs={{8,0},{16,8},{24,16},{0,24},{9,1},{17,9},{25,17},{1,25},{10,2},{18... | collective-permute-start | bytes 786440 | tf_op jit(solution)/shard_map/ppermute | solution.py:239
  44.1 2.3 %collective-permute-start.6 = (bf16[32,16,128]{2,1,0:T(8,128)(2,1)S(1)}, bf16[32,16,128]{2,1,0:T(8,128)(2,1)S(1)}, u32[]{:S(2)}, u32[]{:S(2)}) collective-permute-start(bf16[32,16,128]{2,1,0:T(8,128)(2,1)S(1)} %collective-permute-done.refs_1_), channel_id=1, source_target_pairs={{4,0},{0,4},{5,1},{1,5},{6,2},{2,6},{7,3},{3,7},{12,8},{8,12},{13,... | collective-permute-start | bytes 393224 | tf_op jit(solution)/shard_map/ppermute | solution.py:239
  47.9 1.3 %collective-permute-start.16 = (bf16[32,4096]{1,0:T(8,128)(2,1)S(1)}, bf16[32,4096]{1,0:T(8,128)(2,1)S(1)}, u32[]{:S(2)}, u32[]{:S(2)}) collective-permute-start(bf16[32,4096]{1,0:T(8,128)(2,1)S(1)} %collective-permute-done.11.refs_3_), channel_id=1, source_target_pairs={{4,0},{0,4},{5,1},{1,5},{6,2},{2,6},{7,3},{3,7},{12,8},{8,12},{13,... | collective-permute-start | bytes 786440 | tf_op jit(solution)/shard_map/ppermute | solution.py:239
  49.2 1.9 %collective-permute-start.3 = (bf16[32,64,128]{2,1,0:T(8,128)(2,1)S(1)}, bf16[32,64,128]{2,1,0:T(8,128)(2,1)S(1)}, u32[]{:S(2)}, u32[]{:S(2)}) collective-permute-start(bf16[32,64,128]{2,1,0:T(8,128)(2,1)S(1)} %shard_map.84.refs_0_), channel_id=1, source_target_pairs={{1,0},{2,1},{3,2},{0,3},{5,4},{6,5},{7,6},{4,7},{9,8},{10,9},{11,1... | collective-permute-start | bytes 1572872 | tf_op jit(solution)/shard_map/ppermute | solution.py:239
  53.0 2.3 %shard_map.85.dense_ref = bf16[512,4096]{1,0:T(8,128)(2,1)S(1)} custom-call(s32[8,64]{1,0:T(8,128)S(1)} %bitcast.9, s32[64]{0:T(128)S(1)} %copy-done.7, s32[4]{0:T(128)S(1)} %pad_add_fusion.own_ref, bf16[32,16,128]{2,1,0:T(8,128)(2,1)S(1)} %get-tuple-element.19.refs_0_.refs_2_, bf16[32,16,128]{2,1,0:T(8,128)(2,1)S(1)} %collective-permute-done.refs_1_, ...), custom_call_target="tpu_custom_call" | custom-call | flops 1024 | bytes 1024 | tf_op jit(solution)/shard_map/pallas_call | solution.py:130
  55.3 4.5 %shard_map.88.refs_2_.refs_0_ = bf16[32,16,512]{2,1,0:T(8,128)(2,1)} custom-call(s32[4]{0:T(128)S(1)} %pad_add_fusion.own_ref, bf16[512,4096]{1,0:T(8,128)(2,1)S(1)} %shard_map.85.dense_ref, bf16[64,4096]{1,0:T(8,128)(2,1)S(1)} %shard_map.86.refs_0_, bf16[64,4096]{1,0:T(8,128)(2,1)S(1)} %get-tuple-element.20.refs_1_, ...), custom_call_target="tpu_custom_call" | custom-call | flops 1024 | bytes 1024 | tf_op jit(solution)/shard_map/pallas_call | solution.py:157
  59.8 2.5 %collective-permute-done.3.refs_0_ = bf16[32,64,128]{2,1,0:T(8,128)(2,1)S(1)} collective-permute-done((bf16[32,64,128]{2,1,0:T(8,128)(2,1)S(1)}, bf16[32,64,128]{2,1,0:T(8,128)(2,1)S(1)}, u32[]{:S(2)}, u32[]{:S(2)}) %collective-permute-start.3) | collective-permute-done | bytes 524320 | tf_op jit(solution)/shard_map/ppermute | solution.py:239
  62.4 3.0 %collective-permute-done.4.refs_1_ = bf16[32,64,128]{2,1,0:T(8,128)(2,1)S(1)} collective-permute-done((bf16[32,64,128]{2,1,0:T(8,128)(2,1)S(1)}, bf16[32,64,128]{2,1,0:T(8,128)(2,1)S(1)}, u32[]{:S(2)}, u32[]{:S(2)}) %collective-permute-start.4) | collective-permute-done | bytes 524320 | tf_op jit(solution)/shard_map/ppermute | solution.py:239
  65.4 7.2 %all-to-all-start.1 = ((bf16[32,16,512]{2,1,0:T(8,128)(2,1)}), bf16[32,16,512]{2,1,0:T(8,128)(2,1)S(1)}, u32[]{:S(2)}, u32[]{:S(2)}) async-start(bf16[32,16,512]{2,1,0:T(8,128)(2,1)} %shard_map.90), calls=%async_computation.1 | async-start | bytes 1048576 | tf_op jit(solution)/shard_map/all_to_all | solution.py:252
  72.8 2.6 %collective-permute-start.19 = (bf16[16,64,128]{2,1,0:T(8,128)(2,1)S(1)}, bf16[16,64,128]{2,1,0:T(8,128)(2,1)S(1)}, u32[]{:S(2)}, u32[]{:S(2)}) collective-permute-start(bf16[16,64,128]{2,1,0:T(8,128)(2,1)S(1)} %slice.15), channel_id=1, source_target_pairs={{1,0},{2,1},{3,2},{0,3},{5,4},{6,5},{7,6},{4,7},{9,8},{10,9},{11,1... | collective-permute-start | bytes 786440 | tf_op jit(solution)/shard_map/ppermute | solution.py:239
  75.4 4.4 %collective-permute-done.18.refs_3_ = bf16[16,64,128]{2,1,0:T(8,128)(2,1)S(1)} collective-permute-done((bf16[16,64,128]{2,1,0:T(8,128)(2,1)S(1)}, bf16[16,64,128]{2,1,0:T(8,128)(2,1)S(1)}, u32[]{:S(2)}, u32[]{:S(2)}) %collective-permute-start.18) | collective-permute-done | bytes 262176 | tf_op jit(solution)/shard_map/ppermute | solution.py:239
  79.8 7.8 %all-to-all-done.1.refs_5_ = bf16[32,16,512]{2,1,0:T(8,128)(2,1)S(1)} async-done(((bf16[32,16,512]{2,1,0:T(8,128)(2,1)}), bf16[32,16,512]{2,1,0:T(8,128)(2,1)S(1)}, u32[]{:S(2)}, u32[]{:S(2)}) %all-to-all-start.1) | async-done | bytes 524320 | tf_op jit(solution)/shard_map/all_to_all | solution.py:252
  87.6 3.8 %collective-permute-start.20 = (bf16[32,64,128]{2,1,0:T(8,128)(2,1)S(1)}, bf16[32,64,128]{2,1,0:T(8,128)(2,1)S(1)}, u32[]{:S(2)}, u32[]{:S(2)}) collective-permute-start(bf16[32,64,128]{2,1,0:T(8,128)(2,1)S(1)} %get-tuple-element.24.refs_0_), channel_id=1, source_target_pairs={{4,0},{0,4},{5,1},{1,5},{6,2},{2,6},{7,3},{3,7},{12,8},{8,12},{13,... | collective-permute-start | bytes 1572872 | tf_op jit(solution)/shard_map/ppermute | solution.py:239
  92.4 1.8 %shard_map.92 = (bf16[64,4096]{1,0:T(8,128)(2,1)S(1)}, bf16[64,64,128]{2,1,0:T(8,128)(2,1)S(1)}) custom-call(s32[8,64]{1,0:T(8,128)S(1)} %bitcast.7, s32[64]{0:T(128)S(1)} %copy-done.5, s32[4]{0:T(128)S(1)} %pad_add_fusion.own_ref, bf16[32,64,128]{2,1,0:T(8,128)(2,1)S(1)} %get-tuple-element.24.refs_0_, bf16[32,64,128]{2,1,0:T(8,128)(2,1)S(1)} %get-tuple-element.25.refs_1_, ...), custom_call_target="tpu_custom_call" | custom-call | flops 1024 | bytes 1024 | tf_op jit(solution)/shard_map/pallas_call | solution.py:228
  95.2 2.4 %shard_map.93 = bf16[64,4096]{1,0:T(8,128)(2,1)} custom-call(s32[8,64]{1,0:T(8,128)S(1)} %bitcast.8, s32[64]{0:T(128)S(1)} %copy-done.5, s32[4]{0:T(128)S(1)} %pad_add_fusion.own_ref, bf16[32,64,128]{2,1,0:T(8,128)(2,1)S(1)} %collective-permute-done.20.refs_0_, bf16[32,64,128]{2,1,0:T(8,128)(2,1)S(1)} %collective-permute-done.21.refs_1_, ...), custom_call_target="tpu_custom_call" | custom-call | flops 1024 | bytes 1024 | tf_op jit(solution)/shard_map/pallas_call | solution.py:228
  (63 shorter events, 11.0 us)
Async XLA Ops:
  3.1 30.6 %all-to-all-start = ((bf16[32,80,128]{2,1,0:T(8,128)(2,1)}), bf16[32,80,128]{2,1,0:T(8,128)(2,1)S(1)}, u32[]{:S(2)}, u32[]{:S(2)}) async-start(bf16[32,80,128]{2,1,0:T(8,128)(2,1)} %shard_map.82), calls=%async_computation | async-start | bytes 1310720 | tf_op jit(solution)/shard_map/all_to_all | solution.py:252
  17.3 20.5 %collective-permute-start.10 = (bf16[64,4096]{1,0:T(8,128)(2,1)S(1)}, bf16[64,4096]{1,0:T(8,128)(2,1)S(1)}, u32[]{:S(2)}, u32[]{:S(2)}) collective-permute-start(bf16[64,4096]{1,0:T(8,128)(2,1)S(1)} %shard_map.86.refs_0_), channel_id=1, source_target_pairs={{24,0},{0,8},{8,16},{16,24},{25,1},{1,9},{9,17},{17,25},{26,2},{2,... | collective-permute-start | bytes 1572872 | tf_op jit(solution)/shard_map/ppermute | solution.py:239
  18.6 20.5 %collective-permute-start.9 = (bf16[64,4096]{1,0:T(8,128)(2,1)S(1)}, bf16[64,4096]{1,0:T(8,128)(2,1)S(1)}, u32[]{:S(2)}, u32[]{:S(2)}) collective-permute-start(bf16[64,4096]{1,0:T(8,128)(2,1)S(1)} %shard_map.86.refs_0_), channel_id=1, source_target_pairs={{8,0},{16,8},{24,16},{0,24},{9,1},{17,9},{25,17},{1,25},{10,2},{18... | collective-permute-start | bytes 1572872 | tf_op jit(solution)/shard_map/ppermute | solution.py:239
  20.1 19.2 %collective-permute-start.13 = (bf16[64,4096]{1,0:T(8,128)(2,1)S(1)}, bf16[64,4096]{1,0:T(8,128)(2,1)}, u32[]{:S(2)}, u32[]{:S(2)}) collective-permute-start(bf16[64,4096]{1,0:T(8,128)(2,1)S(1)} %shard_map.86.refs_0_), channel_id=1, source_target_pairs={{4,0},{0,4},{5,1},{1,5},{6,2},{2,6},{7,3},{3,7},{12,8},{8,12},{13,... | collective-permute-start | bytes 1572872 | tf_op jit(solution)/shard_map/ppermute | solution.py:239
  33.7 8.5 %collective-permute-start = (bf16[32,16,128]{2,1,0:T(8,128)(2,1)S(1)}, bf16[32,16,128]{2,1,0:T(8,128)(2,1)S(1)}, u32[]{:S(2)}, u32[]{:S(2)}) collective-permute-start(bf16[32,16,128]{2,1,0:T(8,128)(2,1)S(1)} %get-tuple-element.19.refs_0_.refs_2_), channel_id=1, source_target_pairs={{1,0},{2,1},{3,2},{0,3},{5,4},{6,5},{7,6},{4,7},{9,8},{10,9},{11,1... | collective-permute-start | bytes 393224 | tf_op jit(solution)/shard_map/ppermute | solution.py:239
  36.5 7.5 %collective-permute-start.1 = (bf16[32,16,128]{2,1,0:T(8,128)(2,1)S(1)}, bf16[32,16,128]{2,1,0:T(8,128)(2,1)S(1)}, u32[]{:S(2)}, u32[]{:S(2)}) collective-permute-start(bf16[32,16,128]{2,1,0:T(8,128)(2,1)S(1)} %get-tuple-element.19.refs_0_.refs_2_), channel_id=1, source_target_pairs={{2,0},{3,1},{0,2},{1,3},{6,4},{7,5},{4,6},{5,7},{10,8},{11,9},{8,1... | collective-permute-start | bytes 393224 | tf_op jit(solution)/shard_map/ppermute | solution.py:239
  37.9 8.5 %collective-permute-start.2 = (bf16[32,16,128]{2,1,0:T(8,128)(2,1)S(1)}, bf16[32,16,128]{2,1,0:T(8,128)(2,1)S(1)}, u32[]{:S(2)}, u32[]{:S(2)}) collective-permute-start(bf16[32,16,128]{2,1,0:T(8,128)(2,1)S(1)} %get-tuple-element.19.refs_0_.refs_2_), channel_id=1, source_target_pairs={{3,0},{0,1},{1,2},{2,3},{7,4},{4,5},{5,6},{6,7},{11,8},{8,9},{9,10... | collective-permute-start | bytes 393224 | tf_op jit(solution)/shard_map/ppermute | solution.py:239
  39.2 8.7 %collective-permute-start.11 = (bf16[32,4096]{1,0:T(8,128)(2,1)S(1)}, bf16[32,4096]{1,0:T(8,128)(2,1)S(1)}, u32[]{:S(2)}, u32[]{:S(2)}) collective-permute-start(bf16[32,4096]{1,0:T(8,128)(2,1)S(1)} %slice.12), channel_id=1, source_target_pairs={{24,0},{0,8},{8,16},{16,24},{25,1},{1,9},{9,17},{17,25},{26,2},{2,... | collective-permute-start | bytes 786440 | tf_op jit(solution)/shard_map/ppermute | solution.py:239
  39.3 8.0 %collective-permute-start.5 = (bf16[32,16,128]{2,1,0:T(8,128)(2,1)S(1)}, bf16[32,16,128]{2,1,0:T(8,128)(2,1)S(1)}, u32[]{:S(2)}, u32[]{:S(2)}) collective-permute-start(bf16[32,16,128]{2,1,0:T(8,128)(2,1)S(1)} %get-tuple-element.19.refs_0_.refs_2_), channel_id=1, source_target_pairs={{4,0},{0,4},{5,1},{1,5},{6,2},{2,6},{7,3},{3,7},{12,8},{8,12},{13,... | collective-permute-start | bytes 393224 | tf_op jit(solution)/shard_map/ppermute | solution.py:239
  42.3 8.8 %collective-permute-start.12 = (bf16[32,4096]{1,0:T(8,128)(2,1)S(1)}, bf16[32,4096]{1,0:T(8,128)(2,1)S(1)}, u32[]{:S(2)}, u32[]{:S(2)}) collective-permute-start(bf16[32,4096]{1,0:T(8,128)(2,1)S(1)} %slice.13), channel_id=1, source_target_pairs={{8,0},{16,8},{24,16},{0,24},{9,1},{17,9},{25,17},{1,25},{10,2},{18... | collective-permute-start | bytes 786440 | tf_op jit(solution)/shard_map/ppermute | solution.py:239
  44.1 3.3 %collective-permute-start.6 = (bf16[32,16,128]{2,1,0:T(8,128)(2,1)S(1)}, bf16[32,16,128]{2,1,0:T(8,128)(2,1)S(1)}, u32[]{:S(2)}, u32[]{:S(2)}) collective-permute-start(bf16[32,16,128]{2,1,0:T(8,128)(2,1)S(1)} %collective-permute-done.refs_1_), channel_id=1, source_target_pairs={{4,0},{0,4},{5,1},{1,5},{6,2},{2,6},{7,3},{3,7},{12,8},{8,12},{13,... | collective-permute-start | bytes 393224 | tf_op jit(solution)/shard_map/ppermute | solution.py:239
  47.3 8.0 %collective-permute-start.14 = (bf16[64,4096]{1,0:T(8,128)(2,1)S(1)}, bf16[64,4096]{1,0:T(8,128)(2,1)S(1)}, u32[]{:S(2)}, u32[]{:S(2)}) collective-permute-start(bf16[64,4096]{1,0:T(8,128)(2,1)S(1)} %get-tuple-element.20.refs_1_), channel_id=1, source_target_pairs={{4,0},{0,4},{5,1},{1,5},{6,2},{2,6},{7,3},{3,7},{12,8},{8,12},{13,... | collective-permute-start | bytes 1572872 | tf_op jit(solution)/shard_map/ppermute | solution.py:239
  47.9 4.0 %collective-permute-start.16 = (bf16[32,4096]{1,0:T(8,128)(2,1)S(1)}, bf16[32,4096]{1,0:T(8,128)(2,1)S(1)}, u32[]{:S(2)}, u32[]{:S(2)}) collective-permute-start(bf16[32,4096]{1,0:T(8,128)(2,1)S(1)} %collective-permute-done.11.refs_3_), channel_id=1, source_target_pairs={{4,0},{0,4},{5,1},{1,5},{6,2},{2,6},{7,3},{3,7},{12,8},{8,12},{13,... | collective-permute-start | bytes 786440 | tf_op jit(solution)/shard_map/ppermute | solution.py:239
  49.2 6.1 %collective-permute-start.15 = (bf16[64,4096]{1,0:T(8,128)(2,1)S(1)}, bf16[64,4096]{1,0:T(8,128)(2,1)S(1)}, u32[]{:S(2)}, u32[]{:S(2)}) collective-permute-start(bf16[64,4096]{1,0:T(8,128)(2,1)S(1)} %get-tuple-element.21.refs_2_), channel_id=1, source_target_pairs={{4,0},{0,4},{5,1},{1,5},{6,2},{2,6},{7,3},{3,7},{12,8},{8,12},{13,... | collective-permute-start | bytes 1572872 | tf_op jit(solution)/shard_map/ppermute | solution.py:239
  49.2 13.1 %collective-permute-start.3 = (bf16[32,64,128]{2,1,0:T(8,128)(2,1)S(1)}, bf16[32,64,128]{2,1,0:T(8,128)(2,1)S(1)}, u32[]{:S(2)}, u32[]{:S(2)}) collective-permute-start(bf16[32,64,128]{2,1,0:T(8,128)(2,1)S(1)} %shard_map.84.refs_0_), channel_id=1, source_target_pairs={{1,0},{2,1},{3,2},{0,3},{5,4},{6,5},{7,6},{4,7},{9,8},{10,9},{11,1... | collective-permute-start | bytes 1572872 | tf_op jit(solution)/shard_map/ppermute | solution.py:239
  51.1 14.3 %collective-permute-start.4 = (bf16[32,64,128]{2,1,0:T(8,128)(2,1)S(1)}, bf16[32,64,128]{2,1,0:T(8,128)(2,1)S(1)}, u32[]{:S(2)}, u32[]{:S(2)}) collective-permute-start(bf16[32,64,128]{2,1,0:T(8,128)(2,1)S(1)} %shard_map.84.refs_0_), channel_id=1, source_target_pairs={{3,0},{0,1},{1,2},{2,3},{7,4},{4,5},{5,6},{6,7},{11,8},{8,9},{9,10... | collective-permute-start | bytes 1572872 | tf_op jit(solution)/shard_map/ppermute | solution.py:239
  51.9 3.4 %collective-permute-start.17 = (bf16[32,4096]{1,0:T(8,128)(2,1)S(1)}, bf16[32,4096]{1,0:T(8,128)(2,1)S(1)}, u32[]{:S(2)}, u32[]{:S(2)}) collective-permute-start(bf16[32,4096]{1,0:T(8,128)(2,1)S(1)} %collective-permute-done.12.refs_4_), channel_id=1, source_target_pairs={{4,0},{0,4},{5,1},{1,5},{6,2},{2,6},{7,3},{3,7},{12,8},{8,12},{13,... | collective-permute-start | bytes 786440 | tf_op jit(solution)/shard_map/ppermute | solution.py:239
  65.4 22.2 %all-to-all-start.1 = ((bf16[32,16,512]{2,1,0:T(8,128)(2,1)}), bf16[32,16,512]{2,1,0:T(8,128)(2,1)S(1)}, u32[]{:S(2)}, u32[]{:S(2)}) async-start(bf16[32,16,512]{2,1,0:T(8,128)(2,1)} %shard_map.90), calls=%async_computation.1 | async-start | bytes 1048576 | tf_op jit(solution)/shard_map/all_to_all | solution.py:252
  72.6 7.1 %collective-permute-start.18 = (bf16[16,64,128]{2,1,0:T(8,128)(2,1)S(1)}, bf16[16,64,128]{2,1,0:T(8,128)(2,1)S(1)}, u32[]{:S(2)}, u32[]{:S(2)}) collective-permute-start(bf16[16,64,128]{2,1,0:T(8,128)(2,1)S(1)} %slice.14), channel_id=1, source_target_pairs={{3,0},{0,1},{1,2},{2,3},{7,4},{4,5},{5,6},{6,7},{11,8},{8,9},{9,10... | collective-permute-start | bytes 786440 | tf_op jit(solution)/shard_map/ppermute | solution.py:239
  72.8 7.0 %collective-permute-start.19 = (bf16[16,64,128]{2,1,0:T(8,128)(2,1)S(1)}, bf16[16,64,128]{2,1,0:T(8,128)(2,1)S(1)}, u32[]{:S(2)}, u32[]{:S(2)}) collective-permute-start(bf16[16,64,128]{2,1,0:T(8,128)(2,1)S(1)} %slice.15), channel_id=1, source_target_pairs={{1,0},{2,1},{3,2},{0,3},{5,4},{6,5},{7,6},{4,7},{9,8},{10,9},{11,1... | collective-permute-start | bytes 786440 | tf_op jit(solution)/shard_map/ppermute | solution.py:239
  87.6 7.6 %collective-permute-start.20 = (bf16[32,64,128]{2,1,0:T(8,128)(2,1)S(1)}, bf16[32,64,128]{2,1,0:T(8,128)(2,1)S(1)}, u32[]{:S(2)}, u32[]{:S(2)}) collective-permute-start(bf16[32,64,128]{2,1,0:T(8,128)(2,1)S(1)} %get-tuple-element.24.refs_0_), channel_id=1, source_target_pairs={{4,0},{0,4},{5,1},{1,5},{6,2},{2,6},{7,3},{3,7},{12,8},{8,12},{13,... | collective-permute-start | bytes 1572872 | tf_op jit(solution)/shard_map/ppermute | solution.py:239
  91.4 3.8 %collective-permute-start.21 = (bf16[32,64,128]{2,1,0:T(8,128)(2,1)S(1)}, bf16[32,64,128]{2,1,0:T(8,128)(2,1)S(1)}, u32[]{:S(2)}, u32[]{:S(2)}) collective-permute-start(bf16[32,64,128]{2,1,0:T(8,128)(2,1)S(1)} %get-tuple-element.25.refs_1_), channel_id=1, source_target_pairs={{4,0},{0,4},{5,1},{1,5},{6,2},{2,6},{7,3},{3,7},{12,8},{8,12},{13,... | collective-permute-start | bytes 1572872 | tf_op jit(solution)/shard_map/ppermute | solution.py:239
  91.4 3.8 %collective-permute-start.22 = (bf16[32,64,128]{2,1,0:T(8,128)(2,1)S(1)}, bf16[32,64,128]{2,1,0:T(8,128)(2,1)S(1)}, u32[]{:S(2)}, u32[]{:S(2)}) collective-permute-start(bf16[32,64,128]{2,1,0:T(8,128)(2,1)S(1)} %get-tuple-element.26.refs_2_), channel_id=1, source_target_pairs={{4,0},{0,4},{5,1},{1,5},{6,2},{2,6},{7,3},{3,7},{12,8},{8,12},{13,... | collective-permute-start | bytes 1572872 | tf_op jit(solution)/shard_map/ppermute | solution.py:239
  91.9 3.3 %collective-permute-start.24 = (bf16[16,64,128]{2,1,0:T(8,128)(2,1)S(1)}, bf16[16,64,128]{2,1,0:T(8,128)(2,1)S(1)}, u32[]{:S(2)}, u32[]{:S(2)}) collective-permute-start(bf16[16,64,128]{2,1,0:T(8,128)(2,1)S(1)} %get-tuple-element.28.refs_4_), channel_id=1, source_target_pairs={{4,0},{0,4},{5,1},{1,5},{6,2},{2,6},{7,3},{3,7},{12,8},{8,12},{13,... | collective-permute-start | bytes 786440 | tf_op jit(solution)/shard_map/ppermute | solution.py:239
  (11 other events, 181.9 us)

commit v7 on v6

--- a/solution.py
+++ b/solution.py
@@ -11,6 +11,7 @@
 Z, X, CORES, Y = 8, 4, 2, 4
 SIZES = {"z": Z, "x": X, "core": CORES, "y": Y}
 CHIPS = Z * X
+HALF = CHIPS // 2
 BLOCK, WIDTH, QUARTER = 64, 128, 16
 MOLECULES = CHIPS * CORES
 BASIS = MOLECULES * BLOCK
@@ -64,18 +65,18 @@
     )(own, occ_blocks, virt_blocks)[0]
 
 
-def divide_kernel(both_ref, occ_ref, virt_ref):
+def divide_kernel(both_ref, occ_ref, *virt_refs):
     for chip in range(CHIPS):
         occ_ref[chip] = both_ref[chip, :QUARTER]
-        virt_ref[chip] = both_ref[chip, QUARTER:]
+        virt_refs[chip // HALF][chip % HALF] = both_ref[chip, QUARTER:]
 
 
 def divide(both):
     return call(
         divide_kernel,
-        [(CHIPS, QUARTER, WIDTH), (CHIPS, BLOCK, WIDTH)],
+        [(CHIPS, QUARTER, WIDTH)] + [(HALF, BLOCK, WIDTH)] * 2,
         [VMEM],
-        (VMEM, VMEM),
+        (VMEM,) * 3,
         mib=8,
     )(both)
 
@@ -164,7 +165,7 @@
 
 
 def virtual_kernel(core_off, index_ref, first_ref, own_ref, *refs):
-    panel_refs, refs = refs[: len(PARTS)], refs[len(PARTS) :]
+    panel_refs, refs = refs[: 2 * len(PARTS)], refs[2 * len(PARTS) :]
     if core_off:
         table_ref, before_ref, out_hbm, out_ref, left_ref, right_ref, out_sems = refs
     else:
@@ -185,9 +186,10 @@
             table_ref[half_table + z * X + tile_at] = swap_halves(tile)
 
     def panel(y_off, chip):
+        refs, chip = panel_refs[chip // HALF * len(PARTS) :], chip % HALF
         if y_off == 2:
-            return panel_refs[3 + chip // (CHIPS // 2)][chip % (CHIPS // 2)]
-        return panel_refs[{0: 0, 1: 1, 3: 2}[y_off]][chip]
+            return refs[3 + chip // (HALF // 2)][chip % (HALF // 2)]
+        return refs[{0: 0, 1: 1, 3: 2}[y_off]][chip]
 
     first_half = lax.broadcasted_iota(jnp.int32, (BLOCK, WIDTH), 1) < BLOCK
     written = []
@@ -257,16 +259,16 @@
 ):
     own = jnp.stack([lax.axis_index(axis) for axis in SIZES]).astype(jnp.int32)
     both = exchange(spread(own, occ_blocks, virt_blocks))
-    occ_plane, virt_plane = divide(both)
+    occ_plane, *virt_planes = divide(both)
     pieces = [occ_plane] + [shift(occ_plane, "y", by) for by in range(1, Y)]
     rows = ring(mask_rows(pair_mask, b_tensor), "x", occ_plane)
     rows = rows + [shift(part, "core", 1) for part in rows]
-    (virt_plane,) = tie([virt_plane], *pieces[1:])
+    virt_planes = tie(virt_planes, *pieces[1:])
     pieces = pieces + [shift(piece, "core", 1) for piece in pieces]
     half = occupied(dense_panel(pieces, own, occ_index, second_map), rows, own)
-    mine = ring(virt_plane, "y", half)
+    mine, later = (ring(plane, "y", half) for plane in virt_planes)
     turned = exchange(*tie([half], *mine[1:3]))
-    mine = tie(mine, turned)
+    mine = tie(mine + later, turned)
     other = [shift(panel, "core", 1) for panel in mine]
     known = (own, virt_index, first_map)
     columns, table = virtual(0, mine, *known, turned)

time: 98.2 us -> 102 us (1.039)
  starting transfers between devices: 49.1 us -> 55 us
  waiting for transfers between devices: 31.7 us -> 29.2 us
    all_to_all x2, waiting for transfers between devices: 19.9 us -> 12.1 us  [exchange(): lax.all_to_all(array, ('z', 'x'), split_axis=0, concat_axis=0, tiled=True)]
    ppermute x25 -> x34, waiting for transfers between devices: 11.9 us -> 17.1 us  [shift(): lax.ppermute(array, axis, [((i + by) % size, i) for i in range(size)])]
    ppermute x25 -> x34, starting transfers between devices: 30 us -> 34.1 us  [shift(): lax.ppermute(array, axis, [((i + by) % size, i) for i in range(size)])]
    all_to_all x2, starting transfers between devices: 19.1 us -> 20.9 us  [exchange(): lax.all_to_all(array, ('z', 'x'), split_axis=0, concat_axis=0, tiled=True)]
    unnamed x16 -> x17, local copies, waits for them, and re-layouts: 3.22 us -> 4.02 us
  transfers between devices with their start and end apart: 27 -> 36, of which waited for: 8 -> 9; matrix products, arithmetic and copies ran while one was open for 0% -> 1% of each run, Pallas kernels for 10% -> 8%
where the time goes in v7:
time: 102 us; the launch traced here: 101 us
  starting transfers between devices  55 us (54%)
  waiting for transfers between devices  29.2 us (29%)
  Pallas kernels  12.5 us (12%)
  local copies, waits for them, and re-layouts  4.09 us (4%)
    ppermute x34, starting transfers between devices, shift(): lax.ppermute(array, axis, [((i + by) % size, i) for i in range(size)])  34.1 us
    all_to_all x2, starting transfers between devices, exchange(): lax.all_to_all(array, ('z', 'x'), split_axis=0, concat_axis=0, tiled=True)  20.9 us
    ppermute x34, waiting for transfers between devices, shift(): lax.ppermute(array, axis, [((i + by) % size, i) for i in range(size)])  17.1 us
    all_to_all x2, waiting for transfers between devices, exchange(): lax.all_to_all(array, ('z', 'x'), split_axis=0, concat_axis=0, tiled=True)  12.1 us
    pallas_call x2, Pallas kernels, virtual(): call(functools.partial(virtual_kernel, core_off), [shape] if core_off els...  4.25 us
    unnamed x17, local copies, waits for them, and re-layouts  4.02 us
    pallas_call x1, Pallas kernels, occupied(): call(occupied_kernel, [(CHIPS, QUARTER, lanes)], [SMEM] + [VMEM] * (1 + l...  3.7 us
    pallas_call x1, Pallas kernels, dense_panel(): call(dense_kernel, [shape], [SMEM] * 3 + [VMEM] * len(pieces), (VMEM,), [...  2.34 us
  transfers between devices with their start and end apart: 36, of which 9 were waited for; matrix products, arithmetic and copies ran while one was open for 1% of the time, Pallas kernels for 8%

profile of v7, /device:TPU:1, one launch (start us, length us, event | category | flops | bytes accessed | tf_op | source)
XLA Modules:
  0.0 101.2 jit_solution(346915099172135670)
XLA Ops:
  1.6 1.5 %shard_map.82 = bf16[32,80,128]{2,1,0:T(8,128)(2,1)} custom-call(s32[4]{0:T(128)S(1)} %pad_add_fusion.own_ref, bf16[1,2,64,64]{3,2,1,0:T(8,128)(2,1)S(1)} %copy-done.1, bf16[1,2,64,64]{3,2,1,0:T(8,128)(2,1)S(1)} %copy-done.2), custom_call_target="tpu_custom_call" | custom-call | flops 1024 | bytes 1024 | tf_op jit(solution)/shard_map/pallas_call | solution.py:63
  3.1 11.9 %all-to-all-start = ((bf16[32,80,128]{2,1,0:T(8,128)(2,1)}), bf16[32,80,128]{2,1,0:T(8,128)(2,1)S(1)}, u32[]{:S(2)}, u32[]{:S(2)}) async-start(bf16[32,80,128]{2,1,0:T(8,128)(2,1)} %shard_map.82), calls=%async_computation | async-start | bytes 1310720 | tf_op jit(solution)/shard_map/all_to_all | solution.py:254
  18.7 1.4 %collective-permute-start.9 = (bf16[64,4096]{1,0:T(8,128)(2,1)S(1)}, bf16[64,4096]{1,0:T(8,128)(2,1)S(1)}, u32[]{:S(2)}, u32[]{:S(2)}) collective-permute-start(bf16[64,4096]{1,0:T(8,128)(2,1)S(1)} %shard_map.86.refs_0_), channel_id=1, source_target_pairs={{8,0},{16,8},{24,16},{0,24},{9,1},{17,9},{25,17},{1,25},{10,2},{18... | collective-permute-start | bytes 1572872 | tf_op jit(solution)/shard_map/ppermute | solution.py:241
  20.1 1.5 %collective-permute-start.13 = (bf16[64,4096]{1,0:T(8,128)(2,1)S(1)}, bf16[64,4096]{1,0:T(8,128)(2,1)}, u32[]{:S(2)}, u32[]{:S(2)}) collective-permute-start(bf16[64,4096]{1,0:T(8,128)(2,1)S(1)} %shard_map.86.refs_0_), channel_id=1, source_target_pairs={{4,0},{0,4},{5,1},{1,5},{6,2},{2,6},{7,3},{3,7},{12,8},{8,12},{13,... | collective-permute-start | bytes 1572872 | tf_op jit(solution)/shard_map/ppermute | solution.py:241
  21.6 12.1 %all-to-all-done.both_ref = bf16[32,80,128]{2,1,0:T(8,128)(2,1)S(1)} async-done(((bf16[32,80,128]{2,1,0:T(8,128)(2,1)}), bf16[32,80,128]{2,1,0:T(8,128)(2,1)S(1)}, u32[]{:S(2)}, u32[]{:S(2)}) %all-to-all-start) | async-done | bytes 655392 | tf_op jit(solution)/shard_map/all_to_all | solution.py:254
  33.7 2.8 %collective-permute-start = (bf16[32,16,128]{2,1,0:T(8,128)(2,1)S(1)}, bf16[32,16,128]{2,1,0:T(8,128)(2,1)S(1)}, u32[]{:S(2)}, u32[]{:S(2)}) collective-permute-start(bf16[32,16,128]{2,1,0:T(8,128)(2,1)S(1)} %get-tuple-element.30.refs_0_.refs_2_), channel_id=1, source_target_pairs={{1,0},{2,1},{3,2},{0,3},{5,4},{6,5},{7,6},{4,7},{9,8},{10,9},{11,1... | collective-permute-start | bytes 393224 | tf_op jit(solution)/shard_map/ppermute | solution.py:241
  38.0 3.0 %collective-permute-start.1 = (bf16[32,16,128]{2,1,0:T(8,128)(2,1)S(1)}, bf16[32,16,128]{2,1,0:T(8,128)(2,1)S(1)}, u32[]{:S(2)}, u32[]{:S(2)}) collective-permute-start(bf16[32,16,128]{2,1,0:T(8,128)(2,1)S(1)} %get-tuple-element.30.refs_0_.refs_2_), channel_id=1, source_target_pairs={{2,0},{3,1},{0,2},{1,3},{6,4},{7,5},{4,6},{5,7},{10,8},{11,9},{8,1... | collective-permute-start | bytes 393224 | tf_op jit(solution)/shard_map/ppermute | solution.py:241
  41.4 2.5 %collective-permute-start.5 = (bf16[32,16,128]{2,1,0:T(8,128)(2,1)S(1)}, bf16[32,16,128]{2,1,0:T(8,128)(2,1)S(1)}, u32[]{:S(2)}, u32[]{:S(2)}) collective-permute-start(bf16[32,16,128]{2,1,0:T(8,128)(2,1)S(1)} %get-tuple-element.30.refs_0_.refs_2_), channel_id=1, source_target_pairs={{4,0},{0,4},{5,1},{1,5},{6,2},{2,6},{7,3},{3,7},{12,8},{8,12},{13,... | collective-permute-start | bytes 393224 | tf_op jit(solution)/shard_map/ppermute | solution.py:241
  44.0 2.2 %collective-permute-start.12 = (bf16[32,4096]{1,0:T(8,128)(2,1)S(1)}, bf16[32,4096]{1,0:T(8,128)(2,1)S(1)}, u32[]{:S(2)}, u32[]{:S(2)}) collective-permute-start(bf16[32,4096]{1,0:T(8,128)(2,1)S(1)} %slice.19), channel_id=1, source_target_pairs={{8,0},{16,8},{24,16},{0,24},{9,1},{17,9},{25,17},{1,25},{10,2},{18... | collective-permute-start | bytes 786440 | tf_op jit(solution)/shard_map/ppermute | solution.py:241
  46.3 1.5 %collective-permute-done.2.refs_4_.refs_3_ = bf16[32,16,128]{2,1,0:T(8,128)(2,1)S(1)} collective-permute-done((bf16[32,16,128]{2,1,0:T(8,128)(2,1)S(1)}, bf16[32,16,128]{2,1,0:T(8,128)(2,1)S(1)}, u32[]{:S(2)}, u32[]{:S(2)}) %collective-permute-start.2) | collective-permute-done | bytes 131104 | tf_op jit(solution)/shard_map/ppermute | solution.py:241
  47.8 2.6 %collective-permute-start.14 = (bf16[64,4096]{1,0:T(8,128)(2,1)S(1)}, bf16[64,4096]{1,0:T(8,128)(2,1)S(1)}, u32[]{:S(2)}, u32[]{:S(2)}) collective-permute-start(bf16[64,4096]{1,0:T(8,128)(2,1)S(1)} %get-tuple-element.32.refs_1_), channel_id=1, source_target_pairs={{4,0},{0,4},{5,1},{1,5},{6,2},{2,6},{7,3},{3,7},{12,8},{8,12},{13,... | collective-permute-start | bytes 1572872 | tf_op jit(solution)/shard_map/ppermute | solution.py:241
  52.5 1.8 %collective-permute-start.17 = (bf16[32,4096]{1,0:T(8,128)(2,1)S(1)}, bf16[32,4096]{1,0:T(8,128)(2,1)S(1)}, u32[]{:S(2)}, u32[]{:S(2)}) collective-permute-start(bf16[32,4096]{1,0:T(8,128)(2,1)S(1)} %collective-permute-done.12.refs_4_), channel_id=1, source_target_pairs={{4,0},{0,4},{5,1},{1,5},{6,2},{2,6},{7,3},{3,7},{12,8},{8,12},{13,... | collective-permute-start | bytes 786440 | tf_op jit(solution)/shard_map/ppermute | solution.py:241
  55.7 2.3 %shard_map.85.dense_ref = bf16[512,4096]{1,0:T(8,128)(2,1)S(1)} custom-call(s32[8,64]{1,0:T(8,128)S(1)} %bitcast.9, s32[64]{0:T(128)S(1)} %copy-done.7, s32[4]{0:T(128)S(1)} %pad_add_fusion.own_ref, bf16[32,16,128]{2,1,0:T(8,128)(2,1)S(1)} %get-tuple-element.30.refs_0_.refs_2_, bf16[32,16,128]{2,1,0:T(8,128)(2,1)S(1)} %collective-permute-done.refs_2_.refs_1_, ...), custom_call_target="tpu_custom_call" | custom-call | flops 1024 | bytes 1024 | tf_op jit(solution)/shard_map/pallas_call | solution.py:131
  58.1 3.7 %shard_map.88.refs_2_ = bf16[32,16,512]{2,1,0:T(8,128)(2,1)S(1)} custom-call(s32[4]{0:T(128)S(1)} %pad_add_fusion.own_ref, bf16[512,4096]{1,0:T(8,128)(2,1)S(1)} %shard_map.85.dense_ref, bf16[64,4096]{1,0:T(8,128)(2,1)S(1)} %shard_map.86.refs_0_, bf16[64,4096]{1,0:T(8,128)(2,1)S(1)} %get-tuple-element.32.refs_1_, ...), custom_call_target="tpu_custom_call" | custom-call | flops 1024 | bytes 1024 | tf_op jit(solution)/shard_map/pallas_call | solution.py:158
  62.6 1.8 %collective-permute-done.4.refs_1_ = bf16[16,64,128]{2,1,0:T(8,128)(2,1)S(1)} collective-permute-done((bf16[16,64,128]{2,1,0:T(8,128)(2,1)S(1)}, bf16[16,64,128]{2,1,0:T(8,128)(2,1)S(1)}, u32[]{:S(2)}, u32[]{:S(2)}) %collective-permute-start.4) | collective-permute-done | bytes 262176 | tf_op jit(solution)/shard_map/ppermute | solution.py:241
  64.4 9.0 %all-to-all-start.1 = ((bf16[32,16,512]{2,1,0:T(8,128)(2,1)}), bf16[32,16,512]{2,1,0:T(8,128)(2,1)S(1)}, u32[]{:S(2)}, u32[]{:S(2)}) async-start(bf16[32,16,512]{2,1,0:T(8,128)(2,1)} %shard_map.91), calls=%async_computation.1 | async-start | bytes 1048576 | tf_op jit(solution)/shard_map/all_to_all | solution.py:254
  75.0 4.8 %collective-permute-done.20.refs_0_ = bf16[16,64,128]{2,1,0:T(8,128)(2,1)S(1)} collective-permute-done((bf16[16,64,128]{2,1,0:T(8,128)(2,1)S(1)}, bf16[16,64,128]{2,1,0:T(8,128)(2,1)S(1)}, u32[]{:S(2)}, u32[]{:S(2)}) %collective-permute-start.20) | collective-permute-done | bytes 262176 | tf_op jit(solution)/shard_map/ppermute | solution.py:241
  79.8 2.3 %collective-permute-done.21.refs_1_ = bf16[16,64,128]{2,1,0:T(8,128)(2,1)S(1)} collective-permute-done((bf16[16,64,128]{2,1,0:T(8,128)(2,1)S(1)}, bf16[16,64,128]{2,1,0:T(8,128)(2,1)S(1)}, u32[]{:S(2)}, u32[]{:S(2)}) %collective-permute-start.21) | collective-permute-done | bytes 262176 | tf_op jit(solution)/shard_map/ppermute | solution.py:241
  82.3 2.7 %collective-permute-start.23 = (bf16[8,64,128]{2,1,0:T(8,128)(2,1)S(1)}, bf16[8,64,128]{2,1,0:T(8,128)(2,1)S(1)}, u32[]{:S(2)}, u32[]{:S(2)}) collective-permute-start(bf16[8,64,128]{2,1,0:T(8,128)(2,1)S(1)} %slice.23), channel_id=1, source_target_pairs={{1,0},{2,1},{3,2},{0,3},{5,4},{6,5},{7,6},{4,7},{9,8},{10,9},{11,1... | collective-permute-start | bytes 393224 | tf_op jit(solution)/shard_map/ppermute | solution.py:241
  85.0 2.7 %collective-permute-start.19 = (bf16[8,64,128]{2,1,0:T(8,128)(2,1)S(1)}, bf16[8,64,128]{2,1,0:T(8,128)(2,1)S(1)}, u32[]{:S(2)}, u32[]{:S(2)}) collective-permute-start(bf16[8,64,128]{2,1,0:T(8,128)(2,1)S(1)} %slice.21), channel_id=1, source_target_pairs={{1,0},{2,1},{3,2},{0,3},{5,4},{6,5},{7,6},{4,7},{9,8},{10,9},{11,1... | collective-permute-start | bytes 393224 | tf_op jit(solution)/shard_map/ppermute | solution.py:241
  87.7 3.9 %collective-permute-done.18.refs_3_ = bf16[8,64,128]{2,1,0:T(8,128)(2,1)S(1)} collective-permute-done((bf16[8,64,128]{2,1,0:T(8,128)(2,1)S(1)}, bf16[8,64,128]{2,1,0:T(8,128)(2,1)S(1)}, u32[]{:S(2)}, u32[]{:S(2)}) %collective-permute-start.18) | collective-permute-done | bytes 131104 | tf_op jit(solution)/shard_map/ppermute | solution.py:241
  91.6 2.4 %collective-permute-start.24 = (bf16[16,64,128]{2,1,0:T(8,128)(2,1)S(1)}, bf16[16,64,128]{2,1,0:T(8,128)(2,1)S(1)}, u32[]{:S(2)}, u32[]{:S(2)}) collective-permute-start(bf16[16,64,128]{2,1,0:T(8,128)(2,1)S(1)} %get-tuple-element.39.refs_0_), channel_id=1, source_target_pairs={{4,0},{0,4},{5,1},{1,5},{6,2},{2,6},{7,3},{3,7},{12,8},{8,12},{13,... | collective-permute-start | bytes 786440 | tf_op jit(solution)/shard_map/ppermute | solution.py:241
  96.7 1.9 %shard_map.93 = (bf16[64,4096]{1,0:T(8,128)(2,1)S(1)}, bf16[64,64,128]{2,1,0:T(8,128)(2,1)S(1)}) custom-call(s32[8,64]{1,0:T(8,128)S(1)} %bitcast.7, s32[64]{0:T(128)S(1)} %copy-done.5, s32[4]{0:T(128)S(1)} %pad_add_fusion.own_ref, bf16[16,64,128]{2,1,0:T(8,128)(2,1)S(1)} %get-tuple-element.39.refs_0_, bf16[16,64,128]{2,1,0:T(8,128)(2,1)S(1)} %get-tuple-element.40.refs_1_, ...), custom_call_target="tpu_custom_call" | custom-call | flops 1024 | bytes 1024 | tf_op jit(solution)/shard_map/pallas_call | solution.py:230
  98.7 2.4 %shard_map.94 = bf16[64,4096]{1,0:T(8,128)(2,1)} custom-call(s32[8,64]{1,0:T(8,128)S(1)} %bitcast.8, s32[64]{0:T(128)S(1)} %copy-done.5, s32[4]{0:T(128)S(1)} %pad_add_fusion.own_ref, bf16[16,64,128]{2,1,0:T(8,128)(2,1)S(1)} %collective-permute-done.24.refs_0_, bf16[16,64,128]{2,1,0:T(8,128)(2,1)S(1)} %collective-permute-done.25.refs_1_, ...), custom_call_target="tpu_custom_call" | custom-call | flops 1024 | bytes 1024 | tf_op jit(solution)/shard_map/pallas_call | solution.py:230
  (85 shorter events, 16.1 us)
Async XLA Ops:
  3.1 30.6 %all-to-all-start = ((bf16[32,80,128]{2,1,0:T(8,128)(2,1)}), bf16[32,80,128]{2,1,0:T(8,128)(2,1)S(1)}, u32[]{:S(2)}, u32[]{:S(2)}) async-start(bf16[32,80,128]{2,1,0:T(8,128)(2,1)} %shard_map.82), calls=%async_computation | async-start | bytes 1310720 | tf_op jit(solution)/shard_map/all_to_all | solution.py:254
  17.3 20.5 %collective-permute-start.10 = (bf16[64,4096]{1,0:T(8,128)(2,1)S(1)}, bf16[64,4096]{1,0:T(8,128)(2,1)S(1)}, u32[]{:S(2)}, u32[]{:S(2)}) collective-permute-start(bf16[64,4096]{1,0:T(8,128)(2,1)S(1)} %shard_map.86.refs_0_), channel_id=1, source_target_pairs={{24,0},{0,8},{8,16},{16,24},{25,1},{1,9},{9,17},{17,25},{26,2},{2,... | collective-permute-start | bytes 1572872 | tf_op jit(solution)/shard_map/ppermute | solution.py:241
  18.7 19.2 %collective-permute-start.9 = (bf16[64,4096]{1,0:T(8,128)(2,1)S(1)}, bf16[64,4096]{1,0:T(8,128)(2,1)S(1)}, u32[]{:S(2)}, u32[]{:S(2)}) collective-permute-start(bf16[64,4096]{1,0:T(8,128)(2,1)S(1)} %shard_map.86.refs_0_), channel_id=1, source_target_pairs={{8,0},{16,8},{24,16},{0,24},{9,1},{17,9},{25,17},{1,25},{10,2},{18... | collective-permute-start | bytes 1572872 | tf_op jit(solution)/shard_map/ppermute | solution.py:241
  20.1 21.3 %collective-permute-start.13 = (bf16[64,4096]{1,0:T(8,128)(2,1)S(1)}, bf16[64,4096]{1,0:T(8,128)(2,1)}, u32[]{:S(2)}, u32[]{:S(2)}) collective-permute-start(bf16[64,4096]{1,0:T(8,128)(2,1)S(1)} %shard_map.86.refs_0_), channel_id=1, source_target_pairs={{4,0},{0,4},{5,1},{1,5},{6,2},{2,6},{7,3},{3,7},{12,8},{8,12},{13,... | collective-permute-start | bytes 1572872 | tf_op jit(solution)/shard_map/ppermute | solution.py:241
  33.7 10.2 %collective-permute-start = (bf16[32,16,128]{2,1,0:T(8,128)(2,1)S(1)}, bf16[32,16,128]{2,1,0:T(8,128)(2,1)S(1)}, u32[]{:S(2)}, u32[]{:S(2)}) collective-permute-start(bf16[32,16,128]{2,1,0:T(8,128)(2,1)S(1)} %get-tuple-element.30.refs_0_.refs_2_), channel_id=1, source_target_pairs={{1,0},{2,1},{3,2},{0,3},{5,4},{6,5},{7,6},{4,7},{9,8},{10,9},{11,1... | collective-permute-start | bytes 393224 | tf_op jit(solution)/shard_map/ppermute | solution.py:241
  37.9 13.0 %collective-permute-start.11 = (bf16[32,4096]{1,0:T(8,128)(2,1)S(1)}, bf16[32,4096]{1,0:T(8,128)(2,1)S(1)}, u32[]{:S(2)}, u32[]{:S(2)}) collective-permute-start(bf16[32,4096]{1,0:T(8,128)(2,1)S(1)} %slice.18), channel_id=1, source_target_pairs={{24,0},{0,8},{8,16},{16,24},{25,1},{1,9},{9,17},{17,25},{26,2},{2,... | collective-permute-start | bytes 786440 | tf_op jit(solution)/shard_map/ppermute | solution.py:241
  38.0 6.0 %collective-permute-start.1 = (bf16[32,16,128]{2,1,0:T(8,128)(2,1)S(1)}, bf16[32,16,128]{2,1,0:T(8,128)(2,1)S(1)}, u32[]{:S(2)}, u32[]{:S(2)}) collective-permute-start(bf16[32,16,128]{2,1,0:T(8,128)(2,1)S(1)} %get-tuple-element.30.refs_0_.refs_2_), channel_id=1, source_target_pairs={{2,0},{3,1},{0,2},{1,3},{6,4},{7,5},{4,6},{5,7},{10,8},{11,9},{8,1... | collective-permute-start | bytes 393224 | tf_op jit(solution)/shard_map/ppermute | solution.py:241
  41.0 6.8 %collective-permute-start.2 = (bf16[32,16,128]{2,1,0:T(8,128)(2,1)S(1)}, bf16[32,16,128]{2,1,0:T(8,128)(2,1)S(1)}, u32[]{:S(2)}, u32[]{:S(2)}) collective-permute-start(bf16[32,16,128]{2,1,0:T(8,128)(2,1)S(1)} %get-tuple-element.30.refs_0_.refs_2_), channel_id=1, source_target_pairs={{3,0},{0,1},{1,2},{2,3},{7,4},{4,5},{5,6},{6,7},{11,8},{8,9},{9,10... | collective-permute-start | bytes 393224 | tf_op jit(solution)/shard_map/ppermute | solution.py:241
  41.4 9.0 %collective-permute-start.5 = (bf16[32,16,128]{2,1,0:T(8,128)(2,1)S(1)}, bf16[32,16,128]{2,1,0:T(8,128)(2,1)S(1)}, u32[]{:S(2)}, u32[]{:S(2)}) collective-permute-start(bf16[32,16,128]{2,1,0:T(8,128)(2,1)S(1)} %get-tuple-element.30.refs_0_.refs_2_), channel_id=1, source_target_pairs={{4,0},{0,4},{5,1},{1,5},{6,2},{2,6},{7,3},{3,7},{12,8},{8,12},{13,... | collective-permute-start | bytes 393224 | tf_op jit(solution)/shard_map/ppermute | solution.py:241
  43.9 6.5 %collective-permute-start.6 = (bf16[32,16,128]{2,1,0:T(8,128)(2,1)S(1)}, bf16[32,16,128]{2,1,0:T(8,128)(2,1)S(1)}, u32[]{:S(2)}, u32[]{:S(2)}) collective-permute-start(bf16[32,16,128]{2,1,0:T(8,128)(2,1)S(1)} %collective-permute-done.refs_2_.refs_1_), channel_id=1, source_target_pairs={{4,0},{0,4},{5,1},{1,5},{6,2},{2,6},{7,3},{3,7},{12,8},{8,12},{13,... | collective-permute-start | bytes 393224 | tf_op jit(solution)/shard_map/ppermute | solution.py:241
  44.0 8.4 %collective-permute-start.12 = (bf16[32,4096]{1,0:T(8,128)(2,1)S(1)}, bf16[32,4096]{1,0:T(8,128)(2,1)S(1)}, u32[]{:S(2)}, u32[]{:S(2)}) collective-permute-start(bf16[32,4096]{1,0:T(8,128)(2,1)S(1)} %slice.19), channel_id=1, source_target_pairs={{8,0},{16,8},{24,16},{0,24},{9,1},{17,9},{25,17},{1,25},{10,2},{18... | collective-permute-start | bytes 786440 | tf_op jit(solution)/shard_map/ppermute | solution.py:241
  47.8 10.3 %collective-permute-start.14 = (bf16[64,4096]{1,0:T(8,128)(2,1)S(1)}, bf16[64,4096]{1,0:T(8,128)(2,1)S(1)}, u32[]{:S(2)}, u32[]{:S(2)}) collective-permute-start(bf16[64,4096]{1,0:T(8,128)(2,1)S(1)} %get-tuple-element.32.refs_1_), channel_id=1, source_target_pairs={{4,0},{0,4},{5,1},{1,5},{6,2},{2,6},{7,3},{3,7},{12,8},{8,12},{13,... | collective-permute-start | bytes 1572872 | tf_op jit(solution)/shard_map/ppermute | solution.py:241
  50.5 7.6 %collective-permute-start.15 = (bf16[64,4096]{1,0:T(8,128)(2,1)S(1)}, bf16[64,4096]{1,0:T(8,128)(2,1)S(1)}, u32[]{:S(2)}, u32[]{:S(2)}) collective-permute-start(bf16[64,4096]{1,0:T(8,128)(2,1)S(1)} %get-tuple-element.33.refs_2_), channel_id=1, source_target_pairs={{4,0},{0,4},{5,1},{1,5},{6,2},{2,6},{7,3},{3,7},{12,8},{8,12},{13,... | collective-permute-start | bytes 1572872 | tf_op jit(solution)/shard_map/ppermute | solution.py:241
  52.5 5.6 %collective-permute-start.17 = (bf16[32,4096]{1,0:T(8,128)(2,1)S(1)}, bf16[32,4096]{1,0:T(8,128)(2,1)S(1)}, u32[]{:S(2)}, u32[]{:S(2)}) collective-permute-start(bf16[32,4096]{1,0:T(8,128)(2,1)S(1)} %collective-permute-done.12.refs_4_), channel_id=1, source_target_pairs={{4,0},{0,4},{5,1},{1,5},{6,2},{2,6},{7,3},{3,7},{12,8},{8,12},{13,... | collective-permute-start | bytes 786440 | tf_op jit(solution)/shard_map/ppermute | solution.py:241
  54.3 8.4 %collective-permute-start.3 = (bf16[16,64,128]{2,1,0:T(8,128)(2,1)S(1)}, bf16[16,64,128]{2,1,0:T(8,128)(2,1)S(1)}, u32[]{:S(2)}, u32[]{:S(2)}) collective-permute-start(bf16[16,64,128]{2,1,0:T(8,128)(2,1)S(1)} %get-tuple-element.31.refs_0_), channel_id=1, source_target_pairs={{1,0},{2,1},{3,2},{0,3},{5,4},{6,5},{7,6},{4,7},{9,8},{10,9},{11,1... | collective-permute-start | bytes 786440 | tf_op jit(solution)/shard_map/ppermute | solution.py:241
  55.6 8.7 %collective-permute-start.4 = (bf16[16,64,128]{2,1,0:T(8,128)(2,1)S(1)}, bf16[16,64,128]{2,1,0:T(8,128)(2,1)S(1)}, u32[]{:S(2)}, u32[]{:S(2)}) collective-permute-start(bf16[16,64,128]{2,1,0:T(8,128)(2,1)S(1)} %get-tuple-element.31.refs_0_), channel_id=1, source_target_pairs={{3,0},{0,1},{1,2},{2,3},{7,4},{4,5},{5,6},{6,7},{11,8},{8,9},{9,10... | collective-permute-start | bytes 786440 | tf_op jit(solution)/shard_map/ppermute | solution.py:241
  64.4 27.2 %all-to-all-start.1 = ((bf16[32,16,512]{2,1,0:T(8,128)(2,1)}), bf16[32,16,512]{2,1,0:T(8,128)(2,1)S(1)}, u32[]{:S(2)}, u32[]{:S(2)}) async-start(bf16[32,16,512]{2,1,0:T(8,128)(2,1)} %shard_map.91), calls=%async_computation.1 | async-start | bytes 1048576 | tf_op jit(solution)/shard_map/all_to_all | solution.py:254
  73.4 6.4 %collective-permute-start.20 = (bf16[16,64,128]{2,1,0:T(8,128)(2,1)S(1)}, bf16[16,64,128]{2,1,0:T(8,128)(2,1)S(1)}, u32[]{:S(2)}, u32[]{:S(2)}) collective-permute-start(bf16[16,64,128]{2,1,0:T(8,128)(2,1)S(1)} %get-tuple-element.36.refs_5_), channel_id=1, source_target_pairs={{1,0},{2,1},{3,2},{0,3},{5,4},{6,5},{7,6},{4,7},{9,8},{10,9},{11,1... | collective-permute-start | bytes 786440 | tf_op jit(solution)/shard_map/ppermute | solution.py:241
  74.4 7.8 %collective-permute-start.21 = (bf16[16,64,128]{2,1,0:T(8,128)(2,1)S(1)}, bf16[16,64,128]{2,1,0:T(8,128)(2,1)S(1)}, u32[]{:S(2)}, u32[]{:S(2)}) collective-permute-start(bf16[16,64,128]{2,1,0:T(8,128)(2,1)S(1)} %get-tuple-element.36.refs_5_), channel_id=1, source_target_pairs={{3,0},{0,1},{1,2},{2,3},{7,4},{4,5},{5,6},{6,7},{11,8},{8,9},{9,10... | collective-permute-start | bytes 786440 | tf_op jit(solution)/shard_map/ppermute | solution.py:241
  82.2 5.5 %collective-permute-start.22 = (bf16[8,64,128]{2,1,0:T(8,128)(2,1)S(1)}, bf16[8,64,128]{2,1,0:T(8,128)(2,1)S(1)}, u32[]{:S(2)}, u32[]{:S(2)}) collective-permute-start(bf16[8,64,128]{2,1,0:T(8,128)(2,1)S(1)} %slice.22), channel_id=1, source_target_pairs={{3,0},{0,1},{1,2},{2,3},{7,4},{4,5},{5,6},{6,7},{11,8},{8,9},{9,10... | collective-permute-start | bytes 393224 | tf_op jit(solution)/shard_map/ppermute | solution.py:241
  82.3 5.4 %collective-permute-start.23 = (bf16[8,64,128]{2,1,0:T(8,128)(2,1)S(1)}, bf16[8,64,128]{2,1,0:T(8,128)(2,1)S(1)}, u32[]{:S(2)}, u32[]{:S(2)}) collective-permute-start(bf16[8,64,128]{2,1,0:T(8,128)(2,1)S(1)} %slice.23), channel_id=1, source_target_pairs={{1,0},{2,1},{3,2},{0,3},{5,4},{6,5},{7,6},{4,7},{9,8},{10,9},{11,1... | collective-permute-start | bytes 393224 | tf_op jit(solution)/shard_map/ppermute | solution.py:241
  85.0 6.5 %collective-permute-start.18 = (bf16[8,64,128]{2,1,0:T(8,128)(2,1)S(1)}, bf16[8,64,128]{2,1,0:T(8,128)(2,1)S(1)}, u32[]{:S(2)}, u32[]{:S(2)}) collective-permute-start(bf16[8,64,128]{2,1,0:T(8,128)(2,1)S(1)} %slice.20), channel_id=1, source_target_pairs={{3,0},{0,1},{1,2},{2,3},{7,4},{4,5},{5,6},{6,7},{11,8},{8,9},{9,10... | collective-permute-start | bytes 393224 | tf_op jit(solution)/shard_map/ppermute | solution.py:241
  85.0 6.5 %collective-permute-start.19 = (bf16[8,64,128]{2,1,0:T(8,128)(2,1)S(1)}, bf16[8,64,128]{2,1,0:T(8,128)(2,1)S(1)}, u32[]{:S(2)}, u32[]{:S(2)}) collective-permute-start(bf16[8,64,128]{2,1,0:T(8,128)(2,1)S(1)} %slice.21), channel_id=1, source_target_pairs={{1,0},{2,1},{3,2},{0,3},{5,4},{6,5},{7,6},{4,7},{9,8},{10,9},{11,1... | collective-permute-start | bytes 393224 | tf_op jit(solution)/shard_map/ppermute | solution.py:241
  91.6 4.8 %collective-permute-start.24 = (bf16[16,64,128]{2,1,0:T(8,128)(2,1)S(1)}, bf16[16,64,128]{2,1,0:T(8,128)(2,1)S(1)}, u32[]{:S(2)}, u32[]{:S(2)}) collective-permute-start(bf16[16,64,128]{2,1,0:T(8,128)(2,1)S(1)} %get-tuple-element.39.refs_0_), channel_id=1, source_target_pairs={{4,0},{0,4},{5,1},{1,5},{6,2},{2,6},{7,3},{3,7},{12,8},{8,12},{13,... | collective-permute-start | bytes 786440 | tf_op jit(solution)/shard_map/ppermute | solution.py:241
  (20 other events, 211.2 us)

commit v8 on v6

--- a/solution.py
+++ b/solution.py
@@ -54,13 +54,14 @@
     rows = jnp.concatenate([virt_ref[0, 0], virt_ref[0, 1]], axis=0).astype(jnp.float32)
     virt = rows.T.astype(jnp.bfloat16)
     for z, x in itertools.product(range(Z), range(X)):
-        spread_ref[z * X + x, :QUARTER] = occ[x * QUARTER : (x + 1) * QUARTER]
-        spread_ref[z * X + x, QUARTER:] = virt
+        quarter = slice(x * QUARTER, (x + 1) * QUARTER)
+        spread_ref[z * X + x, :QUARTER] = occ[quarter]
+        spread_ref[z * X + x, QUARTER:] = virt[quarter]
 
 
 def spread(own, occ_blocks, virt_blocks):
     return call(
-        spread_kernel, [(CHIPS, QUARTER + BLOCK, WIDTH)], [SMEM, VMEM, VMEM], (VMEM,), mib=8
+        spread_kernel, [(CHIPS, 2 * QUARTER, WIDTH)], [SMEM, VMEM, VMEM], (VMEM,), mib=8
     )(own, occ_blocks, virt_blocks)[0]
 
 
@@ -73,11 +74,25 @@
 def divide(both):
     return call(
         divide_kernel,
-        [(CHIPS, QUARTER, WIDTH), (CHIPS, BLOCK, WIDTH)],
+        [(CHIPS, QUARTER, WIDTH)] * 2,
         [VMEM],
         (VMEM, VMEM),
         mib=8,
     )(both)
+
+
+def assemble_kernel(own_ref, *refs):
+    *quarter_refs, out_ref = refs
+    for off, ref in enumerate(quarter_refs):
+        rows = pl.ds(pl.multiple_of(((own_ref[1] + off) & (X - 1)) * QUARTER, QUARTER), QUARTER)
+        for chip in range(CHIPS):
+            out_ref[chip, rows, :] = ref[chip]
+
+
+def assemble(own, quarters):
+    return call(
+        assemble_kernel, [(CHIPS, BLOCK, WIDTH)], [SMEM] + [VMEM] * X, (VMEM,), mib=8
+    )(own, *quarters)[0]
 
 
 def tie(arrays, *after):
@@ -257,11 +272,12 @@
 ):
     own = jnp.stack([lax.axis_index(axis) for axis in SIZES]).astype(jnp.int32)
     both = exchange(spread(own, occ_blocks, virt_blocks))
-    occ_plane, virt_plane = divide(both)
+    occ_plane, virt_quarter = divide(both)
     pieces = [occ_plane] + [shift(occ_plane, "y", by) for by in range(1, Y)]
     rows = ring(mask_rows(pair_mask, b_tensor), "x", occ_plane)
     rows = rows + [shift(part, "core", 1) for part in rows]
-    (virt_plane,) = tie([virt_plane], *pieces[1:])
+    quarters = [virt_quarter] + [shift(virt_quarter, "x", by) for by in range(1, X)]
+    virt_plane = assemble(own, quarters)
     pieces = pieces + [shift(piece, "core", 1) for piece in pieces]
     half = occupied(dense_panel(pieces, own, occ_index, second_map), rows, own)
     mine = ring(virt_plane, "y", half)

time: 98.2 us -> 103 us (1.049)
  waiting for transfers between devices: 31.7 us -> 37.1 us
    ppermute x25 -> x28, waiting for transfers between devices: 11.9 us -> 20.6 us  [shift(): lax.ppermute(array, axis, [((i + by) % size, i) for i in range(size)])]
    all_to_all x2, starting transfers between devices: 19.1 us -> 14.9 us  [exchange(): lax.all_to_all(array, ('z', 'x'), split_axis=0, concat_axis=0, tiled=True)]
    all_to_all x2, waiting for transfers between devices: 19.9 us -> 16.5 us  [exchange(): lax.all_to_all(array, ('z', 'x'), split_axis=0, concat_axis=0, tiled=True)]
    ppermute x25 -> x28, starting transfers between devices: 30 us -> 33.3 us  [shift(): lax.ppermute(array, axis, [((i + by) % size, i) for i in range(size)])]
    unnamed x16 -> x20, local copies, waits for them, and re-layouts: 3.22 us -> 3.24 us
  transfers between devices with their start and end apart: 27 -> 30, of which waited for: 8 -> 10; matrix products, arithmetic and copies ran while one was open for 0% -> 0% of each run, Pallas kernels for 10% -> 10%
where the time goes in v8:
time: 103 us; the launch traced here: 102 us
  starting transfers between devices  48.2 us (47%)
  waiting for transfers between devices  37.1 us (36%)
  Pallas kernels  13.1 us (13%)
  local copies, waits for them, and re-layouts  3.31 us (3%)
    ppermute x28, starting transfers between devices, shift(): lax.ppermute(array, axis, [((i + by) % size, i) for i in range(size)])  33.3 us
    ppermute x28, waiting for transfers between devices, shift(): lax.ppermute(array, axis, [((i + by) % size, i) for i in range(size)])  20.6 us
    all_to_all x2, waiting for transfers between devices, exchange(): lax.all_to_all(array, ('z', 'x'), split_axis=0, concat_axis=0, tiled=True)  16.5 us
    all_to_all x2, starting transfers between devices, exchange(): lax.all_to_all(array, ('z', 'x'), split_axis=0, concat_axis=0, tiled=True)  14.9 us
    pallas_call x2, Pallas kernels, virtual(): call(functools.partial(virtual_kernel, core_off), [shape] if core_off els...  4.21 us
    pallas_call x1, Pallas kernels, occupied(): call(occupied_kernel, [(CHIPS, QUARTER, lanes)], [SMEM] + [VMEM] * (1 + l...  3.98 us
    unnamed x20, local copies, waits for them, and re-layouts  3.24 us
    pallas_call x1, Pallas kernels, dense_panel(): call(dense_kernel, [shape], [SMEM] * 3 + [VMEM] * len(pieces), (VMEM,), [...  2.34 us
  transfers between devices with their start and end apart: 30, of which 10 were waited for; matrix products, arithmetic and copies ran while one was open for 0% of the time, Pallas kernels for 10%

profile of v8, /device:TPU:1, one launch (start us, length us, event | category | flops | bytes accessed | tf_op | source)
XLA Modules:
  0.0 102.1 jit_solution(11482378301641969493)
XLA Ops:
  2.3 3.4 %collective-permute-start.12 = (bf16[64,4096]{1,0:T(8,128)(2,1)S(1)}, bf16[64,4096]{1,0:T(8,128)(2,1)S(1)}, u32[]{:S(2)}, u32[]{:S(2)}) collective-permute-start(bf16[64,4096]{1,0:T(8,128)(2,1)S(1)} %shard_map.86.refs_0_), channel_id=1, source_target_pairs={{8,0},{16,8},{24,16},{0,24},{9,1},{17,9},{25,17},{1,25},{10,2},{18... | collective-permute-start | bytes 1572872 | tf_op jit(solution)/shard_map/ppermute | solution.py:254
  7.3 1.3 %shard_map.82 = bf16[32,32,128]{2,1,0:T(8,128)(2,1)} custom-call(s32[4]{0:T(128)S(1)} %pad_add_fusion.own_ref, bf16[1,2,64,64]{3,2,1,0:T(8,128)(2,1)S(1)} %copy-done.3, bf16[1,2,64,64]{3,2,1,0:T(8,128)(2,1)S(1)} %copy-done.4), custom_call_target="tpu_custom_call" | custom-call | flops 1024 | bytes 1024 | tf_op jit(solution)/shard_map/pallas_call | solution.py:63
  8.7 11.0 %all-to-all-start = ((bf16[32,32,128]{2,1,0:T(8,128)(2,1)}), bf16[32,32,128]{2,1,0:T(8,128)(2,1)S(1)}, u32[]{:S(2)}, u32[]{:S(2)}) async-start(bf16[32,32,128]{2,1,0:T(8,128)(2,1)} %shard_map.82), calls=%async_computation | async-start | bytes 524288 | tf_op jit(solution)/shard_map/all_to_all | solution.py:267
  19.7 1.6 %collective-permute-start.16 = (bf16[64,4096]{1,0:T(8,128)(2,1)S(1)}, bf16[64,4096]{1,0:T(8,128)(2,1)S(1)}, u32[]{:S(2)}, u32[]{:S(2)}) collective-permute-start(bf16[64,4096]{1,0:T(8,128)(2,1)S(1)} %shard_map.86.refs_0_), channel_id=1, source_target_pairs={{4,0},{0,4},{5,1},{1,5},{6,2},{2,6},{7,3},{3,7},{12,8},{8,12},{13,... | collective-permute-start | bytes 1572872 | tf_op jit(solution)/shard_map/ppermute | solution.py:254
  21.3 9.0 %all-to-all-done.both_ref = bf16[32,32,128]{2,1,0:T(8,128)(2,1)S(1)} async-done(((bf16[32,32,128]{2,1,0:T(8,128)(2,1)}), bf16[32,32,128]{2,1,0:T(8,128)(2,1)S(1)}, u32[]{:S(2)}, u32[]{:S(2)}) %all-to-all-start) | async-done | bytes 262176 | tf_op jit(solution)/shard_map/all_to_all | solution.py:267
  30.2 3.0 %collective-permute-start.6 = (bf16[32,16,128]{2,1,0:T(8,128)(2,1)S(1)}, bf16[32,16,128]{2,1,0:T(8,128)(2,1)S(1)}, u32[]{:S(2)}, u32[]{:S(2)}) collective-permute-start(bf16[32,16,128]{2,1,0:T(8,128)(2,1)S(1)} %get-tuple-element.19.refs_0_.refs_2_), channel_id=1, source_target_pairs={{2,0},{3,1},{0,2},{1,3},{6,4},{7,5},{4,6},{5,7},{10,8},{11,9},{8,1... | collective-permute-start | bytes 393224 | tf_op jit(solution)/shard_map/ppermute | solution.py:254
  33.6 2.3 %collective-permute-start.5 = (bf16[32,16,128]{2,1,0:T(8,128)(2,1)S(1)}, bf16[32,16,128]{2,1,0:T(8,128)(2,1)S(1)}, u32[]{:S(2)}, u32[]{:S(2)}) collective-permute-start(bf16[32,16,128]{2,1,0:T(8,128)(2,1)S(1)} %get-tuple-element.19.refs_0_.refs_2_), channel_id=1, source_target_pairs={{1,0},{2,1},{3,2},{0,3},{5,4},{6,5},{7,6},{4,7},{9,8},{10,9},{11,1... | collective-permute-start | bytes 393224 | tf_op jit(solution)/shard_map/ppermute | solution.py:254
  35.9 4.1 %collective-permute-start.8 = (bf16[32,16,128]{2,1,0:T(8,128)(2,1)S(1)}, bf16[32,16,128]{2,1,0:T(8,128)(2,1)S(1)}, u32[]{:S(2)}, u32[]{:S(2)}) collective-permute-start(bf16[32,16,128]{2,1,0:T(8,128)(2,1)S(1)} %get-tuple-element.19.refs_0_.refs_2_), channel_id=1, source_target_pairs={{4,0},{0,4},{5,1},{1,5},{6,2},{2,6},{7,3},{3,7},{12,8},{8,12},{13,... | collective-permute-start | bytes 393224 | tf_op jit(solution)/shard_map/ppermute | solution.py:254
  42.4 1.5 %collective-permute-start.2 = (bf16[32,16,128]{2,1,0:T(8,128)(2,1)S(1)}, bf16[32,16,128]{2,1,0:T(8,128)(2,1)S(1)}, u32[]{:S(2)}, u32[]{:S(2)}) collective-permute-start(bf16[32,16,128]{2,1,0:T(8,128)(2,1)S(1)} %get-tuple-element.18.refs_0_), channel_id=1, source_target_pairs={{24,0},{0,8},{8,16},{16,24},{25,1},{1,9},{9,17},{17,25},{26,2},{2,... | collective-permute-start | bytes 393224 | tf_op jit(solution)/shard_map/ppermute | solution.py:254
  45.3 1.3 %collective-permute-start.10 = (bf16[32,16,128]{2,1,0:T(8,128)(2,1)S(1)}, bf16[32,16,128]{2,1,0:T(8,128)(2,1)S(1)}, u32[]{:S(2)}, u32[]{:S(2)}) collective-permute-start(bf16[32,16,128]{2,1,0:T(8,128)(2,1)S(1)} %collective-permute-done.6.refs_2_), channel_id=1, source_target_pairs={{4,0},{0,4},{5,1},{1,5},{6,2},{2,6},{7,3},{3,7},{12,8},{8,12},{13,... | collective-permute-start | bytes 393224 | tf_op jit(solution)/shard_map/ppermute | solution.py:254
  47.6 1.8 %collective-permute-start.11 = (bf16[32,16,128]{2,1,0:T(8,128)(2,1)S(1)}, bf16[32,16,128]{2,1,0:T(8,128)(2,1)S(1)}, u32[]{:S(2)}, u32[]{:S(2)}) collective-permute-start(bf16[32,16,128]{2,1,0:T(8,128)(2,1)S(1)} %collective-permute-done.7.refs_3_), channel_id=1, source_target_pairs={{4,0},{0,4},{5,1},{1,5},{6,2},{2,6},{7,3},{3,7},{12,8},{8,12},{13,... | collective-permute-start | bytes 393224 | tf_op jit(solution)/shard_map/ppermute | solution.py:254
  49.4 7.2 %collective-permute-done.2.refs_3_ = bf16[32,16,128]{2,1,0:T(8,128)(2,1)S(1)} collective-permute-done((bf16[32,16,128]{2,1,0:T(8,128)(2,1)S(1)}, bf16[32,16,128]{2,1,0:T(8,128)(2,1)S(1)}, u32[]{:S(2)}, u32[]{:S(2)}) %collective-permute-start.2) | collective-permute-done | bytes 131104 | tf_op jit(solution)/shard_map/ppermute | solution.py:254
  58.7 1.4 %collective-permute-start.4 = (bf16[32,64,128]{2,1,0:T(8,128)(2,1)S(1)}, bf16[32,64,128]{2,1,0:T(8,128)(2,1)S(1)}, u32[]{:S(2)}, u32[]{:S(2)}) collective-permute-start(bf16[32,64,128]{2,1,0:T(8,128)(2,1)S(1)} %shard_map.84.refs_0_), channel_id=1, source_target_pairs={{3,0},{0,1},{1,2},{2,3},{7,4},{4,5},{5,6},{6,7},{11,8},{8,9},{9,10... | collective-permute-start | bytes 1572872 | tf_op jit(solution)/shard_map/ppermute | solution.py:254
  60.9 2.3 %shard_map.85.dense_ref = bf16[512,4096]{1,0:T(8,128)(2,1)S(1)} custom-call(s32[8,64]{1,0:T(8,128)S(1)} %bitcast.9, s32[64]{0:T(128)S(1)} %copy-done.9, s32[4]{0:T(128)S(1)} %pad_add_fusion.own_ref, bf16[32,16,128]{2,1,0:T(8,128)(2,1)S(1)} %get-tuple-element.19.refs_0_.refs_2_, bf16[32,16,128]{2,1,0:T(8,128)(2,1)S(1)} %collective-permute-done.5.refs_1_, ...), custom_call_target="tpu_custom_call" | custom-call | flops 1024 | bytes 1024 | tf_op jit(solution)/shard_map/pallas_call | solution.py:145
  63.3 4.0 %shard_map.88.refs_2_.refs_0_ = bf16[32,16,512]{2,1,0:T(8,128)(2,1)} custom-call(s32[4]{0:T(128)S(1)} %pad_add_fusion.own_ref, bf16[512,4096]{1,0:T(8,128)(2,1)S(1)} %shard_map.85.dense_ref, bf16[64,4096]{1,0:T(8,128)(2,1)S(1)} %shard_map.86.refs_0_, bf16[64,4096]{1,0:T(8,128)(2,1)S(1)} %get-tuple-element.20.refs_1_, ...), custom_call_target="tpu_custom_call" | custom-call | flops 1024 | bytes 1024 | tf_op jit(solution)/shard_map/pallas_call | solution.py:172
  67.3 4.6 %collective-permute-done.3.refs_0_ = bf16[32,64,128]{2,1,0:T(8,128)(2,1)S(1)} collective-permute-done((bf16[32,64,128]{2,1,0:T(8,128)(2,1)S(1)}, bf16[32,64,128]{2,1,0:T(8,128)(2,1)S(1)}, u32[]{:S(2)}, u32[]{:S(2)}) %collective-permute-start.3) | collective-permute-done | bytes 524320 | tf_op jit(solution)/shard_map/ppermute | solution.py:254
  71.9 1.3 %collective-permute-done.4.refs_1_ = bf16[32,64,128]{2,1,0:T(8,128)(2,1)S(1)} collective-permute-done((bf16[32,64,128]{2,1,0:T(8,128)(2,1)S(1)}, bf16[32,64,128]{2,1,0:T(8,128)(2,1)S(1)}, u32[]{:S(2)}, u32[]{:S(2)}) %collective-permute-start.4) | collective-permute-done | bytes 524320 | tf_op jit(solution)/shard_map/ppermute | solution.py:254
  73.3 3.9 %all-to-all-start.1 = ((bf16[32,16,512]{2,1,0:T(8,128)(2,1)}), bf16[32,16,512]{2,1,0:T(8,128)(2,1)S(1)}, u32[]{:S(2)}, u32[]{:S(2)}) async-start(bf16[32,16,512]{2,1,0:T(8,128)(2,1)} %shard_map.90), calls=%async_computation.1 | async-start | bytes 1048576 | tf_op jit(solution)/shard_map/all_to_all | solution.py:267
  77.3 2.7 %collective-permute-start.22 = (bf16[16,64,128]{2,1,0:T(8,128)(2,1)S(1)}, bf16[16,64,128]{2,1,0:T(8,128)(2,1)S(1)}, u32[]{:S(2)}, u32[]{:S(2)}) collective-permute-start(bf16[16,64,128]{2,1,0:T(8,128)(2,1)S(1)} %slice.15), channel_id=1, source_target_pairs={{1,0},{2,1},{3,2},{0,3},{5,4},{6,5},{7,6},{4,7},{9,8},{10,9},{11,1... | collective-permute-start | bytes 786440 | tf_op jit(solution)/shard_map/ppermute | solution.py:254
  80.0 5.3 %collective-permute-done.21.refs_3_ = bf16[16,64,128]{2,1,0:T(8,128)(2,1)S(1)} collective-permute-done((bf16[16,64,128]{2,1,0:T(8,128)(2,1)S(1)}, bf16[16,64,128]{2,1,0:T(8,128)(2,1)S(1)}, u32[]{:S(2)}, u32[]{:S(2)}) %collective-permute-start.21) | collective-permute-done | bytes 262176 | tf_op jit(solution)/shard_map/ppermute | solution.py:254
  85.2 7.6 %all-to-all-done.1.refs_5_ = bf16[32,16,512]{2,1,0:T(8,128)(2,1)S(1)} async-done(((bf16[32,16,512]{2,1,0:T(8,128)(2,1)}), bf16[32,16,512]{2,1,0:T(8,128)(2,1)S(1)}, u32[]{:S(2)}, u32[]{:S(2)}) %all-to-all-start.1) | async-done | bytes 524320 | tf_op jit(solution)/shard_map/all_to_all | solution.py:267
  92.8 3.0 %collective-permute-start.23 = (bf16[32,64,128]{2,1,0:T(8,128)(2,1)S(1)}, bf16[32,64,128]{2,1,0:T(8,128)(2,1)S(1)}, u32[]{:S(2)}, u32[]{:S(2)}) collective-permute-start(bf16[32,64,128]{2,1,0:T(8,128)(2,1)S(1)} %get-tuple-element.24.refs_0_), channel_id=1, source_target_pairs={{4,0},{0,4},{5,1},{1,5},{6,2},{2,6},{7,3},{3,7},{12,8},{8,12},{13,... | collective-permute-start | bytes 1572872 | tf_op jit(solution)/shard_map/ppermute | solution.py:254
  96.8 1.8 %shard_map.92 = (bf16[64,4096]{1,0:T(8,128)(2,1)S(1)}, bf16[64,64,128]{2,1,0:T(8,128)(2,1)S(1)}) custom-call(s32[8,64]{1,0:T(8,128)S(1)} %bitcast.7, s32[64]{0:T(128)S(1)} %copy-done.7, s32[4]{0:T(128)S(1)} %pad_add_fusion.own_ref, bf16[32,64,128]{2,1,0:T(8,128)(2,1)S(1)} %get-tuple-element.24.refs_0_, bf16[32,64,128]{2,1,0:T(8,128)(2,1)S(1)} %get-tuple-element.25.refs_1_, ...), custom_call_target="tpu_custom_call" | custom-call | flops 1024 | bytes 1024 | tf_op jit(solution)/shard_map/pallas_call | solution.py:243
  99.6 2.4 %shard_map.93 = bf16[64,4096]{1,0:T(8,128)(2,1)} custom-call(s32[8,64]{1,0:T(8,128)S(1)} %bitcast.8, s32[64]{0:T(128)S(1)} %copy-done.7, s32[4]{0:T(128)S(1)} %pad_add_fusion.own_ref, bf16[32,64,128]{2,1,0:T(8,128)(2,1)S(1)} %collective-permute-done.23.refs_0_, bf16[32,64,128]{2,1,0:T(8,128)(2,1)S(1)} %collective-permute-done.24.refs_1_, ...), custom_call_target="tpu_custom_call" | custom-call | flops 1024 | bytes 1024 | tf_op jit(solution)/shard_map/pallas_call | solution.py:243
  (73 shorter events, 14.0 us)
Async XLA Ops:
  2.3 31.3 %collective-permute-start.12 = (bf16[64,4096]{1,0:T(8,128)(2,1)S(1)}, bf16[64,4096]{1,0:T(8,128)(2,1)S(1)}, u32[]{:S(2)}, u32[]{:S(2)}) collective-permute-start(bf16[64,4096]{1,0:T(8,128)(2,1)S(1)} %shard_map.86.refs_0_), channel_id=1, source_target_pairs={{8,0},{16,8},{24,16},{0,24},{9,1},{17,9},{25,17},{1,25},{10,2},{18... | collective-permute-start | bytes 1572872 | tf_op jit(solution)/shard_map/ppermute | solution.py:254
  5.7 30.2 %collective-permute-start.13 = (bf16[64,4096]{1,0:T(8,128)(2,1)S(1)}, bf16[64,4096]{1,0:T(8,128)(2,1)S(1)}, u32[]{:S(2)}, u32[]{:S(2)}) collective-permute-start(bf16[64,4096]{1,0:T(8,128)(2,1)S(1)} %shard_map.86.refs_0_), channel_id=1, source_target_pairs={{24,0},{0,8},{8,16},{16,24},{25,1},{1,9},{9,17},{17,25},{26,2},{2,... | collective-permute-start | bytes 1572872 | tf_op jit(solution)/shard_map/ppermute | solution.py:254
  8.7 21.5 %all-to-all-start = ((bf16[32,32,128]{2,1,0:T(8,128)(2,1)}), bf16[32,32,128]{2,1,0:T(8,128)(2,1)S(1)}, u32[]{:S(2)}, u32[]{:S(2)}) async-start(bf16[32,32,128]{2,1,0:T(8,128)(2,1)} %shard_map.82), calls=%async_computation | async-start | bytes 524288 | tf_op jit(solution)/shard_map/all_to_all | solution.py:267
  19.7 20.4 %collective-permute-start.16 = (bf16[64,4096]{1,0:T(8,128)(2,1)S(1)}, bf16[64,4096]{1,0:T(8,128)(2,1)S(1)}, u32[]{:S(2)}, u32[]{:S(2)}) collective-permute-start(bf16[64,4096]{1,0:T(8,128)(2,1)S(1)} %shard_map.86.refs_0_), channel_id=1, source_target_pairs={{4,0},{0,4},{5,1},{1,5},{6,2},{2,6},{7,3},{3,7},{12,8},{8,12},{13,... | collective-permute-start | bytes 1572872 | tf_op jit(solution)/shard_map/ppermute | solution.py:254
  30.2 11.0 %collective-permute-start.6 = (bf16[32,16,128]{2,1,0:T(8,128)(2,1)S(1)}, bf16[32,16,128]{2,1,0:T(8,128)(2,1)S(1)}, u32[]{:S(2)}, u32[]{:S(2)}) collective-permute-start(bf16[32,16,128]{2,1,0:T(8,128)(2,1)S(1)} %get-tuple-element.19.refs_0_.refs_2_), channel_id=1, source_target_pairs={{2,0},{3,1},{0,2},{1,3},{6,4},{7,5},{4,6},{5,7},{10,8},{11,9},{8,1... | collective-permute-start | bytes 393224 | tf_op jit(solution)/shard_map/ppermute | solution.py:254
  33.2 8.6 %collective-permute-start.7 = (bf16[32,16,128]{2,1,0:T(8,128)(2,1)S(1)}, bf16[32,16,128]{2,1,0:T(8,128)(2,1)S(1)}, u32[]{:S(2)}, u32[]{:S(2)}) collective-permute-start(bf16[32,16,128]{2,1,0:T(8,128)(2,1)S(1)} %get-tuple-element.19.refs_0_.refs_2_), channel_id=1, source_target_pairs={{3,0},{0,1},{1,2},{2,3},{7,4},{4,5},{5,6},{6,7},{11,8},{8,9},{9,10... | collective-permute-start | bytes 393224 | tf_op jit(solution)/shard_map/ppermute | solution.py:254
  33.6 8.7 %collective-permute-start.5 = (bf16[32,16,128]{2,1,0:T(8,128)(2,1)S(1)}, bf16[32,16,128]{2,1,0:T(8,128)(2,1)S(1)}, u32[]{:S(2)}, u32[]{:S(2)}) collective-permute-start(bf16[32,16,128]{2,1,0:T(8,128)(2,1)S(1)} %get-tuple-element.19.refs_0_.refs_2_), channel_id=1, source_target_pairs={{1,0},{2,1},{3,2},{0,3},{5,4},{6,5},{7,6},{4,7},{9,8},{10,9},{11,1... | collective-permute-start | bytes 393224 | tf_op jit(solution)/shard_map/ppermute | solution.py:254
  35.9 8.0 %collective-permute-start.8 = (bf16[32,16,128]{2,1,0:T(8,128)(2,1)S(1)}, bf16[32,16,128]{2,1,0:T(8,128)(2,1)S(1)}, u32[]{:S(2)}, u32[]{:S(2)}) collective-permute-start(bf16[32,16,128]{2,1,0:T(8,128)(2,1)S(1)} %get-tuple-element.19.refs_0_.refs_2_), channel_id=1, source_target_pairs={{4,0},{0,4},{5,1},{1,5},{6,2},{2,6},{7,3},{3,7},{12,8},{8,12},{13,... | collective-permute-start | bytes 393224 | tf_op jit(solution)/shard_map/ppermute | solution.py:254
  40.1 5.2 %collective-permute-start = (bf16[32,16,128]{2,1,0:T(8,128)(2,1)S(1)}, bf16[32,16,128]{2,1,0:T(8,128)(2,1)S(1)}, u32[]{:S(2)}, u32[]{:S(2)}) collective-permute-start(bf16[32,16,128]{2,1,0:T(8,128)(2,1)S(1)} %get-tuple-element.18.refs_0_), channel_id=1, source_target_pairs={{8,0},{16,8},{24,16},{0,24},{9,1},{17,9},{25,17},{1,25},{10,2},{18... | collective-permute-start | bytes 393224 | tf_op jit(solution)/shard_map/ppermute | solution.py:254
  41.2 6.4 %collective-permute-start.1 = (bf16[32,16,128]{2,1,0:T(8,128)(2,1)S(1)}, bf16[32,16,128]{2,1,0:T(8,128)(2,1)S(1)}, u32[]{:S(2)}, u32[]{:S(2)}) collective-permute-start(bf16[32,16,128]{2,1,0:T(8,128)(2,1)S(1)} %get-tuple-element.18.refs_0_), channel_id=1, source_target_pairs={{16,0},{24,8},{0,16},{8,24},{17,1},{25,9},{1,17},{9,25},{18,2},{26... | collective-permute-start | bytes 393224 | tf_op jit(solution)/shard_map/ppermute | solution.py:254
  41.8 16.0 %collective-permute-start.14 = (bf16[32,4096]{1,0:T(8,128)(2,1)S(1)}, bf16[32,4096]{1,0:T(8,128)(2,1)S(1)}, u32[]{:S(2)}, u32[]{:S(2)}) collective-permute-start(bf16[32,4096]{1,0:T(8,128)(2,1)S(1)} %slice.12), channel_id=1, source_target_pairs={{24,0},{0,8},{8,16},{16,24},{25,1},{1,9},{9,17},{17,25},{26,2},{2,... | collective-permute-start | bytes 786440 | tf_op jit(solution)/shard_map/ppermute | solution.py:254
  42.4 14.2 %collective-permute-start.2 = (bf16[32,16,128]{2,1,0:T(8,128)(2,1)S(1)}, bf16[32,16,128]{2,1,0:T(8,128)(2,1)S(1)}, u32[]{:S(2)}, u32[]{:S(2)}) collective-permute-start(bf16[32,16,128]{2,1,0:T(8,128)(2,1)S(1)} %get-tuple-element.18.refs_0_), channel_id=1, source_target_pairs={{24,0},{0,8},{8,16},{16,24},{25,1},{1,9},{9,17},{17,25},{26,2},{2,... | collective-permute-start | bytes 393224 | tf_op jit(solution)/shard_map/ppermute | solution.py:254
  43.9 14.7 %collective-permute-start.15 = (bf16[32,4096]{1,0:T(8,128)(2,1)S(1)}, bf16[32,4096]{1,0:T(8,128)(2,1)S(1)}, u32[]{:S(2)}, u32[]{:S(2)}) collective-permute-start(bf16[32,4096]{1,0:T(8,128)(2,1)S(1)} %slice.13), channel_id=1, source_target_pairs={{8,0},{16,8},{24,16},{0,24},{9,1},{17,9},{25,17},{1,25},{10,2},{18... | collective-permute-start | bytes 786440 | tf_op jit(solution)/shard_map/ppermute | solution.py:254
  45.3 12.4 %collective-permute-start.10 = (bf16[32,16,128]{2,1,0:T(8,128)(2,1)S(1)}, bf16[32,16,128]{2,1,0:T(8,128)(2,1)S(1)}, u32[]{:S(2)}, u32[]{:S(2)}) collective-permute-start(bf16[32,16,128]{2,1,0:T(8,128)(2,1)S(1)} %collective-permute-done.6.refs_2_), channel_id=1, source_target_pairs={{4,0},{0,4},{5,1},{1,5},{6,2},{2,6},{7,3},{3,7},{12,8},{8,12},{13,... | collective-permute-start | bytes 393224 | tf_op jit(solution)/shard_map/ppermute | solution.py:254
  47.6 10.7 %collective-permute-start.11 = (bf16[32,16,128]{2,1,0:T(8,128)(2,1)S(1)}, bf16[32,16,128]{2,1,0:T(8,128)(2,1)S(1)}, u32[]{:S(2)}, u32[]{:S(2)}) collective-permute-start(bf16[32,16,128]{2,1,0:T(8,128)(2,1)S(1)} %collective-permute-done.7.refs_3_), channel_id=1, source_target_pairs={{4,0},{0,4},{5,1},{1,5},{6,2},{2,6},{7,3},{3,7},{12,8},{8,12},{13,... | collective-permute-start | bytes 393224 | tf_op jit(solution)/shard_map/ppermute | solution.py:254
  57.7 5.6 %collective-permute-start.17 = (bf16[64,4096]{1,0:T(8,128)(2,1)S(1)}, bf16[64,4096]{1,0:T(8,128)(2,1)S(1)}, u32[]{:S(2)}, u32[]{:S(2)}) collective-permute-start(bf16[64,4096]{1,0:T(8,128)(2,1)S(1)} %get-tuple-element.20.refs_1_), channel_id=1, source_target_pairs={{4,0},{0,4},{5,1},{1,5},{6,2},{2,6},{7,3},{3,7},{12,8},{8,12},{13,... | collective-permute-start | bytes 1572872 | tf_op jit(solution)/shard_map/ppermute | solution.py:254
  58.3 5.0 %collective-permute-start.18 = (bf16[64,4096]{1,0:T(8,128)(2,1)S(1)}, bf16[64,4096]{1,0:T(8,128)(2,1)S(1)}, u32[]{:S(2)}, u32[]{:S(2)}) collective-permute-start(bf16[64,4096]{1,0:T(8,128)(2,1)S(1)} %get-tuple-element.21.refs_2_), channel_id=1, source_target_pairs={{4,0},{0,4},{5,1},{1,5},{6,2},{2,6},{7,3},{3,7},{12,8},{8,12},{13,... | collective-permute-start | bytes 1572872 | tf_op jit(solution)/shard_map/ppermute | solution.py:254
  58.6 13.4 %collective-permute-start.3 = (bf16[32,64,128]{2,1,0:T(8,128)(2,1)S(1)}, bf16[32,64,128]{2,1,0:T(8,128)(2,1)S(1)}, u32[]{:S(2)}, u32[]{:S(2)}) collective-permute-start(bf16[32,64,128]{2,1,0:T(8,128)(2,1)S(1)} %shard_map.84.refs_0_), channel_id=1, source_target_pairs={{1,0},{2,1},{3,2},{0,3},{5,4},{6,5},{7,6},{4,7},{9,8},{10,9},{11,1... | collective-permute-start | bytes 1572872 | tf_op jit(solution)/shard_map/ppermute | solution.py:254
  58.7 14.6 %collective-permute-start.4 = (bf16[32,64,128]{2,1,0:T(8,128)(2,1)S(1)}, bf16[32,64,128]{2,1,0:T(8,128)(2,1)S(1)}, u32[]{:S(2)}, u32[]{:S(2)}) collective-permute-start(bf16[32,64,128]{2,1,0:T(8,128)(2,1)S(1)} %shard_map.84.refs_0_), channel_id=1, source_target_pairs={{3,0},{0,1},{1,2},{2,3},{7,4},{4,5},{5,6},{6,7},{11,8},{8,9},{9,10... | collective-permute-start | bytes 1572872 | tf_op jit(solution)/shard_map/ppermute | solution.py:254
  73.3 19.5 %all-to-all-start.1 = ((bf16[32,16,512]{2,1,0:T(8,128)(2,1)}), bf16[32,16,512]{2,1,0:T(8,128)(2,1)S(1)}, u32[]{:S(2)}, u32[]{:S(2)}) async-start(bf16[32,16,512]{2,1,0:T(8,128)(2,1)} %shard_map.90), calls=%async_computation.1 | async-start | bytes 1048576 | tf_op jit(solution)/shard_map/all_to_all | solution.py:267
  77.2 8.0 %collective-permute-start.21 = (bf16[16,64,128]{2,1,0:T(8,128)(2,1)S(1)}, bf16[16,64,128]{2,1,0:T(8,128)(2,1)S(1)}, u32[]{:S(2)}, u32[]{:S(2)}) collective-permute-start(bf16[16,64,128]{2,1,0:T(8,128)(2,1)S(1)} %slice.14), channel_id=1, source_target_pairs={{3,0},{0,1},{1,2},{2,3},{7,4},{4,5},{5,6},{6,7},{11,8},{8,9},{9,10... | collective-permute-start | bytes 786440 | tf_op jit(solution)/shard_map/ppermute | solution.py:254
  77.3 7.9 %collective-permute-start.22 = (bf16[16,64,128]{2,1,0:T(8,128)(2,1)S(1)}, bf16[16,64,128]{2,1,0:T(8,128)(2,1)S(1)}, u32[]{:S(2)}, u32[]{:S(2)}) collective-permute-start(bf16[16,64,128]{2,1,0:T(8,128)(2,1)S(1)} %slice.15), channel_id=1, source_target_pairs={{1,0},{2,1},{3,2},{0,3},{5,4},{6,5},{7,6},{4,7},{9,8},{10,9},{11,1... | collective-permute-start | bytes 786440 | tf_op jit(solution)/shard_map/ppermute | solution.py:254
  92.8 6.8 %collective-permute-start.23 = (bf16[32,64,128]{2,1,0:T(8,128)(2,1)S(1)}, bf16[32,64,128]{2,1,0:T(8,128)(2,1)S(1)}, u32[]{:S(2)}, u32[]{:S(2)}) collective-permute-start(bf16[32,64,128]{2,1,0:T(8,128)(2,1)S(1)} %get-tuple-element.24.refs_0_), channel_id=1, source_target_pairs={{4,0},{0,4},{5,1},{1,5},{6,2},{2,6},{7,3},{3,7},{12,8},{8,12},{13,... | collective-permute-start | bytes 1572872 | tf_op jit(solution)/shard_map/ppermute | solution.py:254
  95.8 3.8 %collective-permute-start.24 = (bf16[32,64,128]{2,1,0:T(8,128)(2,1)S(1)}, bf16[32,64,128]{2,1,0:T(8,128)(2,1)S(1)}, u32[]{:S(2)}, u32[]{:S(2)}) collective-permute-start(bf16[32,64,128]{2,1,0:T(8,128)(2,1)S(1)} %get-tuple-element.25.refs_1_), channel_id=1, source_target_pairs={{4,0},{0,4},{5,1},{1,5},{6,2},{2,6},{7,3},{3,7},{12,8},{8,12},{13,... | collective-permute-start | bytes 1572872 | tf_op jit(solution)/shard_map/ppermute | solution.py:254
  (16 other events, 221.3 us)

commit v9 on v8

--- a/solution.py
+++ b/solution.py
@@ -276,12 +276,13 @@
     pieces = [occ_plane] + [shift(occ_plane, "y", by) for by in range(1, Y)]
     rows = ring(mask_rows(pair_mask, b_tensor), "x", occ_plane)
     rows = rows + [shift(part, "core", 1) for part in rows]
+    (virt_quarter,) = tie([virt_quarter], *rows[3:5])
     quarters = [virt_quarter] + [shift(virt_quarter, "x", by) for by in range(1, X)]
     virt_plane = assemble(own, quarters)
     pieces = pieces + [shift(piece, "core", 1) for piece in pieces]
     half = occupied(dense_panel(pieces, own, occ_index, second_map), rows, own)
     mine = ring(virt_plane, "y", half)
-    turned = exchange(*tie([half], *mine[1:3]))
+    turned = exchange(*tie([half], virt_plane))
     mine = tie(mine, turned)
     other = [shift(panel, "core", 1) for panel in mine]
     known = (own, virt_index, first_map)

time: 103 us -> 103 us (level)
  blocking collectives: 0 us -> 21.3 us
  starting transfers between devices: 48.2 us -> 34.8 us
  waiting for transfers between devices: 37.1 us -> 30.1 us
  Pallas kernels: 13.1 us -> 11.6 us
    all_to_all x0 -> x1, blocking collectives: none -> 21.3 us  [exchange(): lax.all_to_all(array, ('z', 'x'), split_axis=0, concat_axis=0, tiled=True)]
    all_to_all x2 -> x1, waiting for transfers between devices: 16.5 us -> 0.01 us  [exchange(): lax.all_to_all(array, ('z', 'x'), split_axis=0, concat_axis=0, tiled=True)]
    all_to_all x2 -> x1, starting transfers between devices: 14.9 us -> 4.02 us  [exchange(): lax.all_to_all(array, ('z', 'x'), split_axis=0, concat_axis=0, tiled=True)]
    ppermute x28, waiting for transfers between devices: 20.6 us -> 30.1 us  [shift(): lax.ppermute(array, axis, [((i + by) % size, i) for i in range(size)])]
    ppermute x28, starting transfers between devices: 33.3 us -> 30.8 us  [shift(): lax.ppermute(array, axis, [((i + by) % size, i) for i in range(size)])]
    unnamed x20 -> x17, local copies, waits for them, and re-layouts: 3.24 us -> 4.02 us
  transfers between devices with their start and end apart: 30 -> 29, of which waited for: 10 -> 11; matrix products, arithmetic and copies ran while one was open for 0% -> 0% of each run, Pallas kernels for 10% -> 5%
where the time goes in v9:
time: 103 us; the launch traced here: 102 us
  starting transfers between devices  34.8 us (34%)
  waiting for transfers between devices  30.1 us (29%)
  blocking collectives  21.3 us (21%)
  Pallas kernels  11.6 us (11%)
  local copies, waits for them, and re-layouts  4.1 us (4%)
    ppermute x28, starting transfers between devices, shift(): lax.ppermute(array, axis, [((i + by) % size, i) for i in range(size)])  30.8 us
    ppermute x28, waiting for transfers between devices, shift(): lax.ppermute(array, axis, [((i + by) % size, i) for i in range(size)])  30.1 us
    all_to_all x1, blocking collectives, exchange(): lax.all_to_all(array, ('z', 'x'), split_axis=0, concat_axis=0, tiled=True)  21.3 us
    pallas_call x2, Pallas kernels, virtual(): call(functools.partial(virtual_kernel, core_off), [shape] if core_off els...  4.21 us
    all_to_all x1, starting transfers between devices, exchange(): lax.all_to_all(array, ('z', 'x'), split_axis=0, concat_axis=0, tiled=True)  4.02 us
    unnamed x17, local copies, waits for them, and re-layouts  4.02 us
    pallas_call x1, Pallas kernels, occupied(): call(occupied_kernel, [(CHIPS, QUARTER, lanes)], [SMEM] + [VMEM] * (1 + l...  3.18 us
    pallas_call x1, Pallas kernels, dense_panel(): call(dense_kernel, [shape], [SMEM] * 3 + [VMEM] * len(pieces), (VMEM,), [...  2.34 us
  transfers between devices with their start and end apart: 29, of which 11 were waited for; matrix products, arithmetic and copies ran while one was open for 0% of the time, Pallas kernels for 5%

profile of v9, /device:TPU:1, one launch (start us, length us, event | category | flops | bytes accessed | tf_op | source)
XLA Modules:
  0.0 102.4 jit_solution(1928881578976313871)
XLA Ops:
  0.0 1.0 %copy-done = bf16[1,64,4096]{2,1,0:T(8,128)(2,1)S(1)} copy-done((bf16[1,64,4096]{2,1,0:T(8,128)(2,1)S(1)}, bf16[1,64,4096]{2,1,0:T(8,128)(2,1)}, u32[]{:S(2)}) %copy-start) | copy-done | bytes 524312
  2.3 3.4 %collective-permute-start = (bf16[64,4096]{1,0:T(8,128)(2,1)S(1)}, bf16[64,4096]{1,0:T(8,128)(2,1)S(1)}, u32[]{:S(2)}, u32[]{:S(2)}) collective-permute-start(bf16[64,4096]{1,0:T(8,128)(2,1)S(1)} %shard_map.84.refs_0_), channel_id=1, source_target_pairs={{8,0},{16,8},{24,16},{0,24},{9,1},{17,9},{25,17},{1,25},{10,2},{18... | collective-permute-start | bytes 1572872 | tf_op jit(solution)/shard_map/ppermute | solution.py:254
  8.0 21.3 %all_to_all.10.both_ref = bf16[32,32,128]{2,1,0:T(8,128)(2,1)S(1)} all-to-all(bf16[32,32,128]{2,1,0:T(8,128)(2,1)S(1)} %shard_map.82), channel_id=1, replica_groups=mesh['z'=8,'x'=4,'core'=2,'y'=4] {'z','x'}, dimensions={0} | all-to-all | bytes 524288 | tf_op jit(solution)/shard_map/all_to_all | solution.py:267
  29.5 2.7 %collective-permute-start.3 = (bf16[32,4096]{1,0:T(8,128)(2,1)S(1)}, bf16[32,4096]{1,0:T(8,128)(2,1)S(1)}, u32[]{:S(2)}, u32[]{:S(2)}) collective-permute-start(bf16[32,4096]{1,0:T(8,128)(2,1)S(1)} %slice.13), channel_id=1, source_target_pairs={{8,0},{16,8},{24,16},{0,24},{9,1},{17,9},{25,17},{1,25},{10,2},{18... | collective-permute-start | bytes 786440 | tf_op jit(solution)/shard_map/ppermute | solution.py:254
  32.2 2.7 %collective-permute-start.9 = (bf16[32,16,128]{2,1,0:T(8,128)(2,1)S(1)}, bf16[32,16,128]{2,1,0:T(8,128)(2,1)S(1)}, u32[]{:S(2)}, u32[]{:S(2)}) collective-permute-start(bf16[32,16,128]{2,1,0:T(8,128)(2,1)S(1)} %get-tuple-element.19.refs_2_.refs_0_), channel_id=1, source_target_pairs={{1,0},{2,1},{3,2},{0,3},{5,4},{6,5},{7,6},{4,7},{9,8},{10,9},{11,1... | collective-permute-start | bytes 393224 | tf_op jit(solution)/shard_map/ppermute | solution.py:254
  36.0 2.3 %collective-permute-done.9.refs_1_ = bf16[32,16,128]{2,1,0:T(8,128)(2,1)S(1)} collective-permute-done((bf16[32,16,128]{2,1,0:T(8,128)(2,1)S(1)}, bf16[32,16,128]{2,1,0:T(8,128)(2,1)S(1)}, u32[]{:S(2)}, u32[]{:S(2)}) %collective-permute-start.9) | collective-permute-done | bytes 131104 | tf_op jit(solution)/shard_map/ppermute | solution.py:254
  38.3 4.7 %collective-permute-start.12 = (bf16[32,16,128]{2,1,0:T(8,128)(2,1)S(1)}, bf16[32,16,128]{2,1,0:T(8,128)(2,1)S(1)}, u32[]{:S(2)}, u32[]{:S(2)}) collective-permute-start(bf16[32,16,128]{2,1,0:T(8,128)(2,1)S(1)} %get-tuple-element.19.refs_2_.refs_0_), channel_id=1, source_target_pairs={{4,0},{0,4},{5,1},{1,5},{6,2},{2,6},{7,3},{3,7},{12,8},{8,12},{13,... | collective-permute-start | bytes 393224 | tf_op jit(solution)/shard_map/ppermute | solution.py:254
  43.0 2.6 %collective-permute-start.13 = (bf16[32,16,128]{2,1,0:T(8,128)(2,1)S(1)}, bf16[32,16,128]{2,1,0:T(8,128)(2,1)S(1)}, u32[]{:S(2)}, u32[]{:S(2)}) collective-permute-start(bf16[32,16,128]{2,1,0:T(8,128)(2,1)S(1)} %collective-permute-done.9.refs_1_), channel_id=1, source_target_pairs={{4,0},{0,4},{5,1},{1,5},{6,2},{2,6},{7,3},{3,7},{12,8},{8,12},{13,... | collective-permute-start | bytes 393224 | tf_op jit(solution)/shard_map/ppermute | solution.py:254
  45.7 1.3 %collective-permute-start.14 = (bf16[32,16,128]{2,1,0:T(8,128)(2,1)S(1)}, bf16[32,16,128]{2,1,0:T(8,128)(2,1)S(1)}, u32[]{:S(2)}, u32[]{:S(2)}) collective-permute-start(bf16[32,16,128]{2,1,0:T(8,128)(2,1)S(1)} %collective-permute-done.10.refs_2_), channel_id=1, source_target_pairs={{4,0},{0,4},{5,1},{1,5},{6,2},{2,6},{7,3},{3,7},{12,8},{8,12},{13,... | collective-permute-start | bytes 393224 | tf_op jit(solution)/shard_map/ppermute | solution.py:254
  49.2 3.4 %collective-permute-done.4.refs_1_ = bf16[32,16,128]{2,1,0:T(8,128)(2,1)S(1)} collective-permute-done((bf16[32,16,128]{2,1,0:T(8,128)(2,1)S(1)}, bf16[32,16,128]{2,1,0:T(8,128)(2,1)S(1)}, u32[]{:S(2)}, u32[]{:S(2)}) %collective-permute-start.4) | collective-permute-done | bytes 131104 | tf_op jit(solution)/shard_map/ppermute | solution.py:254
  52.6 2.9 %collective-permute-done.5.refs_2_ = bf16[32,16,128]{2,1,0:T(8,128)(2,1)S(1)} collective-permute-done((bf16[32,16,128]{2,1,0:T(8,128)(2,1)S(1)}, bf16[32,16,128]{2,1,0:T(8,128)(2,1)S(1)}, u32[]{:S(2)}, u32[]{:S(2)}) %collective-permute-start.5) | collective-permute-done | bytes 131104 | tf_op jit(solution)/shard_map/ppermute | solution.py:254
  56.5 1.1 %collective-permute-done.6.refs_3_ = bf16[32,16,128]{2,1,0:T(8,128)(2,1)S(1)} collective-permute-done((bf16[32,16,128]{2,1,0:T(8,128)(2,1)S(1)}, bf16[32,16,128]{2,1,0:T(8,128)(2,1)S(1)}, u32[]{:S(2)}, u32[]{:S(2)}) %collective-permute-start.6) | collective-permute-done | bytes 131104 | tf_op jit(solution)/shard_map/ppermute | solution.py:254
  57.6 2.5 %collective-permute-start.20 = (bf16[32,4096]{1,0:T(8,128)(2,1)S(1)}, bf16[32,4096]{1,0:T(8,128)(2,1)S(1)}, u32[]{:S(2)}, u32[]{:S(2)}) collective-permute-start(bf16[32,4096]{1,0:T(8,128)(2,1)S(1)} %collective-permute-done.3.refs_2_.refs_4_), channel_id=1, source_target_pairs={{4,0},{0,4},{5,1},{1,5},{6,2},{2,6},{7,3},{3,7},{12,8},{8,12},{13,... | collective-permute-start | bytes 786440 | tf_op jit(solution)/shard_map/ppermute | solution.py:254
  60.1 2.3 %shard_map.88.dense_ref = bf16[512,4096]{1,0:T(8,128)(2,1)S(1)} custom-call(s32[8,64]{1,0:T(8,128)S(1)} %bitcast.9, s32[64]{0:T(128)S(1)} %copy-done.7, s32[4]{0:T(128)S(1)} %pad_add_fusion.own_ref, bf16[32,16,128]{2,1,0:T(8,128)(2,1)S(1)} %get-tuple-element.19.refs_2_.refs_0_, bf16[32,16,128]{2,1,0:T(8,128)(2,1)S(1)} %collective-permute-done.9.refs_1_, ...), custom_call_target="tpu_custom_call" | custom-call | flops 1024 | bytes 1024 | tf_op jit(solution)/shard_map/pallas_call | solution.py:145
  63.1 3.2 %shard_map.89.refs_2_ = bf16[32,16,512]{2,1,0:T(8,128)(2,1)S(1)} custom-call(s32[4]{0:T(128)S(1)} %pad_add_fusion.own_ref, bf16[512,4096]{1,0:T(8,128)(2,1)S(1)} %shard_map.88.dense_ref, bf16[64,4096]{1,0:T(8,128)(2,1)S(1)} %shard_map.84.refs_0_, bf16[64,4096]{1,0:T(8,128)(2,1)S(1)} %get-tuple-element.21.refs_1_, ...), custom_call_target="tpu_custom_call" | custom-call | flops 1024 | bytes 1024 | tf_op jit(solution)/shard_map/pallas_call | solution.py:172
  67.1 4.0 %all-to-all-start.1 = ((bf16[32,16,512]{2,1,0:T(8,128)(2,1)}), bf16[32,16,512]{2,1,0:T(8,128)(2,1)S(1)}, u32[]{:S(2)}, u32[]{:S(2)}) async-start(bf16[32,16,512]{2,1,0:T(8,128)(2,1)} %shard_map.91), calls=%async_computation.1 | async-start | bytes 1048576 | tf_op jit(solution)/shard_map/all_to_all | solution.py:267
  71.5 1.2 %collective-permute-start.8 = (bf16[32,64,128]{2,1,0:T(8,128)(2,1)S(1)}, bf16[32,64,128]{2,1,0:T(8,128)(2,1)S(1)}, u32[]{:S(2)}, u32[]{:S(2)}) collective-permute-start(bf16[32,64,128]{2,1,0:T(8,128)(2,1)S(1)} %shard_map.87.refs_1_.refs_0_), channel_id=1, source_target_pairs={{3,0},{0,1},{1,2},{2,3},{7,4},{4,5},{5,6},{6,7},{11,8},{8,9},{9,10... | collective-permute-start | bytes 1572872 | tf_op jit(solution)/shard_map/ppermute | solution.py:254
  72.7 12.1 %collective-permute-done.7.refs_0_ = bf16[32,64,128]{2,1,0:T(8,128)(2,1)S(1)} collective-permute-done((bf16[32,64,128]{2,1,0:T(8,128)(2,1)S(1)}, bf16[32,64,128]{2,1,0:T(8,128)(2,1)S(1)}, u32[]{:S(2)}, u32[]{:S(2)}) %collective-permute-start.7) | collective-permute-done | bytes 524320 | tf_op jit(solution)/shard_map/ppermute | solution.py:254
  84.8 1.2 %collective-permute-done.8.refs_1_ = bf16[32,64,128]{2,1,0:T(8,128)(2,1)S(1)} collective-permute-done((bf16[32,64,128]{2,1,0:T(8,128)(2,1)S(1)}, bf16[32,64,128]{2,1,0:T(8,128)(2,1)S(1)}, u32[]{:S(2)}, u32[]{:S(2)}) %collective-permute-start.8) | collective-permute-done | bytes 524320 | tf_op jit(solution)/shard_map/ppermute | solution.py:254
  86.1 2.7 %collective-permute-start.22 = (bf16[16,64,128]{2,1,0:T(8,128)(2,1)S(1)}, bf16[16,64,128]{2,1,0:T(8,128)(2,1)S(1)}, u32[]{:S(2)}, u32[]{:S(2)}) collective-permute-start(bf16[16,64,128]{2,1,0:T(8,128)(2,1)S(1)} %slice.15), channel_id=1, source_target_pairs={{1,0},{2,1},{3,2},{0,3},{5,4},{6,5},{7,6},{4,7},{9,8},{10,9},{11,1... | collective-permute-start | bytes 786440 | tf_op jit(solution)/shard_map/ppermute | solution.py:254
  88.8 5.1 %collective-permute-done.21.refs_3_ = bf16[16,64,128]{2,1,0:T(8,128)(2,1)S(1)} collective-permute-done((bf16[16,64,128]{2,1,0:T(8,128)(2,1)S(1)}, bf16[16,64,128]{2,1,0:T(8,128)(2,1)S(1)}, u32[]{:S(2)}, u32[]{:S(2)}) %collective-permute-start.21) | collective-permute-done | bytes 262176 | tf_op jit(solution)/shard_map/ppermute | solution.py:254
  93.9 2.1 %collective-permute-start.23 = (bf16[32,64,128]{2,1,0:T(8,128)(2,1)S(1)}, bf16[32,64,128]{2,1,0:T(8,128)(2,1)S(1)}, u32[]{:S(2)}, u32[]{:S(2)}) collective-permute-start(bf16[32,64,128]{2,1,0:T(8,128)(2,1)S(1)} %get-tuple-element.24.refs_0_), channel_id=1, source_target_pairs={{4,0},{0,4},{5,1},{1,5},{6,2},{2,6},{7,3},{3,7},{12,8},{8,12},{13,... | collective-permute-start | bytes 1572872 | tf_op jit(solution)/shard_map/ppermute | solution.py:254
  97.1 1.8 %shard_map.93 = (bf16[64,4096]{1,0:T(8,128)(2,1)S(1)}, bf16[64,64,128]{2,1,0:T(8,128)(2,1)S(1)}) custom-call(s32[8,64]{1,0:T(8,128)S(1)} %bitcast.7, s32[64]{0:T(128)S(1)} %copy-done.5, s32[4]{0:T(128)S(1)} %pad_add_fusion.own_ref, bf16[32,64,128]{2,1,0:T(8,128)(2,1)S(1)} %get-tuple-element.24.refs_0_, bf16[32,64,128]{2,1,0:T(8,128)(2,1)S(1)} %get-tuple-element.25.refs_1_, ...), custom_call_target="tpu_custom_call" | custom-call | flops 1024 | bytes 1024 | tf_op jit(solution)/shard_map/pallas_call | solution.py:243
  99.9 2.4 %shard_map.94 = bf16[64,4096]{1,0:T(8,128)(2,1)} custom-call(s32[8,64]{1,0:T(8,128)S(1)} %bitcast.8, s32[64]{0:T(128)S(1)} %copy-done.5, s32[4]{0:T(128)S(1)} %pad_add_fusion.own_ref, bf16[32,64,128]{2,1,0:T(8,128)(2,1)S(1)} %collective-permute-done.23.refs_0_, bf16[32,64,128]{2,1,0:T(8,128)(2,1)S(1)} %collective-permute-done.24.refs_1_, ...), custom_call_target="tpu_custom_call" | custom-call | flops 1024 | bytes 1024 | tf_op jit(solution)/shard_map/pallas_call | solution.py:243
  (70 shorter events, 11.8 us)
Async XLA Ops:
  2.3 27.0 %collective-permute-start = (bf16[64,4096]{1,0:T(8,128)(2,1)S(1)}, bf16[64,4096]{1,0:T(8,128)(2,1)S(1)}, u32[]{:S(2)}, u32[]{:S(2)}) collective-permute-start(bf16[64,4096]{1,0:T(8,128)(2,1)S(1)} %shard_map.84.refs_0_), channel_id=1, source_target_pairs={{8,0},{16,8},{24,16},{0,24},{9,1},{17,9},{25,17},{1,25},{10,2},{18... | collective-permute-start | bytes 1572872 | tf_op jit(solution)/shard_map/ppermute | solution.py:254
  5.7 23.6 %collective-permute-start.1 = (bf16[64,4096]{1,0:T(8,128)(2,1)S(1)}, bf16[64,4096]{1,0:T(8,128)(2,1)S(1)}, u32[]{:S(2)}, u32[]{:S(2)}) collective-permute-start(bf16[64,4096]{1,0:T(8,128)(2,1)S(1)} %shard_map.84.refs_0_), channel_id=1, source_target_pairs={{24,0},{0,8},{8,16},{16,24},{25,1},{1,9},{9,17},{17,25},{26,2},{2,... | collective-permute-start | bytes 1572872 | tf_op jit(solution)/shard_map/ppermute | solution.py:254
  29.4 17.6 %collective-permute-start.2 = (bf16[32,4096]{1,0:T(8,128)(2,1)S(1)}, bf16[32,4096]{1,0:T(8,128)(2,1)S(1)}, u32[]{:S(2)}, u32[]{:S(2)}) collective-permute-start(bf16[32,4096]{1,0:T(8,128)(2,1)S(1)} %slice.12), channel_id=1, source_target_pairs={{24,0},{0,8},{8,16},{16,24},{25,1},{1,9},{9,17},{17,25},{26,2},{2,... | collective-permute-start | bytes 786440 | tf_op jit(solution)/shard_map/ppermute | solution.py:254
  29.5 17.5 %collective-permute-start.3 = (bf16[32,4096]{1,0:T(8,128)(2,1)S(1)}, bf16[32,4096]{1,0:T(8,128)(2,1)S(1)}, u32[]{:S(2)}, u32[]{:S(2)}) collective-permute-start(bf16[32,4096]{1,0:T(8,128)(2,1)S(1)} %slice.13), channel_id=1, source_target_pairs={{8,0},{16,8},{24,16},{0,24},{9,1},{17,9},{25,17},{1,25},{10,2},{18... | collective-permute-start | bytes 786440 | tf_op jit(solution)/shard_map/ppermute | solution.py:254
  32.2 6.1 %collective-permute-start.9 = (bf16[32,16,128]{2,1,0:T(8,128)(2,1)S(1)}, bf16[32,16,128]{2,1,0:T(8,128)(2,1)S(1)}, u32[]{:S(2)}, u32[]{:S(2)}) collective-permute-start(bf16[32,16,128]{2,1,0:T(8,128)(2,1)S(1)} %get-tuple-element.19.refs_2_.refs_0_), channel_id=1, source_target_pairs={{1,0},{2,1},{3,2},{0,3},{5,4},{6,5},{7,6},{4,7},{9,8},{10,9},{11,1... | collective-permute-start | bytes 393224 | tf_op jit(solution)/shard_map/ppermute | solution.py:254
  35.0 8.1 %collective-permute-start.10 = (bf16[32,16,128]{2,1,0:T(8,128)(2,1)S(1)}, bf16[32,16,128]{2,1,0:T(8,128)(2,1)S(1)}, u32[]{:S(2)}, u32[]{:S(2)}) collective-permute-start(bf16[32,16,128]{2,1,0:T(8,128)(2,1)S(1)} %get-tuple-element.19.refs_2_.refs_0_), channel_id=1, source_target_pairs={{2,0},{3,1},{0,2},{1,3},{6,4},{7,5},{4,6},{5,7},{10,8},{11,9},{8,1... | collective-permute-start | bytes 393224 | tf_op jit(solution)/shard_map/ppermute | solution.py:254
  35.3 10.4 %collective-permute-start.11 = (bf16[32,16,128]{2,1,0:T(8,128)(2,1)S(1)}, bf16[32,16,128]{2,1,0:T(8,128)(2,1)S(1)}, u32[]{:S(2)}, u32[]{:S(2)}) collective-permute-start(bf16[32,16,128]{2,1,0:T(8,128)(2,1)S(1)} %get-tuple-element.19.refs_2_.refs_0_), channel_id=1, source_target_pairs={{3,0},{0,1},{1,2},{2,3},{7,4},{4,5},{5,6},{6,7},{11,8},{8,9},{9,10... | collective-permute-start | bytes 393224 | tf_op jit(solution)/shard_map/ppermute | solution.py:254
  38.3 9.2 %collective-permute-start.12 = (bf16[32,16,128]{2,1,0:T(8,128)(2,1)S(1)}, bf16[32,16,128]{2,1,0:T(8,128)(2,1)S(1)}, u32[]{:S(2)}, u32[]{:S(2)}) collective-permute-start(bf16[32,16,128]{2,1,0:T(8,128)(2,1)S(1)} %get-tuple-element.19.refs_2_.refs_0_), channel_id=1, source_target_pairs={{4,0},{0,4},{5,1},{1,5},{6,2},{2,6},{7,3},{3,7},{12,8},{8,12},{13,... | collective-permute-start | bytes 393224 | tf_op jit(solution)/shard_map/ppermute | solution.py:254
  43.0 4.5 %collective-permute-start.13 = (bf16[32,16,128]{2,1,0:T(8,128)(2,1)S(1)}, bf16[32,16,128]{2,1,0:T(8,128)(2,1)S(1)}, u32[]{:S(2)}, u32[]{:S(2)}) collective-permute-start(bf16[32,16,128]{2,1,0:T(8,128)(2,1)S(1)} %collective-permute-done.9.refs_1_), channel_id=1, source_target_pairs={{4,0},{0,4},{5,1},{1,5},{6,2},{2,6},{7,3},{3,7},{12,8},{8,12},{13,... | collective-permute-start | bytes 393224 | tf_op jit(solution)/shard_map/ppermute | solution.py:254
  47.0 16.1 %collective-permute-start.16 = (bf16[64,4096]{1,0:T(8,128)(2,1)S(1)}, bf16[64,4096]{1,0:T(8,128)(2,1)S(1)}, u32[]{:S(2)}, u32[]{:S(2)}) collective-permute-start(bf16[64,4096]{1,0:T(8,128)(2,1)S(1)} %shard_map.84.refs_0_), channel_id=1, source_target_pairs={{4,0},{0,4},{5,1},{1,5},{6,2},{2,6},{7,3},{3,7},{12,8},{8,12},{13,... | collective-permute-start | bytes 1572872 | tf_op jit(solution)/shard_map/ppermute | solution.py:254
  47.5 5.1 %collective-permute-start.4 = (bf16[32,16,128]{2,1,0:T(8,128)(2,1)S(1)}, bf16[32,16,128]{2,1,0:T(8,128)(2,1)S(1)}, u32[]{:S(2)}, u32[]{:S(2)}) collective-permute-start(bf16[32,16,128]{2,1,0:T(8,128)(2,1)S(1)} %shard_map.86.refs_0_), channel_id=1, source_target_pairs={{8,0},{16,8},{24,16},{0,24},{9,1},{17,9},{25,17},{1,25},{10,2},{18... | collective-permute-start | bytes 393224 | tf_op jit(solution)/shard_map/ppermute | solution.py:254
  47.5 15.6 %collective-permute-start.17 = (bf16[64,4096]{1,0:T(8,128)(2,1)S(1)}, bf16[64,4096]{1,0:T(8,128)(2,1)S(1)}, u32[]{:S(2)}, u32[]{:S(2)}) collective-permute-start(bf16[64,4096]{1,0:T(8,128)(2,1)S(1)} %get-tuple-element.21.refs_1_), channel_id=1, source_target_pairs={{4,0},{0,4},{5,1},{1,5},{6,2},{2,6},{7,3},{3,7},{12,8},{8,12},{13,... | collective-permute-start | bytes 1572872 | tf_op jit(solution)/shard_map/ppermute | solution.py:254
  48.0 15.1 %collective-permute-start.18 = (bf16[64,4096]{1,0:T(8,128)(2,1)S(1)}, bf16[64,4096]{1,0:T(8,128)(2,1)S(1)}, u32[]{:S(2)}, u32[]{:S(2)}) collective-permute-start(bf16[64,4096]{1,0:T(8,128)(2,1)S(1)} %get-tuple-element.20.refs_2_), channel_id=1, source_target_pairs={{4,0},{0,4},{5,1},{1,5},{6,2},{2,6},{7,3},{3,7},{12,8},{8,12},{13,... | collective-permute-start | bytes 1572872 | tf_op jit(solution)/shard_map/ppermute | solution.py:254
  49.1 6.4 %collective-permute-start.5 = (bf16[32,16,128]{2,1,0:T(8,128)(2,1)S(1)}, bf16[32,16,128]{2,1,0:T(8,128)(2,1)S(1)}, u32[]{:S(2)}, u32[]{:S(2)}) collective-permute-start(bf16[32,16,128]{2,1,0:T(8,128)(2,1)S(1)} %shard_map.86.refs_0_), channel_id=1, source_target_pairs={{16,0},{24,8},{0,16},{8,24},{17,1},{25,9},{1,17},{9,25},{18,2},{26... | collective-permute-start | bytes 393224 | tf_op jit(solution)/shard_map/ppermute | solution.py:254
  52.6 5.0 %collective-permute-start.6 = (bf16[32,16,128]{2,1,0:T(8,128)(2,1)S(1)}, bf16[32,16,128]{2,1,0:T(8,128)(2,1)S(1)}, u32[]{:S(2)}, u32[]{:S(2)}) collective-permute-start(bf16[32,16,128]{2,1,0:T(8,128)(2,1)S(1)} %shard_map.86.refs_0_), channel_id=1, source_target_pairs={{24,0},{0,8},{8,16},{16,24},{25,1},{1,9},{9,17},{17,25},{26,2},{2,... | collective-permute-start | bytes 393224 | tf_op jit(solution)/shard_map/ppermute | solution.py:254
  55.5 7.5 %collective-permute-start.19 = (bf16[32,4096]{1,0:T(8,128)(2,1)S(1)}, bf16[32,4096]{1,0:T(8,128)(2,1)S(1)}, u32[]{:S(2)}, u32[]{:S(2)}) collective-permute-start(bf16[32,4096]{1,0:T(8,128)(2,1)S(1)} %collective-permute-done.2.refs_1_.refs_3_), channel_id=1, source_target_pairs={{4,0},{0,4},{5,1},{1,5},{6,2},{2,6},{7,3},{3,7},{12,8},{8,12},{13,... | collective-permute-start | bytes 786440 | tf_op jit(solution)/shard_map/ppermute | solution.py:254
  57.6 5.5 %collective-permute-start.20 = (bf16[32,4096]{1,0:T(8,128)(2,1)S(1)}, bf16[32,4096]{1,0:T(8,128)(2,1)S(1)}, u32[]{:S(2)}, u32[]{:S(2)}) collective-permute-start(bf16[32,4096]{1,0:T(8,128)(2,1)S(1)} %collective-permute-done.3.refs_2_.refs_4_), channel_id=1, source_target_pairs={{4,0},{0,4},{5,1},{1,5},{6,2},{2,6},{7,3},{3,7},{12,8},{8,12},{13,... | collective-permute-start | bytes 786440 | tf_op jit(solution)/shard_map/ppermute | solution.py:254
  67.1 26.8 %all-to-all-start.1 = ((bf16[32,16,512]{2,1,0:T(8,128)(2,1)}), bf16[32,16,512]{2,1,0:T(8,128)(2,1)S(1)}, u32[]{:S(2)}, u32[]{:S(2)}) async-start(bf16[32,16,512]{2,1,0:T(8,128)(2,1)} %shard_map.91), calls=%async_computation.1 | async-start | bytes 1048576 | tf_op jit(solution)/shard_map/all_to_all | solution.py:267
  71.1 13.6 %collective-permute-start.7 = (bf16[32,64,128]{2,1,0:T(8,128)(2,1)S(1)}, bf16[32,64,128]{2,1,0:T(8,128)(2,1)S(1)}, u32[]{:S(2)}, u32[]{:S(2)}) collective-permute-start(bf16[32,64,128]{2,1,0:T(8,128)(2,1)S(1)} %shard_map.87.refs_1_.refs_0_), channel_id=1, source_target_pairs={{1,0},{2,1},{3,2},{0,3},{5,4},{6,5},{7,6},{4,7},{9,8},{10,9},{11,1... | collective-permute-start | bytes 1572872 | tf_op jit(solution)/shard_map/ppermute | solution.py:254
  71.5 14.4 %collective-permute-start.8 = (bf16[32,64,128]{2,1,0:T(8,128)(2,1)S(1)}, bf16[32,64,128]{2,1,0:T(8,128)(2,1)S(1)}, u32[]{:S(2)}, u32[]{:S(2)}) collective-permute-start(bf16[32,64,128]{2,1,0:T(8,128)(2,1)S(1)} %shard_map.87.refs_1_.refs_0_), channel_id=1, source_target_pairs={{3,0},{0,1},{1,2},{2,3},{7,4},{4,5},{5,6},{6,7},{11,8},{8,9},{9,10... | collective-permute-start | bytes 1572872 | tf_op jit(solution)/shard_map/ppermute | solution.py:254
  86.0 8.0 %collective-permute-start.21 = (bf16[16,64,128]{2,1,0:T(8,128)(2,1)S(1)}, bf16[16,64,128]{2,1,0:T(8,128)(2,1)S(1)}, u32[]{:S(2)}, u32[]{:S(2)}) collective-permute-start(bf16[16,64,128]{2,1,0:T(8,128)(2,1)S(1)} %slice.14), channel_id=1, source_target_pairs={{3,0},{0,1},{1,2},{2,3},{7,4},{4,5},{5,6},{6,7},{11,8},{8,9},{9,10... | collective-permute-start | bytes 786440 | tf_op jit(solution)/shard_map/ppermute | solution.py:254
  86.1 7.9 %collective-permute-start.22 = (bf16[16,64,128]{2,1,0:T(8,128)(2,1)S(1)}, bf16[16,64,128]{2,1,0:T(8,128)(2,1)S(1)}, u32[]{:S(2)}, u32[]{:S(2)}) collective-permute-start(bf16[16,64,128]{2,1,0:T(8,128)(2,1)S(1)} %slice.15), channel_id=1, source_target_pairs={{1,0},{2,1},{3,2},{0,3},{5,4},{6,5},{7,6},{4,7},{9,8},{10,9},{11,1... | collective-permute-start | bytes 786440 | tf_op jit(solution)/shard_map/ppermute | solution.py:254
  93.9 5.9 %collective-permute-start.23 = (bf16[32,64,128]{2,1,0:T(8,128)(2,1)S(1)}, bf16[32,64,128]{2,1,0:T(8,128)(2,1)S(1)}, u32[]{:S(2)}, u32[]{:S(2)}) collective-permute-start(bf16[32,64,128]{2,1,0:T(8,128)(2,1)S(1)} %get-tuple-element.24.refs_0_), channel_id=1, source_target_pairs={{4,0},{0,4},{5,1},{1,5},{6,2},{2,6},{7,3},{3,7},{12,8},{8,12},{13,... | collective-permute-start | bytes 1572872 | tf_op jit(solution)/shard_map/ppermute | solution.py:254
  96.1 3.8 %collective-permute-start.24 = (bf16[32,64,128]{2,1,0:T(8,128)(2,1)S(1)}, bf16[32,64,128]{2,1,0:T(8,128)(2,1)S(1)}, u32[]{:S(2)}, u32[]{:S(2)}) collective-permute-start(bf16[32,64,128]{2,1,0:T(8,128)(2,1)S(1)} %get-tuple-element.25.refs_1_), channel_id=1, source_target_pairs={{4,0},{0,4},{5,1},{1,5},{6,2},{2,6},{7,3},{3,7},{12,8},{8,12},{13,... | collective-permute-start | bytes 1572872 | tf_op jit(solution)/shard_map/ppermute | solution.py:254
  (13 other events, 194.1 us)

commit v10 on v6

--- a/solution.py
+++ b/solution.py
@@ -138,7 +138,7 @@
 
 
 def occupied_kernel(own_ref, dense_ref, *refs):
-    *row_refs, out_ref, rows_ref = refs
+    row_refs, (out_ref, rows_ref) = refs[: CORES * len(PARTS)], refs[-2:]
     x0, core0 = own_ref[1], own_ref[2]
     for core_off in range(CORES):
         for (off, part), ref in zip(PARTS, row_refs[core_off * len(PARTS) :]):
@@ -152,15 +152,15 @@
         out_ref[chip] = product[chip * QUARTER : (chip + 1) * QUARTER]
 
 
-def occupied(dense, rows, own):
+def occupied(dense, rows, own, *early):
     lanes = CORES * X * BLOCK
     return call(
         occupied_kernel,
         [(CHIPS, QUARTER, lanes)],
-        [SMEM] + [VMEM] * (1 + len(rows)),
+        [SMEM] + [VMEM] * (1 + len(rows)) + [ANYWHERE] * len(early),
         (VMEM,),
         [pltpu.VMEM((lanes, BASIS), jnp.bfloat16)],
-    )(own, dense, *rows)[0]
+    )(own, dense, *rows, *early)[0]
 
 
 def virtual_kernel(core_off, index_ref, first_ref, own_ref, *refs):
@@ -239,13 +239,11 @@
     return lax.ppermute(array, axis, [((i + by) % size, i) for i in range(size)])
 
 
-def ring(array, axis, *between):
-    after, before = shift(array, axis, 1), shift(array, axis, -1)
-    if between:
-        after, before = tie([after, before], *between)
-    middle = array.shape[0] // 2
+def second_step(neighbours, axis):
+    after, before = neighbours
+    middle = after.shape[0] // 2
     low, high = shift(before[:middle], axis, -1), shift(after[middle:], axis, 1)
-    return [array, after, before, low, high]
+    return [after, before, low, high]
 
 
 def exchange(array):
@@ -259,13 +257,16 @@
     both = exchange(spread(own, occ_blocks, virt_blocks))
     occ_plane, virt_plane = divide(both)
     pieces = [occ_plane] + [shift(occ_plane, "y", by) for by in range(1, Y)]
-    rows = ring(mask_rows(pair_mask, b_tensor), "x", occ_plane)
+    masked = mask_rows(pair_mask, b_tensor)
+    ahead = [shift(masked, "x", 1), shift(masked, "x", -1)]
+    rows = [masked, *second_step(tie(ahead, occ_plane), "x")]
     rows = rows + [shift(part, "core", 1) for part in rows]
-    (virt_plane,) = tie([virt_plane], *pieces[1:])
+    (virt_plane,) = tie([virt_plane], *rows[1:3])
+    ahead = [shift(virt_plane, "y", 1), shift(virt_plane, "y", -1)]
     pieces = pieces + [shift(piece, "core", 1) for piece in pieces]
-    half = occupied(dense_panel(pieces, own, occ_index, second_map), rows, own)
-    mine = ring(virt_plane, "y", half)
-    turned = exchange(*tie([half], *mine[1:3]))
+    half = occupied(dense_panel(pieces, own, occ_index, second_map), rows, own, *ahead)
+    turned = exchange(half)
+    mine = [virt_plane, *second_step(tie(ahead, half), "y")]
     mine = tie(mine, turned)
     other = [shift(panel, "core", 1) for panel in mine]
     known = (own, virt_index, first_map)

time: 98.2 us -> 98.5 us (level)
  starting transfers between devices: 49.1 us -> 50.4 us
  waiting for transfers between devices: 31.7 us -> 30.6 us
    ppermute x25, starting transfers between devices: 30 us -> 32.9 us  [shift(): lax.ppermute(array, axis, [((i + by) % size, i) for i in range(size)])]
    all_to_all x2, starting transfers between devices: 19.1 us -> 17.5 us  [exchange(): lax.all_to_all(array, ('z', 'x'), split_axis=0, concat_axis=0, tiled=True)]
    ppermute x25, waiting for transfers between devices: 11.9 us -> 10.9 us  [shift(): lax.ppermute(array, axis, [((i + by) % size, i) for i in range(size)])]
  transfers between devices with their start and end apart: 27 -> 27, of which waited for: 8 -> 9; matrix products, arithmetic and copies ran while one was open for 0% -> 0% of each run, Pallas kernels for 10% -> 5%
where the time goes in v10:
time: 98.5 us; the launch traced here: 98 us
  starting transfers between devices  50.4 us (51%)
  waiting for transfers between devices  30.6 us (31%)
  Pallas kernels  13.2 us (13%)
  local copies, waits for them, and re-layouts  3.3 us (3%)
    ppermute x25, starting transfers between devices, shift(): lax.ppermute(array, axis, [((i + by) % size, i) for i in range(size)])  32.9 us
    all_to_all x2, waiting for transfers between devices, exchange(): lax.all_to_all(array, ('z', 'x'), split_axis=0, concat_axis=0, tiled=True)  19.8 us
    all_to_all x2, starting transfers between devices, exchange(): lax.all_to_all(array, ('z', 'x'), split_axis=0, concat_axis=0, tiled=True)  17.5 us
    ppermute x25, waiting for transfers between devices, shift(): lax.ppermute(array, axis, [((i + by) % size, i) for i in range(size)])  10.9 us
    pallas_call x1, Pallas kernels, occupied(): call(occupied_kernel, [(CHIPS, QUARTER, lanes)], [SMEM] + [VMEM] * (1 + l...  4.49 us
    pallas_call x2, Pallas kernels, virtual(): call(functools.partial(virtual_kernel, core_off), [shape] if core_off els...  4.21 us
    unnamed x16, local copies, waits for them, and re-layouts  3.22 us
    pallas_call x1, Pallas kernels, dense_panel(): call(dense_kernel, [shape], [SMEM] * 3 + [VMEM] * len(pieces), (VMEM,), [...  2.34 us
  transfers between devices with their start and end apart: 27, of which 9 were waited for; matrix products, arithmetic and copies ran while one was open for 0% of the time, Pallas kernels for 5%

profile of v10, /device:TPU:1, one launch (start us, length us, event | category | flops | bytes accessed | tf_op | source)
XLA Modules:
  0.0 98.0 jit_solution(4666324096960567480)
XLA Ops:
  1.6 1.5 %shard_map.82 = bf16[32,80,128]{2,1,0:T(8,128)(2,1)} custom-call(s32[4]{0:T(128)S(1)} %pad_add_fusion.own_ref, bf16[1,2,64,64]{3,2,1,0:T(8,128)(2,1)S(1)} %copy-done.1, bf16[1,2,64,64]{3,2,1,0:T(8,128)(2,1)S(1)} %copy-done.2), custom_call_target="tpu_custom_call" | custom-call | flops 1024 | bytes 1024 | tf_op jit(solution)/shard_map/pallas_call | solution.py:62
  3.1 11.9 %all-to-all-start = ((bf16[32,80,128]{2,1,0:T(8,128)(2,1)}), bf16[32,80,128]{2,1,0:T(8,128)(2,1)S(1)}, u32[]{:S(2)}, u32[]{:S(2)}) async-start(bf16[32,80,128]{2,1,0:T(8,128)(2,1)} %shard_map.82), calls=%async_computation | async-start | bytes 1310720 | tf_op jit(solution)/shard_map/all_to_all | solution.py:250
  17.3 2.5 %collective-permute-start = (bf16[64,4096]{1,0:T(8,128)(2,1)S(1)}, bf16[64,4096]{1,0:T(8,128)(2,1)S(1)}, u32[]{:S(2)}, u32[]{:S(2)}) collective-permute-start(bf16[64,4096]{1,0:T(8,128)(2,1)S(1)} %shard_map.84.refs_0_), channel_id=1, source_target_pairs={{8,0},{16,8},{24,16},{0,24},{9,1},{17,9},{25,17},{1,25},{10,2},{18... | collective-permute-start | bytes 1572872 | tf_op jit(solution)/shard_map/ppermute | solution.py:239
  19.9 1.5 %collective-permute-start.13 = (bf16[64,4096]{1,0:T(8,128)(2,1)S(1)}, bf16[64,4096]{1,0:T(8,128)(2,1)}, u32[]{:S(2)}, u32[]{:S(2)}) collective-permute-start(bf16[64,4096]{1,0:T(8,128)(2,1)S(1)} %shard_map.84.refs_0_), channel_id=1, source_target_pairs={{4,0},{0,4},{5,1},{1,5},{6,2},{2,6},{7,3},{3,7},{12,8},{8,12},{13,... | collective-permute-start | bytes 1572872 | tf_op jit(solution)/shard_map/ppermute | solution.py:239
  21.4 12.3 %all-to-all-done.both_ref = bf16[32,80,128]{2,1,0:T(8,128)(2,1)S(1)} async-done(((bf16[32,80,128]{2,1,0:T(8,128)(2,1)}), bf16[32,80,128]{2,1,0:T(8,128)(2,1)S(1)}, u32[]{:S(2)}, u32[]{:S(2)}) %all-to-all-start) | async-done | bytes 655392 | tf_op jit(solution)/shard_map/all_to_all | solution.py:250
  33.7 1.4 %collective-permute-start.6 = (bf16[32,16,128]{2,1,0:T(8,128)(2,1)S(1)}, bf16[32,16,128]{2,1,0:T(8,128)(2,1)S(1)}, u32[]{:S(2)}, u32[]{:S(2)}) collective-permute-start(bf16[32,16,128]{2,1,0:T(8,128)(2,1)S(1)} %get-tuple-element.19.refs_2_.refs_0_), channel_id=1, source_target_pairs={{3,0},{0,1},{1,2},{2,3},{7,4},{4,5},{5,6},{6,7},{11,8},{8,9},{9,10... | collective-permute-start | bytes 393224 | tf_op jit(solution)/shard_map/ppermute | solution.py:239
  35.1 1.5 %collective-permute-start.4 = (bf16[32,16,128]{2,1,0:T(8,128)(2,1)S(1)}, bf16[32,16,128]{2,1,0:T(8,128)(2,1)S(1)}, u32[]{:S(2)}, u32[]{:S(2)}) collective-permute-start(bf16[32,16,128]{2,1,0:T(8,128)(2,1)S(1)} %get-tuple-element.19.refs_2_.refs_0_), channel_id=1, source_target_pairs={{1,0},{2,1},{3,2},{0,3},{5,4},{6,5},{7,6},{4,7},{9,8},{10,9},{11,1... | collective-permute-start | bytes 393224 | tf_op jit(solution)/shard_map/ppermute | solution.py:239
  36.6 2.7 %collective-permute-start.5 = (bf16[32,16,128]{2,1,0:T(8,128)(2,1)S(1)}, bf16[32,16,128]{2,1,0:T(8,128)(2,1)S(1)}, u32[]{:S(2)}, u32[]{:S(2)}) collective-permute-start(bf16[32,16,128]{2,1,0:T(8,128)(2,1)S(1)} %get-tuple-element.19.refs_2_.refs_0_), channel_id=1, source_target_pairs={{2,0},{3,1},{0,2},{1,3},{6,4},{7,5},{4,6},{5,7},{10,8},{11,9},{8,1... | collective-permute-start | bytes 393224 | tf_op jit(solution)/shard_map/ppermute | solution.py:239
  39.3 2.2 %collective-permute-start.7 = (bf16[32,16,128]{2,1,0:T(8,128)(2,1)S(1)}, bf16[32,16,128]{2,1,0:T(8,128)(2,1)S(1)}, u32[]{:S(2)}, u32[]{:S(2)}) collective-permute-start(bf16[32,16,128]{2,1,0:T(8,128)(2,1)S(1)} %get-tuple-element.19.refs_2_.refs_0_), channel_id=1, source_target_pairs={{4,0},{0,4},{5,1},{1,5},{6,2},{2,6},{7,3},{3,7},{12,8},{8,12},{13,... | collective-permute-start | bytes 393224 | tf_op jit(solution)/shard_map/ppermute | solution.py:239
  41.5 1.6 %collective-permute-start.2 = (bf16[32,64,128]{2,1,0:T(8,128)(2,1)S(1)}, bf16[32,64,128]{2,1,0:T(8,128)(2,1)S(1)}, u32[]{:S(2)}, u32[]{:S(2)}) collective-permute-start(bf16[32,64,128]{2,1,0:T(8,128)(2,1)S(1)} %shard_map.86.refs_0_), channel_id=1, source_target_pairs={{1,0},{2,1},{3,2},{0,3},{5,4},{6,5},{7,6},{4,7},{9,8},{10,9},{11,1... | collective-permute-start | bytes 1572872 | tf_op jit(solution)/shard_map/ppermute | solution.py:239
  43.3 1.7 %collective-permute-start.10 = (bf16[32,16,128]{2,1,0:T(8,128)(2,1)S(1)}, bf16[32,16,128]{2,1,0:T(8,128)(2,1)S(1)}, u32[]{:S(2)}, u32[]{:S(2)}) collective-permute-start(bf16[32,16,128]{2,1,0:T(8,128)(2,1)S(1)} %collective-permute-done.6.refs_3_), channel_id=1, source_target_pairs={{4,0},{0,4},{5,1},{1,5},{6,2},{2,6},{7,3},{3,7},{12,8},{8,12},{13,... | collective-permute-start | bytes 393224 | tf_op jit(solution)/shard_map/ppermute | solution.py:239
  46.1 2.2 %collective-permute-start.12 = (bf16[32,4096]{1,0:T(8,128)(2,1)S(1)}, bf16[32,4096]{1,0:T(8,128)(2,1)S(1)}, u32[]{:S(2)}, u32[]{:S(2)}) collective-permute-start(bf16[32,4096]{1,0:T(8,128)(2,1)S(1)} %slice.13), channel_id=1, source_target_pairs={{8,0},{16,8},{24,16},{0,24},{9,1},{17,9},{25,17},{1,25},{10,2},{18... | collective-permute-start | bytes 786440 | tf_op jit(solution)/shard_map/ppermute | solution.py:239
  48.3 3.0 %collective-permute-start.3 = (bf16[32,64,128]{2,1,0:T(8,128)(2,1)S(1)}, bf16[32,64,128]{2,1,0:T(8,128)(2,1)S(1)}, u32[]{:S(2)}, u32[]{:S(2)}) collective-permute-start(bf16[32,64,128]{2,1,0:T(8,128)(2,1)S(1)} %shard_map.86.refs_0_), channel_id=1, source_target_pairs={{3,0},{0,1},{1,2},{2,3},{7,4},{4,5},{5,6},{6,7},{11,8},{8,9},{9,10... | collective-permute-start | bytes 1572872 | tf_op jit(solution)/shard_map/ppermute | solution.py:239
  53.5 1.4 %collective-permute-start.16 = (bf16[32,4096]{1,0:T(8,128)(2,1)S(1)}, bf16[32,4096]{1,0:T(8,128)(2,1)S(1)}, u32[]{:S(2)}, u32[]{:S(2)}) collective-permute-start(bf16[32,4096]{1,0:T(8,128)(2,1)S(1)} %collective-permute-done.11.refs_3_), channel_id=1, source_target_pairs={{4,0},{0,4},{5,1},{1,5},{6,2},{2,6},{7,3},{3,7},{12,8},{8,12},{13,... | collective-permute-start | bytes 786440 | tf_op jit(solution)/shard_map/ppermute | solution.py:239
  56.8 2.3 %shard_map.87.dense_ref = bf16[512,4096]{1,0:T(8,128)(2,1)S(1)} custom-call(s32[8,64]{1,0:T(8,128)S(1)} %bitcast.9, s32[64]{0:T(128)S(1)} %copy-done.7, s32[4]{0:T(128)S(1)} %pad_add_fusion.own_ref, bf16[32,16,128]{2,1,0:T(8,128)(2,1)S(1)} %get-tuple-element.19.refs_2_.refs_0_, bf16[32,16,128]{2,1,0:T(8,128)(2,1)S(1)} %collective-permute-done.4.refs_1_, ...), custom_call_target="tpu_custom_call" | custom-call | flops 1024 | bytes 1024 | tf_op jit(solution)/shard_map/pallas_call | solution.py:130
  59.1 3.5 %collective-permute-done.3.refs_11_.refs_1_ = bf16[32,64,128]{2,1,0:T(8,128)(2,1)S(1)} collective-permute-done((bf16[32,64,128]{2,1,0:T(8,128)(2,1)S(1)}, bf16[32,64,128]{2,1,0:T(8,128)(2,1)S(1)}, u32[]{:S(2)}, u32[]{:S(2)}) %collective-permute-start.3) | collective-permute-done | bytes 524320 | tf_op jit(solution)/shard_map/ppermute | solution.py:239
  62.7 4.5 %shard_map.88.refs_2_ = bf16[32,16,512]{2,1,0:T(8,128)(2,1)} custom-call(s32[4]{0:T(128)S(1)} %pad_add_fusion.own_ref, bf16[512,4096]{1,0:T(8,128)(2,1)S(1)} %shard_map.87.dense_ref, bf16[64,4096]{1,0:T(8,128)(2,1)S(1)} %shard_map.84.refs_0_, bf16[64,4096]{1,0:T(8,128)(2,1)S(1)} %get-tuple-element.20.refs_1_, ...), custom_call_target="tpu_custom_call" | custom-call | flops 1024 | bytes 1024 | tf_op jit(solution)/shard_map/pallas_call | solution.py:157
  67.2 5.7 %all-to-all-start.1 = ((bf16[32,16,512]{2,1,0:T(8,128)(2,1)}), bf16[32,16,512]{2,1,0:T(8,128)(2,1)S(1)}, u32[]{:S(2)}, u32[]{:S(2)}) async-start(bf16[32,16,512]{2,1,0:T(8,128)(2,1)} %shard_map.88.refs_2_), calls=%async_computation.1 | async-start | bytes 1048576 | tf_op jit(solution)/shard_map/all_to_all | solution.py:250
  73.7 2.0 %collective-permute-start.19 = (bf16[16,64,128]{2,1,0:T(8,128)(2,1)S(1)}, bf16[16,64,128]{2,1,0:T(8,128)(2,1)S(1)}, u32[]{:S(2)}, u32[]{:S(2)}) collective-permute-start(bf16[16,64,128]{2,1,0:T(8,128)(2,1)S(1)} %slice.15), channel_id=1, source_target_pairs={{1,0},{2,1},{3,2},{0,3},{5,4},{6,5},{7,6},{4,7},{9,8},{10,9},{11,1... | collective-permute-start | bytes 786440 | tf_op jit(solution)/shard_map/ppermute | solution.py:239
  75.8 5.1 %collective-permute-done.18.refs_3_ = bf16[16,64,128]{2,1,0:T(8,128)(2,1)S(1)} collective-permute-done((bf16[16,64,128]{2,1,0:T(8,128)(2,1)S(1)}, bf16[16,64,128]{2,1,0:T(8,128)(2,1)S(1)}, u32[]{:S(2)}, u32[]{:S(2)}) %collective-permute-start.18) | collective-permute-done | bytes 262176 | tf_op jit(solution)/shard_map/ppermute | solution.py:239
  80.9 7.5 %all-to-all-done.1.refs_5_ = bf16[32,16,512]{2,1,0:T(8,128)(2,1)S(1)} async-done(((bf16[32,16,512]{2,1,0:T(8,128)(2,1)}), bf16[32,16,512]{2,1,0:T(8,128)(2,1)S(1)}, u32[]{:S(2)}, u32[]{:S(2)}) %all-to-all-start.1) | async-done | bytes 524320 | tf_op jit(solution)/shard_map/all_to_all | solution.py:250
  88.3 3.3 %collective-permute-start.20 = (bf16[32,64,128]{2,1,0:T(8,128)(2,1)S(1)}, bf16[32,64,128]{2,1,0:T(8,128)(2,1)S(1)}, u32[]{:S(2)}, u32[]{:S(2)}) collective-permute-start(bf16[32,64,128]{2,1,0:T(8,128)(2,1)S(1)} %get-tuple-element.24.refs_0_), channel_id=1, source_target_pairs={{4,0},{0,4},{5,1},{1,5},{6,2},{2,6},{7,3},{3,7},{12,8},{8,12},{13,... | collective-permute-start | bytes 1572872 | tf_op jit(solution)/shard_map/ppermute | solution.py:239
  92.7 1.8 %shard_map.91 = (bf16[64,4096]{1,0:T(8,128)(2,1)S(1)}, bf16[64,64,128]{2,1,0:T(8,128)(2,1)S(1)}) custom-call(s32[8,64]{1,0:T(8,128)S(1)} %bitcast.7, s32[64]{0:T(128)S(1)} %copy-done.5, s32[4]{0:T(128)S(1)} %pad_add_fusion.own_ref, bf16[32,64,128]{2,1,0:T(8,128)(2,1)S(1)} %get-tuple-element.24.refs_0_, bf16[32,64,128]{2,1,0:T(8,128)(2,1)S(1)} %get-tuple-element.25.refs_1_, ...), custom_call_target="tpu_custom_call" | custom-call | flops 1024 | bytes 1024 | tf_op jit(solution)/shard_map/pallas_call | solution.py:228
  95.4 2.4 %shard_map.92 = bf16[64,4096]{1,0:T(8,128)(2,1)} custom-call(s32[8,64]{1,0:T(8,128)S(1)} %bitcast.8, s32[64]{0:T(128)S(1)} %copy-done.5, s32[4]{0:T(128)S(1)} %pad_add_fusion.own_ref, bf16[32,64,128]{2,1,0:T(8,128)(2,1)S(1)} %collective-permute-done.20.refs_0_, bf16[32,64,128]{2,1,0:T(8,128)(2,1)S(1)} %collective-permute-done.21.refs_1_, ...), custom_call_target="tpu_custom_call" | custom-call | flops 1024 | bytes 1024 | tf_op jit(solution)/shard_map/pallas_call | solution.py:228
  (62 shorter events, 12.2 us)
Async XLA Ops:
  3.1 30.6 %all-to-all-start = ((bf16[32,80,128]{2,1,0:T(8,128)(2,1)}), bf16[32,80,128]{2,1,0:T(8,128)(2,1)S(1)}, u32[]{:S(2)}, u32[]{:S(2)}) async-start(bf16[32,80,128]{2,1,0:T(8,128)(2,1)} %shard_map.82), calls=%async_computation | async-start | bytes 1310720 | tf_op jit(solution)/shard_map/all_to_all | solution.py:250
  17.3 19.3 %collective-permute-start = (bf16[64,4096]{1,0:T(8,128)(2,1)S(1)}, bf16[64,4096]{1,0:T(8,128)(2,1)S(1)}, u32[]{:S(2)}, u32[]{:S(2)}) collective-permute-start(bf16[64,4096]{1,0:T(8,128)(2,1)S(1)} %shard_map.84.refs_0_), channel_id=1, source_target_pairs={{8,0},{16,8},{24,16},{0,24},{9,1},{17,9},{25,17},{1,25},{10,2},{18... | collective-permute-start | bytes 1572872 | tf_op jit(solution)/shard_map/ppermute | solution.py:239
  19.9 19.4 %collective-permute-start.1 = (bf16[64,4096]{1,0:T(8,128)(2,1)S(1)}, bf16[64,4096]{1,0:T(8,128)(2,1)S(1)}, u32[]{:S(2)}, u32[]{:S(2)}) collective-permute-start(bf16[64,4096]{1,0:T(8,128)(2,1)S(1)} %shard_map.84.refs_0_), channel_id=1, source_target_pairs={{24,0},{0,8},{8,16},{16,24},{25,1},{1,9},{9,17},{17,25},{26,2},{2,... | collective-permute-start | bytes 1572872 | tf_op jit(solution)/shard_map/ppermute | solution.py:239
  19.9 21.7 %collective-permute-start.13 = (bf16[64,4096]{1,0:T(8,128)(2,1)S(1)}, bf16[64,4096]{1,0:T(8,128)(2,1)}, u32[]{:S(2)}, u32[]{:S(2)}) collective-permute-start(bf16[64,4096]{1,0:T(8,128)(2,1)S(1)} %shard_map.84.refs_0_), channel_id=1, source_target_pairs={{4,0},{0,4},{5,1},{1,5},{6,2},{2,6},{7,3},{3,7},{12,8},{8,12},{13,... | collective-permute-start | bytes 1572872 | tf_op jit(solution)/shard_map/ppermute | solution.py:239
  33.7 9.4 %collective-permute-start.6 = (bf16[32,16,128]{2,1,0:T(8,128)(2,1)S(1)}, bf16[32,16,128]{2,1,0:T(8,128)(2,1)S(1)}, u32[]{:S(2)}, u32[]{:S(2)}) collective-permute-start(bf16[32,16,128]{2,1,0:T(8,128)(2,1)S(1)} %get-tuple-element.19.refs_2_.refs_0_), channel_id=1, source_target_pairs={{3,0},{0,1},{1,2},{2,3},{7,4},{4,5},{5,6},{6,7},{11,8},{8,9},{9,10... | collective-permute-start | bytes 393224 | tf_op jit(solution)/shard_map/ppermute | solution.py:239
  35.1 8.2 %collective-permute-start.4 = (bf16[32,16,128]{2,1,0:T(8,128)(2,1)S(1)}, bf16[32,16,128]{2,1,0:T(8,128)(2,1)S(1)}, u32[]{:S(2)}, u32[]{:S(2)}) collective-permute-start(bf16[32,16,128]{2,1,0:T(8,128)(2,1)S(1)} %get-tuple-element.19.refs_2_.refs_0_), channel_id=1, source_target_pairs={{1,0},{2,1},{3,2},{0,3},{5,4},{6,5},{7,6},{4,7},{9,8},{10,9},{11,1... | collective-permute-start | bytes 393224 | tf_op jit(solution)/shard_map/ppermute | solution.py:239
  36.6 8.4 %collective-permute-start.5 = (bf16[32,16,128]{2,1,0:T(8,128)(2,1)S(1)}, bf16[32,16,128]{2,1,0:T(8,128)(2,1)S(1)}, u32[]{:S(2)}, u32[]{:S(2)}) collective-permute-start(bf16[32,16,128]{2,1,0:T(8,128)(2,1)S(1)} %get-tuple-element.19.refs_2_.refs_0_), channel_id=1, source_target_pairs={{2,0},{3,1},{0,2},{1,3},{6,4},{7,5},{4,6},{5,7},{10,8},{11,9},{8,1... | collective-permute-start | bytes 393224 | tf_op jit(solution)/shard_map/ppermute | solution.py:239
  39.3 6.7 %collective-permute-start.7 = (bf16[32,16,128]{2,1,0:T(8,128)(2,1)S(1)}, bf16[32,16,128]{2,1,0:T(8,128)(2,1)S(1)}, u32[]{:S(2)}, u32[]{:S(2)}) collective-permute-start(bf16[32,16,128]{2,1,0:T(8,128)(2,1)S(1)} %get-tuple-element.19.refs_2_.refs_0_), channel_id=1, source_target_pairs={{4,0},{0,4},{5,1},{1,5},{6,2},{2,6},{7,3},{3,7},{12,8},{8,12},{13,... | collective-permute-start | bytes 393224 | tf_op jit(solution)/shard_map/ppermute | solution.py:239
  41.5 14.1 %collective-permute-start.2 = (bf16[32,64,128]{2,1,0:T(8,128)(2,1)S(1)}, bf16[32,64,128]{2,1,0:T(8,128)(2,1)S(1)}, u32[]{:S(2)}, u32[]{:S(2)}) collective-permute-start(bf16[32,64,128]{2,1,0:T(8,128)(2,1)S(1)} %shard_map.86.refs_0_), channel_id=1, source_target_pairs={{1,0},{2,1},{3,2},{0,3},{5,4},{6,5},{7,6},{4,7},{9,8},{10,9},{11,1... | collective-permute-start | bytes 1572872 | tf_op jit(solution)/shard_map/ppermute | solution.py:239
  43.1 9.2 %collective-permute-start.11 = (bf16[32,4096]{1,0:T(8,128)(2,1)S(1)}, bf16[32,4096]{1,0:T(8,128)(2,1)S(1)}, u32[]{:S(2)}, u32[]{:S(2)}) collective-permute-start(bf16[32,4096]{1,0:T(8,128)(2,1)S(1)} %slice.12), channel_id=1, source_target_pairs={{24,0},{0,8},{8,16},{16,24},{25,1},{1,9},{9,17},{17,25},{26,2},{2,... | collective-permute-start | bytes 786440 | tf_op jit(solution)/shard_map/ppermute | solution.py:239
  46.0 5.2 %collective-permute-start.9 = (bf16[32,16,128]{2,1,0:T(8,128)(2,1)S(1)}, bf16[32,16,128]{2,1,0:T(8,128)(2,1)S(1)}, u32[]{:S(2)}, u32[]{:S(2)}) collective-permute-start(bf16[32,16,128]{2,1,0:T(8,128)(2,1)S(1)} %collective-permute-done.5.refs_2_), channel_id=1, source_target_pairs={{4,0},{0,4},{5,1},{1,5},{6,2},{2,6},{7,3},{3,7},{12,8},{8,12},{13,... | collective-permute-start | bytes 393224 | tf_op jit(solution)/shard_map/ppermute | solution.py:239
  46.1 7.4 %collective-permute-start.12 = (bf16[32,4096]{1,0:T(8,128)(2,1)S(1)}, bf16[32,4096]{1,0:T(8,128)(2,1)S(1)}, u32[]{:S(2)}, u32[]{:S(2)}) collective-permute-start(bf16[32,4096]{1,0:T(8,128)(2,1)S(1)} %slice.13), channel_id=1, source_target_pairs={{8,0},{16,8},{24,16},{0,24},{9,1},{17,9},{25,17},{1,25},{10,2},{18... | collective-permute-start | bytes 786440 | tf_op jit(solution)/shard_map/ppermute | solution.py:239
  48.3 14.4 %collective-permute-start.3 = (bf16[32,64,128]{2,1,0:T(8,128)(2,1)S(1)}, bf16[32,64,128]{2,1,0:T(8,128)(2,1)S(1)}, u32[]{:S(2)}, u32[]{:S(2)}) collective-permute-start(bf16[32,64,128]{2,1,0:T(8,128)(2,1)S(1)} %shard_map.86.refs_0_), channel_id=1, source_target_pairs={{3,0},{0,1},{1,2},{2,3},{7,4},{4,5},{5,6},{6,7},{11,8},{8,9},{9,10... | collective-permute-start | bytes 1572872 | tf_op jit(solution)/shard_map/ppermute | solution.py:239
  51.2 11.4 %collective-permute-start.14 = (bf16[64,4096]{1,0:T(8,128)(2,1)S(1)}, bf16[64,4096]{1,0:T(8,128)(2,1)S(1)}, u32[]{:S(2)}, u32[]{:S(2)}) collective-permute-start(bf16[64,4096]{1,0:T(8,128)(2,1)S(1)} %get-tuple-element.20.refs_1_), channel_id=1, source_target_pairs={{4,0},{0,4},{5,1},{1,5},{6,2},{2,6},{7,3},{3,7},{12,8},{8,12},{13,... | collective-permute-start | bytes 1572872 | tf_op jit(solution)/shard_map/ppermute | solution.py:239
  52.3 10.4 %collective-permute-start.15 = (bf16[64,4096]{1,0:T(8,128)(2,1)S(1)}, bf16[64,4096]{1,0:T(8,128)(2,1)S(1)}, u32[]{:S(2)}, u32[]{:S(2)}) collective-permute-start(bf16[64,4096]{1,0:T(8,128)(2,1)S(1)} %get-tuple-element.21.refs_2_), channel_id=1, source_target_pairs={{4,0},{0,4},{5,1},{1,5},{6,2},{2,6},{7,3},{3,7},{12,8},{8,12},{13,... | collective-permute-start | bytes 1572872 | tf_op jit(solution)/shard_map/ppermute | solution.py:239
  53.5 9.2 %collective-permute-start.16 = (bf16[32,4096]{1,0:T(8,128)(2,1)S(1)}, bf16[32,4096]{1,0:T(8,128)(2,1)S(1)}, u32[]{:S(2)}, u32[]{:S(2)}) collective-permute-start(bf16[32,4096]{1,0:T(8,128)(2,1)S(1)} %collective-permute-done.11.refs_3_), channel_id=1, source_target_pairs={{4,0},{0,4},{5,1},{1,5},{6,2},{2,6},{7,3},{3,7},{12,8},{8,12},{13,... | collective-permute-start | bytes 786440 | tf_op jit(solution)/shard_map/ppermute | solution.py:239
  55.6 7.1 %collective-permute-start.17 = (bf16[32,4096]{1,0:T(8,128)(2,1)S(1)}, bf16[32,4096]{1,0:T(8,128)(2,1)S(1)}, u32[]{:S(2)}, u32[]{:S(2)}) collective-permute-start(bf16[32,4096]{1,0:T(8,128)(2,1)S(1)} %collective-permute-done.12.refs_4_), channel_id=1, source_target_pairs={{4,0},{0,4},{5,1},{1,5},{6,2},{2,6},{7,3},{3,7},{12,8},{8,12},{13,... | collective-permute-start | bytes 786440 | tf_op jit(solution)/shard_map/ppermute | solution.py:239
  67.2 21.1 %all-to-all-start.1 = ((bf16[32,16,512]{2,1,0:T(8,128)(2,1)}), bf16[32,16,512]{2,1,0:T(8,128)(2,1)S(1)}, u32[]{:S(2)}, u32[]{:S(2)}) async-start(bf16[32,16,512]{2,1,0:T(8,128)(2,1)} %shard_map.88.refs_2_), calls=%async_computation.1 | async-start | bytes 1048576 | tf_op jit(solution)/shard_map/all_to_all | solution.py:250
  72.9 7.9 %collective-permute-start.18 = (bf16[16,64,128]{2,1,0:T(8,128)(2,1)S(1)}, bf16[16,64,128]{2,1,0:T(8,128)(2,1)S(1)}, u32[]{:S(2)}, u32[]{:S(2)}) collective-permute-start(bf16[16,64,128]{2,1,0:T(8,128)(2,1)S(1)} %slice.14), channel_id=1, source_target_pairs={{3,0},{0,1},{1,2},{2,3},{7,4},{4,5},{5,6},{6,7},{11,8},{8,9},{9,10... | collective-permute-start | bytes 786440 | tf_op jit(solution)/shard_map/ppermute | solution.py:239
  73.7 7.1 %collective-permute-start.19 = (bf16[16,64,128]{2,1,0:T(8,128)(2,1)S(1)}, bf16[16,64,128]{2,1,0:T(8,128)(2,1)S(1)}, u32[]{:S(2)}, u32[]{:S(2)}) collective-permute-start(bf16[16,64,128]{2,1,0:T(8,128)(2,1)S(1)} %slice.15), channel_id=1, source_target_pairs={{1,0},{2,1},{3,2},{0,3},{5,4},{6,5},{7,6},{4,7},{9,8},{10,9},{11,1... | collective-permute-start | bytes 786440 | tf_op jit(solution)/shard_map/ppermute | solution.py:239
  88.3 7.1 %collective-permute-start.20 = (bf16[32,64,128]{2,1,0:T(8,128)(2,1)S(1)}, bf16[32,64,128]{2,1,0:T(8,128)(2,1)S(1)}, u32[]{:S(2)}, u32[]{:S(2)}) collective-permute-start(bf16[32,64,128]{2,1,0:T(8,128)(2,1)S(1)} %get-tuple-element.24.refs_0_), channel_id=1, source_target_pairs={{4,0},{0,4},{5,1},{1,5},{6,2},{2,6},{7,3},{3,7},{12,8},{8,12},{13,... | collective-permute-start | bytes 1572872 | tf_op jit(solution)/shard_map/ppermute | solution.py:239
  91.6 3.8 %collective-permute-start.21 = (bf16[32,64,128]{2,1,0:T(8,128)(2,1)S(1)}, bf16[32,64,128]{2,1,0:T(8,128)(2,1)S(1)}, u32[]{:S(2)}, u32[]{:S(2)}) collective-permute-start(bf16[32,64,128]{2,1,0:T(8,128)(2,1)S(1)} %get-tuple-element.25.refs_1_), channel_id=1, source_target_pairs={{4,0},{0,4},{5,1},{1,5},{6,2},{2,6},{7,3},{3,7},{12,8},{8,12},{13,... | collective-permute-start | bytes 1572872 | tf_op jit(solution)/shard_map/ppermute | solution.py:239
  91.6 3.8 %collective-permute-start.22 = (bf16[32,64,128]{2,1,0:T(8,128)(2,1)S(1)}, bf16[32,64,128]{2,1,0:T(8,128)(2,1)S(1)}, u32[]{:S(2)}, u32[]{:S(2)}) collective-permute-start(bf16[32,64,128]{2,1,0:T(8,128)(2,1)S(1)} %get-tuple-element.26.refs_2_), channel_id=1, source_target_pairs={{4,0},{0,4},{5,1},{1,5},{6,2},{2,6},{7,3},{3,7},{12,8},{8,12},{13,... | collective-permute-start | bytes 1572872 | tf_op jit(solution)/shard_map/ppermute | solution.py:239
  92.2 3.3 %collective-permute-start.24 = (bf16[16,64,128]{2,1,0:T(8,128)(2,1)S(1)}, bf16[16,64,128]{2,1,0:T(8,128)(2,1)S(1)}, u32[]{:S(2)}, u32[]{:S(2)}) collective-permute-start(bf16[16,64,128]{2,1,0:T(8,128)(2,1)S(1)} %get-tuple-element.28.refs_4_), channel_id=1, source_target_pairs={{4,0},{0,4},{5,1},{1,5},{6,2},{2,6},{7,3},{3,7},{12,8},{8,12},{13,... | collective-permute-start | bytes 786440 | tf_op jit(solution)/shard_map/ppermute | solution.py:239
  (11 other events, 176.5 us)

commit v11 on v8

--- a/solution.py
+++ b/solution.py
@@ -81,18 +81,16 @@
     )(both)
 
 
-def assemble_kernel(own_ref, *refs):
-    *quarter_refs, out_ref = refs
-    for off, ref in enumerate(quarter_refs):
-        rows = pl.ds(pl.multiple_of(((own_ref[1] + off) & (X - 1)) * QUARTER, QUARTER), QUARTER)
-        for chip in range(CHIPS):
-            out_ref[chip, rows, :] = ref[chip]
-
-
-def assemble(own, quarters):
-    return call(
-        assemble_kernel, [(CHIPS, BLOCK, WIDTH)], [SMEM] + [VMEM] * X, (VMEM,), mib=8
-    )(own, *quarters)[0]
+def stack_kernel(*refs):
+    *parts, out_ref = refs
+    for y, ref in enumerate(parts):
+        out_ref[y] = ref[...]
+
+
+def stack(parts):
+    return call(
+        stack_kernel, [(Y, CHIPS, QUARTER, WIDTH)], [VMEM] * Y, (VMEM,), mib=8
+    )(*parts)[0]
 
 
 def tie(arrays, *after):
@@ -181,10 +179,10 @@
 def virtual_kernel(core_off, index_ref, first_ref, own_ref, *refs):
     panel_refs, refs = refs[: len(PARTS)], refs[len(PARTS) :]
     if core_off:
-        table_ref, before_ref, out_hbm, out_ref, left_ref, right_ref, out_sems = refs
+        table_ref, before_ref, out_hbm, out_ref, panel_ref, left_ref, right_ref, out_sems = refs
     else:
-        rows_ref, out_ref, table_ref, left_ref, right_ref = refs
-    core0, y0 = own_ref[2], own_ref[3]
+        rows_ref, out_ref, table_ref, panel_ref, left_ref, right_ref = refs
+    x0, core0, y0 = (own_ref[i] for i in range(1, 4))
     half_table = CHIPS * CORES // 2
     for slot in range(MOLECULES):
         z, x, core = slot // (X * CORES), slot // CORES % X, slot % CORES
@@ -199,11 +197,10 @@
             table_ref[z * X + tile_at] = tile
             table_ref[half_table + z * X + tile_at] = swap_halves(tile)
 
-    def panel(y_off, chip):
-        if y_off == 2:
-            return panel_refs[3 + chip // (CHIPS // 2)][chip % (CHIPS // 2)]
-        return panel_refs[{0: 0, 1: 1, 3: 2}[y_off]][chip]
-
+    for (off, part), ref in zip(PARTS, panel_refs):
+        place = pl.ds(pl.multiple_of(((x0 + off) & (X - 1)) * QUARTER, QUARTER), QUARTER)
+        for y, chip in itertools.product(range(ref.shape[0]), range(CHIPS)):
+            panel_ref[(part or 0) * (Y // 2) + y, chip, place, :] = ref[y, chip]
     first_half = lax.broadcasted_iota(jnp.int32, (BLOCK, WIDTH), 1) < BLOCK
     written = []
     for z in range(Z):
@@ -215,7 +212,7 @@
                 one = left_ref[index_ref[k, molecule]]
                 two = right_ref[index_ref[k + 1, molecule]]
                 left.append(jnp.where(first_half, table_ref[one], table_ref[two]))
-            right = [panel(y, z * X + x) for y in range(Y)]
+            right = [panel_ref[y, z * X + x] for y in range(Y)]
             found = lax.dot_general(
                 jnp.concatenate(left, axis=1), jnp.concatenate(right, axis=1), NT,
                 preferred_element_type=jnp.float32,
@@ -237,7 +234,8 @@
 
 def virtual(core_off, panels, own, virt_index, first_map, *rest):
     shape, table = (BLOCK, BASIS), (MOLECULES, BLOCK, WIDTH)
-    scratch = [pltpu.SMEM((MOLECULES,), jnp.int32)] * 2
+    scratch = [pltpu.VMEM((Y, CHIPS, BLOCK, WIDTH), jnp.bfloat16)]
+    scratch += [pltpu.SMEM((MOLECULES,), jnp.int32)] * 2
     if core_off:
         scratch = [pltpu.VMEM(shape, jnp.bfloat16), *scratch, pltpu.SemaphoreType.DMA((Z,))]
     return call(
@@ -276,11 +274,10 @@
     pieces = [occ_plane] + [shift(occ_plane, "y", by) for by in range(1, Y)]
     rows = ring(mask_rows(pair_mask, b_tensor), "x", occ_plane)
     rows = rows + [shift(part, "core", 1) for part in rows]
-    quarters = [virt_quarter] + [shift(virt_quarter, "x", by) for by in range(1, X)]
-    virt_plane = assemble(own, quarters)
+    virt_plane = stack([virt_quarter] + [shift(virt_quarter, "y", by) for by in range(1, Y)])
     pieces = pieces + [shift(piece, "core", 1) for piece in pieces]
     half = occupied(dense_panel(pieces, own, occ_index, second_map), rows, own)
-    mine = ring(virt_plane, "y", half)
+    mine = ring(virt_plane, "x", half)
     turned = exchange(*tie([half], *mine[1:3]))
     mine = tie(mine, turned)
     other = [shift(panel, "core", 1) for panel in mine]

time: 103 us -> 97.5 us (0.947)
  waiting for transfers between devices: 37.1 us -> 30.4 us
  starting transfers between devices: 48.2 us -> 49.4 us
    all_to_all x2, waiting for transfers between devices: 16.5 us -> 12.3 us  [exchange(): lax.all_to_all(array, ('z', 'x'), split_axis=0, concat_axis=0, tiled=True)]
    ppermute x28, waiting for transfers between devices: 20.6 us -> 18.1 us  [shift(): lax.ppermute(array, axis, [((i + by) % size, i) for i in range(size)])]
    ppermute x28, starting transfers between devices: 33.3 us -> 34.5 us  [shift(): lax.ppermute(array, axis, [((i + by) % size, i) for i in range(size)])]
  transfers between devices with their start and end apart: 30 -> 30, of which waited for: 10 -> 11; matrix products, arithmetic and copies ran while one was open for 0% -> 0% of each run, Pallas kernels for 10% -> 10%
where the time goes in v11:
time: 97.5 us; the launch traced here: 97.1 us
  starting transfers between devices  49.4 us (51%)
  waiting for transfers between devices  30.4 us (31%)
  Pallas kernels  13.5 us (14%)
  local copies, waits for them, and re-layouts  3.31 us (3%)
    ppermute x28, starting transfers between devices, shift(): lax.ppermute(array, axis, [((i + by) % size, i) for i in range(size)])  34.5 us
    ppermute x28, waiting for transfers between devices, shift(): lax.ppermute(array, axis, [((i + by) % size, i) for i in range(size)])  18.1 us
    all_to_all x2, starting transfers between devices, exchange(): lax.all_to_all(array, ('z', 'x'), split_axis=0, concat_axis=0, tiled=True)  14.9 us
    all_to_all x2, waiting for transfers between devices, exchange(): lax.all_to_all(array, ('z', 'x'), split_axis=0, concat_axis=0, tiled=True)  12.3 us
    pallas_call x2, Pallas kernels, virtual(): call(functools.partial(virtual_kernel, core_off), [shape] if core_off els...  5.16 us
    pallas_call x1, Pallas kernels, occupied(): call(occupied_kernel, [(CHIPS, QUARTER, lanes)], [SMEM] + [VMEM] * (1 + l...  3.98 us
    unnamed x20, local copies, waits for them, and re-layouts  3.24 us
    pallas_call x1, Pallas kernels, dense_panel(): call(dense_kernel, [shape], [SMEM] * 3 + [VMEM] * len(pieces), (VMEM,), [...  2.34 us
  transfers between devices with their start and end apart: 30, of which 11 were waited for; matrix products, arithmetic and copies ran while one was open for 0% of the time, Pallas kernels for 10%

profile of v11, /device:TPU:1, one launch (start us, length us, event | category | flops | bytes accessed | tf_op | source)
XLA Modules:
  0.0 97.1 jit_solution(4411367288962463824)
XLA Ops:
  2.3 3.4 %collective-permute-start.12 = (bf16[64,4096]{1,0:T(8,128)(2,1)S(1)}, bf16[64,4096]{1,0:T(8,128)(2,1)S(1)}, u32[]{:S(2)}, u32[]{:S(2)}) collective-permute-start(bf16[64,4096]{1,0:T(8,128)(2,1)S(1)} %shard_map.86.refs_0_), channel_id=1, source_target_pairs={{8,0},{16,8},{24,16},{0,24},{9,1},{17,9},{25,17},{1,25},{10,2},{18... | collective-permute-start | bytes 1572872 | tf_op jit(solution)/shard_map/ppermute | solution.py:252
  7.3 1.3 %shard_map.82 = bf16[32,32,128]{2,1,0:T(8,128)(2,1)} custom-call(s32[4]{0:T(128)S(1)} %pad_add_fusion.own_ref, bf16[1,2,64,64]{3,2,1,0:T(8,128)(2,1)S(1)} %copy-done.3, bf16[1,2,64,64]{3,2,1,0:T(8,128)(2,1)S(1)} %copy-done.4), custom_call_target="tpu_custom_call" | custom-call | flops 1024 | bytes 1024 | tf_op jit(solution)/shard_map/pallas_call | solution.py:63
  8.7 11.0 %all-to-all-start = ((bf16[32,32,128]{2,1,0:T(8,128)(2,1)}), bf16[32,32,128]{2,1,0:T(8,128)(2,1)S(1)}, u32[]{:S(2)}, u32[]{:S(2)}) async-start(bf16[32,32,128]{2,1,0:T(8,128)(2,1)} %shard_map.82), calls=%async_computation | async-start | bytes 524288 | tf_op jit(solution)/shard_map/all_to_all | solution.py:265
  19.7 1.6 %collective-permute-start.16 = (bf16[64,4096]{1,0:T(8,128)(2,1)S(1)}, bf16[64,4096]{1,0:T(8,128)(2,1)S(1)}, u32[]{:S(2)}, u32[]{:S(2)}) collective-permute-start(bf16[64,4096]{1,0:T(8,128)(2,1)S(1)} %shard_map.86.refs_0_), channel_id=1, source_target_pairs={{4,0},{0,4},{5,1},{1,5},{6,2},{2,6},{7,3},{3,7},{12,8},{8,12},{13,... | collective-permute-start | bytes 1572872 | tf_op jit(solution)/shard_map/ppermute | solution.py:252
  21.3 9.0 %all-to-all-done.both_ref = bf16[32,32,128]{2,1,0:T(8,128)(2,1)S(1)} async-done(((bf16[32,32,128]{2,1,0:T(8,128)(2,1)}), bf16[32,32,128]{2,1,0:T(8,128)(2,1)S(1)}, u32[]{:S(2)}, u32[]{:S(2)}) %all-to-all-start) | async-done | bytes 262176 | tf_op jit(solution)/shard_map/all_to_all | solution.py:265
  30.2 3.0 %collective-permute-start.6 = (bf16[32,16,128]{2,1,0:T(8,128)(2,1)S(1)}, bf16[32,16,128]{2,1,0:T(8,128)(2,1)S(1)}, u32[]{:S(2)}, u32[]{:S(2)}) collective-permute-start(bf16[32,16,128]{2,1,0:T(8,128)(2,1)S(1)} %get-tuple-element.19.refs_0_.refs_2_), channel_id=1, source_target_pairs={{2,0},{3,1},{0,2},{1,3},{6,4},{7,5},{4,6},{5,7},{10,8},{11,9},{8,1... | collective-permute-start | bytes 393224 | tf_op jit(solution)/shard_map/ppermute | solution.py:252
  33.6 2.3 %collective-permute-start.5 = (bf16[32,16,128]{2,1,0:T(8,128)(2,1)S(1)}, bf16[32,16,128]{2,1,0:T(8,128)(2,1)S(1)}, u32[]{:S(2)}, u32[]{:S(2)}) collective-permute-start(bf16[32,16,128]{2,1,0:T(8,128)(2,1)S(1)} %get-tuple-element.19.refs_0_.refs_2_), channel_id=1, source_target_pairs={{1,0},{2,1},{3,2},{0,3},{5,4},{6,5},{7,6},{4,7},{9,8},{10,9},{11,1... | collective-permute-start | bytes 393224 | tf_op jit(solution)/shard_map/ppermute | solution.py:252
  35.9 4.1 %collective-permute-start.8 = (bf16[32,16,128]{2,1,0:T(8,128)(2,1)S(1)}, bf16[32,16,128]{2,1,0:T(8,128)(2,1)S(1)}, u32[]{:S(2)}, u32[]{:S(2)}) collective-permute-start(bf16[32,16,128]{2,1,0:T(8,128)(2,1)S(1)} %get-tuple-element.19.refs_0_.refs_2_), channel_id=1, source_target_pairs={{4,0},{0,4},{5,1},{1,5},{6,2},{2,6},{7,3},{3,7},{12,8},{8,12},{13,... | collective-permute-start | bytes 393224 | tf_op jit(solution)/shard_map/ppermute | solution.py:252
  41.9 2.7 %collective-permute-start.15 = (bf16[32,4096]{1,0:T(8,128)(2,1)S(1)}, bf16[32,4096]{1,0:T(8,128)(2,1)S(1)}, u32[]{:S(2)}, u32[]{:S(2)}) collective-permute-start(bf16[32,4096]{1,0:T(8,128)(2,1)S(1)} %slice.13), channel_id=1, source_target_pairs={{8,0},{16,8},{24,16},{0,24},{9,1},{17,9},{25,17},{1,25},{10,2},{18... | collective-permute-start | bytes 786440 | tf_op jit(solution)/shard_map/ppermute | solution.py:252
  45.3 2.1 %collective-permute-start.10 = (bf16[32,16,128]{2,1,0:T(8,128)(2,1)S(1)}, bf16[32,16,128]{2,1,0:T(8,128)(2,1)S(1)}, u32[]{:S(2)}, u32[]{:S(2)}) collective-permute-start(bf16[32,16,128]{2,1,0:T(8,128)(2,1)S(1)} %collective-permute-done.6.refs_2_), channel_id=1, source_target_pairs={{4,0},{0,4},{5,1},{1,5},{6,2},{2,6},{7,3},{3,7},{12,8},{8,12},{13,... | collective-permute-start | bytes 393224 | tf_op jit(solution)/shard_map/ppermute | solution.py:252
  48.7 1.8 %collective-permute-start.9 = (bf16[32,16,128]{2,1,0:T(8,128)(2,1)S(1)}, bf16[32,16,128]{2,1,0:T(8,128)(2,1)S(1)}, u32[]{:S(2)}, u32[]{:S(2)}) collective-permute-start(bf16[32,16,128]{2,1,0:T(8,128)(2,1)S(1)} %collective-permute-done.5.refs_1_), channel_id=1, source_target_pairs={{4,0},{0,4},{5,1},{1,5},{6,2},{2,6},{7,3},{3,7},{12,8},{8,12},{13,... | collective-permute-start | bytes 393224 | tf_op jit(solution)/shard_map/ppermute | solution.py:252
  51.5 2.0 %collective-permute-start.3 = (bf16[4,32,16,128]{3,2,1,0:T(8,128)(2,1)S(1)}, bf16[4,32,16,128]{3,2,1,0:T(8,128)(2,1)S(1)}, u32[]{:S(2)}, u32[]{:S(2)}) collective-permute-start(bf16[4,32,16,128]{3,2,1,0:T(8,128)(2,1)S(1)} %shard_map.84.refs_0_), channel_id=1, source_target_pairs={{8,0},{16,8},{24,16},{0,24},{9,1},{17,9},{25,17},{1,25},{10,2},{18... | collective-permute-start | bytes 1572872 | tf_op jit(solution)/shard_map/ppermute | solution.py:252
  54.3 2.3 %shard_map.85.dense_ref = bf16[512,4096]{1,0:T(8,128)(2,1)S(1)} custom-call(s32[8,64]{1,0:T(8,128)S(1)} %bitcast.9, s32[64]{0:T(128)S(1)} %copy-done.9, s32[4]{0:T(128)S(1)} %pad_add_fusion.own_ref, bf16[32,16,128]{2,1,0:T(8,128)(2,1)S(1)} %get-tuple-element.19.refs_0_.refs_2_, bf16[32,16,128]{2,1,0:T(8,128)(2,1)S(1)} %collective-permute-done.5.refs_1_, ...), custom_call_target="tpu_custom_call" | custom-call | flops 1024 | bytes 1024 | tf_op jit(solution)/shard_map/pallas_call | solution.py:143
  56.7 4.0 %shard_map.88.refs_2_.refs_0_ = bf16[32,16,512]{2,1,0:T(8,128)(2,1)} custom-call(s32[4]{0:T(128)S(1)} %pad_add_fusion.own_ref, bf16[512,4096]{1,0:T(8,128)(2,1)S(1)} %shard_map.85.dense_ref, bf16[64,4096]{1,0:T(8,128)(2,1)S(1)} %shard_map.86.refs_0_, bf16[64,4096]{1,0:T(8,128)(2,1)S(1)} %get-tuple-element.20.refs_1_, ...), custom_call_target="tpu_custom_call" | custom-call | flops 1024 | bytes 1024 | tf_op jit(solution)/shard_map/pallas_call | solution.py:170
  60.7 4.1 %collective-permute-done.3.refs_0_ = bf16[4,32,16,128]{3,2,1,0:T(8,128)(2,1)S(1)} collective-permute-done((bf16[4,32,16,128]{3,2,1,0:T(8,128)(2,1)S(1)}, bf16[4,32,16,128]{3,2,1,0:T(8,128)(2,1)S(1)}, u32[]{:S(2)}, u32[]{:S(2)}) %collective-permute-start.3) | collective-permute-done | bytes 524320 | tf_op jit(solution)/shard_map/ppermute | solution.py:252
  64.7 2.9 %collective-permute-done.4.refs_1_ = bf16[4,32,16,128]{3,2,1,0:T(8,128)(2,1)S(1)} collective-permute-done((bf16[4,32,16,128]{3,2,1,0:T(8,128)(2,1)S(1)}, bf16[4,32,16,128]{3,2,1,0:T(8,128)(2,1)S(1)}, u32[]{:S(2)}, u32[]{:S(2)}) %collective-permute-start.4) | collective-permute-done | bytes 524320 | tf_op jit(solution)/shard_map/ppermute | solution.py:252
  67.6 3.9 %all-to-all-start.1 = ((bf16[32,16,512]{2,1,0:T(8,128)(2,1)}), bf16[32,16,512]{2,1,0:T(8,128)(2,1)S(1)}, u32[]{:S(2)}, u32[]{:S(2)}) async-start(bf16[32,16,512]{2,1,0:T(8,128)(2,1)} %shard_map.90), calls=%async_computation.1 | async-start | bytes 1048576 | tf_op jit(solution)/shard_map/all_to_all | solution.py:265
  72.8 1.6 %collective-permute-start.22 = (bf16[2,32,16,128]{3,2,1,0:T(8,128)(2,1)S(1)}, bf16[2,32,16,128]{3,2,1,0:T(8,128)(2,1)S(1)}, u32[]{:S(2)}, u32[]{:S(2)}) collective-permute-start(bf16[2,32,16,128]{3,2,1,0:T(8,128)(2,1)S(1)} %slice.15), channel_id=1, source_target_pairs={{8,0},{16,8},{24,16},{0,24},{9,1},{17,9},{25,17},{1,25},{10,2},{18... | collective-permute-start | bytes 786440 | tf_op jit(solution)/shard_map/ppermute | solution.py:252
  74.3 7.6 %collective-permute-done.21.refs_3_ = bf16[2,32,16,128]{3,2,1,0:T(8,128)(2,1)S(1)} collective-permute-done((bf16[2,32,16,128]{3,2,1,0:T(8,128)(2,1)S(1)}, bf16[2,32,16,128]{3,2,1,0:T(8,128)(2,1)S(1)}, u32[]{:S(2)}, u32[]{:S(2)}) %collective-permute-start.21) | collective-permute-done | bytes 262176 | tf_op jit(solution)/shard_map/ppermute | solution.py:252
  81.9 1.6 %collective-permute-done.22.refs_4_ = bf16[2,32,16,128]{3,2,1,0:T(8,128)(2,1)S(1)} collective-permute-done((bf16[2,32,16,128]{3,2,1,0:T(8,128)(2,1)S(1)}, bf16[2,32,16,128]{3,2,1,0:T(8,128)(2,1)S(1)}, u32[]{:S(2)}, u32[]{:S(2)}) %collective-permute-start.22) | collective-permute-done | bytes 262176 | tf_op jit(solution)/shard_map/ppermute | solution.py:252
  83.5 3.3 %all-to-all-done.1.refs_5_ = bf16[32,16,512]{2,1,0:T(8,128)(2,1)S(1)} async-done(((bf16[32,16,512]{2,1,0:T(8,128)(2,1)}), bf16[32,16,512]{2,1,0:T(8,128)(2,1)S(1)}, u32[]{:S(2)}, u32[]{:S(2)}) %all-to-all-start.1) | async-done | bytes 524320 | tf_op jit(solution)/shard_map/all_to_all | solution.py:265
  86.8 3.4 %collective-permute-start.23 = (bf16[4,32,16,128]{3,2,1,0:T(8,128)(2,1)S(1)}, bf16[4,32,16,128]{3,2,1,0:T(8,128)(2,1)S(1)}, u32[]{:S(2)}, u32[]{:S(2)}) collective-permute-start(bf16[4,32,16,128]{3,2,1,0:T(8,128)(2,1)S(1)} %get-tuple-element.24.refs_0_), channel_id=1, source_target_pairs={{4,0},{0,4},{5,1},{1,5},{6,2},{2,6},{7,3},{3,7},{12,8},{8,12},{13,... | collective-permute-start | bytes 1572872 | tf_op jit(solution)/shard_map/ppermute | solution.py:252
  91.3 2.3 %shard_map.92 = (bf16[64,4096]{1,0:T(8,128)(2,1)S(1)}, bf16[64,64,128]{2,1,0:T(8,128)(2,1)S(1)}) custom-call(s32[8,64]{1,0:T(8,128)S(1)} %bitcast.7, s32[64]{0:T(128)S(1)} %copy-done.7, s32[4]{0:T(128)S(1)} %pad_add_fusion.own_ref, bf16[4,32,16,128]{3,2,1,0:T(8,128)(2,1)S(1)} %get-tuple-element.24.refs_0_, ...), custom_call_target="tpu_custom_call" | custom-call | flops 1024 | bytes 1024 | tf_op jit(solution)/shard_map/pallas_call | solution.py:241
  94.0 2.9 %shard_map.93 = bf16[64,4096]{1,0:T(8,128)(2,1)} custom-call(s32[8,64]{1,0:T(8,128)S(1)} %bitcast.8, s32[64]{0:T(128)S(1)} %copy-done.7, s32[4]{0:T(128)S(1)} %pad_add_fusion.own_ref, bf16[4,32,16,128]{3,2,1,0:T(8,128)(2,1)S(1)} %collective-permute-done.23.refs_0_, bf16[4,32,16,128]{3,2,1,0:T(8,128)(2,1)S(1)} %collective-permute-done.24.refs_1_, ...), custom_call_target="tpu_custom_call" | custom-call | flops 1024 | bytes 1024 | tf_op jit(solution)/shard_map/pallas_call | solution.py:241
  (73 shorter events, 12.6 us)
Async XLA Ops:
  2.3 31.3 %collective-permute-start.12 = (bf16[64,4096]{1,0:T(8,128)(2,1)S(1)}, bf16[64,4096]{1,0:T(8,128)(2,1)S(1)}, u32[]{:S(2)}, u32[]{:S(2)}) collective-permute-start(bf16[64,4096]{1,0:T(8,128)(2,1)S(1)} %shard_map.86.refs_0_), channel_id=1, source_target_pairs={{8,0},{16,8},{24,16},{0,24},{9,1},{17,9},{25,17},{1,25},{10,2},{18... | collective-permute-start | bytes 1572872 | tf_op jit(solution)/shard_map/ppermute | solution.py:252
  5.7 30.2 %collective-permute-start.13 = (bf16[64,4096]{1,0:T(8,128)(2,1)S(1)}, bf16[64,4096]{1,0:T(8,128)(2,1)S(1)}, u32[]{:S(2)}, u32[]{:S(2)}) collective-permute-start(bf16[64,4096]{1,0:T(8,128)(2,1)S(1)} %shard_map.86.refs_0_), channel_id=1, source_target_pairs={{24,0},{0,8},{8,16},{16,24},{25,1},{1,9},{9,17},{17,25},{26,2},{2,... | collective-permute-start | bytes 1572872 | tf_op jit(solution)/shard_map/ppermute | solution.py:252
  8.7 21.5 %all-to-all-start = ((bf16[32,32,128]{2,1,0:T(8,128)(2,1)}), bf16[32,32,128]{2,1,0:T(8,128)(2,1)S(1)}, u32[]{:S(2)}, u32[]{:S(2)}) async-start(bf16[32,32,128]{2,1,0:T(8,128)(2,1)} %shard_map.82), calls=%async_computation | async-start | bytes 524288 | tf_op jit(solution)/shard_map/all_to_all | solution.py:265
  19.7 20.4 %collective-permute-start.16 = (bf16[64,4096]{1,0:T(8,128)(2,1)S(1)}, bf16[64,4096]{1,0:T(8,128)(2,1)S(1)}, u32[]{:S(2)}, u32[]{:S(2)}) collective-permute-start(bf16[64,4096]{1,0:T(8,128)(2,1)S(1)} %shard_map.86.refs_0_), channel_id=1, source_target_pairs={{4,0},{0,4},{5,1},{1,5},{6,2},{2,6},{7,3},{3,7},{12,8},{8,12},{13,... | collective-permute-start | bytes 1572872 | tf_op jit(solution)/shard_map/ppermute | solution.py:252
  30.2 10.0 %collective-permute-start.6 = (bf16[32,16,128]{2,1,0:T(8,128)(2,1)S(1)}, bf16[32,16,128]{2,1,0:T(8,128)(2,1)S(1)}, u32[]{:S(2)}, u32[]{:S(2)}) collective-permute-start(bf16[32,16,128]{2,1,0:T(8,128)(2,1)S(1)} %get-tuple-element.19.refs_0_.refs_2_), channel_id=1, source_target_pairs={{2,0},{3,1},{0,2},{1,3},{6,4},{7,5},{4,6},{5,7},{10,8},{11,9},{8,1... | collective-permute-start | bytes 393224 | tf_op jit(solution)/shard_map/ppermute | solution.py:252
  33.2 7.9 %collective-permute-start.7 = (bf16[32,16,128]{2,1,0:T(8,128)(2,1)S(1)}, bf16[32,16,128]{2,1,0:T(8,128)(2,1)S(1)}, u32[]{:S(2)}, u32[]{:S(2)}) collective-permute-start(bf16[32,16,128]{2,1,0:T(8,128)(2,1)S(1)} %get-tuple-element.19.refs_0_.refs_2_), channel_id=1, source_target_pairs={{3,0},{0,1},{1,2},{2,3},{7,4},{4,5},{5,6},{6,7},{11,8},{8,9},{9,10... | collective-permute-start | bytes 393224 | tf_op jit(solution)/shard_map/ppermute | solution.py:252
  33.6 7.5 %collective-permute-start.5 = (bf16[32,16,128]{2,1,0:T(8,128)(2,1)S(1)}, bf16[32,16,128]{2,1,0:T(8,128)(2,1)S(1)}, u32[]{:S(2)}, u32[]{:S(2)}) collective-permute-start(bf16[32,16,128]{2,1,0:T(8,128)(2,1)S(1)} %get-tuple-element.19.refs_0_.refs_2_), channel_id=1, source_target_pairs={{1,0},{2,1},{3,2},{0,3},{5,4},{6,5},{7,6},{4,7},{9,8},{10,9},{11,1... | collective-permute-start | bytes 393224 | tf_op jit(solution)/shard_map/ppermute | solution.py:252
  35.9 5.9 %collective-permute-start.8 = (bf16[32,16,128]{2,1,0:T(8,128)(2,1)S(1)}, bf16[32,16,128]{2,1,0:T(8,128)(2,1)S(1)}, u32[]{:S(2)}, u32[]{:S(2)}) collective-permute-start(bf16[32,16,128]{2,1,0:T(8,128)(2,1)S(1)} %get-tuple-element.19.refs_0_.refs_2_), channel_id=1, source_target_pairs={{4,0},{0,4},{5,1},{1,5},{6,2},{2,6},{7,3},{3,7},{12,8},{8,12},{13,... | collective-permute-start | bytes 393224 | tf_op jit(solution)/shard_map/ppermute | solution.py:252
  40.1 5.2 %collective-permute-start = (bf16[32,16,128]{2,1,0:T(8,128)(2,1)S(1)}, bf16[32,16,128]{2,1,0:T(8,128)(2,1)S(1)}, u32[]{:S(2)}, u32[]{:S(2)}) collective-permute-start(bf16[32,16,128]{2,1,0:T(8,128)(2,1)S(1)} %get-tuple-element.18.refs_0_), channel_id=1, source_target_pairs={{1,0},{2,1},{3,2},{0,3},{5,4},{6,5},{7,6},{4,7},{9,8},{10,9},{11,1... | collective-permute-start | bytes 393224 | tf_op jit(solution)/shard_map/ppermute | solution.py:252
  40.2 7.2 %collective-permute-start.1 = (bf16[32,16,128]{2,1,0:T(8,128)(2,1)S(1)}, bf16[32,16,128]{2,1,0:T(8,128)(2,1)S(1)}, u32[]{:S(2)}, u32[]{:S(2)}) collective-permute-start(bf16[32,16,128]{2,1,0:T(8,128)(2,1)S(1)} %get-tuple-element.18.refs_0_), channel_id=1, source_target_pairs={{2,0},{3,1},{0,2},{1,3},{6,4},{7,5},{4,6},{5,7},{10,8},{11,9},{8,1... | collective-permute-start | bytes 393224 | tf_op jit(solution)/shard_map/ppermute | solution.py:252
  41.2 9.5 %collective-permute-start.14 = (bf16[32,4096]{1,0:T(8,128)(2,1)S(1)}, bf16[32,4096]{1,0:T(8,128)(2,1)S(1)}, u32[]{:S(2)}, u32[]{:S(2)}) collective-permute-start(bf16[32,4096]{1,0:T(8,128)(2,1)S(1)} %slice.12), channel_id=1, source_target_pairs={{24,0},{0,8},{8,16},{16,24},{25,1},{1,9},{9,17},{17,25},{26,2},{2,... | collective-permute-start | bytes 786440 | tf_op jit(solution)/shard_map/ppermute | solution.py:252
  41.2 7.5 %collective-permute-start.2 = (bf16[32,16,128]{2,1,0:T(8,128)(2,1)S(1)}, bf16[32,16,128]{2,1,0:T(8,128)(2,1)S(1)}, u32[]{:S(2)}, u32[]{:S(2)}) collective-permute-start(bf16[32,16,128]{2,1,0:T(8,128)(2,1)S(1)} %get-tuple-element.18.refs_0_), channel_id=1, source_target_pairs={{3,0},{0,1},{1,2},{2,3},{7,4},{4,5},{5,6},{6,7},{11,8},{8,9},{9,10... | collective-permute-start | bytes 393224 | tf_op jit(solution)/shard_map/ppermute | solution.py:252
  41.9 11.7 %collective-permute-start.15 = (bf16[32,4096]{1,0:T(8,128)(2,1)S(1)}, bf16[32,4096]{1,0:T(8,128)(2,1)S(1)}, u32[]{:S(2)}, u32[]{:S(2)}) collective-permute-start(bf16[32,4096]{1,0:T(8,128)(2,1)S(1)} %slice.13), channel_id=1, source_target_pairs={{8,0},{16,8},{24,16},{0,24},{9,1},{17,9},{25,17},{1,25},{10,2},{18... | collective-permute-start | bytes 786440 | tf_op jit(solution)/shard_map/ppermute | solution.py:252
  45.3 5.3 %collective-permute-start.10 = (bf16[32,16,128]{2,1,0:T(8,128)(2,1)S(1)}, bf16[32,16,128]{2,1,0:T(8,128)(2,1)S(1)}, u32[]{:S(2)}, u32[]{:S(2)}) collective-permute-start(bf16[32,16,128]{2,1,0:T(8,128)(2,1)S(1)} %collective-permute-done.6.refs_2_), channel_id=1, source_target_pairs={{4,0},{0,4},{5,1},{1,5},{6,2},{2,6},{7,3},{3,7},{12,8},{8,12},{13,... | collective-permute-start | bytes 393224 | tf_op jit(solution)/shard_map/ppermute | solution.py:252
  50.6 6.0 %collective-permute-start.17 = (bf16[64,4096]{1,0:T(8,128)(2,1)S(1)}, bf16[64,4096]{1,0:T(8,128)(2,1)S(1)}, u32[]{:S(2)}, u32[]{:S(2)}) collective-permute-start(bf16[64,4096]{1,0:T(8,128)(2,1)S(1)} %get-tuple-element.20.refs_1_), channel_id=1, source_target_pairs={{4,0},{0,4},{5,1},{1,5},{6,2},{2,6},{7,3},{3,7},{12,8},{8,12},{13,... | collective-permute-start | bytes 1572872 | tf_op jit(solution)/shard_map/ppermute | solution.py:252
  51.2 5.5 %collective-permute-start.18 = (bf16[64,4096]{1,0:T(8,128)(2,1)S(1)}, bf16[64,4096]{1,0:T(8,128)(2,1)S(1)}, u32[]{:S(2)}, u32[]{:S(2)}) collective-permute-start(bf16[64,4096]{1,0:T(8,128)(2,1)S(1)} %get-tuple-element.21.refs_2_), channel_id=1, source_target_pairs={{4,0},{0,4},{5,1},{1,5},{6,2},{2,6},{7,3},{3,7},{12,8},{8,12},{13,... | collective-permute-start | bytes 1572872 | tf_op jit(solution)/shard_map/ppermute | solution.py:252
  51.5 13.2 %collective-permute-start.3 = (bf16[4,32,16,128]{3,2,1,0:T(8,128)(2,1)S(1)}, bf16[4,32,16,128]{3,2,1,0:T(8,128)(2,1)S(1)}, u32[]{:S(2)}, u32[]{:S(2)}) collective-permute-start(bf16[4,32,16,128]{3,2,1,0:T(8,128)(2,1)S(1)} %shard_map.84.refs_0_), channel_id=1, source_target_pairs={{8,0},{16,8},{24,16},{0,24},{9,1},{17,9},{25,17},{1,25},{10,2},{18... | collective-permute-start | bytes 1572872 | tf_op jit(solution)/shard_map/ppermute | solution.py:252
  53.6 14.1 %collective-permute-start.4 = (bf16[4,32,16,128]{3,2,1,0:T(8,128)(2,1)S(1)}, bf16[4,32,16,128]{3,2,1,0:T(8,128)(2,1)S(1)}, u32[]{:S(2)}, u32[]{:S(2)}) collective-permute-start(bf16[4,32,16,128]{3,2,1,0:T(8,128)(2,1)S(1)} %shard_map.84.refs_0_), channel_id=1, source_target_pairs={{24,0},{0,8},{8,16},{16,24},{25,1},{1,9},{9,17},{17,25},{26,2},{2,... | collective-permute-start | bytes 1572872 | tf_op jit(solution)/shard_map/ppermute | solution.py:252
  67.6 19.2 %all-to-all-start.1 = ((bf16[32,16,512]{2,1,0:T(8,128)(2,1)}), bf16[32,16,512]{2,1,0:T(8,128)(2,1)S(1)}, u32[]{:S(2)}, u32[]{:S(2)}) async-start(bf16[32,16,512]{2,1,0:T(8,128)(2,1)} %shard_map.90), calls=%async_computation.1 | async-start | bytes 1048576 | tf_op jit(solution)/shard_map/all_to_all | solution.py:265
  71.6 10.3 %collective-permute-start.21 = (bf16[2,32,16,128]{3,2,1,0:T(8,128)(2,1)S(1)}, bf16[2,32,16,128]{3,2,1,0:T(8,128)(2,1)S(1)}, u32[]{:S(2)}, u32[]{:S(2)}) collective-permute-start(bf16[2,32,16,128]{3,2,1,0:T(8,128)(2,1)S(1)} %slice.14), channel_id=1, source_target_pairs={{24,0},{0,8},{8,16},{16,24},{25,1},{1,9},{9,17},{17,25},{26,2},{2,... | collective-permute-start | bytes 786440 | tf_op jit(solution)/shard_map/ppermute | solution.py:252
  72.8 10.7 %collective-permute-start.22 = (bf16[2,32,16,128]{3,2,1,0:T(8,128)(2,1)S(1)}, bf16[2,32,16,128]{3,2,1,0:T(8,128)(2,1)S(1)}, u32[]{:S(2)}, u32[]{:S(2)}) collective-permute-start(bf16[2,32,16,128]{3,2,1,0:T(8,128)(2,1)S(1)} %slice.15), channel_id=1, source_target_pairs={{8,0},{16,8},{24,16},{0,24},{9,1},{17,9},{25,17},{1,25},{10,2},{18... | collective-permute-start | bytes 786440 | tf_op jit(solution)/shard_map/ppermute | solution.py:252
  86.8 7.2 %collective-permute-start.23 = (bf16[4,32,16,128]{3,2,1,0:T(8,128)(2,1)S(1)}, bf16[4,32,16,128]{3,2,1,0:T(8,128)(2,1)S(1)}, u32[]{:S(2)}, u32[]{:S(2)}) collective-permute-start(bf16[4,32,16,128]{3,2,1,0:T(8,128)(2,1)S(1)} %get-tuple-element.24.refs_0_), channel_id=1, source_target_pairs={{4,0},{0,4},{5,1},{1,5},{6,2},{2,6},{7,3},{3,7},{12,8},{8,12},{13,... | collective-permute-start | bytes 1572872 | tf_op jit(solution)/shard_map/ppermute | solution.py:252
  90.2 3.8 %collective-permute-start.24 = (bf16[4,32,16,128]{3,2,1,0:T(8,128)(2,1)S(1)}, bf16[4,32,16,128]{3,2,1,0:T(8,128)(2,1)S(1)}, u32[]{:S(2)}, u32[]{:S(2)}) collective-permute-start(bf16[4,32,16,128]{3,2,1,0:T(8,128)(2,1)S(1)} %get-tuple-element.25.refs_1_), channel_id=1, source_target_pairs={{4,0},{0,4},{5,1},{1,5},{6,2},{2,6},{7,3},{3,7},{12,8},{8,12},{13,... | collective-permute-start | bytes 1572872 | tf_op jit(solution)/shard_map/ppermute | solution.py:252
  90.2 3.8 %collective-permute-start.25 = (bf16[4,32,16,128]{3,2,1,0:T(8,128)(2,1)S(1)}, bf16[4,32,16,128]{3,2,1,0:T(8,128)(2,1)S(1)}, u32[]{:S(2)}, u32[]{:S(2)}) collective-permute-start(bf16[4,32,16,128]{3,2,1,0:T(8,128)(2,1)S(1)} %get-tuple-element.26.refs_2_), channel_id=1, source_target_pairs={{4,0},{0,4},{5,1},{1,5},{6,2},{2,6},{7,3},{3,7},{12,8},{8,12},{13,... | collective-permute-start | bytes 1572872 | tf_op jit(solution)/shard_map/ppermute | solution.py:252
  (16 other events, 204.7 us)

commit v12 on v11

--- a/solution.py
+++ b/solution.py
@@ -271,10 +271,12 @@
     own = jnp.stack([lax.axis_index(axis) for axis in SIZES]).astype(jnp.int32)
     both = exchange(spread(own, occ_blocks, virt_blocks))
     occ_plane, virt_quarter = divide(both)
+    sides = [shift(virt_quarter, "y", by) for by in range(1, Y)]
+    virt_plane = stack([virt_quarter] + sides)
+    rows = ring(mask_rows(pair_mask, b_tensor), "x", virt_quarter)
+    rows = rows + [shift(part, "core", 1) for part in rows]
+    (occ_plane,) = tie([occ_plane], *sides)
     pieces = [occ_plane] + [shift(occ_plane, "y", by) for by in range(1, Y)]
-    rows = ring(mask_rows(pair_mask, b_tensor), "x", occ_plane)
-    rows = rows + [shift(part, "core", 1) for part in rows]
-    virt_plane = stack([virt_quarter] + [shift(virt_quarter, "y", by) for by in range(1, Y)])
     pieces = pieces + [shift(piece, "core", 1) for piece in pieces]
     half = occupied(dense_panel(pieces, own, occ_index, second_map), rows, own)
     mine = ring(virt_plane, "x", half)

time: 97.5 us -> 99.9 us (1.025)
  waiting for transfers between devices: 30.4 us -> 33.3 us
    ppermute x28, waiting for transfers between devices: 18.1 us -> 25.2 us  [shift(): lax.ppermute(array, axis, [((i + by) % size, i) for i in range(size)])]
    all_to_all x2, waiting for transfers between devices: 12.3 us -> 8.13 us  [exchange(): lax.all_to_all(array, ('z', 'x'), split_axis=0, concat_axis=0, tiled=True)]
    ppermute x28, starting transfers between devices: 34.5 us -> 32.5 us  [shift(): lax.ppermute(array, axis, [((i + by) % size, i) for i in range(size)])]
    all_to_all x2, starting transfers between devices: 14.9 us -> 16.3 us  [exchange(): lax.all_to_all(array, ('z', 'x'), split_axis=0, concat_axis=0, tiled=True)]
  transfers between devices with their start and end apart: 30 -> 30, of which waited for: 11 -> 11; matrix products, arithmetic and copies ran while one was open for 0% -> 0% of each run, Pallas kernels for 10% -> 9%
where the time goes in v12:
time: 99.9 us; the launch traced here: 99.4 us
  starting transfers between devices  48.9 us (49%)
  waiting for transfers between devices  33.3 us (33%)
  Pallas kernels  13.5 us (14%)
  local copies, waits for them, and re-layouts  3.31 us (3%)
    ppermute x28, starting transfers between devices, shift(): lax.ppermute(array, axis, [((i + by) % size, i) for i in range(size)])  32.5 us
    ppermute x28, waiting for transfers between devices, shift(): lax.ppermute(array, axis, [((i + by) % size, i) for i in range(size)])  25.2 us
    all_to_all x2, starting transfers between devices, exchange(): lax.all_to_all(array, ('z', 'x'), split_axis=0, concat_axis=0, tiled=True)  16.3 us
    all_to_all x2, waiting for transfers between devices, exchange(): lax.all_to_all(array, ('z', 'x'), split_axis=0, concat_axis=0, tiled=True)  8.13 us
    pallas_call x2, Pallas kernels, virtual(): call(functools.partial(virtual_kernel, core_off), [shape] if core_off els...  5.16 us
    pallas_call x1, Pallas kernels, occupied(): call(occupied_kernel, [(CHIPS, QUARTER, lanes)], [SMEM] + [VMEM] * (1 + l...  3.98 us
    unnamed x20, local copies, waits for them, and re-layouts  3.23 us
    pallas_call x1, Pallas kernels, dense_panel(): call(dense_kernel, [shape], [SMEM] * 3 + [VMEM] * len(pieces), (VMEM,), [...  2.34 us
  transfers between devices with their start and end apart: 30, of which 11 were waited for; matrix products, arithmetic and copies ran while one was open for 0% of the time, Pallas kernels for 9%

profile of v12, /device:TPU:1, one launch (start us, length us, event | category | flops | bytes accessed | tf_op | source)
XLA Modules:
  0.0 99.4 jit_solution(2888049089528823932)
XLA Ops:
  1.6 1.3 %shard_map.82 = bf16[32,32,128]{2,1,0:T(8,128)(2,1)} custom-call(s32[4]{0:T(128)S(1)} %pad_add_fusion.own_ref, bf16[1,2,64,64]{3,2,1,0:T(8,128)(2,1)S(1)} %copy-done.3, bf16[1,2,64,64]{3,2,1,0:T(8,128)(2,1)S(1)} %copy-done.4), custom_call_target="tpu_custom_call" | custom-call | flops 1024 | bytes 1024 | tf_op jit(solution)/shard_map/pallas_call | solution.py:63
  2.9 11.9 %all-to-all-start = ((bf16[32,32,128]{2,1,0:T(8,128)(2,1)}), bf16[32,32,128]{2,1,0:T(8,128)(2,1)S(1)}, u32[]{:S(2)}, u32[]{:S(2)}) async-start(bf16[32,32,128]{2,1,0:T(8,128)(2,1)} %shard_map.82), calls=%async_computation | async-start | bytes 524288 | tf_op jit(solution)/shard_map/all_to_all | solution.py:265
  17.2 2.5 %collective-permute-start.12 = (bf16[64,4096]{1,0:T(8,128)(2,1)S(1)}, bf16[64,4096]{1,0:T(8,128)(2,1)S(1)}, u32[]{:S(2)}, u32[]{:S(2)}) collective-permute-start(bf16[64,4096]{1,0:T(8,128)(2,1)S(1)} %shard_map.87.refs_0_), channel_id=1, source_target_pairs={{8,0},{16,8},{24,16},{0,24},{9,1},{17,9},{25,17},{1,25},{10,2},{18... | collective-permute-start | bytes 1572872 | tf_op jit(solution)/shard_map/ppermute | solution.py:252
  19.7 1.5 %collective-permute-start.16 = (bf16[64,4096]{1,0:T(8,128)(2,1)S(1)}, bf16[64,4096]{1,0:T(8,128)(2,1)S(1)}, u32[]{:S(2)}, u32[]{:S(2)}) collective-permute-start(bf16[64,4096]{1,0:T(8,128)(2,1)S(1)} %shard_map.87.refs_0_), channel_id=1, source_target_pairs={{4,0},{0,4},{5,1},{1,5},{6,2},{2,6},{7,3},{3,7},{12,8},{8,12},{13,... | collective-permute-start | bytes 1572872 | tf_op jit(solution)/shard_map/ppermute | solution.py:252
  21.2 4.8 %all-to-all-done.both_ref = bf16[32,32,128]{2,1,0:T(8,128)(2,1)S(1)} async-done(((bf16[32,32,128]{2,1,0:T(8,128)(2,1)}), bf16[32,32,128]{2,1,0:T(8,128)(2,1)S(1)}, u32[]{:S(2)}, u32[]{:S(2)}) %all-to-all-start) | async-done | bytes 262176 | tf_op jit(solution)/shard_map/all_to_all | solution.py:265
  26.0 2.8 %collective-permute-start = (bf16[32,16,128]{2,1,0:T(8,128)(2,1)S(1)}, bf16[32,16,128]{2,1,0:T(8,128)(2,1)S(1)}, u32[]{:S(2)}, u32[]{:S(2)}) collective-permute-start(bf16[32,16,128]{2,1,0:T(8,128)(2,1)S(1)} %get-tuple-element.18.refs_0_.refs_2_), channel_id=1, source_target_pairs={{1,0},{2,1},{3,2},{0,3},{5,4},{6,5},{7,6},{4,7},{9,8},{10,9},{11,1... | collective-permute-start | bytes 393224 | tf_op jit(solution)/shard_map/ppermute | solution.py:252
  29.2 2.7 %collective-permute-done.refs_1_ = bf16[32,16,128]{2,1,0:T(8,128)(2,1)S(1)} collective-permute-done((bf16[32,16,128]{2,1,0:T(8,128)(2,1)S(1)}, bf16[32,16,128]{2,1,0:T(8,128)(2,1)S(1)}, u32[]{:S(2)}, u32[]{:S(2)}) %collective-permute-start) | collective-permute-done | bytes 131104 | tf_op jit(solution)/shard_map/ppermute | solution.py:252
  31.9 2.2 %collective-permute-done.1.refs_2_ = bf16[32,16,128]{2,1,0:T(8,128)(2,1)S(1)} collective-permute-done((bf16[32,16,128]{2,1,0:T(8,128)(2,1)S(1)}, bf16[32,16,128]{2,1,0:T(8,128)(2,1)S(1)}, u32[]{:S(2)}, u32[]{:S(2)}) %collective-permute-start.1) | collective-permute-done | bytes 131104 | tf_op jit(solution)/shard_map/ppermute | solution.py:252
  34.2 4.7 %collective-permute-done.2.refs_3_ = bf16[32,16,128]{2,1,0:T(8,128)(2,1)S(1)} collective-permute-done((bf16[32,16,128]{2,1,0:T(8,128)(2,1)S(1)}, bf16[32,16,128]{2,1,0:T(8,128)(2,1)S(1)}, u32[]{:S(2)}, u32[]{:S(2)}) %collective-permute-start.2) | collective-permute-done | bytes 131104 | tf_op jit(solution)/shard_map/ppermute | solution.py:252
  39.0 2.7 %collective-permute-start.15 = (bf16[32,4096]{1,0:T(8,128)(2,1)S(1)}, bf16[32,4096]{1,0:T(8,128)(2,1)S(1)}, u32[]{:S(2)}, u32[]{:S(2)}) collective-permute-start(bf16[32,4096]{1,0:T(8,128)(2,1)S(1)} %slice.13), channel_id=1, source_target_pairs={{8,0},{16,8},{24,16},{0,24},{9,1},{17,9},{25,17},{1,25},{10,2},{18... | collective-permute-start | bytes 786440 | tf_op jit(solution)/shard_map/ppermute | solution.py:252
  42.8 1.7 %collective-permute-start.5 = (bf16[32,16,128]{2,1,0:T(8,128)(2,1)S(1)}, bf16[32,16,128]{2,1,0:T(8,128)(2,1)S(1)}, u32[]{:S(2)}, u32[]{:S(2)}) collective-permute-start(bf16[32,16,128]{2,1,0:T(8,128)(2,1)S(1)} %shard_map.85.refs_0_), channel_id=1, source_target_pairs={{1,0},{2,1},{3,2},{0,3},{5,4},{6,5},{7,6},{4,7},{9,8},{10,9},{11,1... | collective-permute-start | bytes 393224 | tf_op jit(solution)/shard_map/ppermute | solution.py:252
  44.5 5.6 %collective-permute-start.8 = (bf16[32,16,128]{2,1,0:T(8,128)(2,1)S(1)}, bf16[32,16,128]{2,1,0:T(8,128)(2,1)S(1)}, u32[]{:S(2)}, u32[]{:S(2)}) collective-permute-start(bf16[32,16,128]{2,1,0:T(8,128)(2,1)S(1)} %shard_map.85.refs_0_), channel_id=1, source_target_pairs={{4,0},{0,4},{5,1},{1,5},{6,2},{2,6},{7,3},{3,7},{12,8},{8,12},{13,... | collective-permute-start | bytes 393224 | tf_op jit(solution)/shard_map/ppermute | solution.py:252
  50.1 2.9 %collective-permute-start.10 = (bf16[32,16,128]{2,1,0:T(8,128)(2,1)S(1)}, bf16[32,16,128]{2,1,0:T(8,128)(2,1)S(1)}, u32[]{:S(2)}, u32[]{:S(2)}) collective-permute-start(bf16[32,16,128]{2,1,0:T(8,128)(2,1)S(1)} %collective-permute-done.6.refs_2_), channel_id=1, source_target_pairs={{4,0},{0,4},{5,1},{1,5},{6,2},{2,6},{7,3},{3,7},{12,8},{8,12},{13,... | collective-permute-start | bytes 393224 | tf_op jit(solution)/shard_map/ppermute | solution.py:252
  57.2 2.3 %shard_map.86.dense_ref = bf16[512,4096]{1,0:T(8,128)(2,1)S(1)} custom-call(s32[8,64]{1,0:T(8,128)S(1)} %bitcast.9, s32[64]{0:T(128)S(1)} %copy-done.9, s32[4]{0:T(128)S(1)} %pad_add_fusion.own_ref, bf16[32,16,128]{2,1,0:T(8,128)(2,1)S(1)} %shard_map.85.refs_0_, bf16[32,16,128]{2,1,0:T(8,128)(2,1)S(1)} %collective-permute-done.5.refs_1_, ...), custom_call_target="tpu_custom_call" | custom-call | flops 1024 | bytes 1024 | tf_op jit(solution)/shard_map/pallas_call | solution.py:143
  59.6 4.0 %shard_map.89.refs_2_.refs_0_ = bf16[32,16,512]{2,1,0:T(8,128)(2,1)} custom-call(s32[4]{0:T(128)S(1)} %pad_add_fusion.own_ref, bf16[512,4096]{1,0:T(8,128)(2,1)S(1)} %shard_map.86.dense_ref, bf16[64,4096]{1,0:T(8,128)(2,1)S(1)} %shard_map.87.refs_0_, bf16[64,4096]{1,0:T(8,128)(2,1)S(1)} %get-tuple-element.20.refs_1_, ...), custom_call_target="tpu_custom_call" | custom-call | flops 1024 | bytes 1024 | tf_op jit(solution)/shard_map/pallas_call | solution.py:170
  63.6 4.6 %collective-permute-done.3.refs_0_ = bf16[4,32,16,128]{3,2,1,0:T(8,128)(2,1)S(1)} collective-permute-done((bf16[4,32,16,128]{3,2,1,0:T(8,128)(2,1)S(1)}, bf16[4,32,16,128]{3,2,1,0:T(8,128)(2,1)S(1)}, u32[]{:S(2)}, u32[]{:S(2)}) %collective-permute-start.3) | collective-permute-done | bytes 524320 | tf_op jit(solution)/shard_map/ppermute | solution.py:252
  69.4 4.4 %all-to-all-start.1 = ((bf16[32,16,512]{2,1,0:T(8,128)(2,1)}), bf16[32,16,512]{2,1,0:T(8,128)(2,1)S(1)}, u32[]{:S(2)}, u32[]{:S(2)}) async-start(bf16[32,16,512]{2,1,0:T(8,128)(2,1)} %shard_map.91), calls=%async_computation.1 | async-start | bytes 1048576 | tf_op jit(solution)/shard_map/all_to_all | solution.py:265
  75.2 1.4 %collective-permute-start.22 = (bf16[2,32,16,128]{3,2,1,0:T(8,128)(2,1)S(1)}, bf16[2,32,16,128]{3,2,1,0:T(8,128)(2,1)S(1)}, u32[]{:S(2)}, u32[]{:S(2)}) collective-permute-start(bf16[2,32,16,128]{3,2,1,0:T(8,128)(2,1)S(1)} %slice.15), channel_id=1, source_target_pairs={{8,0},{16,8},{24,16},{0,24},{9,1},{17,9},{25,17},{1,25},{10,2},{18... | collective-permute-start | bytes 786440 | tf_op jit(solution)/shard_map/ppermute | solution.py:252
  76.6 7.4 %collective-permute-done.21.refs_3_ = bf16[2,32,16,128]{3,2,1,0:T(8,128)(2,1)S(1)} collective-permute-done((bf16[2,32,16,128]{3,2,1,0:T(8,128)(2,1)S(1)}, bf16[2,32,16,128]{3,2,1,0:T(8,128)(2,1)S(1)}, u32[]{:S(2)}, u32[]{:S(2)}) %collective-permute-start.21) | collective-permute-done | bytes 262176 | tf_op jit(solution)/shard_map/ppermute | solution.py:252
  84.0 1.8 %collective-permute-done.22.refs_4_ = bf16[2,32,16,128]{3,2,1,0:T(8,128)(2,1)S(1)} collective-permute-done((bf16[2,32,16,128]{3,2,1,0:T(8,128)(2,1)S(1)}, bf16[2,32,16,128]{3,2,1,0:T(8,128)(2,1)S(1)}, u32[]{:S(2)}, u32[]{:S(2)}) %collective-permute-start.22) | collective-permute-done | bytes 262176 | tf_op jit(solution)/shard_map/ppermute | solution.py:252
  85.9 3.3 %all-to-all-done.1.refs_5_ = bf16[32,16,512]{2,1,0:T(8,128)(2,1)S(1)} async-done(((bf16[32,16,512]{2,1,0:T(8,128)(2,1)}), bf16[32,16,512]{2,1,0:T(8,128)(2,1)S(1)}, u32[]{:S(2)}, u32[]{:S(2)}) %all-to-all-start.1) | async-done | bytes 524320 | tf_op jit(solution)/shard_map/all_to_all | solution.py:265
  89.2 3.4 %collective-permute-start.23 = (bf16[4,32,16,128]{3,2,1,0:T(8,128)(2,1)S(1)}, bf16[4,32,16,128]{3,2,1,0:T(8,128)(2,1)S(1)}, u32[]{:S(2)}, u32[]{:S(2)}) collective-permute-start(bf16[4,32,16,128]{3,2,1,0:T(8,128)(2,1)S(1)} %get-tuple-element.24.refs_0_), channel_id=1, source_target_pairs={{4,0},{0,4},{5,1},{1,5},{6,2},{2,6},{7,3},{3,7},{12,8},{8,12},{13,... | collective-permute-start | bytes 1572872 | tf_op jit(solution)/shard_map/ppermute | solution.py:252
  93.6 2.3 %shard_map.93 = (bf16[64,4096]{1,0:T(8,128)(2,1)S(1)}, bf16[64,64,128]{2,1,0:T(8,128)(2,1)S(1)}) custom-call(s32[8,64]{1,0:T(8,128)S(1)} %bitcast.7, s32[64]{0:T(128)S(1)} %copy-done.7, s32[4]{0:T(128)S(1)} %pad_add_fusion.own_ref, bf16[4,32,16,128]{3,2,1,0:T(8,128)(2,1)S(1)} %get-tuple-element.24.refs_0_, ...), custom_call_target="tpu_custom_call" | custom-call | flops 1024 | bytes 1024 | tf_op jit(solution)/shard_map/pallas_call | solution.py:241
  96.4 2.9 %shard_map.94 = bf16[64,4096]{1,0:T(8,128)(2,1)} custom-call(s32[8,64]{1,0:T(8,128)S(1)} %bitcast.8, s32[64]{0:T(128)S(1)} %copy-done.7, s32[4]{0:T(128)S(1)} %pad_add_fusion.own_ref, bf16[4,32,16,128]{3,2,1,0:T(8,128)(2,1)S(1)} %collective-permute-done.23.refs_0_, bf16[4,32,16,128]{3,2,1,0:T(8,128)(2,1)S(1)} %collective-permute-done.24.refs_1_, ...), custom_call_target="tpu_custom_call" | custom-call | flops 1024 | bytes 1024 | tf_op jit(solution)/shard_map/pallas_call | solution.py:241
  (74 shorter events, 13.7 us)
Async XLA Ops:
  2.9 23.1 %all-to-all-start = ((bf16[32,32,128]{2,1,0:T(8,128)(2,1)}), bf16[32,32,128]{2,1,0:T(8,128)(2,1)S(1)}, u32[]{:S(2)}, u32[]{:S(2)}) async-start(bf16[32,32,128]{2,1,0:T(8,128)(2,1)} %shard_map.82), calls=%async_computation | async-start | bytes 524288 | tf_op jit(solution)/shard_map/all_to_all | solution.py:265
  17.2 21.7 %collective-permute-start.12 = (bf16[64,4096]{1,0:T(8,128)(2,1)S(1)}, bf16[64,4096]{1,0:T(8,128)(2,1)S(1)}, u32[]{:S(2)}, u32[]{:S(2)}) collective-permute-start(bf16[64,4096]{1,0:T(8,128)(2,1)S(1)} %shard_map.87.refs_0_), channel_id=1, source_target_pairs={{8,0},{16,8},{24,16},{0,24},{9,1},{17,9},{25,17},{1,25},{10,2},{18... | collective-permute-start | bytes 1572872 | tf_op jit(solution)/shard_map/ppermute | solution.py:252
  19.7 19.2 %collective-permute-start.13 = (bf16[64,4096]{1,0:T(8,128)(2,1)S(1)}, bf16[64,4096]{1,0:T(8,128)(2,1)S(1)}, u32[]{:S(2)}, u32[]{:S(2)}) collective-permute-start(bf16[64,4096]{1,0:T(8,128)(2,1)S(1)} %shard_map.87.refs_0_), channel_id=1, source_target_pairs={{24,0},{0,8},{8,16},{16,24},{25,1},{1,9},{9,17},{17,25},{26,2},{2,... | collective-permute-start | bytes 1572872 | tf_op jit(solution)/shard_map/ppermute | solution.py:252
  19.7 23.1 %collective-permute-start.16 = (bf16[64,4096]{1,0:T(8,128)(2,1)S(1)}, bf16[64,4096]{1,0:T(8,128)(2,1)S(1)}, u32[]{:S(2)}, u32[]{:S(2)}) collective-permute-start(bf16[64,4096]{1,0:T(8,128)(2,1)S(1)} %shard_map.87.refs_0_), channel_id=1, source_target_pairs={{4,0},{0,4},{5,1},{1,5},{6,2},{2,6},{7,3},{3,7},{12,8},{8,12},{13,... | collective-permute-start | bytes 1572872 | tf_op jit(solution)/shard_map/ppermute | solution.py:252
  26.0 5.9 %collective-permute-start = (bf16[32,16,128]{2,1,0:T(8,128)(2,1)S(1)}, bf16[32,16,128]{2,1,0:T(8,128)(2,1)S(1)}, u32[]{:S(2)}, u32[]{:S(2)}) collective-permute-start(bf16[32,16,128]{2,1,0:T(8,128)(2,1)S(1)} %get-tuple-element.18.refs_0_.refs_2_), channel_id=1, source_target_pairs={{1,0},{2,1},{3,2},{0,3},{5,4},{6,5},{7,6},{4,7},{9,8},{10,9},{11,1... | collective-permute-start | bytes 393224 | tf_op jit(solution)/shard_map/ppermute | solution.py:252
  28.8 5.3 %collective-permute-start.1 = (bf16[32,16,128]{2,1,0:T(8,128)(2,1)S(1)}, bf16[32,16,128]{2,1,0:T(8,128)(2,1)S(1)}, u32[]{:S(2)}, u32[]{:S(2)}) collective-permute-start(bf16[32,16,128]{2,1,0:T(8,128)(2,1)S(1)} %get-tuple-element.18.refs_0_.refs_2_), channel_id=1, source_target_pairs={{2,0},{3,1},{0,2},{1,3},{6,4},{7,5},{4,6},{5,7},{10,8},{11,9},{8,1... | collective-permute-start | bytes 393224 | tf_op jit(solution)/shard_map/ppermute | solution.py:252
  31.9 6.9 %collective-permute-start.2 = (bf16[32,16,128]{2,1,0:T(8,128)(2,1)S(1)}, bf16[32,16,128]{2,1,0:T(8,128)(2,1)S(1)}, u32[]{:S(2)}, u32[]{:S(2)}) collective-permute-start(bf16[32,16,128]{2,1,0:T(8,128)(2,1)S(1)} %get-tuple-element.18.refs_0_.refs_2_), channel_id=1, source_target_pairs={{3,0},{0,1},{1,2},{2,3},{7,4},{4,5},{5,6},{6,7},{11,8},{8,9},{9,10... | collective-permute-start | bytes 393224 | tf_op jit(solution)/shard_map/ppermute | solution.py:252
  38.9 5.6 %collective-permute-start.6 = (bf16[32,16,128]{2,1,0:T(8,128)(2,1)S(1)}, bf16[32,16,128]{2,1,0:T(8,128)(2,1)S(1)}, u32[]{:S(2)}, u32[]{:S(2)}) collective-permute-start(bf16[32,16,128]{2,1,0:T(8,128)(2,1)S(1)} %shard_map.85.refs_0_), channel_id=1, source_target_pairs={{2,0},{3,1},{0,2},{1,3},{6,4},{7,5},{4,6},{5,7},{10,8},{11,9},{8,1... | collective-permute-start | bytes 393224 | tf_op jit(solution)/shard_map/ppermute | solution.py:252
  38.9 14.8 %collective-permute-start.14 = (bf16[32,4096]{1,0:T(8,128)(2,1)S(1)}, bf16[32,4096]{1,0:T(8,128)(2,1)S(1)}, u32[]{:S(2)}, u32[]{:S(2)}) collective-permute-start(bf16[32,4096]{1,0:T(8,128)(2,1)S(1)} %slice.12), channel_id=1, source_target_pairs={{24,0},{0,8},{8,16},{16,24},{25,1},{1,9},{9,17},{17,25},{26,2},{2,... | collective-permute-start | bytes 786440 | tf_op jit(solution)/shard_map/ppermute | solution.py:252
  39.0 15.3 %collective-permute-start.15 = (bf16[32,4096]{1,0:T(8,128)(2,1)S(1)}, bf16[32,4096]{1,0:T(8,128)(2,1)S(1)}, u32[]{:S(2)}, u32[]{:S(2)}) collective-permute-start(bf16[32,4096]{1,0:T(8,128)(2,1)S(1)} %slice.13), channel_id=1, source_target_pairs={{8,0},{16,8},{24,16},{0,24},{9,1},{17,9},{25,17},{1,25},{10,2},{18... | collective-permute-start | bytes 786440 | tf_op jit(solution)/shard_map/ppermute | solution.py:252
  41.8 8.3 %collective-permute-start.7 = (bf16[32,16,128]{2,1,0:T(8,128)(2,1)S(1)}, bf16[32,16,128]{2,1,0:T(8,128)(2,1)S(1)}, u32[]{:S(2)}, u32[]{:S(2)}) collective-permute-start(bf16[32,16,128]{2,1,0:T(8,128)(2,1)S(1)} %shard_map.85.refs_0_), channel_id=1, source_target_pairs={{3,0},{0,1},{1,2},{2,3},{7,4},{4,5},{5,6},{6,7},{11,8},{8,9},{9,10... | collective-permute-start | bytes 393224 | tf_op jit(solution)/shard_map/ppermute | solution.py:252
  42.8 10.2 %collective-permute-start.5 = (bf16[32,16,128]{2,1,0:T(8,128)(2,1)S(1)}, bf16[32,16,128]{2,1,0:T(8,128)(2,1)S(1)}, u32[]{:S(2)}, u32[]{:S(2)}) collective-permute-start(bf16[32,16,128]{2,1,0:T(8,128)(2,1)S(1)} %shard_map.85.refs_0_), channel_id=1, source_target_pairs={{1,0},{2,1},{3,2},{0,3},{5,4},{6,5},{7,6},{4,7},{9,8},{10,9},{11,1... | collective-permute-start | bytes 393224 | tf_op jit(solution)/shard_map/ppermute | solution.py:252
  44.5 9.2 %collective-permute-start.8 = (bf16[32,16,128]{2,1,0:T(8,128)(2,1)S(1)}, bf16[32,16,128]{2,1,0:T(8,128)(2,1)S(1)}, u32[]{:S(2)}, u32[]{:S(2)}) collective-permute-start(bf16[32,16,128]{2,1,0:T(8,128)(2,1)S(1)} %shard_map.85.refs_0_), channel_id=1, source_target_pairs={{4,0},{0,4},{5,1},{1,5},{6,2},{2,6},{7,3},{3,7},{12,8},{8,12},{13,... | collective-permute-start | bytes 393224 | tf_op jit(solution)/shard_map/ppermute | solution.py:252
  50.1 4.4 %collective-permute-start.10 = (bf16[32,16,128]{2,1,0:T(8,128)(2,1)S(1)}, bf16[32,16,128]{2,1,0:T(8,128)(2,1)S(1)}, u32[]{:S(2)}, u32[]{:S(2)}) collective-permute-start(bf16[32,16,128]{2,1,0:T(8,128)(2,1)S(1)} %collective-permute-done.6.refs_2_), channel_id=1, source_target_pairs={{4,0},{0,4},{5,1},{1,5},{6,2},{2,6},{7,3},{3,7},{12,8},{8,12},{13,... | collective-permute-start | bytes 393224 | tf_op jit(solution)/shard_map/ppermute | solution.py:252
  53.7 5.9 %collective-permute-start.17 = (bf16[64,4096]{1,0:T(8,128)(2,1)S(1)}, bf16[64,4096]{1,0:T(8,128)(2,1)S(1)}, u32[]{:S(2)}, u32[]{:S(2)}) collective-permute-start(bf16[64,4096]{1,0:T(8,128)(2,1)S(1)} %get-tuple-element.20.refs_1_), channel_id=1, source_target_pairs={{4,0},{0,4},{5,1},{1,5},{6,2},{2,6},{7,3},{3,7},{12,8},{8,12},{13,... | collective-permute-start | bytes 1572872 | tf_op jit(solution)/shard_map/ppermute | solution.py:252
  54.4 5.2 %collective-permute-start.18 = (bf16[64,4096]{1,0:T(8,128)(2,1)S(1)}, bf16[64,4096]{1,0:T(8,128)(2,1)S(1)}, u32[]{:S(2)}, u32[]{:S(2)}) collective-permute-start(bf16[64,4096]{1,0:T(8,128)(2,1)S(1)} %get-tuple-element.21.refs_2_), channel_id=1, source_target_pairs={{4,0},{0,4},{5,1},{1,5},{6,2},{2,6},{7,3},{3,7},{12,8},{8,12},{13,... | collective-permute-start | bytes 1572872 | tf_op jit(solution)/shard_map/ppermute | solution.py:252
  54.8 13.3 %collective-permute-start.3 = (bf16[4,32,16,128]{3,2,1,0:T(8,128)(2,1)S(1)}, bf16[4,32,16,128]{3,2,1,0:T(8,128)(2,1)S(1)}, u32[]{:S(2)}, u32[]{:S(2)}) collective-permute-start(bf16[4,32,16,128]{3,2,1,0:T(8,128)(2,1)S(1)} %shard_map.84.refs_0_), channel_id=1, source_target_pairs={{8,0},{16,8},{24,16},{0,24},{9,1},{17,9},{25,17},{1,25},{10,2},{18... | collective-permute-start | bytes 1572872 | tf_op jit(solution)/shard_map/ppermute | solution.py:252
  55.2 14.1 %collective-permute-start.4 = (bf16[4,32,16,128]{3,2,1,0:T(8,128)(2,1)S(1)}, bf16[4,32,16,128]{3,2,1,0:T(8,128)(2,1)S(1)}, u32[]{:S(2)}, u32[]{:S(2)}) collective-permute-start(bf16[4,32,16,128]{3,2,1,0:T(8,128)(2,1)S(1)} %shard_map.84.refs_0_), channel_id=1, source_target_pairs={{24,0},{0,8},{8,16},{16,24},{25,1},{1,9},{9,17},{17,25},{26,2},{2,... | collective-permute-start | bytes 1572872 | tf_op jit(solution)/shard_map/ppermute | solution.py:252
  69.4 19.8 %all-to-all-start.1 = ((bf16[32,16,512]{2,1,0:T(8,128)(2,1)}), bf16[32,16,512]{2,1,0:T(8,128)(2,1)S(1)}, u32[]{:S(2)}, u32[]{:S(2)}) async-start(bf16[32,16,512]{2,1,0:T(8,128)(2,1)} %shard_map.91), calls=%async_computation.1 | async-start | bytes 1048576 | tf_op jit(solution)/shard_map/all_to_all | solution.py:265
  73.9 10.1 %collective-permute-start.21 = (bf16[2,32,16,128]{3,2,1,0:T(8,128)(2,1)S(1)}, bf16[2,32,16,128]{3,2,1,0:T(8,128)(2,1)S(1)}, u32[]{:S(2)}, u32[]{:S(2)}) collective-permute-start(bf16[2,32,16,128]{3,2,1,0:T(8,128)(2,1)S(1)} %slice.14), channel_id=1, source_target_pairs={{24,0},{0,8},{8,16},{16,24},{25,1},{1,9},{9,17},{17,25},{26,2},{2,... | collective-permute-start | bytes 786440 | tf_op jit(solution)/shard_map/ppermute | solution.py:252
  75.2 10.7 %collective-permute-start.22 = (bf16[2,32,16,128]{3,2,1,0:T(8,128)(2,1)S(1)}, bf16[2,32,16,128]{3,2,1,0:T(8,128)(2,1)S(1)}, u32[]{:S(2)}, u32[]{:S(2)}) collective-permute-start(bf16[2,32,16,128]{3,2,1,0:T(8,128)(2,1)S(1)} %slice.15), channel_id=1, source_target_pairs={{8,0},{16,8},{24,16},{0,24},{9,1},{17,9},{25,17},{1,25},{10,2},{18... | collective-permute-start | bytes 786440 | tf_op jit(solution)/shard_map/ppermute | solution.py:252
  89.2 7.2 %collective-permute-start.23 = (bf16[4,32,16,128]{3,2,1,0:T(8,128)(2,1)S(1)}, bf16[4,32,16,128]{3,2,1,0:T(8,128)(2,1)S(1)}, u32[]{:S(2)}, u32[]{:S(2)}) collective-permute-start(bf16[4,32,16,128]{3,2,1,0:T(8,128)(2,1)S(1)} %get-tuple-element.24.refs_0_), channel_id=1, source_target_pairs={{4,0},{0,4},{5,1},{1,5},{6,2},{2,6},{7,3},{3,7},{12,8},{8,12},{13,... | collective-permute-start | bytes 1572872 | tf_op jit(solution)/shard_map/ppermute | solution.py:252
  92.6 3.8 %collective-permute-start.24 = (bf16[4,32,16,128]{3,2,1,0:T(8,128)(2,1)S(1)}, bf16[4,32,16,128]{3,2,1,0:T(8,128)(2,1)S(1)}, u32[]{:S(2)}, u32[]{:S(2)}) collective-permute-start(bf16[4,32,16,128]{3,2,1,0:T(8,128)(2,1)S(1)} %get-tuple-element.25.refs_1_), channel_id=1, source_target_pairs={{4,0},{0,4},{5,1},{1,5},{6,2},{2,6},{7,3},{3,7},{12,8},{8,12},{13,... | collective-permute-start | bytes 1572872 | tf_op jit(solution)/shard_map/ppermute | solution.py:252
  92.6 3.8 %collective-permute-start.25 = (bf16[4,32,16,128]{3,2,1,0:T(8,128)(2,1)S(1)}, bf16[4,32,16,128]{3,2,1,0:T(8,128)(2,1)S(1)}, u32[]{:S(2)}, u32[]{:S(2)}) collective-permute-start(bf16[4,32,16,128]{3,2,1,0:T(8,128)(2,1)S(1)} %get-tuple-element.26.refs_2_), channel_id=1, source_target_pairs={{4,0},{0,4},{5,1},{1,5},{6,2},{2,6},{7,3},{3,7},{12,8},{8,12},{13,... | collective-permute-start | bytes 1572872 | tf_op jit(solution)/shard_map/ppermute | solution.py:252
  (16 other events, 209.3 us)
